TPU v7x, 128 devices: a whole 4x4x4 slice. The times are simulated.
128 devices in a mesh: px: 16 (over z, x), py: 8 (over y, core).
Axes of the slice: x: 4, y: 4, z: 4, core: 2. Of those that a mesh axis runs over, the one named last changes fastest.
Arguments:
- state_old: float32 [5, 64, 131072], P(None, None, ('px', 'py'))
- level_old: int32 [131072], P(('px', 'py')), may hold values 0 or 1
- morton_old: int32 [131072], P(('px', 'py')), may hold values from -1 to 65535, as said below
- neighbours: int32 [6, 65536], P(None, ('px', 'py')), may hold values from 0 to 65535, as said below
Outputs:
- new_state: float32 [5, 64, 65536], P(None, None, ('px', 'py'))
- rate: float32 [5, 64, 65536], P(None, None, ('px', 'py'))
Inputs may be any that keep to these rules, and one draw needn't show every extreme that they name: `morton_old`: every element 0 to 65535 stands in exactly one slot; the other slots hold -1. The element of old device d goes to new device d, d + 1 or d - 1 along the curve, which closes (device 0 follows the last). Every device sends 1 to 256 elements to the next device, always the lowest-ranked of that device's elements, and 1 to 255 to the previous one, always the highest-ranked of that device's elements; both bounds are reached on some device. `neighbours`: every neighbour of a device's element lies on that device or on a device 1, 2, 3 or 4 steps before or after it along the curve (the curve closes: device 0 follows the last). For each device, exactly 128 of its faces have their neighbour on the next device and exactly 128 on the previous one, and at most 128 on each device 2 to 4 steps away, reached on some device. A face whose neighbour is on the same device never has the element itself as neighbour.
All inputs are finite; a program needn't handle non-finite values. No bound on the sum of `level_old` on one device may be relied on, other than what follows from the above.
Results may differ from a plain program's by a relative error of at most 0.0003.
Values sent between devices are 32-bit elements; how exact they have to be, the bound alone decides.
No kernel may reach another device: no remote copies, remote signals or barrier semaphores. Data moves between devices by JAX's collectives and lax.ppermute only.
A program may use at most 128 MiB of HBM per device.

v0:
```python
import jax
import jax.numpy as jnp
import numpy as np
from jax import lax
from jax.experimental import pallas as pl
from jax.experimental.pallas import tpu as pltpu
from jax.sharding import PartitionSpec as P

FIELDS = 5
DOFS = 64
ROWS = FIELDS * DOFS
NEW_DEV = 512
HALF = NEW_DEV // 2
OLD_CAP = 1024
CAP = 128
TRACE_ROWS = FIELDS * 16
MOVED_ROWS = ROWS + 8
BLOCKS = NEW_DEV // 128

HEAT = 1.4
SPEED = 4.0
DT = 0.0002
AXES = ("px", "py")
F32 = jnp.float32
BF16 = jnp.bfloat16
I32 = jnp.int32

STEPS = (2, 3, 4, 1, -1, -2, -3, -4)


def derivative_table():
    points = np.array([-1.0, -1.0 / np.sqrt(5.0), 1.0 / np.sqrt(5.0), 1.0])
    weights = np.array(
        [1.0 / np.prod([points[c] - points[o] for o in range(4) if o != c]) for c in range(4)]
    )
    table = np.zeros((4, 4))
    for r in range(4):
        for c in range(4):
            if r != c:
                table[r, c] = weights[c] / weights[r] / (points[r] - points[c])
        table[r, r] = -np.sum(table[r])
    return table


def stacked_table():
    d = derivative_table().astype(np.float32).astype(np.float64)
    one = np.eye(4)
    full = np.concatenate(
        [
            np.kron(np.kron(d, one), one),
            np.kron(np.kron(one, d), one),
            np.kron(np.kron(one, one), d),
        ],
        axis=1,
    ).astype(np.float32)
    high = full.astype(jnp.bfloat16)
    low = (full - high.astype(np.float32)).astype(jnp.bfloat16)
    return np.concatenate([high, low], axis=0)


def split(x):
    high = x.astype(BF16)
    low = (x - high.astype(F32)).astype(BF16)
    return high, low


def dot(a, b):
    return lax.dot_general(a, b, (((1,), (0,)), ((), ())), preferred_element_type=F32)


def dot_nt(a, b):
    return lax.dot_general(a, b, (((1,), (1,)), ((), ())), preferred_element_type=F32)


def one_hot_rows(size, row):
    spots = lax.broadcasted_iota(I32, (size, row.shape[1]), 0)
    return jnp.where(spots == row, 1.0, 0.0).astype(BF16)


def relay_slots(me, morton):
    occupied = morton >= 0
    owner = morton >> 9
    slot = morton & (NEW_DEV - 1)
    gap = (owner - me) & 127
    even = (me & 1) == 0
    to_next = occupied & (gap == 1)
    to_prior = occupied & (gap == 127)
    home = jnp.where(occupied & (gap == 0), slot, -1)
    ahead = jnp.where(to_next, slot, -1)
    behind = jnp.where(to_prior, slot - HALF, -1)
    sib = jnp.where(even, ahead, behind)
    far = jnp.where(even, behind, ahead)
    return sib, far, home


def stacked_rows(state, level):
    high, low = split(state)
    lev = jnp.broadcast_to(level.astype(F32), (16, OLD_CAP)).astype(BF16)
    return jnp.concatenate([high, low, lev], axis=0)


def store_moved(ref, got):
    ref[0:ROWS, :] = got[0:ROWS] + got[ROWS : 2 * ROWS]
    ref[ROWS : ROWS + 8, :] = got[2 * ROWS : 2 * ROWS + 8]


def pack_kernel(me_ref, state_ref, level_ref, morton_ref, far_ref, sib_ref):
    sib, far, _ = relay_slots(me_ref[0], morton_ref[...])
    lhs = stacked_rows(state_ref[...], level_ref[...])
    store_moved(far_ref, dot_nt(lhs, one_hot_rows(HALF, far)))
    store_moved(sib_ref, dot_nt(lhs, one_hot_rows(HALF, sib)))


def home_kernel(me_ref, state_ref, level_ref, morton_ref, home_ref):
    _, _, home = relay_slots(me_ref[0], morton_ref[...])
    lhs = stacked_rows(state_ref[...], level_ref[...])
    got = dot_nt(lhs, one_hot_rows(NEW_DEV, home))
    for c in range(BLOCKS):
        store_moved(home_ref.at[c], got[:, 128 * c : 128 * c + 128])


def request_kernel(me_ref, links_ref, ask_ref, near_ref, far_ref):
    me = me_ref[0]
    links = links_ref[...]
    owner = links >> 9
    slot = links & (NEW_DEV - 1)
    gap = ((owner - me + 192) & 127) - 64
    gap = jnp.where((me & 1) == 0, gap, -gap)
    near_ref[...] = jnp.where(gap == 0, slot, -1)
    b = lax.broadcasted_iota(I32, (8, NEW_DEV), 0)
    step_of = jnp.where(b < 3, b + 2, jnp.where(b == 3, 1, 3 - b))
    masks = [jnp.where(gap[f : f + 1, :] == step_of, 1.0, 0.0) for f in range(6)]
    k = lax.broadcasted_iota(I32, (NEW_DEV, NEW_DEV), 0)
    j = lax.broadcasted_iota(I32, (NEW_DEV, NEW_DEV), 1)
    upper = jnp.where(k <= j, 1.0, 0.0).astype(BF16)
    counts = dot(jnp.concatenate(masks, axis=0).astype(BF16), upper)
    offset = jnp.full((8, 1), -1.0, F32)
    bf = b.astype(F32)
    total = jnp.zeros((16, CAP), F32)
    for f in range(6):
        run = counts[8 * f : 8 * f + 8, :]
        here = gap[f : f + 1, :] != 0
        rank = jnp.sum(masks[f] * (run + offset), axis=0, keepdims=True)
        bucket = jnp.sum(masks[f] * bf, axis=0, keepdims=True)
        offset = offset + run[:, NEW_DEV - 1 : NEW_DEV]
        rank = jnp.where(here, rank.astype(I32), -1)
        far_ref[f : f + 1, :] = jnp.where(here, bucket.astype(I32) * CAP + rank, -1)
        s = slot[f : f + 1, :]
        low = (s & 255).astype(F32)
        high = ((s >> 8) + 2 * (f ^ 1)).astype(F32)
        lhs = jnp.concatenate([masks[f] * low, masks[f] * high], axis=0).astype(BF16)
        total = total + dot_nt(lhs, one_hot_rows(CAP, rank))
    ask_ref[...] = total[0:8].astype(I32) + 256 * total[8:16].astype(I32)


def lower_half(shape):
    return lax.broadcasted_iota(I32, shape, 0) < 4


def trace(ref, c, v, f):
    a, s = f // 2, f % 2
    at = v * DOFS
    if a == 0:
        return ref[c, at + 48 * s : at + 48 * s + 16, :]
    if a == 1:
        out = []
        for h in range(2):
            r = at + 32 * h + 8 * s
            x = ref[c, r : r + 8, :]
            y = ref[c, r + 16 : r + 24, :]
            low = lower_half(x.shape)
            if s == 0:
                out.append(jnp.where(low, x, pltpu.roll(y, 4, 0)))
            else:
                out.append(jnp.where(low, pltpu.roll(x, 4, 0), y))
        return jnp.concatenate(out, axis=0)
    return ref[c, pl.ds(at + 3 * s, 16, stride=4), :]


def add_on_face(ref, c, v, f, x):
    a, s = f // 2, f % 2
    at = v * DOFS
    if a == 0:
        ref[c, at + 48 * s : at + 48 * s + 16, :] += x
    elif a == 1:
        for h in range(2):
            y = x[8 * h : 8 * h + 8, :]
            low = lower_half(y.shape)
            keep = low if s == 0 else ~low
            turned = pltpu.roll(y, 4, 0)
            first, second = (y, turned) if s == 0 else (turned, y)
            r = at + 32 * h + 8 * s
            ref[c, r : r + 8, :] += jnp.where(keep, first, 0.0)
            ref[c, r + 16 : r + 24, :] += jnp.where(keep, second, 0.0)
    else:
        spot = (c, pl.ds(at + 3 * s, 16, stride=4), slice(None))
        ref[spot] = ref[spot] + x


def wide(ref, rows):
    return jnp.concatenate([ref[c, 0:rows, :] for c in range(ref.shape[0])], axis=1)


def pressure_of(w, u):
    return (HEAT - 1.0) * (w[4] - 0.5 * (w[1] * u[0] + w[2] * u[1] + w[3] * u[2]))


def axis_flux(w, u, p, a):
    un = u[a]
    out = [w[1 + a]]
    for c in range(3):
        m = w[1 + c] * un
        out.append(m + p if c == a else m)
    out.append((w[4] + p) * un)
    return out


def side_term(w, a, sign):
    u = [w[1 + c] / w[0] for c in range(3)]
    p = pressure_of(w, u)
    flux = axis_flux(w, u, p, a)
    return [(sign * flux[v]) - SPEED * w[v] for v in range(FIELDS)]


def reply(fields, ask_ref, got_ref, own_ref, swap_ref):
    ask = ask_ref[...]
    code = jnp.concatenate([ask[t : t + 1, :] for t in range(8)], axis=1)
    hot = one_hot_rows(NEW_DEV, code & (NEW_DEV - 1))
    high, low = split(fields)
    both = dot(jnp.concatenate([high, low], axis=0), hot)
    for t in range(8):
        spot = slice(CAP * t, CAP * t + CAP)
        got_ref[t] = both[0:ROWS, spot] + both[ROWS:, spot]
    for t in range(8):
        face = ask[t : t + 1, :] >> 9
        for v in range(FIELDS):
            x = trace(got_ref, t, v, 0)
            for f in range(1, 6):
                x = jnp.where(face == f, trace(got_ref, t, v, f), x)
            if t < 3:
                own_ref[t, 16 * v : 16 * v + 16, :] = x
            else:
                swap_ref[t - 3, 16 * v : 16 * v + 16, :] = x


def first_kernel(me_ref, home_ref, far_ref, sib_ref, ask_ref, start_ref, own_ref, swap_ref, got_ref):
    even = (me_ref[0] & 1) == 0
    for c in range(2):
        spot = slice(128 * c, 128 * c + 128)
        sib = sib_ref[:, spot]
        far = far_ref[:, spot]
        start_ref[c] = home_ref[c] + jnp.where(even, far, sib)
        start_ref[c + 2] = home_ref[c + 2] + jnp.where(even, sib, far)
    reply(wide(start_ref, ROWS), ask_ref, got_ref, own_ref, swap_ref)


def near_kernel(table_ref, fields_ref, near_ref, part_ref, high_ref, low_ref):
    for c in range(BLOCKS):
        spot = slice(128 * c, 128 * c + 128)
        w = [fields_ref[c, DOFS * v : DOFS * v + DOFS, :] for v in range(FIELDS)]
        u = [w[1 + i] / w[0] for i in range(3)]
        p = pressure_of(w, u)
        for a in range(3):
            flux = axis_flux(w, u, p, a)
            for v in range(FIELDS):
                high, low = split(flux[v])
                high_ref[v, DOFS * a : DOFS * a + DOFS, spot] = high
                low_ref[v, DOFS * a : DOFS * a + DOFS, spot] = low
    table = table_ref[...]
    for v in range(FIELDS):
        x = dot(table, high_ref[v])
        x = x[0:DOFS] + x[DOFS:] + dot(table[0:DOFS], low_ref[v])
        for c in range(BLOCKS):
            part_ref[c, DOFS * v : DOFS * v + DOFS, :] = x[:, 128 * c : 128 * c + 128]
    for f in range(6):
        a, sign = f // 2, 1.0 if f % 2 else -1.0
        mine = near_ref[f : f + 1, :]
        hot = one_hot_rows(NEW_DEV, mine)
        across = jnp.concatenate(
            [
                jnp.concatenate([trace(fields_ref, c, v, f ^ 1) for v in range(FIELDS)], axis=0)
                for c in range(BLOCKS)
            ],
            axis=1,
        )
        high, low = split(across)
        both = dot(jnp.concatenate([high, low], axis=0), hot)
        for c in range(BLOCKS):
            spot = slice(128 * c, 128 * c + 128)
            outer = both[0:TRACE_ROWS, spot] + both[TRACE_ROWS:, spot]
            there = mine[:, spot] >= 0
            plus = side_term(outer_fields(outer, there), a, sign)
            minus = side_term([trace(fields_ref, c, v, f) for v in range(FIELDS)], a, sign)
            for v in range(FIELDS):
                add_on_face(part_ref, c, v, f, 3.0 * (jnp.where(there, plus[v], 0.0) - minus[v]))


def outer_fields(outer, there):
    w = [outer[16 * v : 16 * v + 16] for v in range(FIELDS)]
    w[0] = jnp.where(there, w[0], 1.0)
    return w


def add_far(part_ref, far_ref, ghosts, sum_ref, lhs_ref):
    for t in range(8):
        high, low = split(ghosts[t])
        lhs_ref[0:TRACE_ROWS, CAP * t : CAP * t + CAP] = high
        lhs_ref[TRACE_ROWS:, CAP * t : CAP * t + CAP] = low
    sum_ref[...] = part_ref[...]
    lhs = lhs_ref[...]
    for f in range(6):
        a, sign = f // 2, 1.0 if f % 2 else -1.0
        place = far_ref[f : f + 1, :]
        both = dot(lhs, one_hot_rows(8 * CAP, place))
        for c in range(BLOCKS):
            spot = slice(128 * c, 128 * c + 128)
            outer = both[0:TRACE_ROWS, spot] + both[TRACE_ROWS:, spot]
            there = place[:, spot] >= 0
            plus = side_term(outer_fields(outer, there), a, sign)
            for v in range(FIELDS):
                add_on_face(sum_ref, c, v, f, 3.0 * jnp.where(there, plus[v], 0.0))


def metric_of(start_ref, c):
    return jnp.where(start_ref[c, ROWS : ROWS + 1, :] > 0.5, 2.0, 1.0)


def ghosts_of(a_ref, b_ref, swap_ref, post_ref):
    return [post_ref[1], post_ref[0], post_ref[2], swap_ref[0], a_ref[2], a_ref[0], b_ref[1], b_ref[0]]


def second_kernel(start_ref, part_ref, far_ref, ask_ref, a_ref, b_ref, swap_ref, post_ref,
                  section_ref, own_ref, out_ref, sum_ref, lhs_ref, got_ref):
    add_far(part_ref, far_ref, ghosts_of(a_ref, b_ref, swap_ref, post_ref), sum_ref, lhs_ref)
    for c in range(BLOCKS):
        section_ref[c] = start_ref[c, 0:ROWS, :] - (DT * metric_of(start_ref, c)) * sum_ref[c]
    reply(wide(section_ref, ROWS), ask_ref, got_ref, own_ref, out_ref)


def last_kernel(start_ref, section_ref, part_ref, far_ref, a_ref, b_ref, swap_ref, post_ref,
                state_ref, rate_ref, sum_ref, lhs_ref):
    add_far(part_ref, far_ref, ghosts_of(a_ref, b_ref, swap_ref, post_ref), sum_ref, lhs_ref)
    for c in range(BLOCKS):
        spot = slice(128 * c, 128 * c + 128)
        rate = -metric_of(start_ref, c) * sum_ref[c]
        rate_ref[:, spot] = rate
        state_ref[:, spot] = 0.5 * start_ref[c, 0:ROWS, :] + 0.5 * (section_ref[c] + DT * rate)


VM = pl.BlockSpec(memory_space=pltpu.VMEM)
SM = pl.BlockSpec(memory_space=pltpu.SMEM)


def call(kernel, outs, args, scalars=0, scratch=(), flops=0):
    return pl.pallas_call(
        kernel,
        out_shape=[jax.ShapeDtypeStruct(s, d) for s, d in outs],
        in_specs=[SM] * scalars + [VM] * (len(args) - scalars),
        out_specs=[VM] * len(outs),
        scratch_shapes=[pltpu.VMEM(s, d) for s, d in scratch],
        compiler_params=pltpu.CompilerParams(vmem_limit_bytes=40 * 2**20),
        cost_estimate=pl.CostEstimate(flops=flops, bytes_accessed=2**20, transcendentals=0),
    )(*args)


def swap_cores(x):
    n = lax.axis_size(AXES)
    return lax.ppermute(x, AXES, [(i, i ^ 1) for i in range(n)])


def swap_chips(x):
    n = lax.axis_size(AXES)
    return lax.ppermute(x, AXES, [(i, (i + (1 if i % 2 else -1)) % n) for i in range(n)])


def outward(x, by):
    n = lax.axis_size(AXES)
    return lax.ppermute(x, AXES, [(i, (i + (by if i % 2 == 0 else -by)) % n) for i in range(n)])


def exchange(own, swap):
    got = swap_cores(swap)
    b = outward(jnp.concatenate([own[2:3], got[3:5]], axis=0), 4)
    a = outward(jnp.concatenate([own[0:2], got[1:3]], axis=0), 2)
    post = swap_cores(jnp.concatenate([a[1:2], a[3:4], b[2:3]], axis=0))
    return a, b, got, post


def body(state_old, level_old, morton_old, neighbours):
    me = lax.axis_index(AXES).astype(I32).reshape(1)
    state = state_old.reshape(ROWS, OLD_CAP)
    level = level_old.reshape(1, OLD_CAP)
    morton = morton_old.reshape(1, OLD_CAP)

    ask, near, far = call(
        request_kernel,
        [((8, CAP), I32), ((6, NEW_DEV), I32), ((6, NEW_DEV), I32)],
        (me, neighbours),
        1,
    )
    ask = ask.reshape(8, 1, CAP)
    asked = jnp.concatenate(list(g for g in ghosts_of(*exchange(ask[0:3], ask[3:8]))), axis=0)

    to_far, to_sib = call(
        pack_kernel, [((MOVED_ROWS, HALF), F32)] * 2, (me, state, level, morton), 1
    )
    from_far = swap_chips(to_far)
    from_sib = swap_cores(to_sib)
    (home,) = call(home_kernel, [((BLOCKS, MOVED_ROWS, 128), F32)], (me, state, level, morton), 1)

    chunks = [((3, TRACE_ROWS, CAP), F32), ((5, TRACE_ROWS, CAP), F32)]
    got_scratch = ((8, ROWS, CAP), F32)
    sum_scratch = ((BLOCKS, ROWS, 128), F32)
    lhs_scratch = ((2 * TRACE_ROWS, 8 * CAP), BF16)
    table = jnp.asarray(stacked_table())

    def near_part(fields):
        return call(
            near_kernel,
            [((BLOCKS, ROWS, 128), F32)],
            (table, fields, near),
            0,
            [((FIELDS, 3 * DOFS, NEW_DEV), BF16)] * 2,
            flops=10**9,
        )[0]

    start, own, swap = call(
        first_kernel,
        [((BLOCKS, MOVED_ROWS, 128), F32)] + chunks,
        (me, home, from_far, from_sib, asked),
        1,
        [got_scratch],
    )
    came = exchange(own, swap)
    part = near_part(start)
    section, own, swap = call(
        second_kernel,
        [((BLOCKS, ROWS, 128), F32)] + chunks,
        (start, part, far, asked) + came,
        0,
        [sum_scratch, lhs_scratch, got_scratch],
    )
    came = exchange(own, swap)
    part = near_part(section)
    new_state, rate = call(
        last_kernel,
        [((ROWS, NEW_DEV), F32)] * 2,
        (start, section, part, far) + came,
        0,
        [sum_scratch, lhs_scratch],
    )
    shape = (FIELDS, DOFS, NEW_DEV)
    return new_state.reshape(shape), rate.reshape(shape)


def solution(mesh):
    wide = P(None, None, AXES)
    return jax.shard_map(
        body,
        mesh=mesh,
        in_specs=(wide, P(AXES), P(AXES), P(None, AXES)),
        out_specs=(wide, wide),
        check_vma=False,
    )
```

profile of v0, /device:TPU:1, one launch (start us, length us, event | category | flops | bytes accessed | tf_op | source)
XLA Modules:
  0.0 67.1 jit_solution(5528971592616243725)
XLA Ops:
  0.6 0.7 %copy-done.3 = s32[6,512]{1,0:T(8,128)S(1)} copy-done((s32[6,512]{1,0:T(8,128)S(1)}, s32[6,512]{1,0:T(8,128)}, u32[]{:S(2)}) %copy-start.3) | copy-done | bytes 12312
  1.4 0.7 %shard_map.70 = (s32[8,128]{1,0:T(8,128)S(1)}, s32[6,512]{1,0:T(8,128)S(1)}, s32[6,512]{1,0:T(8,128)S(1)}) custom-call(s32[1]{0:T(128)} %bitcast.me_ref, s32[6,512]{1,0:T(8,128)S(1)} %copy-done.3), custom_call_target="tpu_custom_call" | custom-call | bytes 1048576 | tf_op jit(solution)/shard_map/pallas_call | solution.py:355
  2.1 1.5 %collective-permute-start.2 = (s32[5,1,128]{2,0,1:T(8,128)S(1)}, s32[5,1,128]{2,0,1:T(8,128)S(1)}, u32[]{:S(2)}, u32[]{:S(2)}) collective-permute-start(s32[5,1,128]{2,0,1:T(8,128)S(1)} %slice_bitcast_fusion), channel_id=1, source_target_pairs={{0,1},{1,0},{2,3},{3,2},{4,5},{5,4},{6,7},{7,6},{8,9},{9,8},{10,11... | collective-permute-start | bytes 7688 | tf_op jit(solution)/shard_map/ppermute | solution.py:368
  3.5 1.3 %copy-done = f32[5,64,1024]{2,1,0:T(8,128)S(1)} copy-done((f32[5,64,1024]{2,1,0:T(8,128)S(1)}, f32[5,64,1024]{2,1,0:T(8,128)}, u32[]{:S(2)}) %copy-start) | copy-done | bytes 1310744
  4.9 0.7 %copy-done.1 = s32[1024]{0:T(1024)S(1)} copy-done((s32[1024]{0:T(1024)S(1)}, s32[1024]{0:T(1024)}, u32[]{:S(2)}) %copy-start.1) | copy-done | bytes 4120
  5.5 0.7 %copy-done.2 = s32[1024]{0:T(1024)S(1)} copy-done((s32[1024]{0:T(1024)S(1)}, s32[1024]{0:T(1024)}, u32[]{:S(2)}) %copy-start.2) | copy-done | bytes 4120
  6.2 0.9 %shard_map.69 = (f32[328,256]{1,0:T(8,128)S(1)}, f32[328,256]{1,0:T(8,128)S(1)}) custom-call(s32[1]{0:T(128)} %bitcast.me_ref, f32[320,1024]{1,0:T(8,128)S(1)} %bitcast.30, s32[1,1024]{1,0:T(1,128)S(1)} %bitcast.32, s32[1,1024]{1,0:T(1,128)S(1)} %bitcast.34), custom_call_target="tpu_custom_call" | custom-call | bytes 1048576 | tf_op jit(solution)/shard_map/pallas_call | solution.py:355
  7.1 1.4 %collective-permute-start = (f32[328,256]{1,0:T(8,128)S(1)}, f32[328,256]{1,0:T(8,128)S(1)}, u32[]{:S(2)}, u32[]{:S(2)}) collective-permute-start(f32[328,256]{1,0:T(8,128)S(1)} %get-tuple-element.15), channel_id=1, source_target_pairs={{0,127},{1,2},{2,1},{3,4},{4,3},{5,6},{6,5},{7,8},{8,7},{9,10},{10... | collective-permute-start | bytes 1007624 | tf_op jit(solution)/shard_map/ppermute | solution.py:373
  8.5 7.6 %collective-permute-start.1 = (f32[328,256]{1,0:T(8,128)S(1)}, f32[328,256]{1,0:T(8,128)S(1)}, u32[]{:S(2)}, u32[]{:S(2)}) collective-permute-start(f32[328,256]{1,0:T(8,128)S(1)} %get-tuple-element.16), channel_id=1, source_target_pairs={{0,1},{1,0},{2,3},{3,2},{4,5},{5,4},{6,7},{7,6},{8,9},{9,8},{10,11... | collective-permute-start | bytes 1007624 | tf_op jit(solution)/shard_map/ppermute | solution.py:368
  16.1 0.9 %shard_map.68.home_ref = f32[4,328,128]{2,1,0:T(8,128)S(1)} custom-call(s32[1]{0:T(128)} %bitcast.me_ref, f32[320,1024]{1,0:T(8,128)S(1)} %bitcast.31, s32[1,1024]{1,0:T(1,128)S(1)} %bitcast.33, s32[1,1024]{1,0:T(1,128)S(1)} %bitcast.35), custom_call_target="tpu_custom_call" | custom-call | bytes 1048576 | tf_op jit(solution)/shard_map/pallas_call | solution.py:355
  17.0 0.8 %collective-permute-start.4 = (s32[3,1,128]{2,0,1:T(4,128)S(1)}, s32[3,1,128]{2,0,1:T(4,128)S(1)}, u32[]{:S(2)}, u32[]{:S(2)}) collective-permute-start(s32[3,1,128]{2,0,1:T(4,128)S(1)} %pad_add_fusion.1), channel_id=1, source_target_pairs={{0,4},{1,125},{2,6},{3,127},{4,8},{5,1},{6,10},{7,3},{8,12},{9,5},... | collective-permute-start | bytes 4616 | tf_op jit(solution)/shard_map/ppermute | solution.py:378
  17.8 1.1 %collective-permute-start.3 = (s32[4,1,128]{2,0,1:T(4,128)S(1)}, s32[4,1,128]{2,0,1:T(4,128)S(1)}, u32[]{:S(2)}, u32[]{:S(2)}) collective-permute-start(s32[4,1,128]{2,0,1:T(4,128)S(1)} %pad_add_fusion), channel_id=1, source_target_pairs={{0,2},{1,127},{2,4},{3,1},{4,6},{5,3},{6,8},{7,5},{8,10},{9,7},{10... | collective-permute-start | bytes 6152 | tf_op jit(solution)/shard_map/ppermute | solution.py:378
  18.9 2.2 %collective-permute-done.4 = s32[3,1,128]{2,0,1:T(4,128)S(1)} collective-permute-done((s32[3,1,128]{2,0,1:T(4,128)S(1)}, s32[3,1,128]{2,0,1:T(4,128)S(1)}, u32[]{:S(2)}, u32[]{:S(2)}) %collective-permute-start.4) | collective-permute-done | bytes 1568 | tf_op jit(solution)/shard_map/ppermute | solution.py:378
  21.1 5.4 %collective-permute-start.5 = (s32[3,1,128]{2,0,1:T(4,128)S(1)}, s32[3,1,128]{2,0,1:T(4,128)S(1)}, u32[]{:S(2)}, u32[]{:S(2)}) collective-permute-start(s32[3,1,128]{2,0,1:T(4,128)S(1)} %pad_add_fusion.2), channel_id=1, source_target_pairs={{0,1},{1,0},{2,3},{3,2},{4,5},{5,4},{6,7},{7,6},{8,9},{9,8},{10,11... | collective-permute-start | bytes 4616 | tf_op jit(solution)/shard_map/ppermute | solution.py:368
  26.5 0.8 %collective-permute-done.5 = s32[3,1,128]{2,0,1:T(4,128)S(1)} collective-permute-done((s32[3,1,128]{2,0,1:T(4,128)S(1)}, s32[3,1,128]{2,0,1:T(4,128)S(1)}, u32[]{:S(2)}, u32[]{:S(2)}) %collective-permute-start.5) | collective-permute-done | bytes 1568 | tf_op jit(solution)/shard_map/ppermute | solution.py:368
  27.4 1.0 %shard_map.71 = (f32[4,328,128]{2,1,0:T(8,128)S(1)}, f32[3,80,128]{2,1,0:T(8,128)S(1)}, f32[5,80,128]{2,1,0:T(8,128)S(1)}) custom-call(s32[1]{0:T(128)} %bitcast.me_ref, f32[4,328,128]{2,1,0:T(8,128)S(1)} %shard_map.68.home_ref, f32[328,256]{1,0:T(8,128)S(1)} %collective-permute-done.far_ref, f32[328,256]{1,0:T(8,128)S(1)} %collective-permute-done.1.sib_ref, ...), custom_call_target="tpu_custom_call" | custom-call | bytes 1048576 | tf_op jit(solution)/shard_map/pallas_call | solution.py:355
  28.4 0.4 collective-permute-start.6
  28.8 1.1 %collective-permute-done.6.swap_ref = f32[5,80,128]{2,1,0:T(8,128)S(1)} collective-permute-done((f32[5,80,128]{2,1,0:T(8,128)S(1)}, f32[5,80,128]{2,1,0:T(8,128)S(1)}, u32[]{:S(2)}, u32[]{:S(2)}) %collective-permute-start.6) | collective-permute-done | bytes 204832 | tf_op jit(solution)/shard_map/ppermute | solution.py:368
  30.0 0.8 %collective-permute-start.7 = (f32[4,80,128]{2,1,0:T(8,128)S(1)}, f32[4,80,128]{2,1,0:T(8,128)S(1)}, u32[]{:S(2)}, u32[]{:S(2)}) collective-permute-start(f32[4,80,128]{2,1,0:T(8,128)S(1)} %pad_maximum_fusion), channel_id=1, source_target_pairs={{0,2},{1,127},{2,4},{3,1},{4,6},{5,3},{6,8},{7,5},{8,10},{9,7},{10... | collective-permute-start | bytes 491528 | tf_op jit(solution)/shard_map/ppermute | solution.py:378
  30.8 1.1 %collective-permute-start.8 = (f32[3,80,128]{2,1,0:T(8,128)S(1)}, f32[3,80,128]{2,1,0:T(8,128)S(1)}, u32[]{:S(2)}, u32[]{:S(2)}) collective-permute-start(f32[3,80,128]{2,1,0:T(8,128)S(1)} %pad_maximum_fusion.2), channel_id=1, source_target_pairs={{0,4},{1,125},{2,6},{3,127},{4,8},{5,1},{6,10},{7,3},{8,12},{9,5},... | collective-permute-start | bytes 368648 | tf_op jit(solution)/shard_map/ppermute | solution.py:378
  31.9 5.3 %collective-permute-done.8.b_ref = f32[3,80,128]{2,1,0:T(8,128)S(1)} collective-permute-done((f32[3,80,128]{2,1,0:T(8,128)S(1)}, f32[3,80,128]{2,1,0:T(8,128)S(1)}, u32[]{:S(2)}, u32[]{:S(2)}) %collective-permute-start.8) | collective-permute-done | bytes 122912 | tf_op jit(solution)/shard_map/ppermute | solution.py:378
  37.2 5.3 %collective-permute-start.9 = (f32[3,80,128]{2,1,0:T(8,128)S(1)}, f32[3,80,128]{2,1,0:T(8,128)S(1)}, u32[]{:S(2)}, u32[]{:S(2)}) collective-permute-start(f32[3,80,128]{2,1,0:T(8,128)S(1)} %pad_maximum_fusion.3), channel_id=1, source_target_pairs={{0,1},{1,0},{2,3},{3,2},{4,5},{5,4},{6,7},{7,6},{8,9},{9,8},{10,11... | collective-permute-start | bytes 368648 | tf_op jit(solution)/shard_map/ppermute | solution.py:368
  42.6 2.2 %shard_map.72.part_ref = f32[4,320,128]{2,1,0:T(8,128)S(1)} custom-call(bf16[128,192]{1,0:T(8,128)(2,1)S(1)} %copy-done.4, f32[4,328,128]{2,1,0:T(8,128)S(1)} %get-tuple-element.18.fields_ref.start_ref, s32[6,512]{1,0:T(8,128)S(1)} %get-tuple-element.19.near_ref), custom_call_target="tpu_custom_call" | custom-call | flops 1000000000 | bytes 1048576 | tf_op jit(solution)/shard_map/pallas_call | solution.py:355
  44.8 2.8 %shard_map.73 = (f32[4,320,128]{2,1,0:T(8,128)S(1)}, f32[3,80,128]{2,1,0:T(8,128)S(1)}, f32[5,80,128]{2,1,0:T(8,128)S(1)}) custom-call(f32[4,328,128]{2,1,0:T(8,128)S(1)} %get-tuple-element.18.fields_ref.start_ref, f32[4,320,128]{2,1,0:T(8,128)S(1)} %shard_map.72.part_ref, s32[6,512]{1,0:T(8,128)S(1)} %get-tuple-element.20.far_ref, ...), custom_call_target="tpu_custom_call" | custom-call | bytes 1048576 | tf_op jit(solution)/shard_map/pallas_call | solution.py:355
  47.6 0.1 collective-permute-start.10
  47.7 1.4 %collective-permute-done.10.swap_ref = f32[5,80,128]{2,1,0:T(8,128)S(1)} collective-permute-done((f32[5,80,128]{2,1,0:T(8,128)S(1)}, f32[5,80,128]{2,1,0:T(8,128)S(1)}, u32[]{:S(2)}, u32[]{:S(2)}) %collective-permute-start.10) | collective-permute-done | bytes 204832 | tf_op jit(solution)/shard_map/ppermute | solution.py:368
  49.2 1.6 %collective-permute-start.11 = (f32[4,80,128]{2,1,0:T(8,128)S(1)}, f32[4,80,128]{2,1,0:T(8,128)S(1)}, u32[]{:S(2)}, u32[]{:S(2)}) collective-permute-start(f32[4,80,128]{2,1,0:T(8,128)S(1)} %pad_maximum_fusion.1), channel_id=1, source_target_pairs={{0,2},{1,127},{2,4},{3,1},{4,6},{5,3},{6,8},{7,5},{8,10},{9,7},{10... | collective-permute-start | bytes 491528 | tf_op jit(solution)/shard_map/ppermute | solution.py:378
  50.8 0.1 collective-permute-start.12
  50.9 5.2 %collective-permute-done.12.b_ref = f32[3,80,128]{2,1,0:T(8,128)S(1)} collective-permute-done((f32[3,80,128]{2,1,0:T(8,128)S(1)}, f32[3,80,128]{2,1,0:T(8,128)S(1)}, u32[]{:S(2)}, u32[]{:S(2)}) %collective-permute-start.12) | collective-permute-done | bytes 122912 | tf_op jit(solution)/shard_map/ppermute | solution.py:378
  56.2 5.6 %collective-permute-start.13 = (f32[3,80,128]{2,1,0:T(8,128)S(1)}, f32[3,80,128]{2,1,0:T(8,128)S(1)}, u32[]{:S(2)}, u32[]{:S(2)}) collective-permute-start(f32[3,80,128]{2,1,0:T(8,128)S(1)} %pad_maximum_fusion.5), channel_id=1, source_target_pairs={{0,1},{1,0},{2,3},{3,2},{4,5},{5,4},{6,7},{7,6},{8,9},{9,8},{10,11... | collective-permute-start | bytes 368648 | tf_op jit(solution)/shard_map/ppermute | solution.py:368
  61.7 2.2 %shard_map.74.part_ref = f32[4,320,128]{2,1,0:T(8,128)S(1)} custom-call(bf16[128,192]{1,0:T(8,128)(2,1)S(1)} %copy-done.4, f32[4,320,128]{2,1,0:T(8,128)S(1)} %get-tuple-element.23.fields_ref.section_ref, s32[6,512]{1,0:T(8,128)S(1)} %get-tuple-element.19.near_ref), custom_call_target="tpu_custom_call" | custom-call | flops 1000000000 | bytes 1048576 | tf_op jit(solution)/shard_map/pallas_call | solution.py:355
  64.0 3.1 %shard_map.75 = (f32[320,512]{1,0:T(8,128)}, f32[320,512]{1,0:T(8,128)}) custom-call(f32[4,328,128]{2,1,0:T(8,128)S(1)} %get-tuple-element.18.fields_ref.start_ref, f32[4,320,128]{2,1,0:T(8,128)S(1)} %get-tuple-element.23.fields_ref.section_ref, f32[4,320,128]{2,1,0:T(8,128)S(1)} %shard_map.74.part_ref, s32[6,512]{1,0:T(8,128)S(1)} %get-tuple-element.20.far_ref, ...), custom_call_target="tpu_custom_call" | custom-call | bytes 1048576 | tf_op jit(solution)/shard_map/pallas_call | solution.py:355
  (42 shorter events, 0.3 us)
Async XLA Ops:
  0.6 0.7 %copy-start.3 = (s32[6,512]{1,0:T(8,128)S(1)}, s32[6,512]{1,0:T(8,128)}, u32[]{:S(2)}) copy-start(s32[6,512]{1,0:T(8,128)} %links_ref.1) | copy-start | bytes 36868
  2.1 14.9 %collective-permute-start.2 = (s32[5,1,128]{2,0,1:T(8,128)S(1)}, s32[5,1,128]{2,0,1:T(8,128)S(1)}, u32[]{:S(2)}, u32[]{:S(2)}) collective-permute-start(s32[5,1,128]{2,0,1:T(8,128)S(1)} %slice_bitcast_fusion), channel_id=1, source_target_pairs={{0,1},{1,0},{2,3},{3,2},{4,5},{5,4},{6,7},{7,6},{8,9},{9,8},{10,11... | collective-permute-start | bytes 7688 | tf_op jit(solution)/shard_map/ppermute | solution.py:368
  3.5 1.3 %copy-start = (f32[5,64,1024]{2,1,0:T(8,128)S(1)}, f32[5,64,1024]{2,1,0:T(8,128)}, u32[]{:S(2)}) copy-start(f32[5,64,1024]{2,1,0:T(8,128)} %param.5) | copy-start | bytes 3932164
  4.8 0.7 %copy-start.1 = (s32[1024]{0:T(1024)S(1)}, s32[1024]{0:T(1024)}, u32[]{:S(2)}) copy-start(s32[1024]{0:T(1024)} %param.6) | copy-start | bytes 12292
  5.5 0.7 %copy-start.2 = (s32[1024]{0:T(1024)S(1)}, s32[1024]{0:T(1024)}, u32[]{:S(2)}) copy-start(s32[1024]{0:T(1024)} %param.7) | copy-start | bytes 12292
  7.1 20.3 %collective-permute-start = (f32[328,256]{1,0:T(8,128)S(1)}, f32[328,256]{1,0:T(8,128)S(1)}, u32[]{:S(2)}, u32[]{:S(2)}) collective-permute-start(f32[328,256]{1,0:T(8,128)S(1)} %get-tuple-element.15), channel_id=1, source_target_pairs={{0,127},{1,2},{2,1},{3,4},{4,3},{5,6},{6,5},{7,8},{8,7},{9,10},{10... | collective-permute-start | bytes 1007624 | tf_op jit(solution)/shard_map/ppermute | solution.py:373
  8.5 18.9 %collective-permute-start.1 = (f32[328,256]{1,0:T(8,128)S(1)}, f32[328,256]{1,0:T(8,128)S(1)}, u32[]{:S(2)}, u32[]{:S(2)}) collective-permute-start(f32[328,256]{1,0:T(8,128)S(1)} %get-tuple-element.16), channel_id=1, source_target_pairs={{0,1},{1,0},{2,3},{3,2},{4,5},{5,4},{6,7},{7,6},{8,9},{9,8},{10,11... | collective-permute-start | bytes 1007624 | tf_op jit(solution)/shard_map/ppermute | solution.py:368
  17.0 4.0 %collective-permute-start.4 = (s32[3,1,128]{2,0,1:T(4,128)S(1)}, s32[3,1,128]{2,0,1:T(4,128)S(1)}, u32[]{:S(2)}, u32[]{:S(2)}) collective-permute-start(s32[3,1,128]{2,0,1:T(4,128)S(1)} %pad_add_fusion.1), channel_id=1, source_target_pairs={{0,4},{1,125},{2,6},{3,127},{4,8},{5,1},{6,10},{7,3},{8,12},{9,5},... | collective-permute-start | bytes 4616 | tf_op jit(solution)/shard_map/ppermute | solution.py:378
  17.8 3.2 %collective-permute-start.3 = (s32[4,1,128]{2,0,1:T(4,128)S(1)}, s32[4,1,128]{2,0,1:T(4,128)S(1)}, u32[]{:S(2)}, u32[]{:S(2)}) collective-permute-start(s32[4,1,128]{2,0,1:T(4,128)S(1)} %pad_add_fusion), channel_id=1, source_target_pairs={{0,2},{1,127},{2,4},{3,1},{4,6},{5,3},{6,8},{7,5},{8,10},{9,7},{10... | collective-permute-start | bytes 6152 | tf_op jit(solution)/shard_map/ppermute | solution.py:378
  21.1 6.3 %collective-permute-start.5 = (s32[3,1,128]{2,0,1:T(4,128)S(1)}, s32[3,1,128]{2,0,1:T(4,128)S(1)}, u32[]{:S(2)}, u32[]{:S(2)}) collective-permute-start(s32[3,1,128]{2,0,1:T(4,128)S(1)} %pad_add_fusion.2), channel_id=1, source_target_pairs={{0,1},{1,0},{2,3},{3,2},{4,5},{5,4},{6,7},{7,6},{8,9},{9,8},{10,11... | collective-permute-start | bytes 4616 | tf_op jit(solution)/shard_map/ppermute | solution.py:368
  27.4 15.2 %copy-start.4 = (bf16[128,192]{1,0:T(8,128)(2,1)S(1)}, bf16[128,192]{1,0:T(8,128)(2,1)}, u32[]{:S(2)}) copy-start(bf16[128,192]{1,0:T(8,128)(2,1)} %constant.13.clone.table_ref) | copy-start | bytes 147460
  28.4 1.5 %collective-permute-start.6 = (f32[5,80,128]{2,1,0:T(8,128)S(1)}, f32[5,80,128]{2,1,0:T(8,128)S(1)}, u32[]{:S(2)}, u32[]{:S(2)}) collective-permute-start(f32[5,80,128]{2,1,0:T(8,128)S(1)} %get-tuple-element.22), channel_id=1, source_target_pairs={{0,1},{1,0},{2,3},{3,2},{4,5},{5,4},{6,7},{7,6},{8,9},{9,8},{10,11... | collective-permute-start | bytes 614408 | tf_op jit(solution)/shard_map/ppermute | solution.py:368
  30.0 7.2 %collective-permute-start.7 = (f32[4,80,128]{2,1,0:T(8,128)S(1)}, f32[4,80,128]{2,1,0:T(8,128)S(1)}, u32[]{:S(2)}, u32[]{:S(2)}) collective-permute-start(f32[4,80,128]{2,1,0:T(8,128)S(1)} %pad_maximum_fusion), channel_id=1, source_target_pairs={{0,2},{1,127},{2,4},{3,1},{4,6},{5,3},{6,8},{7,5},{8,10},{9,7},{10... | collective-permute-start | bytes 491528 | tf_op jit(solution)/shard_map/ppermute | solution.py:378
  30.8 6.4 %collective-permute-start.8 = (f32[3,80,128]{2,1,0:T(8,128)S(1)}, f32[3,80,128]{2,1,0:T(8,128)S(1)}, u32[]{:S(2)}, u32[]{:S(2)}) collective-permute-start(f32[3,80,128]{2,1,0:T(8,128)S(1)} %pad_maximum_fusion.2), channel_id=1, source_target_pairs={{0,4},{1,125},{2,6},{3,127},{4,8},{5,1},{6,10},{7,3},{8,12},{9,5},... | collective-permute-start | bytes 368648 | tf_op jit(solution)/shard_map/ppermute | solution.py:378
  37.2 7.6 %collective-permute-start.9 = (f32[3,80,128]{2,1,0:T(8,128)S(1)}, f32[3,80,128]{2,1,0:T(8,128)S(1)}, u32[]{:S(2)}, u32[]{:S(2)}) collective-permute-start(f32[3,80,128]{2,1,0:T(8,128)S(1)} %pad_maximum_fusion.3), channel_id=1, source_target_pairs={{0,1},{1,0},{2,3},{3,2},{4,5},{5,4},{6,7},{7,6},{8,9},{9,8},{10,11... | collective-permute-start | bytes 368648 | tf_op jit(solution)/shard_map/ppermute | solution.py:368
  47.6 1.5 %collective-permute-start.10 = (f32[5,80,128]{2,1,0:T(8,128)S(1)}, f32[5,80,128]{2,1,0:T(8,128)S(1)}, u32[]{:S(2)}, u32[]{:S(2)}) collective-permute-start(f32[5,80,128]{2,1,0:T(8,128)S(1)} %get-tuple-element.25), channel_id=1, source_target_pairs={{0,1},{1,0},{2,3},{3,2},{4,5},{5,4},{6,7},{7,6},{8,9},{9,8},{10,11... | collective-permute-start | bytes 614408 | tf_op jit(solution)/shard_map/ppermute | solution.py:368
  49.2 7.0 %collective-permute-start.11 = (f32[4,80,128]{2,1,0:T(8,128)S(1)}, f32[4,80,128]{2,1,0:T(8,128)S(1)}, u32[]{:S(2)}, u32[]{:S(2)}) collective-permute-start(f32[4,80,128]{2,1,0:T(8,128)S(1)} %pad_maximum_fusion.1), channel_id=1, source_target_pairs={{0,2},{1,127},{2,4},{3,1},{4,6},{5,3},{6,8},{7,5},{8,10},{9,7},{10... | collective-permute-start | bytes 491528 | tf_op jit(solution)/shard_map/ppermute | solution.py:378
  50.8 5.3 %collective-permute-start.12 = (f32[3,80,128]{2,1,0:T(8,128)S(1)}, f32[3,80,128]{2,1,0:T(8,128)S(1)}, u32[]{:S(2)}, u32[]{:S(2)}) collective-permute-start(f32[3,80,128]{2,1,0:T(8,128)S(1)} %pad_maximum_fusion.4), channel_id=1, source_target_pairs={{0,4},{1,125},{2,6},{3,127},{4,8},{5,1},{6,10},{7,3},{8,12},{9,5},... | collective-permute-start | bytes 368648 | tf_op jit(solution)/shard_map/ppermute | solution.py:378
  56.2 7.8 %collective-permute-start.13 = (f32[3,80,128]{2,1,0:T(8,128)S(1)}, f32[3,80,128]{2,1,0:T(8,128)S(1)}, u32[]{:S(2)}, u32[]{:S(2)}) collective-permute-start(f32[3,80,128]{2,1,0:T(8,128)S(1)} %pad_maximum_fusion.5), channel_id=1, source_target_pairs={{0,1},{1,0},{2,3},{3,2},{4,5},{5,4},{6,7},{7,6},{8,9},{9,8},{10,11... | collective-permute-start | bytes 368648 | tf_op jit(solution)/shard_map/ppermute | solution.py:368
where the time goes:
time: 67.4 us; the launch traced here: 67.1 us
  starting transfers between devices  32.7 us (49%)
  waiting for transfers between devices  16.1 us (24%)
  Pallas kernels  13.8 us (20%)
  local copies, waits for them, and re-layouts  3.53 us (5%)
  between operations  0.85 us (1%)
    ppermute x7, starting transfers between devices, swap_cores(): return lax.ppermute(x, AXES, [(i, i ^ 1) for i in range(n)])  25.9 us
    pallas_call x8, Pallas kernels, call(): pl.pallas_call(kernel, out_shape=[jax.ShapeDtypeStruct(s, d) for s, d in...  13.8 us
    ppermute x6, waiting for transfers between devices, outward(): lax.ppermute(x, AXES, [(i, (i + (by if i % 2 == 0 else -by)) % n) for i i...  12.7 us
    ppermute x6, starting transfers between devices, outward(): lax.ppermute(x, AXES, [(i, (i + (by if i % 2 == 0 else -by)) % n) for i i...  5.45 us
    unnamed x10, local copies, waits for them, and re-layouts  3.4 us
    ppermute x7, waiting for transfers between devices, swap_cores(): return lax.ppermute(x, AXES, [(i, i ^ 1) for i in range(n)])  3.34 us
    ppermute x1, starting transfers between devices, swap_chips(): lax.ppermute(x, AXES, [(i, (i + (1 if i % 2 else -1)) % n) for i in range...  1.35 us
  transfers between devices with their start and end apart: 14, of which 6 were waited for; matrix products, arithmetic and copies ran while one was open for 0% of the time, Pallas kernels for 9%

commit v1 on v0

--- a/solution.py
+++ b/solution.py
@@ -93,35 +93,43 @@
     return sib, far, home
 
 
-def stacked_rows(state, level):
-    high, low = split(state)
-    lev = jnp.broadcast_to(level.astype(F32), (16, OLD_CAP)).astype(BF16)
-    return jnp.concatenate([high, low, lev], axis=0)
-
-
 def store_moved(ref, got):
     ref[0:ROWS, :] = got[0:ROWS] + got[ROWS : 2 * ROWS]
     ref[ROWS : ROWS + 8, :] = got[2 * ROWS : 2 * ROWS + 8]
 
 
-def pack_kernel(me_ref, state_ref, level_ref, morton_ref, far_ref, sib_ref):
-    sib, far, _ = relay_slots(me_ref[0], morton_ref[...])
-    lhs = stacked_rows(state_ref[...], level_ref[...])
-    store_moved(far_ref, dot_nt(lhs, one_hot_rows(HALF, far)))
-    store_moved(sib_ref, dot_nt(lhs, one_hot_rows(HALF, sib)))
-
-
-def home_kernel(me_ref, state_ref, level_ref, morton_ref, home_ref):
-    _, _, home = relay_slots(me_ref[0], morton_ref[...])
-    lhs = stacked_rows(state_ref[...], level_ref[...])
-    got = dot_nt(lhs, one_hot_rows(NEW_DEV, home))
+def prepare_kernel(me_ref, links_hbm, state_hbm, level_hbm, morton_hbm, ask_ref, near_ref, far_ref,
+                   slots_ref, rows_ref, links_ref, state_ref, level_ref, morton_ref, sems):
+    pairs = ((links_hbm, links_ref), (morton_hbm, morton_ref), (level_hbm, level_ref), (state_hbm, state_ref))
+    copies = [pltpu.make_async_copy(src, dst, sems.at[i]) for i, (src, dst) in enumerate(pairs)]
+    for copy in copies:
+        copy.start()
+    copies[0].wait()
+    requests(me_ref[0], links_ref[...], ask_ref, near_ref, far_ref)
+    copies[1].wait()
+    for i, row in enumerate(relay_slots(me_ref[0], morton_ref[...])):
+        slots_ref[i : i + 1, :] = row
+    copies[2].wait()
+    rows_ref[2 * ROWS :, :] = jnp.broadcast_to(level_ref[...].astype(F32), (16, OLD_CAP)).astype(BF16)
+    copies[3].wait()
+    high, low = split(state_ref[...])
+    rows_ref[0:ROWS, :] = high
+    rows_ref[ROWS : 2 * ROWS, :] = low
+
+
+def pack_kernel(rows_ref, slots_ref, far_ref, sib_ref):
+    lhs = rows_ref[...]
+    store_moved(far_ref, dot_nt(lhs, one_hot_rows(HALF, slots_ref[1:2, :])))
+    store_moved(sib_ref, dot_nt(lhs, one_hot_rows(HALF, slots_ref[0:1, :])))
+
+
+def home_kernel(rows_ref, slots_ref, home_ref):
+    got = dot_nt(rows_ref[...], one_hot_rows(NEW_DEV, slots_ref[2:3, :]))
     for c in range(BLOCKS):
         store_moved(home_ref.at[c], got[:, 128 * c : 128 * c + 128])
 
 
-def request_kernel(me_ref, links_ref, ask_ref, near_ref, far_ref):
-    me = me_ref[0]
-    links = links_ref[...]
+def requests(me, links, ask_ref, near_ref, far_ref):
     owner = links >> 9
     slot = links & (NEW_DEV - 1)
     gap = ((owner - me + 192) & 127) - 64
@@ -215,10 +223,11 @@
     return out
 
 
-def side_term(w, a, sign):
+def side_term(w, f):
+    sign = 1.0 if f % 2 else -1.0
     u = [w[1 + c] / w[0] for c in range(3)]
     p = pressure_of(w, u)
-    flux = axis_flux(w, u, p, a)
+    flux = axis_flux(w, u, p, f // 2)
     return [(sign * flux[v]) - SPEED * w[v] for v in range(FIELDS)]
 
 
@@ -254,7 +263,7 @@
     reply(wide(start_ref, ROWS), ask_ref, got_ref, own_ref, swap_ref)
 
 
-def near_kernel(table_ref, fields_ref, near_ref, part_ref, high_ref, low_ref):
+def near_kernel(table_ref, fields_ref, near_ref, part_ref, outer_ref, high_ref, low_ref):
     for c in range(BLOCKS):
         spot = slice(128 * c, 128 * c + 128)
         w = [fields_ref[c, DOFS * v : DOFS * v + DOFS, :] for v in range(FIELDS)]
@@ -273,9 +282,7 @@
         for c in range(BLOCKS):
             part_ref[c, DOFS * v : DOFS * v + DOFS, :] = x[:, 128 * c : 128 * c + 128]
     for f in range(6):
-        a, sign = f // 2, 1.0 if f % 2 else -1.0
-        mine = near_ref[f : f + 1, :]
-        hot = one_hot_rows(NEW_DEV, mine)
+        hot = one_hot_rows(NEW_DEV, near_ref[f : f + 1, :])
         across = jnp.concatenate(
             [
                 jnp.concatenate([trace(fields_ref, c, v, f ^ 1) for v in range(FIELDS)], axis=0)
@@ -285,61 +292,56 @@
         )
         high, low = split(across)
         both = dot(jnp.concatenate([high, low], axis=0), hot)
+        outer_ref[f] = both[0:TRACE_ROWS] + both[TRACE_ROWS:]
+    for c in range(BLOCKS):
+        for f in range(6):
+            minus = side_term([trace(fields_ref, c, v, f) for v in range(FIELDS)], f)
+            for v in range(FIELDS):
+                add_on_face(part_ref, c, v, f, -3.0 * minus[v])
+
+
+def ghost_rows(ghosts):
+    parts = [split(g) for g in ghosts]
+    high = jnp.concatenate([p[0] for p in parts], axis=1)
+    low = jnp.concatenate([p[1] for p in parts], axis=1)
+    return jnp.concatenate([high, low], axis=0)
+
+
+def direct_kernel(outer_ref, far_ref, a_ref, b_ref, swap_ref, sum_ref):
+    lhs = ghost_rows([swap_ref[0], a_ref[2], a_ref[0], b_ref[1], b_ref[0]])
+    for f in range(6):
+        both = dot(lhs, one_hot_rows(5 * CAP, far_ref[f : f + 1, :] - 3 * CAP))
+        sum_ref[f] = outer_ref[f] + both[0:TRACE_ROWS] + both[TRACE_ROWS:]
+
+
+def add_outer(part_ref, outer_ref, far_ref, post_ref, sum_ref):
+    lhs = ghost_rows([post_ref[1], post_ref[0], post_ref[2]])
+    sum_ref[...] = part_ref[...]
+    for f in range(6):
+        both = dot(lhs, one_hot_rows(3 * CAP, far_ref[f : f + 1, :]))
         for c in range(BLOCKS):
             spot = slice(128 * c, 128 * c + 128)
-            outer = both[0:TRACE_ROWS, spot] + both[TRACE_ROWS:, spot]
-            there = mine[:, spot] >= 0
-            plus = side_term(outer_fields(outer, there), a, sign)
-            minus = side_term([trace(fields_ref, c, v, f) for v in range(FIELDS)], a, sign)
+            outer = outer_ref[f, :, spot] + both[0:TRACE_ROWS, spot] + both[TRACE_ROWS:, spot]
+            plus = side_term([outer[16 * v : 16 * v + 16] for v in range(FIELDS)], f)
             for v in range(FIELDS):
-                add_on_face(part_ref, c, v, f, 3.0 * (jnp.where(there, plus[v], 0.0) - minus[v]))
-
-
-def outer_fields(outer, there):
-    w = [outer[16 * v : 16 * v + 16] for v in range(FIELDS)]
-    w[0] = jnp.where(there, w[0], 1.0)
-    return w
-
-
-def add_far(part_ref, far_ref, ghosts, sum_ref, lhs_ref):
-    for t in range(8):
-        high, low = split(ghosts[t])
-        lhs_ref[0:TRACE_ROWS, CAP * t : CAP * t + CAP] = high
-        lhs_ref[TRACE_ROWS:, CAP * t : CAP * t + CAP] = low
-    sum_ref[...] = part_ref[...]
-    lhs = lhs_ref[...]
-    for f in range(6):
-        a, sign = f // 2, 1.0 if f % 2 else -1.0
-        place = far_ref[f : f + 1, :]
-        both = dot(lhs, one_hot_rows(8 * CAP, place))
-        for c in range(BLOCKS):
-            spot = slice(128 * c, 128 * c + 128)
-            outer = both[0:TRACE_ROWS, spot] + both[TRACE_ROWS:, spot]
-            there = place[:, spot] >= 0
-            plus = side_term(outer_fields(outer, there), a, sign)
-            for v in range(FIELDS):
-                add_on_face(sum_ref, c, v, f, 3.0 * jnp.where(there, plus[v], 0.0))
+                add_on_face(sum_ref, c, v, f, 3.0 * plus[v])
 
 
 def metric_of(start_ref, c):
     return jnp.where(start_ref[c, ROWS : ROWS + 1, :] > 0.5, 2.0, 1.0)
 
 
-def ghosts_of(a_ref, b_ref, swap_ref, post_ref):
-    return [post_ref[1], post_ref[0], post_ref[2], swap_ref[0], a_ref[2], a_ref[0], b_ref[1], b_ref[0]]
-
-
-def second_kernel(start_ref, part_ref, far_ref, ask_ref, a_ref, b_ref, swap_ref, post_ref,
-                  section_ref, own_ref, out_ref, sum_ref, lhs_ref, got_ref):
-    add_far(part_ref, far_ref, ghosts_of(a_ref, b_ref, swap_ref, post_ref), sum_ref, lhs_ref)
+def second_kernel(start_ref, part_ref, outer_ref, far_ref, ask_ref, post_ref,
+                  section_ref, own_ref, out_ref, sum_ref, got_ref):
+    add_outer(part_ref, outer_ref, far_ref, post_ref, sum_ref)
     for c in range(BLOCKS):
         section_ref[c] = start_ref[c, 0:ROWS, :] - (DT * metric_of(start_ref, c)) * sum_ref[c]
     reply(wide(section_ref, ROWS), ask_ref, got_ref, own_ref, out_ref)
 
 
-def last_kernel(start_ref, section_ref, part_ref, far_ref, a_ref, b_ref, swap_ref, post_ref,
-                state_ref, rate_ref, sum_ref, lhs_ref):
-    add_far(part_ref, far_ref, ghosts_of(a_ref, b_ref, swap_ref, post_ref), sum_ref, lhs_ref)
+def last_kernel(start_ref, section_ref, part_ref, outer_ref, far_ref, post_ref,
+                state_ref, rate_ref, sum_ref):
+    add_outer(part_ref, outer_ref, far_ref, post_ref, sum_ref)
     for c in range(BLOCKS):
         spot = slice(128 * c, 128 * c + 128)
         rate = -metric_of(start_ref, c) * sum_ref[c]
@@ -349,15 +351,16 @@
 
 VM = pl.BlockSpec(memory_space=pltpu.VMEM)
 SM = pl.BlockSpec(memory_space=pltpu.SMEM)
-
-
-def call(kernel, outs, args, scalars=0, scratch=(), flops=0):
+HB = pl.BlockSpec(memory_space=pltpu.HBM)
+
+
+def call(kernel, outs, args, specs=None, scratch=(), flops=10**6):
     return pl.pallas_call(
         kernel,
         out_shape=[jax.ShapeDtypeStruct(s, d) for s, d in outs],
-        in_specs=[SM] * scalars + [VM] * (len(args) - scalars),
+        in_specs=specs or [VM] * len(args),
         out_specs=[VM] * len(outs),
-        scratch_shapes=[pltpu.VMEM(s, d) for s, d in scratch],
+        scratch_shapes=[pltpu.VMEM(*s) if isinstance(s, tuple) else s for s in scratch],
         compiler_params=pltpu.CompilerParams(vmem_limit_bytes=40 * 2**20),
         cost_estimate=pl.CostEstimate(flops=flops, bytes_accessed=2**20, transcendentals=0),
     )(*args)
@@ -378,12 +381,14 @@
     return lax.ppermute(x, AXES, [(i, (i + (by if i % 2 == 0 else -by)) % n) for i in range(n)])
 
 
-def exchange(own, swap):
-    got = swap_cores(swap)
+def outward_pair(own, got):
     b = outward(jnp.concatenate([own[2:3], got[3:5]], axis=0), 4)
     a = outward(jnp.concatenate([own[0:2], got[1:3]], axis=0), 2)
-    post = swap_cores(jnp.concatenate([a[1:2], a[3:4], b[2:3]], axis=0))
-    return a, b, got, post
+    return a, b
+
+
+def swap_back(a, b):
+    return swap_cores(jnp.concatenate([a[1:2], a[3:4], b[2:3]], axis=0))
 
 
 def body(state_old, level_old, morton_old, neighbours):
@@ -392,62 +397,82 @@
     level = level_old.reshape(1, OLD_CAP)
     morton = morton_old.reshape(1, OLD_CAP)
 
-    ask, near, far = call(
-        request_kernel,
-        [((8, CAP), I32), ((6, NEW_DEV), I32), ((6, NEW_DEV), I32)],
-        (me, neighbours),
-        1,
+    ask, near, far, slots, rows = call(
+        prepare_kernel,
+        [
+            ((8, CAP), I32),
+            ((6, NEW_DEV), I32),
+            ((6, NEW_DEV), I32),
+            ((3, OLD_CAP), I32),
+            ((2 * ROWS + 16, OLD_CAP), BF16),
+        ],
+        (me, neighbours, state, level, morton),
+        [SM, HB, HB, HB, HB],
+        [
+            ((6, NEW_DEV), I32),
+            ((ROWS, OLD_CAP), F32),
+            ((1, OLD_CAP), I32),
+            ((1, OLD_CAP), I32),
+            pltpu.SemaphoreType.DMA((4,)),
+        ],
     )
     ask = ask.reshape(8, 1, CAP)
-    asked = jnp.concatenate(list(g for g in ghosts_of(*exchange(ask[0:3], ask[3:8]))), axis=0)
-
-    to_far, to_sib = call(
-        pack_kernel, [((MOVED_ROWS, HALF), F32)] * 2, (me, state, level, morton), 1
-    )
+    got = swap_cores(ask[3:8])
+    to_far, to_sib = call(pack_kernel, [((MOVED_ROWS, HALF), F32)] * 2, (rows, slots))
+    got, to_far = lax.optimization_barrier((got, to_far))
+    a, b = outward_pair(ask[0:3], got)
     from_far = swap_chips(to_far)
     from_sib = swap_cores(to_sib)
-    (home,) = call(home_kernel, [((BLOCKS, MOVED_ROWS, 128), F32)], (me, state, level, morton), 1)
+    (home,) = call(home_kernel, [((BLOCKS, MOVED_ROWS, 128), F32)], (rows, slots))
+    post = swap_back(a, b)
+    asked = jnp.concatenate(
+        [post[1], post[0], post[2], got[0], a[2], a[0], b[1], b[0]], axis=0
+    )
 
     chunks = [((3, TRACE_ROWS, CAP), F32), ((5, TRACE_ROWS, CAP), F32)]
     got_scratch = ((8, ROWS, CAP), F32)
-    sum_scratch = ((BLOCKS, ROWS, 128), F32)
-    lhs_scratch = ((2 * TRACE_ROWS, 8 * CAP), BF16)
+    blocks = ((BLOCKS, ROWS, 128), F32)
+    sides = ((6, TRACE_ROWS, NEW_DEV), F32)
     table = jnp.asarray(stacked_table())
 
-    def near_part(fields):
-        return call(
+    def neighbours_of(fields, own, swap):
+        got = swap_cores(swap)
+        a, b = outward_pair(own, got)
+        part, outer = call(
             near_kernel,
-            [((BLOCKS, ROWS, 128), F32)],
+            [blocks, sides],
             (table, fields, near),
-            0,
+            None,
             [((FIELDS, 3 * DOFS, NEW_DEV), BF16)] * 2,
             flops=10**9,
-        )[0]
+        )
+        a, b, outer = lax.optimization_barrier((a, b, outer))
+        post = swap_back(a, b)
+        (outer,) = call(direct_kernel, [sides], (outer, far, a, b, got), flops=10**9)
+        return part, outer, far, post
 
     start, own, swap = call(
         first_kernel,
         [((BLOCKS, MOVED_ROWS, 128), F32)] + chunks,
         (me, home, from_far, from_sib, asked),
-        1,
+        [SM, VM, VM, VM, VM],
         [got_scratch],
     )
-    came = exchange(own, swap)
-    part = near_part(start)
+    part, outer, far, post = neighbours_of(start, own, swap)
     section, own, swap = call(
         second_kernel,
-        [((BLOCKS, ROWS, 128), F32)] + chunks,
-        (start, part, far, asked) + came,
-        0,
-        [sum_scratch, lhs_scratch, got_scratch],
-    )
-    came = exchange(own, swap)
-    part = near_part(section)
+        [blocks] + chunks,
+        (start, part, outer, far, asked, post),
+        None,
+        [blocks, got_scratch],
+    )
+    part, outer, far, post = neighbours_of(section, own, swap)
     new_state, rate = call(
         last_kernel,
         [((ROWS, NEW_DEV), F32)] * 2,
-        (start, section, part, far) + came,
-        0,
-        [sum_scratch, lhs_scratch],
+        (start, section, part, outer, far, post),
+        None,
+        [blocks],
     )
     shape = (FIELDS, DOFS, NEW_DEV)
     return new_state.reshape(shape), rate.reshape(shape)

time: 67.4 us -> 61.3 us (0.909)
  starting transfers between devices: 32.7 us -> 28.2 us
  waiting for transfers between devices: 16.1 us -> 14.2 us
    ppermute x7, starting transfers between devices: 25.9 us -> 8.86 us  [swap_cores(): return lax.ppermute(x, AXES, [(i, i ^ 1) for i in range(n)])]
    ppermute x6, starting transfers between devices: 5.45 us -> 19.3 us  [outward(): lax.ppermute(x, AXES, [(i, (i + (by if i % 2 == 0 else -by)) % n) for i i...]
    ppermute x6, waiting for transfers between devices: 12.7 us -> 8.84 us  [outward(): lax.ppermute(x, AXES, [(i, (i + (by if i % 2 == 0 else -by)) % n) for i i...]
    ppermute x1, waiting for transfers between devices: 0.01 us -> 2.33 us  [swap_chips(): lax.ppermute(x, AXES, [(i, (i + (1 if i % 2 else -1)) % n) for i in range...]
    ppermute x1, starting transfers between devices: 1.35 us -> 0.01 us  [swap_chips(): lax.ppermute(x, AXES, [(i, (i + (1 if i % 2 else -1)) % n) for i in range...]
    pallas_call x8 -> x10, Pallas kernels: 13.8 us -> 14.2 us  [call(): pl.pallas_call(kernel, out_shape=[jax.ShapeDtypeStruct(s, d) for s, d in...]
  transfers between devices with their start and end apart: 14 -> 14, of which waited for: 6 -> 7; matrix products, arithmetic and copies ran while one was open for 0% -> 0% of each run, Pallas kernels for 9% -> 13%
where the time goes in v1:
time: 61.3 us; the launch traced here: 61 us
  starting transfers between devices  28.2 us (46%)
  Pallas kernels  14.2 us (23%)
  waiting for transfers between devices  14.2 us (23%)
  local copies, waits for them, and re-layouts  3.53 us (6%)
  between operations  0.87 us (1%)
    ppermute x6, starting transfers between devices, outward(): lax.ppermute(x, AXES, [(i, (i + (by if i % 2 == 0 else -by)) % n) for i i...  19.3 us
    pallas_call x10, Pallas kernels, call(): pl.pallas_call(kernel, out_shape=[jax.ShapeDtypeStruct(s, d) for s, d in...  14.2 us
    ppermute x7, starting transfers between devices, swap_cores(): return lax.ppermute(x, AXES, [(i, i ^ 1) for i in range(n)])  8.86 us
    ppermute x6, waiting for transfers between devices, outward(): lax.ppermute(x, AXES, [(i, (i + (by if i % 2 == 0 else -by)) % n) for i i...  8.84 us
    unnamed x10, local copies, waits for them, and re-layouts  3.41 us
    ppermute x7, waiting for transfers between devices, swap_cores(): return lax.ppermute(x, AXES, [(i, i ^ 1) for i in range(n)])  2.99 us
    ppermute x1, waiting for transfers between devices, swap_chips(): lax.ppermute(x, AXES, [(i, (i + (1 if i % 2 else -1)) % n) for i in range...  2.33 us
  transfers between devices with their start and end apart: 14, of which 7 were waited for; matrix products, arithmetic and copies ran while one was open for 0% of the time, Pallas kernels for 13%

profile of v1, /device:TPU:1, one launch (start us, length us, event | category | flops | bytes accessed | tf_op | source)
XLA Modules:
  0.0 61.0 jit_solution(10262420428349052410)
XLA Ops:
  0.6 1.3 %copy-done = f32[5,64,1024]{2,1,0:T(8,128)S(1)} copy-done((f32[5,64,1024]{2,1,0:T(8,128)S(1)}, f32[5,64,1024]{2,1,0:T(8,128)}, u32[]{:S(2)}) %copy-start) | copy-done | bytes 1310744
  2.0 0.7 %copy-done.1 = s32[6,512]{1,0:T(8,128)S(1)} copy-done((s32[6,512]{1,0:T(8,128)S(1)}, s32[6,512]{1,0:T(8,128)}, u32[]{:S(2)}) %copy-start.1) | copy-done | bytes 12312
  2.7 0.7 %copy-done.2 = s32[1024]{0:T(1024)S(1)} copy-done((s32[1024]{0:T(1024)S(1)}, s32[1024]{0:T(1024)}, u32[]{:S(2)}) %copy-start.2) | copy-done | bytes 4120
  3.4 0.7 %copy-done.3 = s32[1024]{0:T(1024)S(1)} copy-done((s32[1024]{0:T(1024)S(1)}, s32[1024]{0:T(1024)}, u32[]{:S(2)}) %copy-start.3) | copy-done | bytes 4120
  4.0 1.1 %shard_map.68 = (s32[8,128]{1,0:T(8,128)S(1)}, s32[6,512]{1,0:T(8,128)S(1)}, s32[6,512]{1,0:T(8,128)S(1)}, s32[3,1024]{1,0:T(4,128)S(1)}, bf16[656,1024]{1,0:T(8,128)(2,1)S(1)}) custom-call(s32[1]{0:T(128)} %bitcast.me_ref, s32[6,512]{1,0:T(8,128)S(1)} %copy-done.1, f32[320,1024]{1,0:T(8,128)S(1)} %bitcast.30, s32[1,1024]{1,0:T(1,128)S(1)} %bitcast.31, ...), custom_call_target="tpu_custom_call" | custom-call | flops 1000000 | bytes 1048576 | tf_op jit(solution)/shard_map/pallas_call | solution.py:358
  5.1 1.5 %collective-permute-start = (s32[5,1,128]{2,0,1:T(8,128)S(1)}, s32[5,1,128]{2,0,1:T(8,128)S(1)}, u32[]{:S(2)}, u32[]{:S(2)}) collective-permute-start(s32[5,1,128]{2,0,1:T(8,128)S(1)} %slice_bitcast_fusion), channel_id=1, source_target_pairs={{0,1},{1,0},{2,3},{3,2},{4,5},{5,4},{6,7},{7,6},{8,9},{9,8},{10,11... | collective-permute-start | bytes 7688 | tf_op jit(solution)/shard_map/ppermute | solution.py:371
  6.6 0.9 %shard_map.70 = (f32[328,256]{1,0:T(8,128)S(1)}, f32[328,256]{1,0:T(8,128)S(1)}) custom-call(bf16[656,1024]{1,0:T(8,128)(2,1)S(1)} %get-tuple-element.29.rows_ref, s32[3,1024]{1,0:T(4,128)S(1)} %get-tuple-element.30.slots_ref), custom_call_target="tpu_custom_call" | custom-call | flops 1000000 | bytes 1048576 | tf_op jit(solution)/shard_map/pallas_call | solution.py:358
  7.6 0.9 %shard_map.69.home_ref = f32[4,328,128]{2,1,0:T(8,128)S(1)} custom-call(bf16[656,1024]{1,0:T(8,128)(2,1)S(1)} %get-tuple-element.29.rows_ref, s32[3,1024]{1,0:T(4,128)S(1)} %get-tuple-element.30.slots_ref), custom_call_target="tpu_custom_call" | custom-call | flops 1000000 | bytes 1048576 | tf_op jit(solution)/shard_map/pallas_call | solution.py:358
  8.6 8.7 %collective-permute-start.4 = (s32[3,1,128]{2,0,1:T(4,128)S(1)}, s32[3,1,128]{2,0,1:T(4,128)S(1)}, u32[]{:S(2)}, u32[]{:S(2)}) collective-permute-start(s32[3,1,128]{2,0,1:T(4,128)S(1)} %pad_add_fusion.1), channel_id=1, source_target_pairs={{0,4},{1,125},{2,6},{3,127},{4,8},{5,1},{6,10},{7,3},{8,12},{9,5},... | collective-permute-start | bytes 4616 | tf_op jit(solution)/shard_map/ppermute | solution.py:381
  17.3 0.8 %collective-permute-start.3 = (s32[4,1,128]{2,0,1:T(4,128)S(1)}, s32[4,1,128]{2,0,1:T(4,128)S(1)}, u32[]{:S(2)}, u32[]{:S(2)}) collective-permute-start(s32[4,1,128]{2,0,1:T(4,128)S(1)} %pad_add_fusion), channel_id=1, source_target_pairs={{0,2},{1,127},{2,4},{3,1},{4,6},{5,3},{6,8},{7,5},{8,10},{9,7},{10... | collective-permute-start | bytes 6152 | tf_op jit(solution)/shard_map/ppermute | solution.py:381
  18.1 1.9 %collective-permute-done.3 = s32[4,1,128]{2,0,1:T(4,128)S(1)} collective-permute-done((s32[4,1,128]{2,0,1:T(4,128)S(1)}, s32[4,1,128]{2,0,1:T(4,128)S(1)}, u32[]{:S(2)}, u32[]{:S(2)}) %collective-permute-start.3) | collective-permute-done | bytes 2080 | tf_op jit(solution)/shard_map/ppermute | solution.py:381
  20.1 1.5 %collective-permute-start.5 = (s32[3,1,128]{2,0,1:T(4,128)S(1)}, s32[3,1,128]{2,0,1:T(4,128)S(1)}, u32[]{:S(2)}, u32[]{:S(2)}) collective-permute-start(s32[3,1,128]{2,0,1:T(4,128)S(1)} %pad_add_fusion.2), channel_id=1, source_target_pairs={{0,1},{1,0},{2,3},{3,2},{4,5},{5,4},{6,7},{7,6},{8,9},{9,8},{10,11... | collective-permute-start | bytes 4616 | tf_op jit(solution)/shard_map/ppermute | solution.py:371
  21.5 0.8 %collective-permute-done.5 = s32[3,1,128]{2,0,1:T(4,128)S(1)} collective-permute-done((s32[3,1,128]{2,0,1:T(4,128)S(1)}, s32[3,1,128]{2,0,1:T(4,128)S(1)}, u32[]{:S(2)}, u32[]{:S(2)}) %collective-permute-start.5) | collective-permute-done | bytes 1568 | tf_op jit(solution)/shard_map/ppermute | solution.py:371
  22.4 2.3 %collective-permute-done.1.far_ref = f32[328,256]{1,0:T(8,128)S(1)} collective-permute-done((f32[328,256]{1,0:T(8,128)S(1)}, f32[328,256]{1,0:T(8,128)S(1)}, u32[]{:S(2)}, u32[]{:S(2)}) %collective-permute-start.1) | collective-permute-done | bytes 335904 | tf_op jit(solution)/shard_map/ppermute | solution.py:376
  24.7 1.0 %shard_map.71 = (f32[4,328,128]{2,1,0:T(8,128)S(1)}, f32[3,80,128]{2,1,0:T(8,128)S(1)}, f32[5,80,128]{2,1,0:T(8,128)S(1)}) custom-call(s32[1]{0:T(128)} %bitcast.me_ref, f32[4,328,128]{2,1,0:T(8,128)S(1)} %shard_map.69.home_ref, f32[328,256]{1,0:T(8,128)S(1)} %collective-permute-done.1.far_ref, f32[328,256]{1,0:T(8,128)S(1)} %collective-permute-done.2.sib_ref, ...), custom_call_target="tpu_custom_call" | custom-call | flops 1000000 | bytes 1048576 | tf_op jit(solution)/shard_map/pallas_call | solution.py:358
  25.7 0.5 collective-permute-start.6
  26.2 1.1 %collective-permute-done.6.swap_ref = f32[5,80,128]{2,1,0:T(8,128)S(1)} collective-permute-done((f32[5,80,128]{2,1,0:T(8,128)S(1)}, f32[5,80,128]{2,1,0:T(8,128)S(1)}, u32[]{:S(2)}, u32[]{:S(2)}) %collective-permute-start.6) | collective-permute-done | bytes 204832 | tf_op jit(solution)/shard_map/ppermute | solution.py:371
  27.3 5.5 %collective-permute-start.7 = (f32[4,80,128]{2,1,0:T(8,128)S(1)}, f32[4,80,128]{2,1,0:T(8,128)S(1)}, u32[]{:S(2)}, u32[]{:S(2)}) collective-permute-start(f32[4,80,128]{2,1,0:T(8,128)S(1)} %pad_maximum_fusion), channel_id=1, source_target_pairs={{0,2},{1,127},{2,4},{3,1},{4,6},{5,3},{6,8},{7,5},{8,10},{9,7},{10... | collective-permute-start | bytes 491528 | tf_op jit(solution)/shard_map/ppermute | solution.py:381
  33.0 2.1 %shard_map.72 = (f32[4,320,128]{2,1,0:T(8,128)S(1)}, f32[6,80,512]{2,1,0:T(8,128)S(1)}) custom-call(bf16[128,192]{1,0:T(8,128)(2,1)S(1)} %copy-done.4, f32[4,328,128]{2,1,0:T(8,128)S(1)} %get-tuple-element.36.fields_ref.start_ref, s32[6,512]{1,0:T(8,128)S(1)} %get-tuple-element.37.near_ref), custom_call_target="tpu_custom_call" | custom-call | flops 1000000000 | bytes 1048576 | tf_op jit(solution)/shard_map/pallas_call | solution.py:358
  35.1 3.6 %collective-permute-done.8.b_ref = f32[3,80,128]{2,1,0:T(8,128)S(1)} collective-permute-done((f32[3,80,128]{2,1,0:T(8,128)S(1)}, f32[3,80,128]{2,1,0:T(8,128)S(1)}, u32[]{:S(2)}, u32[]{:S(2)}) %collective-permute-start.8) | collective-permute-done | bytes 122912 | tf_op jit(solution)/shard_map/ppermute | solution.py:381
  38.8 1.9 %collective-permute-start.9 = (f32[3,80,128]{2,1,0:T(8,128)S(1)}, f32[3,80,128]{2,1,0:T(8,128)S(1)}, u32[]{:S(2)}, u32[]{:S(2)}) collective-permute-start(f32[3,80,128]{2,1,0:T(8,128)S(1)} %pad_maximum_fusion.3), channel_id=1, source_target_pairs={{0,1},{1,0},{2,3},{3,2},{4,5},{5,4},{6,7},{7,6},{8,9},{9,8},{10,11... | collective-permute-start | bytes 368648 | tf_op jit(solution)/shard_map/ppermute | solution.py:371
  40.7 1.0 %shard_map.73.outer_ref = f32[6,80,512]{2,1,0:T(8,128)S(1)} custom-call(f32[6,80,512]{2,1,0:T(8,128)S(1)} %get-tuple-element.42.outer_ref, s32[6,512]{1,0:T(8,128)S(1)} %get-tuple-element.43.far_ref, f32[4,80,128]{2,1,0:T(8,128)S(1)} %collective-permute-done.7.a_ref, f32[3,80,128]{2,1,0:T(8,128)S(1)} %collective-permute-done.8.b_ref, ...), custom_call_target="tpu_custom_call" | custom-call | flops 1000000000 | bytes 1048576 | tf_op jit(solution)/shard_map/pallas_call | solution.py:358
  41.6 1.9 %shard_map.74 = (f32[4,320,128]{2,1,0:T(8,128)S(1)}, f32[3,80,128]{2,1,0:T(8,128)S(1)}, f32[5,80,128]{2,1,0:T(8,128)S(1)}) custom-call(f32[4,328,128]{2,1,0:T(8,128)S(1)} %get-tuple-element.36.fields_ref.start_ref, f32[4,320,128]{2,1,0:T(8,128)S(1)} %get-tuple-element.38.part_ref, f32[6,80,512]{2,1,0:T(8,128)S(1)} %shard_map.73.outer_ref, ...), custom_call_target="tpu_custom_call" | custom-call | flops 1000000 | bytes 1048576 | tf_op jit(solution)/shard_map/pallas_call | solution.py:358
  43.6 0.4 collective-permute-start.10
  44.0 1.1 %collective-permute-done.10.swap_ref = f32[5,80,128]{2,1,0:T(8,128)S(1)} collective-permute-done((f32[5,80,128]{2,1,0:T(8,128)S(1)}, f32[5,80,128]{2,1,0:T(8,128)S(1)}, u32[]{:S(2)}, u32[]{:S(2)}) %collective-permute-start.10) | collective-permute-done | bytes 204832 | tf_op jit(solution)/shard_map/ppermute | solution.py:371
  45.1 3.8 %collective-permute-start.11 = (f32[4,80,128]{2,1,0:T(8,128)S(1)}, f32[4,80,128]{2,1,0:T(8,128)S(1)}, u32[]{:S(2)}, u32[]{:S(2)}) collective-permute-start(f32[4,80,128]{2,1,0:T(8,128)S(1)} %pad_maximum_fusion.1), channel_id=1, source_target_pairs={{0,2},{1,127},{2,4},{3,1},{4,6},{5,3},{6,8},{7,5},{8,10},{9,7},{10... | collective-permute-start | bytes 491528 | tf_op jit(solution)/shard_map/ppermute | solution.py:381
  48.9 0.4 collective-permute-start.12
  49.3 2.1 %shard_map.75 = (f32[4,320,128]{2,1,0:T(8,128)S(1)}, f32[6,80,512]{2,1,0:T(8,128)S(1)}) custom-call(bf16[128,192]{1,0:T(8,128)(2,1)S(1)} %copy-done.4, f32[4,320,128]{2,1,0:T(8,128)S(1)} %get-tuple-element.46.fields_ref.section_ref, s32[6,512]{1,0:T(8,128)S(1)} %get-tuple-element.37.near_ref), custom_call_target="tpu_custom_call" | custom-call | flops 1000000000 | bytes 1048576 | tf_op jit(solution)/shard_map/pallas_call | solution.py:358
  51.5 3.2 %collective-permute-done.12.b_ref = f32[3,80,128]{2,1,0:T(8,128)S(1)} collective-permute-done((f32[3,80,128]{2,1,0:T(8,128)S(1)}, f32[3,80,128]{2,1,0:T(8,128)S(1)}, u32[]{:S(2)}, u32[]{:S(2)}) %collective-permute-start.12) | collective-permute-done | bytes 122912 | tf_op jit(solution)/shard_map/ppermute | solution.py:381
  54.7 3.0 %collective-permute-start.13 = (f32[3,80,128]{2,1,0:T(8,128)S(1)}, f32[3,80,128]{2,1,0:T(8,128)S(1)}, u32[]{:S(2)}, u32[]{:S(2)}) collective-permute-start(f32[3,80,128]{2,1,0:T(8,128)S(1)} %pad_maximum_fusion.5), channel_id=1, source_target_pairs={{0,1},{1,0},{2,3},{3,2},{4,5},{5,4},{6,7},{7,6},{8,9},{9,8},{10,11... | collective-permute-start | bytes 368648 | tf_op jit(solution)/shard_map/ppermute | solution.py:371
  57.7 1.0 %shard_map.76.outer_ref = f32[6,80,512]{2,1,0:T(8,128)S(1)} custom-call(f32[6,80,512]{2,1,0:T(8,128)S(1)} %get-tuple-element.51.outer_ref, s32[6,512]{1,0:T(8,128)S(1)} %get-tuple-element.43.far_ref, f32[4,80,128]{2,1,0:T(8,128)S(1)} %collective-permute-done.11.a_ref, f32[3,80,128]{2,1,0:T(8,128)S(1)} %collective-permute-done.12.b_ref, ...), custom_call_target="tpu_custom_call" | custom-call | flops 1000000000 | bytes 1048576 | tf_op jit(solution)/shard_map/pallas_call | solution.py:358
  58.7 2.3 %shard_map.77 = (f32[320,512]{1,0:T(8,128)}, f32[320,512]{1,0:T(8,128)}) custom-call(f32[4,328,128]{2,1,0:T(8,128)S(1)} %get-tuple-element.36.fields_ref.start_ref, f32[4,320,128]{2,1,0:T(8,128)S(1)} %get-tuple-element.46.fields_ref.section_ref, f32[4,320,128]{2,1,0:T(8,128)S(1)} %get-tuple-element.47.part_ref, f32[6,80,512]{2,1,0:T(8,128)S(1)} %shard_map.76.outer_ref, ...), custom_call_target="tpu_custom_call" | custom-call | flops 1000000 | bytes 1048576 | tf_op jit(solution)/shard_map/pallas_call | solution.py:358
  (44 shorter events, 0.4 us)
Async XLA Ops:
  0.6 1.3 %copy-start = (f32[5,64,1024]{2,1,0:T(8,128)S(1)}, f32[5,64,1024]{2,1,0:T(8,128)}, u32[]{:S(2)}) copy-start(f32[5,64,1024]{2,1,0:T(8,128)} %param.5) | copy-start | bytes 3932164
  2.0 0.7 %copy-start.1 = (s32[6,512]{1,0:T(8,128)S(1)}, s32[6,512]{1,0:T(8,128)}, u32[]{:S(2)}) copy-start(s32[6,512]{1,0:T(8,128)} %links_hbm.1) | copy-start | bytes 36868
  2.7 0.7 %copy-start.2 = (s32[1024]{0:T(1024)S(1)}, s32[1024]{0:T(1024)}, u32[]{:S(2)}) copy-start(s32[1024]{0:T(1024)} %param.6) | copy-start | bytes 12292
  3.4 0.7 %copy-start.3 = (s32[1024]{0:T(1024)S(1)}, s32[1024]{0:T(1024)}, u32[]{:S(2)}) copy-start(s32[1024]{0:T(1024)} %param.7) | copy-start | bytes 12292
  5.1 3.4 %collective-permute-start = (s32[5,1,128]{2,0,1:T(8,128)S(1)}, s32[5,1,128]{2,0,1:T(8,128)S(1)}, u32[]{:S(2)}, u32[]{:S(2)}) collective-permute-start(s32[5,1,128]{2,0,1:T(8,128)S(1)} %slice_bitcast_fusion), channel_id=1, source_target_pairs={{0,1},{1,0},{2,3},{3,2},{4,5},{5,4},{6,7},{7,6},{8,9},{9,8},{10,11... | collective-permute-start | bytes 7688 | tf_op jit(solution)/shard_map/ppermute | solution.py:371
  7.5 14.9 %collective-permute-start.2 = (f32[328,256]{1,0:T(8,128)S(1)}, f32[328,256]{1,0:T(8,128)S(1)}, u32[]{:S(2)}, u32[]{:S(2)}) collective-permute-start(f32[328,256]{1,0:T(8,128)S(1)} %get-tuple-element.34), channel_id=1, source_target_pairs={{0,1},{1,0},{2,3},{3,2},{4,5},{5,4},{6,7},{7,6},{8,9},{9,8},{10,11... | collective-permute-start | bytes 1007624 | tf_op jit(solution)/shard_map/ppermute | solution.py:371
  8.5 24.4 %copy-start.4 = (bf16[128,192]{1,0:T(8,128)(2,1)S(1)}, bf16[128,192]{1,0:T(8,128)(2,1)}, u32[]{:S(2)}) copy-start(bf16[128,192]{1,0:T(8,128)(2,1)} %constant.13.clone.table_ref) | copy-start | bytes 147460
  8.6 9.5 %collective-permute-start.4 = (s32[3,1,128]{2,0,1:T(4,128)S(1)}, s32[3,1,128]{2,0,1:T(4,128)S(1)}, u32[]{:S(2)}, u32[]{:S(2)}) collective-permute-start(s32[3,1,128]{2,0,1:T(4,128)S(1)} %pad_add_fusion.1), channel_id=1, source_target_pairs={{0,4},{1,125},{2,6},{3,127},{4,8},{5,1},{6,10},{7,3},{8,12},{9,5},... | collective-permute-start | bytes 4616 | tf_op jit(solution)/shard_map/ppermute | solution.py:381
  17.3 2.7 %collective-permute-start.3 = (s32[4,1,128]{2,0,1:T(4,128)S(1)}, s32[4,1,128]{2,0,1:T(4,128)S(1)}, u32[]{:S(2)}, u32[]{:S(2)}) collective-permute-start(s32[4,1,128]{2,0,1:T(4,128)S(1)} %pad_add_fusion), channel_id=1, source_target_pairs={{0,2},{1,127},{2,4},{3,1},{4,6},{5,3},{6,8},{7,5},{8,10},{9,7},{10... | collective-permute-start | bytes 6152 | tf_op jit(solution)/shard_map/ppermute | solution.py:381
  18.1 6.6 %collective-permute-start.1 = (f32[328,256]{1,0:T(8,128)S(1)}, f32[328,256]{1,0:T(8,128)S(1)}, u32[]{:S(2)}, u32[]{:S(2)}) collective-permute-start(f32[328,256]{1,0:T(8,128)S(1)} %get-tuple-element.33), channel_id=1, source_target_pairs={{0,127},{1,2},{2,1},{3,4},{4,3},{5,6},{6,5},{7,8},{8,7},{9,10},{10... | collective-permute-start | bytes 1007624 | tf_op jit(solution)/shard_map/ppermute | solution.py:376
  20.1 2.3 %collective-permute-start.5 = (s32[3,1,128]{2,0,1:T(4,128)S(1)}, s32[3,1,128]{2,0,1:T(4,128)S(1)}, u32[]{:S(2)}, u32[]{:S(2)}) collective-permute-start(s32[3,1,128]{2,0,1:T(4,128)S(1)} %pad_add_fusion.2), channel_id=1, source_target_pairs={{0,1},{1,0},{2,3},{3,2},{4,5},{5,4},{6,7},{7,6},{8,9},{9,8},{10,11... | collective-permute-start | bytes 4616 | tf_op jit(solution)/shard_map/ppermute | solution.py:371
  25.7 1.6 %collective-permute-start.6 = (f32[5,80,128]{2,1,0:T(8,128)S(1)}, f32[5,80,128]{2,1,0:T(8,128)S(1)}, u32[]{:S(2)}, u32[]{:S(2)}) collective-permute-start(f32[5,80,128]{2,1,0:T(8,128)S(1)} %get-tuple-element.40), channel_id=1, source_target_pairs={{0,1},{1,0},{2,3},{3,2},{4,5},{5,4},{6,7},{7,6},{8,9},{9,8},{10,11... | collective-permute-start | bytes 614408 | tf_op jit(solution)/shard_map/ppermute | solution.py:371
  27.3 11.4 %collective-permute-start.7 = (f32[4,80,128]{2,1,0:T(8,128)S(1)}, f32[4,80,128]{2,1,0:T(8,128)S(1)}, u32[]{:S(2)}, u32[]{:S(2)}) collective-permute-start(f32[4,80,128]{2,1,0:T(8,128)S(1)} %pad_maximum_fusion), channel_id=1, source_target_pairs={{0,2},{1,127},{2,4},{3,1},{4,6},{5,3},{6,8},{7,5},{8,10},{9,7},{10... | collective-permute-start | bytes 491528 | tf_op jit(solution)/shard_map/ppermute | solution.py:381
  32.9 5.9 %collective-permute-start.8 = (f32[3,80,128]{2,1,0:T(8,128)S(1)}, f32[3,80,128]{2,1,0:T(8,128)S(1)}, u32[]{:S(2)}, u32[]{:S(2)}) collective-permute-start(f32[3,80,128]{2,1,0:T(8,128)S(1)} %pad_maximum_fusion.2), channel_id=1, source_target_pairs={{0,4},{1,125},{2,6},{3,127},{4,8},{5,1},{6,10},{7,3},{8,12},{9,5},... | collective-permute-start | bytes 368648 | tf_op jit(solution)/shard_map/ppermute | solution.py:381
  38.8 2.9 %collective-permute-start.9 = (f32[3,80,128]{2,1,0:T(8,128)S(1)}, f32[3,80,128]{2,1,0:T(8,128)S(1)}, u32[]{:S(2)}, u32[]{:S(2)}) collective-permute-start(f32[3,80,128]{2,1,0:T(8,128)S(1)} %pad_maximum_fusion.3), channel_id=1, source_target_pairs={{0,1},{1,0},{2,3},{3,2},{4,5},{5,4},{6,7},{7,6},{8,9},{9,8},{10,11... | collective-permute-start | bytes 368648 | tf_op jit(solution)/shard_map/ppermute | solution.py:371
  43.6 1.5 %collective-permute-start.10 = (f32[5,80,128]{2,1,0:T(8,128)S(1)}, f32[5,80,128]{2,1,0:T(8,128)S(1)}, u32[]{:S(2)}, u32[]{:S(2)}) collective-permute-start(f32[5,80,128]{2,1,0:T(8,128)S(1)} %get-tuple-element.49), channel_id=1, source_target_pairs={{0,1},{1,0},{2,3},{3,2},{4,5},{5,4},{6,7},{7,6},{8,9},{9,8},{10,11... | collective-permute-start | bytes 614408 | tf_op jit(solution)/shard_map/ppermute | solution.py:371
  45.1 9.6 %collective-permute-start.11 = (f32[4,80,128]{2,1,0:T(8,128)S(1)}, f32[4,80,128]{2,1,0:T(8,128)S(1)}, u32[]{:S(2)}, u32[]{:S(2)}) collective-permute-start(f32[4,80,128]{2,1,0:T(8,128)S(1)} %pad_maximum_fusion.1), channel_id=1, source_target_pairs={{0,2},{1,127},{2,4},{3,1},{4,6},{5,3},{6,8},{7,5},{8,10},{9,7},{10... | collective-permute-start | bytes 491528 | tf_op jit(solution)/shard_map/ppermute | solution.py:381
  48.9 5.8 %collective-permute-start.12 = (f32[3,80,128]{2,1,0:T(8,128)S(1)}, f32[3,80,128]{2,1,0:T(8,128)S(1)}, u32[]{:S(2)}, u32[]{:S(2)}) collective-permute-start(f32[3,80,128]{2,1,0:T(8,128)S(1)} %pad_maximum_fusion.4), channel_id=1, source_target_pairs={{0,4},{1,125},{2,6},{3,127},{4,8},{5,1},{6,10},{7,3},{8,12},{9,5},... | collective-permute-start | bytes 368648 | tf_op jit(solution)/shard_map/ppermute | solution.py:381
  54.7 4.0 %collective-permute-start.13 = (f32[3,80,128]{2,1,0:T(8,128)S(1)}, f32[3,80,128]{2,1,0:T(8,128)S(1)}, u32[]{:S(2)}, u32[]{:S(2)}) collective-permute-start(f32[3,80,128]{2,1,0:T(8,128)S(1)} %pad_maximum_fusion.5), channel_id=1, source_target_pairs={{0,1},{1,0},{2,3},{3,2},{4,5},{5,4},{6,7},{7,6},{8,9},{9,8},{10,11... | collective-permute-start | bytes 368648 | tf_op jit(solution)/shard_map/ppermute | solution.py:371

commit v2 on v1

--- a/solution.py
+++ b/solution.py
@@ -26,6 +26,8 @@
 I32 = jnp.int32
 
 STEPS = (2, 3, 4, 1, -1, -2, -3, -4)
+
+OPEN_VMEM = 54
 
 
 def derivative_table():
@@ -98,8 +100,14 @@
     ref[ROWS : ROWS + 8, :] = got[2 * ROWS : 2 * ROWS + 8]
 
 
-def prepare_kernel(me_ref, links_hbm, state_hbm, level_hbm, morton_hbm, ask_ref, near_ref, far_ref,
-                   slots_ref, rows_ref, links_ref, state_ref, level_ref, morton_ref, sems):
+def relay_rows(state, level):
+    high, low = split(state)
+    lev = jnp.broadcast_to(level.astype(F32), (16, OLD_CAP)).astype(BF16)
+    return jnp.concatenate([high, low, lev], axis=0)
+
+
+def open_kernel(me_ref, links_hbm, state_hbm, level_hbm, morton_hbm, ask_ref, near_ref, far_ref,
+                to_far_ref, to_sib_ref, links_ref, state_ref, level_ref, morton_ref, sems):
     pairs = ((links_hbm, links_ref), (morton_hbm, morton_ref), (level_hbm, level_ref), (state_hbm, state_ref))
     copies = [pltpu.make_async_copy(src, dst, sems.at[i]) for i, (src, dst) in enumerate(pairs)]
     for copy in copies:
@@ -107,24 +115,17 @@
     copies[0].wait()
     requests(me_ref[0], links_ref[...], ask_ref, near_ref, far_ref)
     copies[1].wait()
-    for i, row in enumerate(relay_slots(me_ref[0], morton_ref[...])):
-        slots_ref[i : i + 1, :] = row
+    sib, far, _ = relay_slots(me_ref[0], morton_ref[...])
     copies[2].wait()
-    rows_ref[2 * ROWS :, :] = jnp.broadcast_to(level_ref[...].astype(F32), (16, OLD_CAP)).astype(BF16)
     copies[3].wait()
-    high, low = split(state_ref[...])
-    rows_ref[0:ROWS, :] = high
-    rows_ref[ROWS : 2 * ROWS, :] = low
-
-
-def pack_kernel(rows_ref, slots_ref, far_ref, sib_ref):
-    lhs = rows_ref[...]
-    store_moved(far_ref, dot_nt(lhs, one_hot_rows(HALF, slots_ref[1:2, :])))
-    store_moved(sib_ref, dot_nt(lhs, one_hot_rows(HALF, slots_ref[0:1, :])))
-
-
-def home_kernel(rows_ref, slots_ref, home_ref):
-    got = dot_nt(rows_ref[...], one_hot_rows(NEW_DEV, slots_ref[2:3, :]))
+    lhs = relay_rows(state_ref[...], level_ref[...])
+    store_moved(to_far_ref, dot_nt(lhs, one_hot_rows(HALF, far)))
+    store_moved(to_sib_ref, dot_nt(lhs, one_hot_rows(HALF, sib)))
+
+
+def home_kernel(me_ref, state_ref, level_ref, morton_ref, home_ref):
+    _, _, home = relay_slots(me_ref[0], morton_ref[...])
+    got = dot_nt(relay_rows(state_ref[...], level_ref[...]), one_hot_rows(NEW_DEV, home))
     for c in range(BLOCKS):
         store_moved(home_ref.at[c], got[:, 128 * c : 128 * c + 128])
 
@@ -354,14 +355,14 @@
 HB = pl.BlockSpec(memory_space=pltpu.HBM)
 
 
-def call(kernel, outs, args, specs=None, scratch=(), flops=10**6):
+def call(kernel, outs, args, specs=None, scratch=(), flops=10**6, vmem=40):
     return pl.pallas_call(
         kernel,
         out_shape=[jax.ShapeDtypeStruct(s, d) for s, d in outs],
         in_specs=specs or [VM] * len(args),
         out_specs=[VM] * len(outs),
         scratch_shapes=[pltpu.VMEM(*s) if isinstance(s, tuple) else s for s in scratch],
-        compiler_params=pltpu.CompilerParams(vmem_limit_bytes=40 * 2**20),
+        compiler_params=pltpu.CompilerParams(vmem_limit_bytes=vmem * 2**20),
         cost_estimate=pl.CostEstimate(flops=flops, bytes_accessed=2**20, transcendentals=0),
     )(*args)
 
@@ -397,14 +398,14 @@
     level = level_old.reshape(1, OLD_CAP)
     morton = morton_old.reshape(1, OLD_CAP)
 
-    ask, near, far, slots, rows = call(
-        prepare_kernel,
+    ask, near, far, to_far, to_sib = call(
+        open_kernel,
         [
             ((8, CAP), I32),
             ((6, NEW_DEV), I32),
             ((6, NEW_DEV), I32),
-            ((3, OLD_CAP), I32),
-            ((2 * ROWS + 16, OLD_CAP), BF16),
+            ((MOVED_ROWS, HALF), F32),
+            ((MOVED_ROWS, HALF), F32),
         ],
         (me, neighbours, state, level, morton),
         [SM, HB, HB, HB, HB],
@@ -415,15 +416,19 @@
             ((1, OLD_CAP), I32),
             pltpu.SemaphoreType.DMA((4,)),
         ],
-    )
+        vmem=OPEN_VMEM,
+    )
+    from_far = swap_chips(to_far)
+    from_sib = swap_cores(to_sib)
     ask = ask.reshape(8, 1, CAP)
     got = swap_cores(ask[3:8])
-    to_far, to_sib = call(pack_kernel, [((MOVED_ROWS, HALF), F32)] * 2, (rows, slots))
-    got, to_far = lax.optimization_barrier((got, to_far))
+    (home,) = call(
+        home_kernel,
+        [((BLOCKS, MOVED_ROWS, 128), F32)],
+        (me, state, level, morton),
+        [SM, VM, VM, VM],
+    )
     a, b = outward_pair(ask[0:3], got)
-    from_far = swap_chips(to_far)
-    from_sib = swap_cores(to_sib)
-    (home,) = call(home_kernel, [((BLOCKS, MOVED_ROWS, 128), F32)], (rows, slots))
     post = swap_back(a, b)
     asked = jnp.concatenate(
         [post[1], post[0], post[2], got[0], a[2], a[0], b[1], b[0]], axis=0

time: 61.3 us -> 63.6 us (1.038)
  starting transfers between devices: 28.2 us -> 32.9 us
  waiting for transfers between devices: 14.2 us -> 11.5 us
  Pallas kernels: 14.2 us -> 15.7 us
  local copies, waits for them, and re-layouts: 3.53 us -> 2.2 us
    ppermute x7, starting transfers between devices: 8.86 us -> 26.1 us  [swap_cores(): return lax.ppermute(x, AXES, [(i, i ^ 1) for i in range(n)])]
    ppermute x6, starting transfers between devices: 19.3 us -> 5.61 us  [outward(): lax.ppermute(x, AXES, [(i, (i + (by if i % 2 == 0 else -by)) % n) for i i...]
    unnamed x10 -> x12, local copies, waits for them, and re-layouts: 3.41 us -> 0.03 us
    ppermute x1, waiting for transfers between devices: 2.33 us -> 0.01 us  [swap_chips(): lax.ppermute(x, AXES, [(i, (i + (1 if i % 2 else -1)) % n) for i in range...]
    pallas_call x10 -> x9, Pallas kernels: 14.2 us -> 15.7 us  [call(): pl.pallas_call(kernel, out_shape=[jax.ShapeDtypeStruct(s, d) for s, d in...]
    ppermute x1, starting transfers between devices: 0.01 us -> 1.25 us  [swap_chips(): lax.ppermute(x, AXES, [(i, (i + (1 if i % 2 else -1)) % n) for i in range...]
    slice x1, local copies, waits for them, and re-layouts: 0.01 us -> 0.69 us  [body(): got = swap_cores(ask[3:8])]
    slice x4, local copies, waits for them, and re-layouts: 0.02 us -> 0.7 us  [outward_pair(): a = outward(jnp.concatenate([own[0:2], got[1:3]], axis=0), 2)]
  transfers between devices with their start and end apart: 14 -> 14, of which waited for: 7 -> 6; matrix products, arithmetic and copies ran while one was open for 0% -> 2% of each run, Pallas kernels for 13% -> 11%
where the time goes in v2:
time: 63.6 us; the launch traced here: 63.4 us
  starting transfers between devices  32.9 us (52%)
  Pallas kernels  15.7 us (25%)
  waiting for transfers between devices  11.5 us (18%)
  local copies, waits for them, and re-layouts  2.2 us (3%)
  between operations  0.86 us (1%)
    ppermute x7, starting transfers between devices, swap_cores(): return lax.ppermute(x, AXES, [(i, i ^ 1) for i in range(n)])  26.1 us
    pallas_call x9, Pallas kernels, call(): pl.pallas_call(kernel, out_shape=[jax.ShapeDtypeStruct(s, d) for s, d in...  15.7 us
    ppermute x6, waiting for transfers between devices, outward(): lax.ppermute(x, AXES, [(i, (i + (by if i % 2 == 0 else -by)) % n) for i i...  8.51 us
    ppermute x6, starting transfers between devices, outward(): lax.ppermute(x, AXES, [(i, (i + (by if i % 2 == 0 else -by)) % n) for i i...  5.61 us
    ppermute x7, waiting for transfers between devices, swap_cores(): return lax.ppermute(x, AXES, [(i, i ^ 1) for i in range(n)])  3.02 us
  transfers between devices with their start and end apart: 14, of which 6 were waited for; matrix products, arithmetic and copies ran while one was open for 2% of the time, Pallas kernels for 11%

profile of v2, /device:TPU:1, one launch (start us, length us, event | category | flops | bytes accessed | tf_op | source)
XLA Modules:
  0.0 63.4 jit_solution(1434716952268274654)
XLA Ops:
  0.7 3.5 %shard_map.69 = (s32[8,128]{1,0:T(8,128)}, s32[6,512]{1,0:T(8,128)}, s32[6,512]{1,0:T(8,128)}, f32[328,256]{1,0:T(8,128)}, f32[328,256]{1,0:T(8,128)}) custom-call(s32[1]{0:T(128)} %bitcast.me_ref, s32[6,512]{1,0:T(8,128)} %links_hbm.1, f32[320,1024]{1,0:T(8,128)} %bitcast.30, s32[1,1024]{1,0:T(1,128)} %bitcast.32, s32[1,1024]{1,0:T(1,128)} %bitcast.34), custom_call_target="tpu_custom_call" | custom-call | flops 1000000 | bytes 1048576 | tf_op jit(solution)/shard_map/pallas_call | solution.py:359
  4.2 0.7 %slice_bitcast_fusion = s32[5,1,128]{2,0,1:T(8,128)S(1)} fusion(s32[8,128]{1,0:T(8,128)} %get-tuple-element.27), kind=kLoop, calls=%fused_computation.6 | loop fusion | bytes 5120 | tf_op jit(solution)/shard_map/slice | solution.py:424
  4.9 1.4 %collective-permute-start.2 = (s32[5,1,128]{2,0,1:T(8,128)S(1)}, s32[5,1,128]{2,0,1:T(8,128)S(1)}, u32[]{:S(2)}, u32[]{:S(2)}) collective-permute-start(s32[5,1,128]{2,0,1:T(8,128)S(1)} %slice_bitcast_fusion), channel_id=1, source_target_pairs={{0,1},{1,0},{2,3},{3,2},{4,5},{5,4},{6,7},{7,6},{8,9},{9,8},{10,11... | collective-permute-start | bytes 7688 | tf_op jit(solution)/shard_map/ppermute | solution.py:372
  6.3 1.2 %collective-permute-start = (f32[328,256]{1,0:T(8,128)}, f32[328,256]{1,0:T(8,128)S(1)}, u32[]{:S(2)}, u32[]{:S(2)}) collective-permute-start(f32[328,256]{1,0:T(8,128)} %get-tuple-element.25), channel_id=1, source_target_pairs={{0,127},{1,2},{2,1},{3,4},{4,3},{5,6},{6,5},{7,8},{8,7},{9,10},{10... | collective-permute-start | bytes 1007624 | tf_op jit(solution)/shard_map/ppermute | solution.py:377
  7.6 7.6 %collective-permute-start.1 = (f32[328,256]{1,0:T(8,128)}, f32[328,256]{1,0:T(8,128)S(1)}, u32[]{:S(2)}, u32[]{:S(2)}) collective-permute-start(f32[328,256]{1,0:T(8,128)} %get-tuple-element.26), channel_id=1, source_target_pairs={{0,1},{1,0},{2,3},{3,2},{4,5},{5,4},{6,7},{7,6},{8,9},{9,8},{10,11... | collective-permute-start | bytes 1007624 | tf_op jit(solution)/shard_map/ppermute | solution.py:372
  15.2 0.7 %slice_bitcast_fusion.1 = s32[2,1,128]{2,0,1:T(2,128)S(1)} fusion(s32[8,128]{1,0:T(8,128)} %get-tuple-element.27), kind=kLoop, calls=%fused_computation.10 | loop fusion | bytes 2048 | tf_op jit(solution)/shard_map/slice | solution.py:387
  15.9 0.7 %slice_bitcast_fusion.10 = s32[1,1,128]{2,0,1:T(1,128)S(1)} fusion(s32[8,128]{1,0:T(8,128)} %get-tuple-element.27), kind=kLoop, calls=%fused_computation.19 | loop fusion | bytes 1024 | tf_op jit(solution)/shard_map/slice | solution.py:386
  16.6 0.9 %shard_map.68.home_ref = f32[4,328,128]{2,1,0:T(8,128)S(1)} custom-call(s32[1]{0:T(128)} %bitcast.me_ref, f32[320,1024]{1,0:T(8,128)S(1)} %bitcast.31, s32[1,1024]{1,0:T(1,128)S(1)} %bitcast.33, s32[1,1024]{1,0:T(1,128)S(1)} %bitcast.35), custom_call_target="tpu_custom_call" | custom-call | flops 1000000 | bytes 1048576 | tf_op jit(solution)/shard_map/pallas_call | solution.py:359
  17.5 0.7 %collective-permute-start.4 = (s32[3,1,128]{2,0,1:T(4,128)S(1)}, s32[3,1,128]{2,0,1:T(4,128)S(1)}, u32[]{:S(2)}, u32[]{:S(2)}) collective-permute-start(s32[3,1,128]{2,0,1:T(4,128)S(1)} %pad_add_fusion.1), channel_id=1, source_target_pairs={{0,4},{1,125},{2,6},{3,127},{4,8},{5,1},{6,10},{7,3},{8,12},{9,5},... | collective-permute-start | bytes 4616 | tf_op jit(solution)/shard_map/ppermute | solution.py:382
  18.3 1.1 %collective-permute-start.3 = (s32[4,1,128]{2,0,1:T(4,128)S(1)}, s32[4,1,128]{2,0,1:T(4,128)S(1)}, u32[]{:S(2)}, u32[]{:S(2)}) collective-permute-start(s32[4,1,128]{2,0,1:T(4,128)S(1)} %pad_add_fusion), channel_id=1, source_target_pairs={{0,2},{1,127},{2,4},{3,1},{4,6},{5,3},{6,8},{7,5},{8,10},{9,7},{10... | collective-permute-start | bytes 6152 | tf_op jit(solution)/shard_map/ppermute | solution.py:382
  19.4 2.2 %collective-permute-done.4 = s32[3,1,128]{2,0,1:T(4,128)S(1)} collective-permute-done((s32[3,1,128]{2,0,1:T(4,128)S(1)}, s32[3,1,128]{2,0,1:T(4,128)S(1)}, u32[]{:S(2)}, u32[]{:S(2)}) %collective-permute-start.4) | collective-permute-done | bytes 1568 | tf_op jit(solution)/shard_map/ppermute | solution.py:382
  21.6 5.4 %collective-permute-start.5 = (s32[3,1,128]{2,0,1:T(4,128)S(1)}, s32[3,1,128]{2,0,1:T(4,128)S(1)}, u32[]{:S(2)}, u32[]{:S(2)}) collective-permute-start(s32[3,1,128]{2,0,1:T(4,128)S(1)} %pad_add_fusion.2), channel_id=1, source_target_pairs={{0,1},{1,0},{2,3},{3,2},{4,5},{5,4},{6,7},{7,6},{8,9},{9,8},{10,11... | collective-permute-start | bytes 4616 | tf_op jit(solution)/shard_map/ppermute | solution.py:372
  27.0 0.8 %collective-permute-done.5 = s32[3,1,128]{2,0,1:T(4,128)S(1)} collective-permute-done((s32[3,1,128]{2,0,1:T(4,128)S(1)}, s32[3,1,128]{2,0,1:T(4,128)S(1)}, u32[]{:S(2)}, u32[]{:S(2)}) %collective-permute-start.5) | collective-permute-done | bytes 1568 | tf_op jit(solution)/shard_map/ppermute | solution.py:372
  27.9 1.0 %shard_map.70 = (f32[4,328,128]{2,1,0:T(8,128)S(1)}, f32[3,80,128]{2,1,0:T(8,128)S(1)}, f32[5,80,128]{2,1,0:T(8,128)S(1)}) custom-call(s32[1]{0:T(128)} %bitcast.me_ref, f32[4,328,128]{2,1,0:T(8,128)S(1)} %shard_map.68.home_ref, f32[328,256]{1,0:T(8,128)S(1)} %collective-permute-done.far_ref, f32[328,256]{1,0:T(8,128)S(1)} %collective-permute-done.1.sib_ref, ...), custom_call_target="tpu_custom_call" | custom-call | flops 1000000 | bytes 1048576 | tf_op jit(solution)/shard_map/pallas_call | solution.py:359
  28.9 0.4 collective-permute-start.6
  29.3 1.1 %collective-permute-done.6.swap_ref = f32[5,80,128]{2,1,0:T(8,128)S(1)} collective-permute-done((f32[5,80,128]{2,1,0:T(8,128)S(1)}, f32[5,80,128]{2,1,0:T(8,128)S(1)}, u32[]{:S(2)}, u32[]{:S(2)}) %collective-permute-start.6) | collective-permute-done | bytes 204832 | tf_op jit(solution)/shard_map/ppermute | solution.py:372
  30.5 0.7 %collective-permute-start.7 = (f32[4,80,128]{2,1,0:T(8,128)S(1)}, f32[4,80,128]{2,1,0:T(8,128)S(1)}, u32[]{:S(2)}, u32[]{:S(2)}) collective-permute-start(f32[4,80,128]{2,1,0:T(8,128)S(1)} %pad_maximum_fusion), channel_id=1, source_target_pairs={{0,2},{1,127},{2,4},{3,1},{4,6},{5,3},{6,8},{7,5},{8,10},{9,7},{10... | collective-permute-start | bytes 491528 | tf_op jit(solution)/shard_map/ppermute | solution.py:382
  31.2 1.2 %collective-permute-start.8 = (f32[3,80,128]{2,1,0:T(8,128)S(1)}, f32[3,80,128]{2,1,0:T(8,128)S(1)}, u32[]{:S(2)}, u32[]{:S(2)}) collective-permute-start(f32[3,80,128]{2,1,0:T(8,128)S(1)} %pad_maximum_fusion.2), channel_id=1, source_target_pairs={{0,4},{1,125},{2,6},{3,127},{4,8},{5,1},{6,10},{7,3},{8,12},{9,5},... | collective-permute-start | bytes 368648 | tf_op jit(solution)/shard_map/ppermute | solution.py:382
  32.4 2.1 %shard_map.71 = (f32[4,320,128]{2,1,0:T(8,128)S(1)}, f32[6,80,512]{2,1,0:T(8,128)S(1)}) custom-call(bf16[128,192]{1,0:T(8,128)(2,1)S(1)} %copy-done.5, f32[4,328,128]{2,1,0:T(8,128)S(1)} %get-tuple-element.28.fields_ref.start_ref, s32[6,512]{1,0:T(8,128)S(1)} %copy-done.4), custom_call_target="tpu_custom_call" | custom-call | flops 1000000000 | bytes 1048576 | tf_op jit(solution)/shard_map/pallas_call | solution.py:359
  34.5 3.2 %collective-permute-done.8.b_ref = f32[3,80,128]{2,1,0:T(8,128)S(1)} collective-permute-done((f32[3,80,128]{2,1,0:T(8,128)S(1)}, f32[3,80,128]{2,1,0:T(8,128)S(1)}, u32[]{:S(2)}, u32[]{:S(2)}) %collective-permute-start.8) | collective-permute-done | bytes 122912 | tf_op jit(solution)/shard_map/ppermute | solution.py:382
  37.7 5.3 %collective-permute-start.9 = (f32[3,80,128]{2,1,0:T(8,128)S(1)}, f32[3,80,128]{2,1,0:T(8,128)S(1)}, u32[]{:S(2)}, u32[]{:S(2)}) collective-permute-start(f32[3,80,128]{2,1,0:T(8,128)S(1)} %pad_maximum_fusion.3), channel_id=1, source_target_pairs={{0,1},{1,0},{2,3},{3,2},{4,5},{5,4},{6,7},{7,6},{8,9},{9,8},{10,11... | collective-permute-start | bytes 368648 | tf_op jit(solution)/shard_map/ppermute | solution.py:372
  43.1 1.0 %shard_map.72.outer_ref = f32[6,80,512]{2,1,0:T(8,128)S(1)} custom-call(f32[6,80,512]{2,1,0:T(8,128)S(1)} %get-tuple-element.34.outer_ref, s32[6,512]{1,0:T(8,128)S(1)} %copy-done.1, f32[4,80,128]{2,1,0:T(8,128)S(1)} %collective-permute-done.7.a_ref, f32[3,80,128]{2,1,0:T(8,128)S(1)} %collective-permute-done.8.b_ref, ...), custom_call_target="tpu_custom_call" | custom-call | flops 1000000000 | bytes 1048576 | tf_op jit(solution)/shard_map/pallas_call | solution.py:359
  44.0 1.9 %shard_map.73 = (f32[4,320,128]{2,1,0:T(8,128)S(1)}, f32[3,80,128]{2,1,0:T(8,128)S(1)}, f32[5,80,128]{2,1,0:T(8,128)S(1)}) custom-call(f32[4,328,128]{2,1,0:T(8,128)S(1)} %get-tuple-element.28.fields_ref.start_ref, f32[4,320,128]{2,1,0:T(8,128)S(1)} %get-tuple-element.30.part_ref, f32[6,80,512]{2,1,0:T(8,128)S(1)} %shard_map.72.outer_ref, ...), custom_call_target="tpu_custom_call" | custom-call | flops 1000000 | bytes 1048576 | tf_op jit(solution)/shard_map/pallas_call | solution.py:359
  45.9 0.4 collective-permute-start.10
  46.4 1.1 %collective-permute-done.10.swap_ref = f32[5,80,128]{2,1,0:T(8,128)S(1)} collective-permute-done((f32[5,80,128]{2,1,0:T(8,128)S(1)}, f32[5,80,128]{2,1,0:T(8,128)S(1)}, u32[]{:S(2)}, u32[]{:S(2)}) %collective-permute-start.10) | collective-permute-done | bytes 204832 | tf_op jit(solution)/shard_map/ppermute | solution.py:372
  47.5 1.6 %collective-permute-start.11 = (f32[4,80,128]{2,1,0:T(8,128)S(1)}, f32[4,80,128]{2,1,0:T(8,128)S(1)}, u32[]{:S(2)}, u32[]{:S(2)}) collective-permute-start(f32[4,80,128]{2,1,0:T(8,128)S(1)} %pad_maximum_fusion.1), channel_id=1, source_target_pairs={{0,2},{1,127},{2,4},{3,1},{4,6},{5,3},{6,8},{7,5},{8,10},{9,7},{10... | collective-permute-start | bytes 491528 | tf_op jit(solution)/shard_map/ppermute | solution.py:382
  49.2 0.3 collective-permute-start.12
  49.4 2.1 %shard_map.74 = (f32[4,320,128]{2,1,0:T(8,128)S(1)}, f32[6,80,512]{2,1,0:T(8,128)S(1)}) custom-call(bf16[128,192]{1,0:T(8,128)(2,1)S(1)} %copy-done.5, f32[4,320,128]{2,1,0:T(8,128)S(1)} %get-tuple-element.38.fields_ref.section_ref, s32[6,512]{1,0:T(8,128)S(1)} %copy-done.4), custom_call_target="tpu_custom_call" | custom-call | flops 1000000000 | bytes 1048576 | tf_op jit(solution)/shard_map/pallas_call | solution.py:359
  51.6 3.1 %collective-permute-done.12.b_ref = f32[3,80,128]{2,1,0:T(8,128)S(1)} collective-permute-done((f32[3,80,128]{2,1,0:T(8,128)S(1)}, f32[3,80,128]{2,1,0:T(8,128)S(1)}, u32[]{:S(2)}, u32[]{:S(2)}) %collective-permute-start.12) | collective-permute-done | bytes 122912 | tf_op jit(solution)/shard_map/ppermute | solution.py:382
  54.7 5.4 %collective-permute-start.13 = (f32[3,80,128]{2,1,0:T(8,128)S(1)}, f32[3,80,128]{2,1,0:T(8,128)S(1)}, u32[]{:S(2)}, u32[]{:S(2)}) collective-permute-start(f32[3,80,128]{2,1,0:T(8,128)S(1)} %pad_maximum_fusion.5), channel_id=1, source_target_pairs={{0,1},{1,0},{2,3},{3,2},{4,5},{5,4},{6,7},{7,6},{8,9},{9,8},{10,11... | collective-permute-start | bytes 368648 | tf_op jit(solution)/shard_map/ppermute | solution.py:372
  60.1 1.0 %shard_map.75.outer_ref = f32[6,80,512]{2,1,0:T(8,128)S(1)} custom-call(f32[6,80,512]{2,1,0:T(8,128)S(1)} %get-tuple-element.43.outer_ref, s32[6,512]{1,0:T(8,128)S(1)} %copy-done.1, f32[4,80,128]{2,1,0:T(8,128)S(1)} %collective-permute-done.11.a_ref, f32[3,80,128]{2,1,0:T(8,128)S(1)} %collective-permute-done.12.b_ref, ...), custom_call_target="tpu_custom_call" | custom-call | flops 1000000000 | bytes 1048576 | tf_op jit(solution)/shard_map/pallas_call | solution.py:359
  61.1 2.3 %shard_map.76 = (f32[320,512]{1,0:T(8,128)}, f32[320,512]{1,0:T(8,128)}) custom-call(f32[4,328,128]{2,1,0:T(8,128)S(1)} %get-tuple-element.28.fields_ref.start_ref, f32[4,320,128]{2,1,0:T(8,128)S(1)} %get-tuple-element.38.fields_ref.section_ref, f32[4,320,128]{2,1,0:T(8,128)S(1)} %get-tuple-element.39.part_ref, f32[6,80,512]{2,1,0:T(8,128)S(1)} %shard_map.75.outer_ref, ...), custom_call_target="tpu_custom_call" | custom-call | flops 1000000 | bytes 1048576 | tf_op jit(solution)/shard_map/pallas_call | solution.py:359
  (45 shorter events, 0.3 us)
Async XLA Ops:
  0.6 15.9 %copy-start.3 = (s32[1024]{0:T(1024)S(1)}, s32[1024]{0:T(1024)}, u32[]{:S(2)}) copy-start(s32[1024]{0:T(1024)} %param.7) | copy-start | bytes 12292
  0.6 15.9 %copy-start.2 = (s32[1024]{0:T(1024)S(1)}, s32[1024]{0:T(1024)}, u32[]{:S(2)}) copy-start(s32[1024]{0:T(1024)} %param.6) | copy-start | bytes 12292
  0.7 15.9 %copy-start = (f32[5,64,1024]{2,1,0:T(8,128)S(1)}, f32[5,64,1024]{2,1,0:T(8,128)}, u32[]{:S(2)}) copy-start(f32[5,64,1024]{2,1,0:T(8,128)} %param.5) | copy-start | bytes 3932164
  4.9 12.6 %collective-permute-start.2 = (s32[5,1,128]{2,0,1:T(8,128)S(1)}, s32[5,1,128]{2,0,1:T(8,128)S(1)}, u32[]{:S(2)}, u32[]{:S(2)}) collective-permute-start(s32[5,1,128]{2,0,1:T(8,128)S(1)} %slice_bitcast_fusion), channel_id=1, source_target_pairs={{0,1},{1,0},{2,3},{3,2},{4,5},{5,4},{6,7},{7,6},{8,9},{9,8},{10,11... | collective-permute-start | bytes 7688 | tf_op jit(solution)/shard_map/ppermute | solution.py:372
  6.3 21.6 %collective-permute-start = (f32[328,256]{1,0:T(8,128)}, f32[328,256]{1,0:T(8,128)S(1)}, u32[]{:S(2)}, u32[]{:S(2)}) collective-permute-start(f32[328,256]{1,0:T(8,128)} %get-tuple-element.25), channel_id=1, source_target_pairs={{0,127},{1,2},{2,1},{3,4},{4,3},{5,6},{6,5},{7,8},{8,7},{9,10},{10... | collective-permute-start | bytes 1007624 | tf_op jit(solution)/shard_map/ppermute | solution.py:377
  7.6 20.3 %collective-permute-start.1 = (f32[328,256]{1,0:T(8,128)}, f32[328,256]{1,0:T(8,128)S(1)}, u32[]{:S(2)}, u32[]{:S(2)}) collective-permute-start(f32[328,256]{1,0:T(8,128)} %get-tuple-element.26), channel_id=1, source_target_pairs={{0,1},{1,0},{2,3},{3,2},{4,5},{5,4},{6,7},{7,6},{8,9},{9,8},{10,11... | collective-permute-start | bytes 1007624 | tf_op jit(solution)/shard_map/ppermute | solution.py:372
  17.5 14.9 %copy-start.4 = (s32[6,512]{1,0:T(8,128)S(1)}, s32[6,512]{1,0:T(8,128)}, u32[]{:S(2)}) copy-start(s32[6,512]{1,0:T(8,128)} %get-tuple-element.29.near_ref) | copy-start | bytes 36868
  17.5 14.9 %copy-start.5 = (bf16[128,192]{1,0:T(8,128)(2,1)S(1)}, bf16[128,192]{1,0:T(8,128)(2,1)}, u32[]{:S(2)}) copy-start(bf16[128,192]{1,0:T(8,128)(2,1)} %constant.13.clone.table_ref) | copy-start | bytes 147460
  17.5 4.0 %collective-permute-start.4 = (s32[3,1,128]{2,0,1:T(4,128)S(1)}, s32[3,1,128]{2,0,1:T(4,128)S(1)}, u32[]{:S(2)}, u32[]{:S(2)}) collective-permute-start(s32[3,1,128]{2,0,1:T(4,128)S(1)} %pad_add_fusion.1), channel_id=1, source_target_pairs={{0,4},{1,125},{2,6},{3,127},{4,8},{5,1},{6,10},{7,3},{8,12},{9,5},... | collective-permute-start | bytes 4616 | tf_op jit(solution)/shard_map/ppermute | solution.py:382
  18.3 3.3 %collective-permute-start.3 = (s32[4,1,128]{2,0,1:T(4,128)S(1)}, s32[4,1,128]{2,0,1:T(4,128)S(1)}, u32[]{:S(2)}, u32[]{:S(2)}) collective-permute-start(s32[4,1,128]{2,0,1:T(4,128)S(1)} %pad_add_fusion), channel_id=1, source_target_pairs={{0,2},{1,127},{2,4},{3,1},{4,6},{5,3},{6,8},{7,5},{8,10},{9,7},{10... | collective-permute-start | bytes 6152 | tf_op jit(solution)/shard_map/ppermute | solution.py:382
  21.6 6.3 %collective-permute-start.5 = (s32[3,1,128]{2,0,1:T(4,128)S(1)}, s32[3,1,128]{2,0,1:T(4,128)S(1)}, u32[]{:S(2)}, u32[]{:S(2)}) collective-permute-start(s32[3,1,128]{2,0,1:T(4,128)S(1)} %pad_add_fusion.2), channel_id=1, source_target_pairs={{0,1},{1,0},{2,3},{3,2},{4,5},{5,4},{6,7},{7,6},{8,9},{9,8},{10,11... | collective-permute-start | bytes 4616 | tf_op jit(solution)/shard_map/ppermute | solution.py:372
  28.9 1.5 %collective-permute-start.6 = (f32[5,80,128]{2,1,0:T(8,128)S(1)}, f32[5,80,128]{2,1,0:T(8,128)S(1)}, u32[]{:S(2)}, u32[]{:S(2)}) collective-permute-start(f32[5,80,128]{2,1,0:T(8,128)S(1)} %get-tuple-element.32), channel_id=1, source_target_pairs={{0,1},{1,0},{2,3},{3,2},{4,5},{5,4},{6,7},{7,6},{8,9},{9,8},{10,11... | collective-permute-start | bytes 614408 | tf_op jit(solution)/shard_map/ppermute | solution.py:372
  30.5 7.2 %collective-permute-start.7 = (f32[4,80,128]{2,1,0:T(8,128)S(1)}, f32[4,80,128]{2,1,0:T(8,128)S(1)}, u32[]{:S(2)}, u32[]{:S(2)}) collective-permute-start(f32[4,80,128]{2,1,0:T(8,128)S(1)} %pad_maximum_fusion), channel_id=1, source_target_pairs={{0,2},{1,127},{2,4},{3,1},{4,6},{5,3},{6,8},{7,5},{8,10},{9,7},{10... | collective-permute-start | bytes 491528 | tf_op jit(solution)/shard_map/ppermute | solution.py:382
  31.2 6.5 %collective-permute-start.8 = (f32[3,80,128]{2,1,0:T(8,128)S(1)}, f32[3,80,128]{2,1,0:T(8,128)S(1)}, u32[]{:S(2)}, u32[]{:S(2)}) collective-permute-start(f32[3,80,128]{2,1,0:T(8,128)S(1)} %pad_maximum_fusion.2), channel_id=1, source_target_pairs={{0,4},{1,125},{2,6},{3,127},{4,8},{5,1},{6,10},{7,3},{8,12},{9,5},... | collective-permute-start | bytes 368648 | tf_op jit(solution)/shard_map/ppermute | solution.py:382
  32.4 10.7 %copy-start.1 = (s32[6,512]{1,0:T(8,128)S(1)}, s32[6,512]{1,0:T(8,128)}, u32[]{:S(2)}) copy-start(s32[6,512]{1,0:T(8,128)} %get-tuple-element.35.far_ref) | copy-start | bytes 36868
  37.7 6.3 %collective-permute-start.9 = (f32[3,80,128]{2,1,0:T(8,128)S(1)}, f32[3,80,128]{2,1,0:T(8,128)S(1)}, u32[]{:S(2)}, u32[]{:S(2)}) collective-permute-start(f32[3,80,128]{2,1,0:T(8,128)S(1)} %pad_maximum_fusion.3), channel_id=1, source_target_pairs={{0,1},{1,0},{2,3},{3,2},{4,5},{5,4},{6,7},{7,6},{8,9},{9,8},{10,11... | collective-permute-start | bytes 368648 | tf_op jit(solution)/shard_map/ppermute | solution.py:372
  45.9 1.5 %collective-permute-start.10 = (f32[5,80,128]{2,1,0:T(8,128)S(1)}, f32[5,80,128]{2,1,0:T(8,128)S(1)}, u32[]{:S(2)}, u32[]{:S(2)}) collective-permute-start(f32[5,80,128]{2,1,0:T(8,128)S(1)} %get-tuple-element.41), channel_id=1, source_target_pairs={{0,1},{1,0},{2,3},{3,2},{4,5},{5,4},{6,7},{7,6},{8,9},{9,8},{10,11... | collective-permute-start | bytes 614408 | tf_op jit(solution)/shard_map/ppermute | solution.py:372
  47.5 7.1 %collective-permute-start.11 = (f32[4,80,128]{2,1,0:T(8,128)S(1)}, f32[4,80,128]{2,1,0:T(8,128)S(1)}, u32[]{:S(2)}, u32[]{:S(2)}) collective-permute-start(f32[4,80,128]{2,1,0:T(8,128)S(1)} %pad_maximum_fusion.1), channel_id=1, source_target_pairs={{0,2},{1,127},{2,4},{3,1},{4,6},{5,3},{6,8},{7,5},{8,10},{9,7},{10... | collective-permute-start | bytes 491528 | tf_op jit(solution)/shard_map/ppermute | solution.py:382
  49.2 5.5 %collective-permute-start.12 = (f32[3,80,128]{2,1,0:T(8,128)S(1)}, f32[3,80,128]{2,1,0:T(8,128)S(1)}, u32[]{:S(2)}, u32[]{:S(2)}) collective-permute-start(f32[3,80,128]{2,1,0:T(8,128)S(1)} %pad_maximum_fusion.4), channel_id=1, source_target_pairs={{0,4},{1,125},{2,6},{3,127},{4,8},{5,1},{6,10},{7,3},{8,12},{9,5},... | collective-permute-start | bytes 368648 | tf_op jit(solution)/shard_map/ppermute | solution.py:382
  54.7 6.4 %collective-permute-start.13 = (f32[3,80,128]{2,1,0:T(8,128)S(1)}, f32[3,80,128]{2,1,0:T(8,128)S(1)}, u32[]{:S(2)}, u32[]{:S(2)}) collective-permute-start(f32[3,80,128]{2,1,0:T(8,128)S(1)} %pad_maximum_fusion.5), channel_id=1, source_target_pairs={{0,1},{1,0},{2,3},{3,2},{4,5},{5,4},{6,7},{7,6},{8,9},{9,8},{10,11... | collective-permute-start | bytes 368648 | tf_op jit(solution)/shard_map/ppermute | solution.py:372

commit v3 on v2

--- a/solution.py
+++ b/solution.py
@@ -26,8 +26,6 @@
 I32 = jnp.int32
 
 STEPS = (2, 3, 4, 1, -1, -2, -3, -4)
-
-OPEN_VMEM = 54
 
 
 def derivative_table():
@@ -106,21 +104,28 @@
     return jnp.concatenate([high, low, lev], axis=0)
 
 
-def open_kernel(me_ref, links_hbm, state_hbm, level_hbm, morton_hbm, ask_ref, near_ref, far_ref,
-                to_far_ref, to_sib_ref, links_ref, state_ref, level_ref, morton_ref, sems):
+def open_kernel(me_ref, links_hbm, state_hbm, level_hbm, morton_hbm, own_ask_ref, swap_ask_ref, near_ref, far_ref,
+                state_ref, level_ref, morton_ref, links_ref, sems):
     pairs = ((links_hbm, links_ref), (morton_hbm, morton_ref), (level_hbm, level_ref), (state_hbm, state_ref))
     copies = [pltpu.make_async_copy(src, dst, sems.at[i]) for i, (src, dst) in enumerate(pairs)]
     for copy in copies:
         copy.start()
     copies[0].wait()
-    requests(me_ref[0], links_ref[...], ask_ref, near_ref, far_ref)
-    copies[1].wait()
+    ask = requests(me_ref[0], links_ref[...], near_ref, far_ref)
+    for t in range(8):
+        if t < 3:
+            own_ask_ref[t] = ask[t : t + 1]
+        else:
+            swap_ask_ref[t - 3] = ask[t : t + 1]
+    for copy in copies[1:]:
+        copy.wait()
+
+
+def pack_kernel(me_ref, state_ref, level_ref, morton_ref, far_ref, sib_ref):
     sib, far, _ = relay_slots(me_ref[0], morton_ref[...])
-    copies[2].wait()
-    copies[3].wait()
     lhs = relay_rows(state_ref[...], level_ref[...])
-    store_moved(to_far_ref, dot_nt(lhs, one_hot_rows(HALF, far)))
-    store_moved(to_sib_ref, dot_nt(lhs, one_hot_rows(HALF, sib)))
+    store_moved(far_ref, dot_nt(lhs, one_hot_rows(HALF, far)))
+    store_moved(sib_ref, dot_nt(lhs, one_hot_rows(HALF, sib)))
 
 
 def home_kernel(me_ref, state_ref, level_ref, morton_ref, home_ref):
@@ -130,7 +135,7 @@
         store_moved(home_ref.at[c], got[:, 128 * c : 128 * c + 128])
 
 
-def requests(me, links, ask_ref, near_ref, far_ref):
+def requests(me, links, near_ref, far_ref):
     owner = links >> 9
     slot = links & (NEW_DEV - 1)
     gap = ((owner - me + 192) & 127) - 64
@@ -159,7 +164,7 @@
         high = ((s >> 8) + 2 * (f ^ 1)).astype(F32)
         lhs = jnp.concatenate([masks[f] * low, masks[f] * high], axis=0).astype(BF16)
         total = total + dot_nt(lhs, one_hot_rows(CAP, rank))
-    ask_ref[...] = total[0:8].astype(I32) + 256 * total[8:16].astype(I32)
+    return total[0:8].astype(I32) + 256 * total[8:16].astype(I32)
 
 
 def lower_half(shape):
@@ -232,28 +237,29 @@
     return [(sign * flux[v]) - SPEED * w[v] for v in range(FIELDS)]
 
 
-def reply(fields, ask_ref, got_ref, own_ref, swap_ref):
-    ask = ask_ref[...]
-    code = jnp.concatenate([ask[t : t + 1, :] for t in range(8)], axis=1)
+def reply(fields, ask, got_ref, out_ref):
+    chunks = ask.shape[0]
+    code = jnp.concatenate([ask[t : t + 1, :] for t in range(chunks)], axis=1)
     hot = one_hot_rows(NEW_DEV, code & (NEW_DEV - 1))
     high, low = split(fields)
     both = dot(jnp.concatenate([high, low], axis=0), hot)
-    for t in range(8):
+    for t in range(chunks):
         spot = slice(CAP * t, CAP * t + CAP)
         got_ref[t] = both[0:ROWS, spot] + both[ROWS:, spot]
-    for t in range(8):
+    for t in range(chunks):
         face = ask[t : t + 1, :] >> 9
         for v in range(FIELDS):
             x = trace(got_ref, t, v, 0)
             for f in range(1, 6):
                 x = jnp.where(face == f, trace(got_ref, t, v, f), x)
-            if t < 3:
-                own_ref[t, 16 * v : 16 * v + 16, :] = x
-            else:
-                swap_ref[t - 3, 16 * v : 16 * v + 16, :] = x
-
-
-def first_kernel(me_ref, home_ref, far_ref, sib_ref, ask_ref, start_ref, own_ref, swap_ref, got_ref):
+            out_ref[t, 16 * v : 16 * v + 16, :] = x
+
+
+def own_kernel(fields_ref, ask_ref, own_ref, got_ref):
+    reply(wide(fields_ref, ROWS), ask_ref[0:3, :], got_ref, own_ref)
+
+
+def first_kernel(me_ref, home_ref, far_ref, sib_ref, ask_ref, start_ref, swap_ref, got_ref):
     even = (me_ref[0] & 1) == 0
     for c in range(2):
         spot = slice(128 * c, 128 * c + 128)
@@ -261,7 +267,7 @@
         far = far_ref[:, spot]
         start_ref[c] = home_ref[c] + jnp.where(even, far, sib)
         start_ref[c + 2] = home_ref[c + 2] + jnp.where(even, sib, far)
-    reply(wide(start_ref, ROWS), ask_ref, got_ref, own_ref, swap_ref)
+    reply(wide(start_ref, ROWS), ask_ref[3:8, :], got_ref, swap_ref)
 
 
 def near_kernel(table_ref, fields_ref, near_ref, part_ref, outer_ref, high_ref, low_ref):
@@ -315,17 +321,20 @@
         sum_ref[f] = outer_ref[f] + both[0:TRACE_ROWS] + both[TRACE_ROWS:]
 
 
-def add_outer(part_ref, outer_ref, far_ref, post_ref, sum_ref):
+def place_rest(outer_ref, far_ref, post_ref, side_ref):
     lhs = ghost_rows([post_ref[1], post_ref[0], post_ref[2]])
-    sum_ref[...] = part_ref[...]
     for f in range(6):
         both = dot(lhs, one_hot_rows(3 * CAP, far_ref[f : f + 1, :]))
-        for c in range(BLOCKS):
-            spot = slice(128 * c, 128 * c + 128)
-            outer = outer_ref[f, :, spot] + both[0:TRACE_ROWS, spot] + both[TRACE_ROWS:, spot]
-            plus = side_term([outer[16 * v : 16 * v + 16] for v in range(FIELDS)], f)
-            for v in range(FIELDS):
-                add_on_face(sum_ref, c, v, f, 3.0 * plus[v])
+        side_ref[f] = outer_ref[f] + both[0:TRACE_ROWS] + both[TRACE_ROWS:]
+
+
+def add_outer(part_ref, side_ref, sum_ref, c):
+    sum_ref[c] = part_ref[c]
+    for f in range(6):
+        outer = side_ref[f, :, 128 * c : 128 * c + 128]
+        plus = side_term([outer[16 * v : 16 * v + 16] for v in range(FIELDS)], f)
+        for v in range(FIELDS):
+            add_on_face(sum_ref, c, v, f, 3.0 * plus[v])
 
 
 def metric_of(start_ref, c):
@@ -333,21 +342,29 @@
 
 
 def second_kernel(start_ref, part_ref, outer_ref, far_ref, ask_ref, post_ref,
-                  section_ref, own_ref, out_ref, sum_ref, got_ref):
-    add_outer(part_ref, outer_ref, far_ref, post_ref, sum_ref)
+                  section_ref, swap_ref, side_ref, sum_ref, got_ref):
+    place_rest(outer_ref, far_ref, post_ref, side_ref)
     for c in range(BLOCKS):
+        add_outer(part_ref, side_ref, sum_ref, c)
         section_ref[c] = start_ref[c, 0:ROWS, :] - (DT * metric_of(start_ref, c)) * sum_ref[c]
-    reply(wide(section_ref, ROWS), ask_ref, got_ref, own_ref, out_ref)
+    reply(wide(section_ref, ROWS), ask_ref[3:8, :], got_ref, swap_ref)
 
 
 def last_kernel(start_ref, section_ref, part_ref, outer_ref, far_ref, post_ref,
-                state_ref, rate_ref, sum_ref):
-    add_outer(part_ref, outer_ref, far_ref, post_ref, sum_ref)
+                state_hbm, rate_hbm, side_ref, sum_ref, state_ref, rate_ref, sems):
+    place_rest(outer_ref, far_ref, post_ref, side_ref)
+    copies = []
     for c in range(BLOCKS):
-        spot = slice(128 * c, 128 * c + 128)
+        add_outer(part_ref, side_ref, sum_ref, c)
         rate = -metric_of(start_ref, c) * sum_ref[c]
-        rate_ref[:, spot] = rate
-        state_ref[:, spot] = 0.5 * start_ref[c, 0:ROWS, :] + 0.5 * (section_ref[c] + DT * rate)
+        rate_ref[c] = rate
+        state_ref[c] = 0.5 * start_ref[c, 0:ROWS, :] + 0.5 * (section_ref[c] + DT * rate)
+        for i, (src, dst) in enumerate(((rate_ref, rate_hbm), (state_ref, state_hbm))):
+            copy = pltpu.make_async_copy(src.at[c], dst.at[:, pl.ds(128 * c, 128)], sems.at[i, c])
+            copy.start()
+            copies.append(copy)
+    for copy in copies:
+        copy.wait()
 
 
 VM = pl.BlockSpec(memory_space=pltpu.VMEM)
@@ -355,14 +372,14 @@
 HB = pl.BlockSpec(memory_space=pltpu.HBM)
 
 
-def call(kernel, outs, args, specs=None, scratch=(), flops=10**6, vmem=40):
+def call(kernel, outs, args, specs=None, scratch=(), flops=10**6, outs_in=None):
     return pl.pallas_call(
         kernel,
         out_shape=[jax.ShapeDtypeStruct(s, d) for s, d in outs],
         in_specs=specs or [VM] * len(args),
-        out_specs=[VM] * len(outs),
+        out_specs=[outs_in or VM] * len(outs),
         scratch_shapes=[pltpu.VMEM(*s) if isinstance(s, tuple) else s for s in scratch],
-        compiler_params=pltpu.CompilerParams(vmem_limit_bytes=vmem * 2**20),
+        compiler_params=pltpu.CompilerParams(vmem_limit_bytes=40 * 2**20),
         cost_estimate=pl.CostEstimate(flops=flops, bytes_accessed=2**20, transcendentals=0),
     )(*args)
 
@@ -394,54 +411,58 @@
 
 def body(state_old, level_old, morton_old, neighbours):
     me = lax.axis_index(AXES).astype(I32).reshape(1)
-    state = state_old.reshape(ROWS, OLD_CAP)
-    level = level_old.reshape(1, OLD_CAP)
-    morton = morton_old.reshape(1, OLD_CAP)
-
-    ask, near, far, to_far, to_sib = call(
+    inputs = [
+        pltpu.with_memory_space_constraint(x, pltpu.HBM)
+        for x in (
+            neighbours,
+            state_old.reshape(ROWS, OLD_CAP),
+            level_old.reshape(1, OLD_CAP),
+            morton_old.reshape(1, OLD_CAP),
+        )
+    ]
+    own_ask, swap_ask, near, far, state, level, morton = call(
         open_kernel,
         [
-            ((8, CAP), I32),
+            ((3, 1, CAP), I32),
+            ((5, 1, CAP), I32),
             ((6, NEW_DEV), I32),
-            ((6, NEW_DEV), I32),
-            ((MOVED_ROWS, HALF), F32),
-            ((MOVED_ROWS, HALF), F32),
-        ],
-        (me, neighbours, state, level, morton),
-        [SM, HB, HB, HB, HB],
-        [
             ((6, NEW_DEV), I32),
             ((ROWS, OLD_CAP), F32),
             ((1, OLD_CAP), I32),
             ((1, OLD_CAP), I32),
-            pltpu.SemaphoreType.DMA((4,)),
         ],
-        vmem=OPEN_VMEM,
-    )
+        (me, *inputs),
+        [SM, HB, HB, HB, HB],
+        [((6, NEW_DEV), I32), pltpu.SemaphoreType.DMA((4,))],
+    )
+    got = swap_cores(swap_ask)
+    relay = [SM, VM, VM, VM]
+    to_far, to_sib = call(pack_kernel, [((MOVED_ROWS, HALF), F32)] * 2, (me, state, level, morton), relay)
+    got, to_far, to_sib, morton = lax.optimization_barrier((got, to_far, to_sib, morton))
+    a, b = outward_pair(own_ask, got)
     from_far = swap_chips(to_far)
     from_sib = swap_cores(to_sib)
-    ask = ask.reshape(8, 1, CAP)
-    got = swap_cores(ask[3:8])
-    (home,) = call(
-        home_kernel,
-        [((BLOCKS, MOVED_ROWS, 128), F32)],
-        (me, state, level, morton),
-        [SM, VM, VM, VM],
-    )
-    a, b = outward_pair(ask[0:3], got)
+    (home,) = call(home_kernel, [((BLOCKS, MOVED_ROWS, 128), F32)], (me, state, level, morton), relay)
     post = swap_back(a, b)
     asked = jnp.concatenate(
         [post[1], post[0], post[2], got[0], a[2], a[0], b[1], b[0]], axis=0
     )
 
-    chunks = [((3, TRACE_ROWS, CAP), F32), ((5, TRACE_ROWS, CAP), F32)]
-    got_scratch = ((8, ROWS, CAP), F32)
+    swapped = ((5, TRACE_ROWS, CAP), F32)
+    got_scratch = ((5, ROWS, CAP), F32)
     blocks = ((BLOCKS, ROWS, 128), F32)
     sides = ((6, TRACE_ROWS, NEW_DEV), F32)
     table = jnp.asarray(stacked_table())
 
-    def neighbours_of(fields, own, swap):
+    def neighbours_of(fields, swap):
         got = swap_cores(swap)
+        (own,) = call(
+            own_kernel,
+            [((3, TRACE_ROWS, CAP), F32)],
+            (fields, asked),
+            None,
+            [((3, ROWS, CAP), F32)],
+        )
         a, b = outward_pair(own, got)
         part, outer = call(
             near_kernel,
@@ -456,28 +477,29 @@
         (outer,) = call(direct_kernel, [sides], (outer, far, a, b, got), flops=10**9)
         return part, outer, far, post
 
-    start, own, swap = call(
+    start, swap = call(
         first_kernel,
-        [((BLOCKS, MOVED_ROWS, 128), F32)] + chunks,
+        [((BLOCKS, MOVED_ROWS, 128), F32), swapped],
         (me, home, from_far, from_sib, asked),
         [SM, VM, VM, VM, VM],
         [got_scratch],
     )
-    part, outer, far, post = neighbours_of(start, own, swap)
-    section, own, swap = call(
+    part, outer, far, post = neighbours_of(start, swap)
+    section, swap = call(
         second_kernel,
-        [blocks] + chunks,
+        [blocks, swapped],
         (start, part, outer, far, asked, post),
         None,
-        [blocks, got_scratch],
-    )
-    part, outer, far, post = neighbours_of(section, own, swap)
+        [sides, blocks, got_scratch],
+    )
+    part, outer, far, post = neighbours_of(section, swap)
     new_state, rate = call(
         last_kernel,
         [((ROWS, NEW_DEV), F32)] * 2,
         (start, section, part, outer, far, post),
         None,
-        [blocks],
+        [sides, blocks, blocks, blocks, pltpu.SemaphoreType.DMA((2, BLOCKS))],
+        outs_in=HB,
     )
     shape = (FIELDS, DOFS, NEW_DEV)
     return new_state.reshape(shape), rate.reshape(shape)

time: 63.6 us -> 56.8 us (0.89)
  starting transfers between devices: 32.9 us -> 28.2 us
  local copies, waits for them, and re-layouts: 2.2 us -> 0.12 us
    ppermute x7, starting transfers between devices: 26.1 us -> 8.93 us  [swap_cores(): return lax.ppermute(x, AXES, [(i, i ^ 1) for i in range(n)])]
    ppermute x6, starting transfers between devices: 5.61 us -> 19.3 us  [outward(): lax.ppermute(x, AXES, [(i, (i + (by if i % 2 == 0 else -by)) % n) for i i...]
    ppermute x1, waiting for transfers between devices: 0.01 us -> 2.61 us  [swap_chips(): lax.ppermute(x, AXES, [(i, (i + (1 if i % 2 else -1)) % n) for i in range...]
    ppermute x7, waiting for transfers between devices: 3.02 us -> 1.36 us  [swap_cores(): return lax.ppermute(x, AXES, [(i, i ^ 1) for i in range(n)])]
    ppermute x1, starting transfers between devices: 1.25 us -> 0.01 us  [swap_chips(): lax.ppermute(x, AXES, [(i, (i + (1 if i % 2 else -1)) % n) for i in range...]
    slice x1 -> x0, local copies, waits for them, and re-layouts: 0.69 us -> none  [body(): got = swap_cores(ask[3:8])]
    slice x4, local copies, waits for them, and re-layouts: 0.7 us -> 0.02 us  [outward_pair(): a = outward(jnp.concatenate([own[0:2], got[1:3]], axis=0), 2)]
    slice x5, local copies, waits for them, and re-layouts: 0.72 us -> 0.03 us  [outward_pair(): b = outward(jnp.concatenate([own[2:3], got[3:5]], axis=0), 4)]
  transfers between devices with their start and end apart: 14 -> 14, of which waited for: 6 -> 6; matrix products, arithmetic and copies ran while one was open for 2% -> 0% of each run, Pallas kernels for 11% -> 16%
where the time goes in v3:
time: 56.8 us; the launch traced here: 56.6 us
  starting transfers between devices  28.2 us (50%)
  Pallas kernels  15.2 us (27%)
  waiting for transfers between devices  12 us (21%)
  between operations  1.05 us (2%)
    ppermute x6, starting transfers between devices, outward(): lax.ppermute(x, AXES, [(i, (i + (by if i % 2 == 0 else -by)) % n) for i i...  19.3 us
    pallas_call x12, Pallas kernels, call(): pl.pallas_call(kernel, out_shape=[jax.ShapeDtypeStruct(s, d) for s, d in...  15.2 us
    ppermute x7, starting transfers between devices, swap_cores(): return lax.ppermute(x, AXES, [(i, i ^ 1) for i in range(n)])  8.93 us
    ppermute x6, waiting for transfers between devices, outward(): lax.ppermute(x, AXES, [(i, (i + (by if i % 2 == 0 else -by)) % n) for i i...  8.04 us
    ppermute x1, waiting for transfers between devices, swap_chips(): lax.ppermute(x, AXES, [(i, (i + (1 if i % 2 else -1)) % n) for i in range...  2.61 us
    ppermute x7, waiting for transfers between devices, swap_cores(): return lax.ppermute(x, AXES, [(i, i ^ 1) for i in range(n)])  1.36 us
  transfers between devices with their start and end apart: 14, of which 6 were waited for; matrix products, arithmetic and copies ran while one was open for 0% of the time, Pallas kernels for 16%

profile of v3, /device:TPU:1, one launch (start us, length us, event | category | flops | bytes accessed | tf_op | source)
XLA Modules:
  0.0 56.6 jit_solution(16174451416394043160)
XLA Ops:
  0.6 1.5 %shard_map.68 = (s32[3,1,128]{2,1,0:T(1,128)S(1)}, s32[5,1,128]{2,1,0:T(1,128)S(1)}, s32[6,512]{1,0:T(8,128)S(1)}, s32[6,512]{1,0:T(8,128)S(1)}, f32[320,1024]{1...) custom-call(s32[1]{0:T(128)} %bitcast.me_ref, s32[6,512]{1,0:T(8,128)} %links_hbm.1, f32[320,1024]{1,0:T(8,128)} %bitcast.22, ...), custom_call_target="tpu_custom_call" | custom-call | flops 1000000 | bytes 1048576 | tf_op jit(solution)/shard_map/pallas_call | solution.py:376
  2.1 1.5 %collective-permute-start = (s32[5,1,128]{2,1,0:T(1,128)S(1)}, s32[5,1,128]{2,1,0:T(1,128)S(1)}, u32[]{:S(2)}, u32[]{:S(2)}) collective-permute-start(s32[5,1,128]{2,1,0:T(1,128)S(1)} %get-tuple-element.33), channel_id=1, source_target_pairs={{0,1},{1,0},{2,3},{3,2},{4,5},{5,4},{6,7},{7,6},{8,9},{9,8},{10,11... | collective-permute-start | bytes 7688 | tf_op jit(solution)/shard_map/ppermute | solution.py:389
  3.6 0.9 %shard_map.69 = (f32[328,256]{1,0:T(8,128)S(1)}, f32[328,256]{1,0:T(8,128)S(1)}) custom-call(s32[1]{0:T(128)} %bitcast.me_ref, f32[320,1024]{1,0:T(8,128)S(1)} %get-tuple-element.31.state_ref, s32[1,1024]{1,0:T(1,128)S(1)} %get-tuple-element.32.level_ref, s32[1,1024]{1,0:T(1,128)S(1)} %get-tuple-element.37.morton_ref), custom_call_target="tpu_custom_call" | custom-call | flops 1000000 | bytes 1048576 | tf_op jit(solution)/shard_map/pallas_call | solution.py:376
  4.6 8.7 %collective-permute-start.4 = (s32[3,1,128]{2,1,0:T(1,128)S(1)}, s32[3,1,128]{2,1,0:T(1,128)S(1)}, u32[]{:S(2)}, u32[]{:S(2)}) collective-permute-start(s32[3,1,128]{2,1,0:T(1,128)S(1)} %pad_add_fusion.1), channel_id=1, source_target_pairs={{0,4},{1,125},{2,6},{3,127},{4,8},{5,1},{6,10},{7,3},{8,12},{9,5},... | collective-permute-start | bytes 4616 | tf_op jit(solution)/shard_map/ppermute | solution.py:399
  13.3 0.8 %collective-permute-start.3 = (s32[4,1,128]{2,1,0:T(1,128)S(1)}, s32[4,1,128]{2,1,0:T(1,128)S(1)}, u32[]{:S(2)}, u32[]{:S(2)}) collective-permute-start(s32[4,1,128]{2,1,0:T(1,128)S(1)} %pad_add_fusion), channel_id=1, source_target_pairs={{0,2},{1,127},{2,4},{3,1},{4,6},{5,3},{6,8},{7,5},{8,10},{9,7},{10... | collective-permute-start | bytes 6152 | tf_op jit(solution)/shard_map/ppermute | solution.py:399
  14.1 0.4 collective-permute-start.2
  14.5 1.5 %collective-permute-done.3 = s32[4,1,128]{2,1,0:T(1,128)S(1)} collective-permute-done((s32[4,1,128]{2,1,0:T(1,128)S(1)}, s32[4,1,128]{2,1,0:T(1,128)S(1)}, u32[]{:S(2)}, u32[]{:S(2)}) %collective-permute-start.3) | collective-permute-done | bytes 2080 | tf_op jit(solution)/shard_map/ppermute | solution.py:399
  16.1 1.1 %collective-permute-start.5 = (s32[3,1,128]{2,1,0:T(1,128)S(1)}, s32[3,1,128]{2,1,0:T(1,128)S(1)}, u32[]{:S(2)}, u32[]{:S(2)}) collective-permute-start(s32[3,1,128]{2,1,0:T(1,128)S(1)} %pad_add_fusion.2), channel_id=1, source_target_pairs={{0,1},{1,0},{2,3},{3,2},{4,5},{5,4},{6,7},{7,6},{8,9},{9,8},{10,11... | collective-permute-start | bytes 4616 | tf_op jit(solution)/shard_map/ppermute | solution.py:389
  17.1 0.9 %shard_map.70.home_ref = f32[4,328,128]{2,1,0:T(8,128)S(1)} custom-call(s32[1]{0:T(128)} %bitcast.me_ref, f32[320,1024]{1,0:T(8,128)S(1)} %get-tuple-element.31.state_ref, s32[1,1024]{1,0:T(1,128)S(1)} %get-tuple-element.32.level_ref, s32[1,1024]{1,0:T(1,128)S(1)} %get-tuple-element.37.morton_ref), custom_call_target="tpu_custom_call" | custom-call | flops 1000000 | bytes 1048576 | tf_op jit(solution)/shard_map/pallas_call | solution.py:376
  18.1 2.6 %collective-permute-done.1.far_ref = f32[328,256]{1,0:T(8,128)S(1)} collective-permute-done((f32[328,256]{1,0:T(8,128)S(1)}, f32[328,256]{1,0:T(8,128)S(1)}, u32[]{:S(2)}, u32[]{:S(2)}) %collective-permute-start.1) | collective-permute-done | bytes 335904 | tf_op jit(solution)/shard_map/ppermute | solution.py:394
  20.7 0.8 %shard_map.71 = (f32[4,328,128]{2,1,0:T(8,128)S(1)}, f32[5,80,128]{2,1,0:T(8,128)S(1)}) custom-call(s32[1]{0:T(128)} %bitcast.me_ref, f32[4,328,128]{2,1,0:T(8,128)S(1)} %shard_map.70.home_ref, f32[328,256]{1,0:T(8,128)S(1)} %collective-permute-done.1.far_ref, f32[328,256]{1,0:T(8,128)S(1)} %collective-permute-done.2.sib_ref, s32[8,128]{1,0:T(8,128)S(1)} %concatenate.33.ask_ref), custom_call_target="tpu_custom_call" | custom-call | flops 1000000 | bytes 1048576 | tf_op jit(solution)/shard_map/pallas_call | solution.py:376
  21.5 0.2 collective-permute-start.6
  21.7 0.5 shard_map.73
  22.2 0.8 %collective-permute-done.6.swap_ref = f32[5,80,128]{2,1,0:T(8,128)S(1)} collective-permute-done((f32[5,80,128]{2,1,0:T(8,128)S(1)}, f32[5,80,128]{2,1,0:T(8,128)S(1)}, u32[]{:S(2)}, u32[]{:S(2)}) %collective-permute-start.6) | collective-permute-done | bytes 204832 | tf_op jit(solution)/shard_map/ppermute | solution.py:389
  23.0 5.5 %collective-permute-start.7 = (f32[4,80,128]{2,1,0:T(8,128)S(1)}, f32[4,80,128]{2,1,0:T(8,128)S(1)}, u32[]{:S(2)}, u32[]{:S(2)}) collective-permute-start(f32[4,80,128]{2,1,0:T(8,128)S(1)} %pad_maximum_fusion), channel_id=1, source_target_pairs={{0,2},{1,127},{2,4},{3,1},{4,6},{5,3},{6,8},{7,5},{8,10},{9,7},{10... | collective-permute-start | bytes 491528 | tf_op jit(solution)/shard_map/ppermute | solution.py:399
  28.6 0.1 collective-permute-start.8
  28.7 2.1 %shard_map.72 = (f32[4,320,128]{2,1,0:T(8,128)S(1)}, f32[6,80,512]{2,1,0:T(8,128)S(1)}) custom-call(bf16[128,192]{1,0:T(8,128)(2,1)S(1)} %copy-done, f32[4,328,128]{2,1,0:T(8,128)S(1)} %get-tuple-element.42.fields_ref.start_ref, s32[6,512]{1,0:T(8,128)S(1)} %get-tuple-element.43.near_ref), custom_call_target="tpu_custom_call" | custom-call | flops 1000000000 | bytes 1048576 | tf_op jit(solution)/shard_map/pallas_call | solution.py:376
  30.8 3.4 %collective-permute-done.8.b_ref = f32[3,80,128]{2,1,0:T(8,128)S(1)} collective-permute-done((f32[3,80,128]{2,1,0:T(8,128)S(1)}, f32[3,80,128]{2,1,0:T(8,128)S(1)}, u32[]{:S(2)}, u32[]{:S(2)}) %collective-permute-start.8) | collective-permute-done | bytes 122912 | tf_op jit(solution)/shard_map/ppermute | solution.py:399
  34.2 2.2 %collective-permute-start.9 = (f32[3,80,128]{2,1,0:T(8,128)S(1)}, f32[3,80,128]{2,1,0:T(8,128)S(1)}, u32[]{:S(2)}, u32[]{:S(2)}) collective-permute-start(f32[3,80,128]{2,1,0:T(8,128)S(1)} %pad_maximum_fusion.3), channel_id=1, source_target_pairs={{0,1},{1,0},{2,3},{3,2},{4,5},{5,4},{6,7},{7,6},{8,9},{9,8},{10,11... | collective-permute-start | bytes 368648 | tf_op jit(solution)/shard_map/ppermute | solution.py:389
  36.4 1.0 %shard_map.74.outer_ref = f32[6,80,512]{2,1,0:T(8,128)S(1)} custom-call(f32[6,80,512]{2,1,0:T(8,128)S(1)} %get-tuple-element.47.outer_ref, s32[6,512]{1,0:T(8,128)S(1)} %get-tuple-element.48.far_ref, f32[4,80,128]{2,1,0:T(8,128)S(1)} %collective-permute-done.7.a_ref, f32[3,80,128]{2,1,0:T(8,128)S(1)} %collective-permute-done.8.b_ref, ...), custom_call_target="tpu_custom_call" | custom-call | flops 1000000000 | bytes 1048576 | tf_op jit(solution)/shard_map/pallas_call | solution.py:376
  37.4 1.7 %shard_map.75 = (f32[4,320,128]{2,1,0:T(8,128)S(1)}, f32[5,80,128]{2,1,0:T(8,128)S(1)}) custom-call(f32[4,328,128]{2,1,0:T(8,128)S(1)} %get-tuple-element.42.fields_ref.start_ref, f32[4,320,128]{2,1,0:T(8,128)S(1)} %get-tuple-element.44.part_ref, f32[6,80,512]{2,1,0:T(8,128)S(1)} %shard_map.74.outer_ref, s32[6,512]{1,0:T(8,128)S(1)} %get-tuple-element.48.far_ref, ...), custom_call_target="tpu_custom_call" | custom-call | flops 1000000 | bytes 1048576 | tf_op jit(solution)/shard_map/pallas_call | solution.py:376
  39.1 0.4 collective-permute-start.10
  39.5 0.5 shard_map.77
  40.1 0.5 collective-permute-done.10.swap_ref
  40.6 3.6 %collective-permute-start.11 = (f32[4,80,128]{2,1,0:T(8,128)S(1)}, f32[4,80,128]{2,1,0:T(8,128)S(1)}, u32[]{:S(2)}, u32[]{:S(2)}) collective-permute-start(f32[4,80,128]{2,1,0:T(8,128)S(1)} %pad_maximum_fusion.1), channel_id=1, source_target_pairs={{0,2},{1,127},{2,4},{3,1},{4,6},{5,3},{6,8},{7,5},{8,10},{9,7},{10... | collective-permute-start | bytes 491528 | tf_op jit(solution)/shard_map/ppermute | solution.py:399
  44.3 0.6 collective-permute-start.12
  44.8 2.1 %shard_map.76 = (f32[4,320,128]{2,1,0:T(8,128)S(1)}, f32[6,80,512]{2,1,0:T(8,128)S(1)}) custom-call(bf16[128,192]{1,0:T(8,128)(2,1)S(1)} %copy-done, f32[4,320,128]{2,1,0:T(8,128)S(1)} %get-tuple-element.51.fields_ref.section_ref, s32[6,512]{1,0:T(8,128)S(1)} %get-tuple-element.43.near_ref), custom_call_target="tpu_custom_call" | custom-call | flops 1000000000 | bytes 1048576 | tf_op jit(solution)/shard_map/pallas_call | solution.py:376
  46.9 3.1 %collective-permute-done.12.b_ref = f32[3,80,128]{2,1,0:T(8,128)S(1)} collective-permute-done((f32[3,80,128]{2,1,0:T(8,128)S(1)}, f32[3,80,128]{2,1,0:T(8,128)S(1)}, u32[]{:S(2)}, u32[]{:S(2)}) %collective-permute-start.12) | collective-permute-done | bytes 122912 | tf_op jit(solution)/shard_map/ppermute | solution.py:399
  50.1 3.1 %collective-permute-start.13 = (f32[3,80,128]{2,1,0:T(8,128)S(1)}, f32[3,80,128]{2,1,0:T(8,128)S(1)}, u32[]{:S(2)}, u32[]{:S(2)}) collective-permute-start(f32[3,80,128]{2,1,0:T(8,128)S(1)} %pad_maximum_fusion.5), channel_id=1, source_target_pairs={{0,1},{1,0},{2,3},{3,2},{4,5},{5,4},{6,7},{7,6},{8,9},{9,8},{10,11... | collective-permute-start | bytes 368648 | tf_op jit(solution)/shard_map/ppermute | solution.py:389
  53.2 1.0 %shard_map.78.outer_ref = f32[6,80,512]{2,1,0:T(8,128)S(1)} custom-call(f32[6,80,512]{2,1,0:T(8,128)S(1)} %get-tuple-element.55.outer_ref, s32[6,512]{1,0:T(8,128)S(1)} %get-tuple-element.48.far_ref, f32[4,80,128]{2,1,0:T(8,128)S(1)} %collective-permute-done.11.a_ref, f32[3,80,128]{2,1,0:T(8,128)S(1)} %collective-permute-done.12.b_ref, ...), custom_call_target="tpu_custom_call" | custom-call | flops 1000000000 | bytes 1048576 | tf_op jit(solution)/shard_map/pallas_call | solution.py:376
  54.2 0.0 collective-permute-done.13.post_ref
  54.2 2.3 %shard_map.79 = (f32[320,512]{1,0:T(8,128)}, f32[320,512]{1,0:T(8,128)}) custom-call(f32[4,328,128]{2,1,0:T(8,128)S(1)} %get-tuple-element.42.fields_ref.start_ref, f32[4,320,128]{2,1,0:T(8,128)S(1)} %get-tuple-element.51.fields_ref.section_ref, f32[4,320,128]{2,1,0:T(8,128)S(1)} %get-tuple-element.52.part_ref, f32[6,80,512]{2,1,0:T(8,128)S(1)} %shard_map.78.outer_ref, ...), custom_call_target="tpu_custom_call" | custom-call | flops 1000000 | bytes 1048576 | tf_op jit(solution)/shard_map/pallas_call | solution.py:376
  (37 shorter events, 0.2 us)
Async XLA Ops:
  2.1 2.4 %collective-permute-start = (s32[5,1,128]{2,1,0:T(1,128)S(1)}, s32[5,1,128]{2,1,0:T(1,128)S(1)}, u32[]{:S(2)}, u32[]{:S(2)}) collective-permute-start(s32[5,1,128]{2,1,0:T(1,128)S(1)} %get-tuple-element.33), channel_id=1, source_target_pairs={{0,1},{1,0},{2,3},{3,2},{4,5},{5,4},{6,7},{7,6},{8,9},{9,8},{10,11... | collective-permute-start | bytes 7688 | tf_op jit(solution)/shard_map/ppermute | solution.py:389
  4.6 9.9 %collective-permute-start.4 = (s32[3,1,128]{2,1,0:T(1,128)S(1)}, s32[3,1,128]{2,1,0:T(1,128)S(1)}, u32[]{:S(2)}, u32[]{:S(2)}) collective-permute-start(s32[3,1,128]{2,1,0:T(1,128)S(1)} %pad_add_fusion.1), channel_id=1, source_target_pairs={{0,4},{1,125},{2,6},{3,127},{4,8},{5,1},{6,10},{7,3},{8,12},{9,5},... | collective-permute-start | bytes 4616 | tf_op jit(solution)/shard_map/ppermute | solution.py:399
  13.3 2.7 %collective-permute-start.3 = (s32[4,1,128]{2,1,0:T(1,128)S(1)}, s32[4,1,128]{2,1,0:T(1,128)S(1)}, u32[]{:S(2)}, u32[]{:S(2)}) collective-permute-start(s32[4,1,128]{2,1,0:T(1,128)S(1)} %pad_add_fusion), channel_id=1, source_target_pairs={{0,2},{1,127},{2,4},{3,1},{4,6},{5,3},{6,8},{7,5},{8,10},{9,7},{10... | collective-permute-start | bytes 6152 | tf_op jit(solution)/shard_map/ppermute | solution.py:399
  14.1 6.6 %collective-permute-start.1 = (f32[328,256]{1,0:T(8,128)S(1)}, f32[328,256]{1,0:T(8,128)S(1)}, u32[]{:S(2)}, u32[]{:S(2)}) collective-permute-start(f32[328,256]{1,0:T(8,128)S(1)} %get-tuple-element.38), channel_id=1, source_target_pairs={{0,127},{1,2},{2,1},{3,4},{4,3},{5,6},{6,5},{7,8},{8,7},{9,10},{10... | collective-permute-start | bytes 1007624 | tf_op jit(solution)/shard_map/ppermute | solution.py:394
  14.1 6.6 %collective-permute-start.2 = (f32[328,256]{1,0:T(8,128)S(1)}, f32[328,256]{1,0:T(8,128)S(1)}, u32[]{:S(2)}, u32[]{:S(2)}) collective-permute-start(f32[328,256]{1,0:T(8,128)S(1)} %get-tuple-element.39), channel_id=1, source_target_pairs={{0,1},{1,0},{2,3},{3,2},{4,5},{5,4},{6,7},{7,6},{8,9},{9,8},{10,11... | collective-permute-start | bytes 1007624 | tf_op jit(solution)/shard_map/ppermute | solution.py:389
  16.1 2.0 %collective-permute-start.5 = (s32[3,1,128]{2,1,0:T(1,128)S(1)}, s32[3,1,128]{2,1,0:T(1,128)S(1)}, u32[]{:S(2)}, u32[]{:S(2)}) collective-permute-start(s32[3,1,128]{2,1,0:T(1,128)S(1)} %pad_add_fusion.2), channel_id=1, source_target_pairs={{0,1},{1,0},{2,3},{3,2},{4,5},{5,4},{6,7},{7,6},{8,9},{9,8},{10,11... | collective-permute-start | bytes 4616 | tf_op jit(solution)/shard_map/ppermute | solution.py:389
  21.5 7.2 %copy-start = (bf16[128,192]{1,0:T(8,128)(2,1)S(1)}, bf16[128,192]{1,0:T(8,128)(2,1)}, u32[]{:S(2)}) copy-start(bf16[128,192]{1,0:T(8,128)(2,1)} %constant.13.clone.table_ref) | copy-start | bytes 147460
  21.5 1.5 %collective-permute-start.6 = (f32[5,80,128]{2,1,0:T(8,128)S(1)}, f32[5,80,128]{2,1,0:T(8,128)S(1)}, u32[]{:S(2)}, u32[]{:S(2)}) collective-permute-start(f32[5,80,128]{2,1,0:T(8,128)S(1)} %get-tuple-element.45), channel_id=1, source_target_pairs={{0,1},{1,0},{2,3},{3,2},{4,5},{5,4},{6,7},{7,6},{8,9},{9,8},{10,11... | collective-permute-start | bytes 614408 | tf_op jit(solution)/shard_map/ppermute | solution.py:389
  23.0 11.1 %collective-permute-start.7 = (f32[4,80,128]{2,1,0:T(8,128)S(1)}, f32[4,80,128]{2,1,0:T(8,128)S(1)}, u32[]{:S(2)}, u32[]{:S(2)}) collective-permute-start(f32[4,80,128]{2,1,0:T(8,128)S(1)} %pad_maximum_fusion), channel_id=1, source_target_pairs={{0,2},{1,127},{2,4},{3,1},{4,6},{5,3},{6,8},{7,5},{8,10},{9,7},{10... | collective-permute-start | bytes 491528 | tf_op jit(solution)/shard_map/ppermute | solution.py:399
  28.6 5.6 %collective-permute-start.8 = (f32[3,80,128]{2,1,0:T(8,128)S(1)}, f32[3,80,128]{2,1,0:T(8,128)S(1)}, u32[]{:S(2)}, u32[]{:S(2)}) collective-permute-start(f32[3,80,128]{2,1,0:T(8,128)S(1)} %pad_maximum_fusion.2), channel_id=1, source_target_pairs={{0,4},{1,125},{2,6},{3,127},{4,8},{5,1},{6,10},{7,3},{8,12},{9,5},... | collective-permute-start | bytes 368648 | tf_op jit(solution)/shard_map/ppermute | solution.py:399
  34.2 3.2 %collective-permute-start.9 = (f32[3,80,128]{2,1,0:T(8,128)S(1)}, f32[3,80,128]{2,1,0:T(8,128)S(1)}, u32[]{:S(2)}, u32[]{:S(2)}) collective-permute-start(f32[3,80,128]{2,1,0:T(8,128)S(1)} %pad_maximum_fusion.3), channel_id=1, source_target_pairs={{0,1},{1,0},{2,3},{3,2},{4,5},{5,4},{6,7},{7,6},{8,9},{9,8},{10,11... | collective-permute-start | bytes 368648 | tf_op jit(solution)/shard_map/ppermute | solution.py:389
  39.1 1.5 %collective-permute-start.10 = (f32[5,80,128]{2,1,0:T(8,128)S(1)}, f32[5,80,128]{2,1,0:T(8,128)S(1)}, u32[]{:S(2)}, u32[]{:S(2)}) collective-permute-start(f32[5,80,128]{2,1,0:T(8,128)S(1)} %get-tuple-element.53), channel_id=1, source_target_pairs={{0,1},{1,0},{2,3},{3,2},{4,5},{5,4},{6,7},{7,6},{8,9},{9,8},{10,11... | collective-permute-start | bytes 614408 | tf_op jit(solution)/shard_map/ppermute | solution.py:389
  40.6 9.4 %collective-permute-start.11 = (f32[4,80,128]{2,1,0:T(8,128)S(1)}, f32[4,80,128]{2,1,0:T(8,128)S(1)}, u32[]{:S(2)}, u32[]{:S(2)}) collective-permute-start(f32[4,80,128]{2,1,0:T(8,128)S(1)} %pad_maximum_fusion.1), channel_id=1, source_target_pairs={{0,2},{1,127},{2,4},{3,1},{4,6},{5,3},{6,8},{7,5},{8,10},{9,7},{10... | collective-permute-start | bytes 491528 | tf_op jit(solution)/shard_map/ppermute | solution.py:399
  44.3 5.8 %collective-permute-start.12 = (f32[3,80,128]{2,1,0:T(8,128)S(1)}, f32[3,80,128]{2,1,0:T(8,128)S(1)}, u32[]{:S(2)}, u32[]{:S(2)}) collective-permute-start(f32[3,80,128]{2,1,0:T(8,128)S(1)} %pad_maximum_fusion.4), channel_id=1, source_target_pairs={{0,4},{1,125},{2,6},{3,127},{4,8},{5,1},{6,10},{7,3},{8,12},{9,5},... | collective-permute-start | bytes 368648 | tf_op jit(solution)/shard_map/ppermute | solution.py:399
  50.1 4.1 %collective-permute-start.13 = (f32[3,80,128]{2,1,0:T(8,128)S(1)}, f32[3,80,128]{2,1,0:T(8,128)S(1)}, u32[]{:S(2)}, u32[]{:S(2)}) collective-permute-start(f32[3,80,128]{2,1,0:T(8,128)S(1)} %pad_maximum_fusion.5), channel_id=1, source_target_pairs={{0,1},{1,0},{2,3},{3,2},{4,5},{5,4},{6,7},{7,6},{8,9},{9,8},{10,11... | collective-permute-start | bytes 368648 | tf_op jit(solution)/shard_map/ppermute | solution.py:389

commit v4 on v3

--- a/solution.py
+++ b/solution.py
@@ -237,10 +237,12 @@
     return [(sign * flux[v]) - SPEED * w[v] for v in range(FIELDS)]
 
 
-def reply(fields, ask, got_ref, out_ref):
+def asked_code(ask):
+    return jnp.concatenate([ask[t : t + 1, :] for t in range(ask.shape[0])], axis=1)
+
+
+def reply(fields, ask, hot, got_ref, out_ref):
     chunks = ask.shape[0]
-    code = jnp.concatenate([ask[t : t + 1, :] for t in range(chunks)], axis=1)
-    hot = one_hot_rows(NEW_DEV, code & (NEW_DEV - 1))
     high, low = split(fields)
     both = dot(jnp.concatenate([high, low], axis=0), hot)
     for t in range(chunks):
@@ -255,11 +257,19 @@
             out_ref[t, 16 * v : 16 * v + 16, :] = x
 
 
+def hot_kernel(far_ref, ask_ref, rest_ref, reply_ref):
+    for f in range(6):
+        rest_ref[f] = one_hot_rows(3 * CAP, far_ref[f : f + 1, :])
+    reply_ref[...] = one_hot_rows(NEW_DEV, asked_code(ask_ref[3:8, :]) & (NEW_DEV - 1))
+
+
 def own_kernel(fields_ref, ask_ref, own_ref, got_ref):
-    reply(wide(fields_ref, ROWS), ask_ref[0:3, :], got_ref, own_ref)
-
-
-def first_kernel(me_ref, home_ref, far_ref, sib_ref, ask_ref, start_ref, swap_ref, got_ref):
+    ask = ask_ref[0:3, :]
+    hot = one_hot_rows(NEW_DEV, asked_code(ask) & (NEW_DEV - 1))
+    reply(wide(fields_ref, ROWS), ask, hot, got_ref, own_ref)
+
+
+def first_kernel(me_ref, home_ref, far_ref, sib_ref, ask_ref, hot_ref, start_ref, swap_ref, got_ref):
     even = (me_ref[0] & 1) == 0
     for c in range(2):
         spot = slice(128 * c, 128 * c + 128)
@@ -267,10 +277,10 @@
         far = far_ref[:, spot]
         start_ref[c] = home_ref[c] + jnp.where(even, far, sib)
         start_ref[c + 2] = home_ref[c + 2] + jnp.where(even, sib, far)
-    reply(wide(start_ref, ROWS), ask_ref[3:8, :], got_ref, swap_ref)
-
-
-def near_kernel(table_ref, fields_ref, near_ref, part_ref, outer_ref, high_ref, low_ref):
+    reply(wide(start_ref, ROWS), ask_ref[3:8, :], hot_ref[...], got_ref, swap_ref)
+
+
+def near_kernel(table_ref, fields_ref, near_ref, part_ref, high_ref, low_ref):
     for c in range(BLOCKS):
         spot = slice(128 * c, 128 * c + 128)
         w = [fields_ref[c, DOFS * v : DOFS * v + DOFS, :] for v in range(FIELDS)]
@@ -299,63 +309,83 @@
         )
         high, low = split(across)
         both = dot(jnp.concatenate([high, low], axis=0), hot)
-        outer_ref[f] = both[0:TRACE_ROWS] + both[TRACE_ROWS:]
-    for c in range(BLOCKS):
-        for f in range(6):
+        for c in range(BLOCKS):
+            spot = slice(128 * c, 128 * c + 128)
+            outer = both[0:TRACE_ROWS, spot] + both[TRACE_ROWS:, spot]
+            there = near_ref[f : f + 1, spot] >= 0
+            w = [outer[16 * v : 16 * v + 16] for v in range(FIELDS)]
+            w[0] = jnp.where(there, w[0], 1.0)
+            plus = side_term(w, f)
             minus = side_term([trace(fields_ref, c, v, f) for v in range(FIELDS)], f)
             for v in range(FIELDS):
-                add_on_face(part_ref, c, v, f, -3.0 * minus[v])
-
-
-def ghost_rows(ghosts):
-    parts = [split(g) for g in ghosts]
+                add_on_face(part_ref, c, v, f, 3.0 * (jnp.where(there, plus[v], 0.0) - minus[v]))
+
+
+def ghost_terms(ghost, ask):
+    face = (ask >> 9) ^ 1
+    axis = face >> 1
+    sign = jnp.where((face & 1) == 1, 3.0, -3.0)
+    w = [ghost[16 * v : 16 * v + 16] for v in range(FIELDS)]
+    u = [w[1 + c] / w[0] for c in range(3)]
+    p = pressure_of(w, u)
+
+    def along(x):
+        return jnp.where(axis == 0, x[0], jnp.where(axis == 1, x[1], x[2]))
+
+    un = along(u)
+    flux = [along(w[1:4])]
+    for c in range(3):
+        flux.append(w[1 + c] * un + jnp.where(axis == c, p, 0.0))
+    flux.append((w[4] + p) * un)
+    return jnp.concatenate([sign * flux[v] - (3.0 * SPEED) * w[v] for v in range(FIELDS)], axis=0)
+
+
+def ghost_rows(ghosts, ask_ref):
+    parts = [split(ghost_terms(g, ask_ref[t])) for t, g in enumerate(ghosts)]
     high = jnp.concatenate([p[0] for p in parts], axis=1)
     low = jnp.concatenate([p[1] for p in parts], axis=1)
     return jnp.concatenate([high, low], axis=0)
 
 
-def direct_kernel(outer_ref, far_ref, a_ref, b_ref, swap_ref, sum_ref):
-    lhs = ghost_rows([swap_ref[0], a_ref[2], a_ref[0], b_ref[1], b_ref[0]])
+def add_ghosts(sum_ref, lhs, hot_of):
     for f in range(6):
-        both = dot(lhs, one_hot_rows(5 * CAP, far_ref[f : f + 1, :] - 3 * CAP))
-        sum_ref[f] = outer_ref[f] + both[0:TRACE_ROWS] + both[TRACE_ROWS:]
-
-
-def place_rest(outer_ref, far_ref, post_ref, side_ref):
-    lhs = ghost_rows([post_ref[1], post_ref[0], post_ref[2]])
-    for f in range(6):
-        both = dot(lhs, one_hot_rows(3 * CAP, far_ref[f : f + 1, :]))
-        side_ref[f] = outer_ref[f] + both[0:TRACE_ROWS] + both[TRACE_ROWS:]
-
-
-def add_outer(part_ref, side_ref, sum_ref, c):
-    sum_ref[c] = part_ref[c]
-    for f in range(6):
-        outer = side_ref[f, :, 128 * c : 128 * c + 128]
-        plus = side_term([outer[16 * v : 16 * v + 16] for v in range(FIELDS)], f)
-        for v in range(FIELDS):
-            add_on_face(sum_ref, c, v, f, 3.0 * plus[v])
+        both = dot(lhs, hot_of(f))
+        for c in range(BLOCKS):
+            spot = slice(128 * c, 128 * c + 128)
+            term = both[0:TRACE_ROWS, spot] + both[TRACE_ROWS:, spot]
+            for v in range(FIELDS):
+                add_on_face(sum_ref, c, v, f, term[16 * v : 16 * v + 16])
+
+
+def direct_kernel(part_ref, far_ref, ask_ref, a_ref, b_ref, swap_ref, sum_ref):
+    lhs = ghost_rows([swap_ref[0], a_ref[2], a_ref[0], b_ref[1], b_ref[0]], ask_ref)
+    sum_ref[...] = part_ref[...]
+    add_ghosts(sum_ref, lhs, lambda f: one_hot_rows(5 * CAP, far_ref[f : f + 1, :] - 3 * CAP))
+
+
+def add_rest(part_ref, rest_ref, ask_ref, post_ref, sum_ref):
+    lhs = ghost_rows([post_ref[1], post_ref[0], post_ref[2]], ask_ref)
+    sum_ref[...] = part_ref[...]
+    add_ghosts(sum_ref, lhs, lambda f: rest_ref[f])
 
 
 def metric_of(start_ref, c):
     return jnp.where(start_ref[c, ROWS : ROWS + 1, :] > 0.5, 2.0, 1.0)
 
 
-def second_kernel(start_ref, part_ref, outer_ref, far_ref, ask_ref, post_ref,
-                  section_ref, swap_ref, side_ref, sum_ref, got_ref):
-    place_rest(outer_ref, far_ref, post_ref, side_ref)
+def second_kernel(start_ref, part_ref, rest_ref, own_ask_ref, post_ref, ask_ref, hot_ref,
+                  section_ref, swap_ref, sum_ref, got_ref):
+    add_rest(part_ref, rest_ref, own_ask_ref, post_ref, sum_ref)
     for c in range(BLOCKS):
-        add_outer(part_ref, side_ref, sum_ref, c)
         section_ref[c] = start_ref[c, 0:ROWS, :] - (DT * metric_of(start_ref, c)) * sum_ref[c]
-    reply(wide(section_ref, ROWS), ask_ref[3:8, :], got_ref, swap_ref)
-
-
-def last_kernel(start_ref, section_ref, part_ref, outer_ref, far_ref, post_ref,
-                state_hbm, rate_hbm, side_ref, sum_ref, state_ref, rate_ref, sems):
-    place_rest(outer_ref, far_ref, post_ref, side_ref)
+    reply(wide(section_ref, ROWS), ask_ref[3:8, :], hot_ref[...], got_ref, swap_ref)
+
+
+def last_kernel(start_ref, section_ref, part_ref, rest_ref, own_ask_ref, post_ref,
+                state_hbm, rate_hbm, sum_ref, state_ref, rate_ref, sems):
+    add_rest(part_ref, rest_ref, own_ask_ref, post_ref, sum_ref)
     copies = []
     for c in range(BLOCKS):
-        add_outer(part_ref, side_ref, sum_ref, c)
         rate = -metric_of(start_ref, c) * sum_ref[c]
         rate_ref[c] = rate
         state_ref[c] = 0.5 * start_ref[c, 0:ROWS, :] + 0.5 * (section_ref[c] + DT * rate)
@@ -379,7 +409,7 @@
         in_specs=specs or [VM] * len(args),
         out_specs=[outs_in or VM] * len(outs),
         scratch_shapes=[pltpu.VMEM(*s) if isinstance(s, tuple) else s for s in scratch],
-        compiler_params=pltpu.CompilerParams(vmem_limit_bytes=40 * 2**20),
+        compiler_params=pltpu.CompilerParams(vmem_limit_bytes=24 * 2**20),
         cost_estimate=pl.CostEstimate(flops=flops, bytes_accessed=2**20, transcendentals=0),
     )(*args)
 
@@ -448,10 +478,15 @@
         [post[1], post[0], post[2], got[0], a[2], a[0], b[1], b[0]], axis=0
     )
 
+    rest_hot, reply_hot = call(
+        hot_kernel,
+        [((6, 3 * CAP, NEW_DEV), BF16), ((NEW_DEV, 5 * CAP), BF16)],
+        (far, asked),
+        flops=10**9,
+    )
     swapped = ((5, TRACE_ROWS, CAP), F32)
     got_scratch = ((5, ROWS, CAP), F32)
     blocks = ((BLOCKS, ROWS, 128), F32)
-    sides = ((6, TRACE_ROWS, NEW_DEV), F32)
     table = jnp.asarray(stacked_table())
 
     def neighbours_of(fields, swap):
@@ -464,41 +499,41 @@
             [((3, ROWS, CAP), F32)],
         )
         a, b = outward_pair(own, got)
-        part, outer = call(
+        (part,) = call(
             near_kernel,
-            [blocks, sides],
+            [blocks],
             (table, fields, near),
             None,
             [((FIELDS, 3 * DOFS, NEW_DEV), BF16)] * 2,
             flops=10**9,
         )
-        a, b, outer = lax.optimization_barrier((a, b, outer))
+        a, b, part = lax.optimization_barrier((a, b, part))
         post = swap_back(a, b)
-        (outer,) = call(direct_kernel, [sides], (outer, far, a, b, got), flops=10**9)
-        return part, outer, far, post
+        (part,) = call(direct_kernel, [blocks], (part, far, swap_ask, a, b, got), flops=10**9)
+        return part, rest_hot, own_ask, post
 
     start, swap = call(
         first_kernel,
         [((BLOCKS, MOVED_ROWS, 128), F32), swapped],
-        (me, home, from_far, from_sib, asked),
-        [SM, VM, VM, VM, VM],
+        (me, home, from_far, from_sib, asked, reply_hot),
+        [SM, VM, VM, VM, VM, VM],
         [got_scratch],
     )
-    part, outer, far, post = neighbours_of(start, swap)
+    ghosts = neighbours_of(start, swap)
     section, swap = call(
         second_kernel,
         [blocks, swapped],
-        (start, part, outer, far, asked, post),
+        (start, *ghosts, asked, reply_hot),
         None,
-        [sides, blocks, got_scratch],
-    )
-    part, outer, far, post = neighbours_of(section, swap)
+        [blocks, got_scratch],
+    )
+    ghosts = neighbours_of(section, swap)
     new_state, rate = call(
         last_kernel,
         [((ROWS, NEW_DEV), F32)] * 2,
-        (start, section, part, outer, far, post),
+        (start, section, *ghosts),
         None,
-        [sides, blocks, blocks, blocks, pltpu.SemaphoreType.DMA((2, BLOCKS))],
+        [blocks, blocks, blocks, pltpu.SemaphoreType.DMA((2, BLOCKS))],
         outs_in=HB,
     )
     shape = (FIELDS, DOFS, NEW_DEV)

time: 56.8 us -> 56.5 us (level)
  Pallas kernels: 15.2 us -> 15.8 us
    pallas_call x12 -> x13, Pallas kernels: 15.2 us -> 15.8 us  [call(): pl.pallas_call(kernel, out_shape=[jax.ShapeDtypeStruct(s, d) for s, d in...]
  transfers between devices with their start and end apart: 14 -> 14, of which waited for: 6 -> 6; matrix products, arithmetic and copies ran while one was open for 0% -> 0% of each run, Pallas kernels for 16% -> 18%
where the time goes in v4:
time: 56.5 us; the launch traced here: 56.4 us
  starting transfers between devices  27.8 us (49%)
  Pallas kernels  15.8 us (28%)
  waiting for transfers between devices  11.5 us (20%)
  between operations  1.06 us (2%)
    ppermute x6, starting transfers between devices, outward(): lax.ppermute(x, AXES, [(i, (i + (by if i % 2 == 0 else -by)) % n) for i i...  19.1 us
    pallas_call x13, Pallas kernels, call(): pl.pallas_call(kernel, out_shape=[jax.ShapeDtypeStruct(s, d) for s, d in...  15.8 us
    ppermute x7, starting transfers between devices, swap_cores(): return lax.ppermute(x, AXES, [(i, i ^ 1) for i in range(n)])  8.69 us
    ppermute x6, waiting for transfers between devices, outward(): lax.ppermute(x, AXES, [(i, (i + (by if i % 2 == 0 else -by)) % n) for i i...  7.82 us
    ppermute x1, waiting for transfers between devices, swap_chips(): lax.ppermute(x, AXES, [(i, (i + (1 if i % 2 else -1)) % n) for i in range...  2.1 us
    ppermute x7, waiting for transfers between devices, swap_cores(): return lax.ppermute(x, AXES, [(i, i ^ 1) for i in range(n)])  1.62 us
  transfers between devices with their start and end apart: 14, of which 6 were waited for; matrix products, arithmetic and copies ran while one was open for 0% of the time, Pallas kernels for 18%

profile of v4, /device:TPU:1, one launch (start us, length us, event | category | flops | bytes accessed | tf_op | source)
XLA Modules:
  0.0 56.4 jit_solution(851998956757576512)
XLA Ops:
  0.6 1.5 %shard_map.68 = (s32[3,1,128]{2,1,0:T(1,128)S(1)}, s32[5,1,128]{2,1,0:T(1,128)S(1)}, s32[6,512]{1,0:T(8,128)S(1)}, s32[6,512]{1,0:T(8,128)S(1)}, f32[320,1024]{1...) custom-call(s32[1]{0:T(128)} %bitcast.me_ref, s32[6,512]{1,0:T(8,128)} %links_hbm.1, f32[320,1024]{1,0:T(8,128)} %bitcast.22, ...), custom_call_target="tpu_custom_call" | custom-call | flops 1000000 | bytes 1048576 | tf_op jit(solution)/shard_map/pallas_call | solution.py:406
  2.1 1.5 %collective-permute-start = (s32[5,1,128]{2,1,0:T(1,128)S(1)}, s32[5,1,128]{2,1,0:T(1,128)S(1)}, u32[]{:S(2)}, u32[]{:S(2)}) collective-permute-start(s32[5,1,128]{2,1,0:T(1,128)S(1)} %get-tuple-element.31.ask_ref), channel_id=1, source_target_pairs={{0,1},{1,0},{2,3},{3,2},{4,5},{5,4},{6,7},{7,6},{8,9},{9,8},{10,11... | collective-permute-start | bytes 7688 | tf_op jit(solution)/shard_map/ppermute | solution.py:419
  3.6 0.9 %shard_map.69 = (f32[328,256]{1,0:T(8,128)S(1)}, f32[328,256]{1,0:T(8,128)S(1)}) custom-call(s32[1]{0:T(128)} %bitcast.me_ref, f32[320,1024]{1,0:T(8,128)S(1)} %get-tuple-element.29.state_ref, s32[1,1024]{1,0:T(1,128)S(1)} %get-tuple-element.30.level_ref, s32[1,1024]{1,0:T(1,128)S(1)} %get-tuple-element.35.morton_ref), custom_call_target="tpu_custom_call" | custom-call | flops 1000000 | bytes 1048576 | tf_op jit(solution)/shard_map/pallas_call | solution.py:406
  4.6 8.7 %collective-permute-start.4 = (s32[3,1,128]{2,1,0:T(1,128)S(1)}, s32[3,1,128]{2,1,0:T(1,128)S(1)}, u32[]{:S(2)}, u32[]{:S(2)}) collective-permute-start(s32[3,1,128]{2,1,0:T(1,128)S(1)} %pad_add_fusion.1), channel_id=1, source_target_pairs={{0,4},{1,125},{2,6},{3,127},{4,8},{5,1},{6,10},{7,3},{8,12},{9,5},... | collective-permute-start | bytes 4616 | tf_op jit(solution)/shard_map/ppermute | solution.py:429
  13.3 0.8 %collective-permute-start.3 = (s32[4,1,128]{2,1,0:T(1,128)S(1)}, s32[4,1,128]{2,1,0:T(1,128)S(1)}, u32[]{:S(2)}, u32[]{:S(2)}) collective-permute-start(s32[4,1,128]{2,1,0:T(1,128)S(1)} %pad_add_fusion), channel_id=1, source_target_pairs={{0,2},{1,127},{2,4},{3,1},{4,6},{5,3},{6,8},{7,5},{8,10},{9,7},{10... | collective-permute-start | bytes 6152 | tf_op jit(solution)/shard_map/ppermute | solution.py:429
  14.1 0.4 collective-permute-start.2
  14.5 1.5 %collective-permute-done.3 = s32[4,1,128]{2,1,0:T(1,128)S(1)} collective-permute-done((s32[4,1,128]{2,1,0:T(1,128)S(1)}, s32[4,1,128]{2,1,0:T(1,128)S(1)}, u32[]{:S(2)}, u32[]{:S(2)}) %collective-permute-start.3) | collective-permute-done | bytes 2080 | tf_op jit(solution)/shard_map/ppermute | solution.py:429
  16.1 1.1 %collective-permute-start.5 = (s32[3,1,128]{2,1,0:T(1,128)S(1)}, s32[3,1,128]{2,1,0:T(1,128)S(1)}, u32[]{:S(2)}, u32[]{:S(2)}) collective-permute-start(s32[3,1,128]{2,1,0:T(1,128)S(1)} %pad_add_fusion.2), channel_id=1, source_target_pairs={{0,1},{1,0},{2,3},{3,2},{4,5},{5,4},{6,7},{7,6},{8,9},{9,8},{10,11... | collective-permute-start | bytes 4616 | tf_op jit(solution)/shard_map/ppermute | solution.py:419
  17.1 0.9 %shard_map.70.home_ref = f32[4,328,128]{2,1,0:T(8,128)S(1)} custom-call(s32[1]{0:T(128)} %bitcast.me_ref, f32[320,1024]{1,0:T(8,128)S(1)} %get-tuple-element.29.state_ref, s32[1,1024]{1,0:T(1,128)S(1)} %get-tuple-element.30.level_ref, s32[1,1024]{1,0:T(1,128)S(1)} %get-tuple-element.35.morton_ref), custom_call_target="tpu_custom_call" | custom-call | flops 1000000 | bytes 1048576 | tf_op jit(solution)/shard_map/pallas_call | solution.py:406
  18.1 0.5 shard_map.71
  18.6 2.1 %collective-permute-done.1.far_ref = f32[328,256]{1,0:T(8,128)S(1)} collective-permute-done((f32[328,256]{1,0:T(8,128)S(1)}, f32[328,256]{1,0:T(8,128)S(1)}, u32[]{:S(2)}, u32[]{:S(2)}) %collective-permute-start.1) | collective-permute-done | bytes 335904 | tf_op jit(solution)/shard_map/ppermute | solution.py:424
  20.7 0.7 %shard_map.72 = (f32[4,328,128]{2,1,0:T(8,128)S(1)}, f32[5,80,128]{2,1,0:T(8,128)S(1)}) custom-call(s32[1]{0:T(128)} %bitcast.me_ref, f32[4,328,128]{2,1,0:T(8,128)S(1)} %shard_map.70.home_ref, f32[328,256]{1,0:T(8,128)S(1)} %collective-permute-done.1.far_ref, f32[328,256]{1,0:T(8,128)S(1)} %collective-permute-done.2.sib_ref, ...), custom_call_target="tpu_custom_call" | custom-call | flops 1000000 | bytes 1048576 | tf_op jit(solution)/shard_map/pallas_call | solution.py:406
  21.4 0.2 collective-permute-start.6
  21.6 0.5 shard_map.73
  22.2 0.8 %collective-permute-done.6.swap_ref = f32[5,80,128]{2,1,0:T(8,128)S(1)} collective-permute-done((f32[5,80,128]{2,1,0:T(8,128)S(1)}, f32[5,80,128]{2,1,0:T(8,128)S(1)}, u32[]{:S(2)}, u32[]{:S(2)}) %collective-permute-start.6) | collective-permute-done | bytes 204832 | tf_op jit(solution)/shard_map/ppermute | solution.py:419
  23.0 5.5 %collective-permute-start.7 = (f32[4,80,128]{2,1,0:T(8,128)S(1)}, f32[4,80,128]{2,1,0:T(8,128)S(1)}, u32[]{:S(2)}, u32[]{:S(2)}) collective-permute-start(f32[4,80,128]{2,1,0:T(8,128)S(1)} %pad_maximum_fusion), channel_id=1, source_target_pairs={{0,2},{1,127},{2,4},{3,1},{4,6},{5,3},{6,8},{7,5},{8,10},{9,7},{10... | collective-permute-start | bytes 491528 | tf_op jit(solution)/shard_map/ppermute | solution.py:429
  28.5 0.1 collective-permute-start.8
  28.6 2.2 %shard_map.74.part_ref = f32[4,320,128]{2,1,0:T(8,128)S(1)} custom-call(bf16[128,192]{1,0:T(8,128)(2,1)S(1)} %copy-done, f32[4,328,128]{2,1,0:T(8,128)S(1)} %get-tuple-element.42.fields_ref.start_ref, s32[6,512]{1,0:T(8,128)S(1)} %get-tuple-element.44.near_ref), custom_call_target="tpu_custom_call" | custom-call | flops 1000000000 | bytes 1048576 | tf_op jit(solution)/shard_map/pallas_call | solution.py:406
  30.8 3.3 %collective-permute-done.8.b_ref = f32[3,80,128]{2,1,0:T(8,128)S(1)} collective-permute-done((f32[3,80,128]{2,1,0:T(8,128)S(1)}, f32[3,80,128]{2,1,0:T(8,128)S(1)}, u32[]{:S(2)}, u32[]{:S(2)}) %collective-permute-start.8) | collective-permute-done | bytes 122912 | tf_op jit(solution)/shard_map/ppermute | solution.py:429
  34.2 2.2 %collective-permute-start.9 = (f32[3,80,128]{2,1,0:T(8,128)S(1)}, f32[3,80,128]{2,1,0:T(8,128)S(1)}, u32[]{:S(2)}, u32[]{:S(2)}) collective-permute-start(f32[3,80,128]{2,1,0:T(8,128)S(1)} %pad_maximum_fusion.3), channel_id=1, source_target_pairs={{0,1},{1,0},{2,3},{3,2},{4,5},{5,4},{6,7},{7,6},{8,9},{9,8},{10,11... | collective-permute-start | bytes 368648 | tf_op jit(solution)/shard_map/ppermute | solution.py:419
  36.4 1.2 %shard_map.75.part_ref = f32[4,320,128]{2,1,0:T(8,128)S(1)} custom-call(f32[4,320,128]{2,1,0:T(8,128)S(1)} %shard_map.74.part_ref, s32[6,512]{1,0:T(8,128)S(1)} %get-tuple-element.40.far_ref, s32[5,1,128]{2,1,0:T(1,128)S(1)} %get-tuple-element.31.ask_ref, f32[4,80,128]{2,1,0:T(8,128)S(1)} %collective-permute-done.7.a_ref, ...), custom_call_target="tpu_custom_call" | custom-call | flops 1000000000 | bytes 1048576 | tf_op jit(solution)/shard_map/pallas_call | solution.py:406
  37.6 1.5 %shard_map.76 = (f32[4,320,128]{2,1,0:T(8,128)S(1)}, f32[5,80,128]{2,1,0:T(8,128)S(1)}) custom-call(f32[4,328,128]{2,1,0:T(8,128)S(1)} %get-tuple-element.42.fields_ref.start_ref, f32[4,320,128]{2,1,0:T(8,128)S(1)} %shard_map.75.part_ref, bf16[6,384,512]{2,1,0:T(8,128)(2,1)S(1)} %get-tuple-element.48.rest_ref, ...), custom_call_target="tpu_custom_call" | custom-call | flops 1000000 | bytes 1048576 | tf_op jit(solution)/shard_map/pallas_call | solution.py:406
  39.1 0.2 collective-permute-start.10
  39.3 0.5 shard_map.77
  39.8 0.8 %collective-permute-done.10.swap_ref = f32[5,80,128]{2,1,0:T(8,128)S(1)} collective-permute-done((f32[5,80,128]{2,1,0:T(8,128)S(1)}, f32[5,80,128]{2,1,0:T(8,128)S(1)}, u32[]{:S(2)}, u32[]{:S(2)}) %collective-permute-start.10) | collective-permute-done | bytes 204832 | tf_op jit(solution)/shard_map/ppermute | solution.py:419
  40.7 3.4 %collective-permute-start.11 = (f32[4,80,128]{2,1,0:T(8,128)S(1)}, f32[4,80,128]{2,1,0:T(8,128)S(1)}, u32[]{:S(2)}, u32[]{:S(2)}) collective-permute-start(f32[4,80,128]{2,1,0:T(8,128)S(1)} %pad_maximum_fusion.1), channel_id=1, source_target_pairs={{0,2},{1,127},{2,4},{3,1},{4,6},{5,3},{6,8},{7,5},{8,10},{9,7},{10... | collective-permute-start | bytes 491528 | tf_op jit(solution)/shard_map/ppermute | solution.py:429
  44.1 0.6 %collective-permute-start.12 = (f32[3,80,128]{2,1,0:T(8,128)S(1)}, f32[3,80,128]{2,1,0:T(8,128)S(1)}, u32[]{:S(2)}, u32[]{:S(2)}) collective-permute-start(f32[3,80,128]{2,1,0:T(8,128)S(1)} %pad_maximum_fusion.4), channel_id=1, source_target_pairs={{0,4},{1,125},{2,6},{3,127},{4,8},{5,1},{6,10},{7,3},{8,12},{9,5},... | collective-permute-start | bytes 368648 | tf_op jit(solution)/shard_map/ppermute | solution.py:429
  44.6 2.2 %shard_map.78.part_ref = f32[4,320,128]{2,1,0:T(8,128)S(1)} custom-call(bf16[128,192]{1,0:T(8,128)(2,1)S(1)} %copy-done, f32[4,320,128]{2,1,0:T(8,128)S(1)} %get-tuple-element.49.fields_ref.section_ref, s32[6,512]{1,0:T(8,128)S(1)} %get-tuple-element.44.near_ref), custom_call_target="tpu_custom_call" | custom-call | flops 1000000000 | bytes 1048576 | tf_op jit(solution)/shard_map/pallas_call | solution.py:406
  46.8 3.0 %collective-permute-done.12.b_ref = f32[3,80,128]{2,1,0:T(8,128)S(1)} collective-permute-done((f32[3,80,128]{2,1,0:T(8,128)S(1)}, f32[3,80,128]{2,1,0:T(8,128)S(1)}, u32[]{:S(2)}, u32[]{:S(2)}) %collective-permute-start.12) | collective-permute-done | bytes 122912 | tf_op jit(solution)/shard_map/ppermute | solution.py:429
  49.9 3.2 %collective-permute-start.13 = (f32[3,80,128]{2,1,0:T(8,128)S(1)}, f32[3,80,128]{2,1,0:T(8,128)S(1)}, u32[]{:S(2)}, u32[]{:S(2)}) collective-permute-start(f32[3,80,128]{2,1,0:T(8,128)S(1)} %pad_maximum_fusion.5), channel_id=1, source_target_pairs={{0,1},{1,0},{2,3},{3,2},{4,5},{5,4},{6,7},{7,6},{8,9},{9,8},{10,11... | collective-permute-start | bytes 368648 | tf_op jit(solution)/shard_map/ppermute | solution.py:419
  53.0 1.2 %shard_map.79.part_ref = f32[4,320,128]{2,1,0:T(8,128)S(1)} custom-call(f32[4,320,128]{2,1,0:T(8,128)S(1)} %shard_map.78.part_ref, s32[6,512]{1,0:T(8,128)S(1)} %get-tuple-element.40.far_ref, s32[5,1,128]{2,1,0:T(1,128)S(1)} %get-tuple-element.31.ask_ref, f32[4,80,128]{2,1,0:T(8,128)S(1)} %collective-permute-done.11.a_ref, ...), custom_call_target="tpu_custom_call" | custom-call | flops 1000000000 | bytes 1048576 | tf_op jit(solution)/shard_map/pallas_call | solution.py:406
  54.3 1.9 %shard_map.80 = (f32[320,512]{1,0:T(8,128)}, f32[320,512]{1,0:T(8,128)}) custom-call(f32[4,328,128]{2,1,0:T(8,128)S(1)} %get-tuple-element.42.fields_ref.start_ref, f32[4,320,128]{2,1,0:T(8,128)S(1)} %get-tuple-element.49.fields_ref.section_ref, f32[4,320,128]{2,1,0:T(8,128)S(1)} %shard_map.79.part_ref, bf16[6,384,512]{2,1,0:T(8,128)(2,1)S(1)} %get-tuple-element.48.rest_ref, ...), custom_call_target="tpu_custom_call" | custom-call | flops 1000000 | bytes 1048576 | tf_op jit(solution)/shard_map/pallas_call | solution.py:406
  (38 shorter events, 0.2 us)
Async XLA Ops:
  2.1 2.4 %collective-permute-start = (s32[5,1,128]{2,1,0:T(1,128)S(1)}, s32[5,1,128]{2,1,0:T(1,128)S(1)}, u32[]{:S(2)}, u32[]{:S(2)}) collective-permute-start(s32[5,1,128]{2,1,0:T(1,128)S(1)} %get-tuple-element.31.ask_ref), channel_id=1, source_target_pairs={{0,1},{1,0},{2,3},{3,2},{4,5},{5,4},{6,7},{7,6},{8,9},{9,8},{10,11... | collective-permute-start | bytes 7688 | tf_op jit(solution)/shard_map/ppermute | solution.py:419
  4.6 9.9 %collective-permute-start.4 = (s32[3,1,128]{2,1,0:T(1,128)S(1)}, s32[3,1,128]{2,1,0:T(1,128)S(1)}, u32[]{:S(2)}, u32[]{:S(2)}) collective-permute-start(s32[3,1,128]{2,1,0:T(1,128)S(1)} %pad_add_fusion.1), channel_id=1, source_target_pairs={{0,4},{1,125},{2,6},{3,127},{4,8},{5,1},{6,10},{7,3},{8,12},{9,5},... | collective-permute-start | bytes 4616 | tf_op jit(solution)/shard_map/ppermute | solution.py:429
  13.3 2.7 %collective-permute-start.3 = (s32[4,1,128]{2,1,0:T(1,128)S(1)}, s32[4,1,128]{2,1,0:T(1,128)S(1)}, u32[]{:S(2)}, u32[]{:S(2)}) collective-permute-start(s32[4,1,128]{2,1,0:T(1,128)S(1)} %pad_add_fusion), channel_id=1, source_target_pairs={{0,2},{1,127},{2,4},{3,1},{4,6},{5,3},{6,8},{7,5},{8,10},{9,7},{10... | collective-permute-start | bytes 6152 | tf_op jit(solution)/shard_map/ppermute | solution.py:429
  14.1 6.6 %collective-permute-start.1 = (f32[328,256]{1,0:T(8,128)S(1)}, f32[328,256]{1,0:T(8,128)S(1)}, u32[]{:S(2)}, u32[]{:S(2)}) collective-permute-start(f32[328,256]{1,0:T(8,128)S(1)} %get-tuple-element.36), channel_id=1, source_target_pairs={{0,127},{1,2},{2,1},{3,4},{4,3},{5,6},{6,5},{7,8},{8,7},{9,10},{10... | collective-permute-start | bytes 1007624 | tf_op jit(solution)/shard_map/ppermute | solution.py:424
  14.1 6.6 %collective-permute-start.2 = (f32[328,256]{1,0:T(8,128)S(1)}, f32[328,256]{1,0:T(8,128)S(1)}, u32[]{:S(2)}, u32[]{:S(2)}) collective-permute-start(f32[328,256]{1,0:T(8,128)S(1)} %get-tuple-element.37), channel_id=1, source_target_pairs={{0,1},{1,0},{2,3},{3,2},{4,5},{5,4},{6,7},{7,6},{8,9},{9,8},{10,11... | collective-permute-start | bytes 1007624 | tf_op jit(solution)/shard_map/ppermute | solution.py:419
  16.1 2.0 %collective-permute-start.5 = (s32[3,1,128]{2,1,0:T(1,128)S(1)}, s32[3,1,128]{2,1,0:T(1,128)S(1)}, u32[]{:S(2)}, u32[]{:S(2)}) collective-permute-start(s32[3,1,128]{2,1,0:T(1,128)S(1)} %pad_add_fusion.2), channel_id=1, source_target_pairs={{0,1},{1,0},{2,3},{3,2},{4,5},{5,4},{6,7},{7,6},{8,9},{9,8},{10,11... | collective-permute-start | bytes 4616 | tf_op jit(solution)/shard_map/ppermute | solution.py:419
  21.4 7.2 %copy-start = (bf16[128,192]{1,0:T(8,128)(2,1)S(1)}, bf16[128,192]{1,0:T(8,128)(2,1)}, u32[]{:S(2)}) copy-start(bf16[128,192]{1,0:T(8,128)(2,1)} %constant.13.clone.table_ref) | copy-start | bytes 147460
  21.4 1.5 %collective-permute-start.6 = (f32[5,80,128]{2,1,0:T(8,128)S(1)}, f32[5,80,128]{2,1,0:T(8,128)S(1)}, u32[]{:S(2)}, u32[]{:S(2)}) collective-permute-start(f32[5,80,128]{2,1,0:T(8,128)S(1)} %get-tuple-element.43), channel_id=1, source_target_pairs={{0,1},{1,0},{2,3},{3,2},{4,5},{5,4},{6,7},{7,6},{8,9},{9,8},{10,11... | collective-permute-start | bytes 614408 | tf_op jit(solution)/shard_map/ppermute | solution.py:419
  23.0 11.1 %collective-permute-start.7 = (f32[4,80,128]{2,1,0:T(8,128)S(1)}, f32[4,80,128]{2,1,0:T(8,128)S(1)}, u32[]{:S(2)}, u32[]{:S(2)}) collective-permute-start(f32[4,80,128]{2,1,0:T(8,128)S(1)} %pad_maximum_fusion), channel_id=1, source_target_pairs={{0,2},{1,127},{2,4},{3,1},{4,6},{5,3},{6,8},{7,5},{8,10},{9,7},{10... | collective-permute-start | bytes 491528 | tf_op jit(solution)/shard_map/ppermute | solution.py:429
  28.5 5.6 %collective-permute-start.8 = (f32[3,80,128]{2,1,0:T(8,128)S(1)}, f32[3,80,128]{2,1,0:T(8,128)S(1)}, u32[]{:S(2)}, u32[]{:S(2)}) collective-permute-start(f32[3,80,128]{2,1,0:T(8,128)S(1)} %pad_maximum_fusion.2), channel_id=1, source_target_pairs={{0,4},{1,125},{2,6},{3,127},{4,8},{5,1},{6,10},{7,3},{8,12},{9,5},... | collective-permute-start | bytes 368648 | tf_op jit(solution)/shard_map/ppermute | solution.py:429
  34.2 3.4 %collective-permute-start.9 = (f32[3,80,128]{2,1,0:T(8,128)S(1)}, f32[3,80,128]{2,1,0:T(8,128)S(1)}, u32[]{:S(2)}, u32[]{:S(2)}) collective-permute-start(f32[3,80,128]{2,1,0:T(8,128)S(1)} %pad_maximum_fusion.3), channel_id=1, source_target_pairs={{0,1},{1,0},{2,3},{3,2},{4,5},{5,4},{6,7},{7,6},{8,9},{9,8},{10,11... | collective-permute-start | bytes 368648 | tf_op jit(solution)/shard_map/ppermute | solution.py:419
  39.1 1.5 %collective-permute-start.10 = (f32[5,80,128]{2,1,0:T(8,128)S(1)}, f32[5,80,128]{2,1,0:T(8,128)S(1)}, u32[]{:S(2)}, u32[]{:S(2)}) collective-permute-start(f32[5,80,128]{2,1,0:T(8,128)S(1)} %get-tuple-element.50), channel_id=1, source_target_pairs={{0,1},{1,0},{2,3},{3,2},{4,5},{5,4},{6,7},{7,6},{8,9},{9,8},{10,11... | collective-permute-start | bytes 614408 | tf_op jit(solution)/shard_map/ppermute | solution.py:419
  40.7 9.2 %collective-permute-start.11 = (f32[4,80,128]{2,1,0:T(8,128)S(1)}, f32[4,80,128]{2,1,0:T(8,128)S(1)}, u32[]{:S(2)}, u32[]{:S(2)}) collective-permute-start(f32[4,80,128]{2,1,0:T(8,128)S(1)} %pad_maximum_fusion.1), channel_id=1, source_target_pairs={{0,2},{1,127},{2,4},{3,1},{4,6},{5,3},{6,8},{7,5},{8,10},{9,7},{10... | collective-permute-start | bytes 491528 | tf_op jit(solution)/shard_map/ppermute | solution.py:429
  44.1 5.8 %collective-permute-start.12 = (f32[3,80,128]{2,1,0:T(8,128)S(1)}, f32[3,80,128]{2,1,0:T(8,128)S(1)}, u32[]{:S(2)}, u32[]{:S(2)}) collective-permute-start(f32[3,80,128]{2,1,0:T(8,128)S(1)} %pad_maximum_fusion.4), channel_id=1, source_target_pairs={{0,4},{1,125},{2,6},{3,127},{4,8},{5,1},{6,10},{7,3},{8,12},{9,5},... | collective-permute-start | bytes 368648 | tf_op jit(solution)/shard_map/ppermute | solution.py:429
  49.9 4.4 %collective-permute-start.13 = (f32[3,80,128]{2,1,0:T(8,128)S(1)}, f32[3,80,128]{2,1,0:T(8,128)S(1)}, u32[]{:S(2)}, u32[]{:S(2)}) collective-permute-start(f32[3,80,128]{2,1,0:T(8,128)S(1)} %pad_maximum_fusion.5), channel_id=1, source_target_pairs={{0,1},{1,0},{2,3},{3,2},{4,5},{5,4},{6,7},{7,6},{8,9},{9,8},{10,11... | collective-permute-start | bytes 368648 | tf_op jit(solution)/shard_map/ppermute | solution.py:419

commit v5 on v4

--- a/solution.py
+++ b/solution.py
@@ -121,10 +121,15 @@
         copy.wait()
 
 
-def pack_kernel(me_ref, state_ref, level_ref, morton_ref, far_ref, sib_ref):
-    sib, far, _ = relay_slots(me_ref[0], morton_ref[...])
+def far_kernel(me_ref, state_ref, level_ref, morton_ref, far_ref):
+    _, far, _ = relay_slots(me_ref[0], morton_ref[...])
     lhs = relay_rows(state_ref[...], level_ref[...])
     store_moved(far_ref, dot_nt(lhs, one_hot_rows(HALF, far)))
+
+
+def sib_kernel(me_ref, state_ref, level_ref, morton_ref, sib_ref):
+    sib, _, _ = relay_slots(me_ref[0], morton_ref[...])
+    lhs = relay_rows(state_ref[...], level_ref[...])
     store_moved(sib_ref, dot_nt(lhs, one_hot_rows(HALF, sib)))
 
 
@@ -241,7 +246,7 @@
     return jnp.concatenate([ask[t : t + 1, :] for t in range(ask.shape[0])], axis=1)
 
 
-def reply(fields, ask, hot, got_ref, out_ref):
+def reply(fields, ask, hot, got_ref, outs):
     chunks = ask.shape[0]
     high, low = split(fields)
     both = dot(jnp.concatenate([high, low], axis=0), hot)
@@ -254,19 +259,20 @@
             x = trace(got_ref, t, v, 0)
             for f in range(1, 6):
                 x = jnp.where(face == f, trace(got_ref, t, v, f), x)
-            out_ref[t, 16 * v : 16 * v + 16, :] = x
+            outs[t][16 * v : 16 * v + 16, :] = x
 
 
 def hot_kernel(far_ref, ask_ref, rest_ref, reply_ref):
     for f in range(6):
         rest_ref[f] = one_hot_rows(3 * CAP, far_ref[f : f + 1, :])
-    reply_ref[...] = one_hot_rows(NEW_DEV, asked_code(ask_ref[3:8, :]) & (NEW_DEV - 1))
-
-
-def own_kernel(fields_ref, ask_ref, own_ref, got_ref):
-    ask = ask_ref[0:3, :]
+    reply_ref[...] = one_hot_rows(NEW_DEV, asked_code(ask_ref[4:8, :]) & (NEW_DEV - 1))
+
+
+def own_kernel(fields_ref, ask_ref, a_ref, b_ref, sib_ref, got_ref):
+    ask = ask_ref[0:4, :]
     hot = one_hot_rows(NEW_DEV, asked_code(ask) & (NEW_DEV - 1))
-    reply(wide(fields_ref, ROWS), ask, hot, got_ref, own_ref)
+    outs = [a_ref.at[0], a_ref.at[1], b_ref.at[0], sib_ref.at[0]]
+    reply(wide(fields_ref, ROWS), ask, hot, got_ref, outs)
 
 
 def first_kernel(me_ref, home_ref, far_ref, sib_ref, ask_ref, hot_ref, start_ref, swap_ref, got_ref):
@@ -277,7 +283,7 @@
         far = far_ref[:, spot]
         start_ref[c] = home_ref[c] + jnp.where(even, far, sib)
         start_ref[c + 2] = home_ref[c + 2] + jnp.where(even, sib, far)
-    reply(wide(start_ref, ROWS), ask_ref[3:8, :], hot_ref[...], got_ref, swap_ref)
+    reply(wide(start_ref, ROWS), ask_ref[4:8, :], hot_ref[...], got_ref, [swap_ref.at[t] for t in range(4)])
 
 
 def near_kernel(table_ref, fields_ref, near_ref, part_ref, high_ref, low_ref):
@@ -347,52 +353,52 @@
     return jnp.concatenate([high, low], axis=0)
 
 
-def add_ghosts(sum_ref, lhs, hot_of):
+def add_ghosts(sum_ref, lhs, hot_of, blocks=range(BLOCKS)):
     for f in range(6):
         both = dot(lhs, hot_of(f))
-        for c in range(BLOCKS):
-            spot = slice(128 * c, 128 * c + 128)
+        for i, c in enumerate(blocks):
+            spot = slice(128 * i, 128 * i + 128)
             term = both[0:TRACE_ROWS, spot] + both[TRACE_ROWS:, spot]
             for v in range(FIELDS):
                 add_on_face(sum_ref, c, v, f, term[16 * v : 16 * v + 16])
 
 
-def direct_kernel(part_ref, far_ref, ask_ref, a_ref, b_ref, swap_ref, sum_ref):
-    lhs = ghost_rows([swap_ref[0], a_ref[2], a_ref[0], b_ref[1], b_ref[0]], ask_ref)
+def direct_kernel(part_ref, far_ref, ask_ref, a_ref, b_ref, sib_ref, sum_ref):
+    lhs = ghost_rows([sib_ref[0], a_ref[2], a_ref[0], b_ref[1], b_ref[0]], ask_ref)
     sum_ref[...] = part_ref[...]
     add_ghosts(sum_ref, lhs, lambda f: one_hot_rows(5 * CAP, far_ref[f : f + 1, :] - 3 * CAP))
 
 
-def add_rest(part_ref, rest_ref, ask_ref, post_ref, sum_ref):
-    lhs = ghost_rows([post_ref[1], post_ref[0], post_ref[2]], ask_ref)
+def metric_of(start_ref, c):
+    return jnp.where(start_ref[c, ROWS : ROWS + 1, :] > 0.5, 2.0, 1.0)
+
+
+def second_kernel(start_ref, part_ref, rest_ref, own_ask_ref, post_ref, ask_ref, hot_ref,
+                  section_ref, swap_ref, sum_ref, got_ref):
+    lhs = ghost_rows([post_ref[1], post_ref[0], post_ref[2]], own_ask_ref)
     sum_ref[...] = part_ref[...]
     add_ghosts(sum_ref, lhs, lambda f: rest_ref[f])
-
-
-def metric_of(start_ref, c):
-    return jnp.where(start_ref[c, ROWS : ROWS + 1, :] > 0.5, 2.0, 1.0)
-
-
-def second_kernel(start_ref, part_ref, rest_ref, own_ask_ref, post_ref, ask_ref, hot_ref,
-                  section_ref, swap_ref, sum_ref, got_ref):
-    add_rest(part_ref, rest_ref, own_ask_ref, post_ref, sum_ref)
     for c in range(BLOCKS):
         section_ref[c] = start_ref[c, 0:ROWS, :] - (DT * metric_of(start_ref, c)) * sum_ref[c]
-    reply(wide(section_ref, ROWS), ask_ref[3:8, :], hot_ref[...], got_ref, swap_ref)
+    reply(wide(section_ref, ROWS), ask_ref[4:8, :], hot_ref[...], got_ref, [swap_ref.at[t] for t in range(4)])
 
 
 def last_kernel(start_ref, section_ref, part_ref, rest_ref, own_ask_ref, post_ref,
                 state_hbm, rate_hbm, sum_ref, state_ref, rate_ref, sems):
-    add_rest(part_ref, rest_ref, own_ask_ref, post_ref, sum_ref)
+    lhs = ghost_rows([post_ref[1], post_ref[0], post_ref[2]], own_ask_ref)
+    sum_ref[...] = part_ref[...]
     copies = []
-    for c in range(BLOCKS):
-        rate = -metric_of(start_ref, c) * sum_ref[c]
-        rate_ref[c] = rate
-        state_ref[c] = 0.5 * start_ref[c, 0:ROWS, :] + 0.5 * (section_ref[c] + DT * rate)
-        for i, (src, dst) in enumerate(((rate_ref, rate_hbm), (state_ref, state_hbm))):
-            copy = pltpu.make_async_copy(src.at[c], dst.at[:, pl.ds(128 * c, 128)], sems.at[i, c])
-            copy.start()
-            copies.append(copy)
+    for half in range(2):
+        pair = (2 * half, 2 * half + 1)
+        add_ghosts(sum_ref, lhs, lambda f: rest_ref[f, :, HALF * half : HALF * half + HALF], pair)
+        for c in pair:
+            rate = -metric_of(start_ref, c) * sum_ref[c]
+            rate_ref[c] = rate
+            state_ref[c] = 0.5 * start_ref[c, 0:ROWS, :] + 0.5 * (section_ref[c] + DT * rate)
+            for i, (src, dst) in enumerate(((rate_ref, rate_hbm), (state_ref, state_hbm))):
+                copy = pltpu.make_async_copy(src.at[c], dst.at[:, pl.ds(128 * c, 128)], sems.at[i, c])
+                copy.start()
+                copies.append(copy)
     for copy in copies:
         copy.wait()
 
@@ -430,8 +436,8 @@
 
 
 def outward_pair(own, got):
-    b = outward(jnp.concatenate([own[2:3], got[3:5]], axis=0), 4)
-    a = outward(jnp.concatenate([own[0:2], got[1:3]], axis=0), 2)
+    b = outward(jnp.concatenate([own[1], got[2:4]], axis=0), 4)
+    a = outward(jnp.concatenate([own[0], got[0:2]], axis=0), 2)
     return a, b
 
 
@@ -467,10 +473,13 @@
     )
     got = swap_cores(swap_ask)
     relay = [SM, VM, VM, VM]
-    to_far, to_sib = call(pack_kernel, [((MOVED_ROWS, HALF), F32)] * 2, (me, state, level, morton), relay)
-    got, to_far, to_sib, morton = lax.optimization_barrier((got, to_far, to_sib, morton))
-    a, b = outward_pair(own_ask, got)
+    moved = ((MOVED_ROWS, HALF), F32)
+    (to_far,) = call(far_kernel, [moved], (me, state, level, morton), relay)
+    got, to_far = lax.optimization_barrier((got, to_far))
+    a, b = outward_pair((own_ask[0:2], own_ask[2:3]), got[1:5])
     from_far = swap_chips(to_far)
+    a, morton = lax.optimization_barrier((a, morton))
+    (to_sib,) = call(sib_kernel, [moved], (me, state, level, morton), relay, flops=10**9)
     from_sib = swap_cores(to_sib)
     (home,) = call(home_kernel, [((BLOCKS, MOVED_ROWS, 128), F32)], (me, state, level, morton), relay)
     post = swap_back(a, b)
@@ -480,23 +489,24 @@
 
     rest_hot, reply_hot = call(
         hot_kernel,
-        [((6, 3 * CAP, NEW_DEV), BF16), ((NEW_DEV, 5 * CAP), BF16)],
+        [((6, 3 * CAP, NEW_DEV), BF16), ((NEW_DEV, 4 * CAP), BF16)],
         (far, asked),
         flops=10**9,
     )
-    swapped = ((5, TRACE_ROWS, CAP), F32)
-    got_scratch = ((5, ROWS, CAP), F32)
+    swapped = ((4, TRACE_ROWS, CAP), F32)
+    got_scratch = ((4, ROWS, CAP), F32)
     blocks = ((BLOCKS, ROWS, 128), F32)
     table = jnp.asarray(stacked_table())
 
     def neighbours_of(fields, swap):
         got = swap_cores(swap)
-        (own,) = call(
+        *own, sib = call(
             own_kernel,
-            [((3, TRACE_ROWS, CAP), F32)],
+            [((2, TRACE_ROWS, CAP), F32), ((1, TRACE_ROWS, CAP), F32), ((1, TRACE_ROWS, CAP), F32)],
             (fields, asked),
             None,
-            [((3, ROWS, CAP), F32)],
+            [got_scratch],
+            flops=10**9,
         )
         a, b = outward_pair(own, got)
         (part,) = call(
@@ -507,9 +517,11 @@
             [((FIELDS, 3 * DOFS, NEW_DEV), BF16)] * 2,
             flops=10**9,
         )
+        sib, part = lax.optimization_barrier((sib, part))
+        sib = swap_cores(sib)
         a, b, part = lax.optimization_barrier((a, b, part))
         post = swap_back(a, b)
-        (part,) = call(direct_kernel, [blocks], (part, far, swap_ask, a, b, got), flops=10**9)
+        (part,) = call(direct_kernel, [blocks], (part, far, swap_ask, a, b, sib), flops=10**9)
         return part, rest_hot, own_ask, post
 
     start, swap = call(

time: 56.5 us -> 55.9 us (0.989)
    ppermute x1, waiting for transfers between devices: 2.1 us -> 1.27 us  [swap_chips(): lax.ppermute(x, AXES, [(i, (i + (1 if i % 2 else -1)) % n) for i in range...]
    pallas_call x13 -> x14, Pallas kernels: 15.8 us -> 15.5 us  [call(): pl.pallas_call(kernel, out_shape=[jax.ShapeDtypeStruct(s, d) for s, d in...]
    ppermute x7 -> x9, starting transfers between devices: 8.69 us -> 8.76 us  [swap_cores(): return lax.ppermute(x, AXES, [(i, i ^ 1) for i in range(n)])]
    ppermute x7 -> x9, waiting for transfers between devices: 1.62 us -> 1.59 us  [swap_cores(): return lax.ppermute(x, AXES, [(i, i ^ 1) for i in range(n)])]
  transfers between devices with their start and end apart: 14 -> 16, of which waited for: 6 -> 7; matrix products, arithmetic and copies ran while one was open for 0% -> 0% of each run, Pallas kernels for 18% -> 19%
where the time goes in v5:
time: 55.9 us; the launch traced here: 55.7 us
  starting transfers between devices  27.8 us (50%)
  Pallas kernels  15.5 us (28%)
  waiting for transfers between devices  11.2 us (20%)
  between operations  1.04 us (2%)
    ppermute x6, starting transfers between devices, outward(): lax.ppermute(x, AXES, [(i, (i + (by if i % 2 == 0 else -by)) % n) for i i...  19 us
    pallas_call x14, Pallas kernels, call(): pl.pallas_call(kernel, out_shape=[jax.ShapeDtypeStruct(s, d) for s, d in...  15.5 us
    ppermute x9, starting transfers between devices, swap_cores(): return lax.ppermute(x, AXES, [(i, i ^ 1) for i in range(n)])  8.76 us
    ppermute x6, waiting for transfers between devices, outward(): lax.ppermute(x, AXES, [(i, (i + (by if i % 2 == 0 else -by)) % n) for i i...  8.36 us
    ppermute x9, waiting for transfers between devices, swap_cores(): return lax.ppermute(x, AXES, [(i, i ^ 1) for i in range(n)])  1.59 us
    ppermute x1, waiting for transfers between devices, swap_chips(): lax.ppermute(x, AXES, [(i, (i + (1 if i % 2 else -1)) % n) for i in range...  1.27 us
  transfers between devices with their start and end apart: 16, of which 7 were waited for; matrix products, arithmetic and copies ran while one was open for 0% of the time, Pallas kernels for 19%

profile of v5, /device:TPU:1, one launch (start us, length us, event | category | flops | bytes accessed | tf_op | source)
XLA Modules:
  0.0 55.7 jit_solution(6203237366996895859)
XLA Ops:
  0.6 1.5 %shard_map.68 = (s32[3,1,128]{2,1,0:T(1,128)S(1)}, s32[5,1,128]{2,1,0:T(1,128)S(1)}, s32[6,512]{1,0:T(8,128)S(1)}, s32[6,512]{1,0:T(8,128)S(1)}, f32[320,1024]{1...) custom-call(s32[1]{0:T(128)} %bitcast.me_ref, s32[6,512]{1,0:T(8,128)} %links_hbm.1, f32[320,1024]{1,0:T(8,128)} %bitcast.22, ...), custom_call_target="tpu_custom_call" | custom-call | flops 1000000 | bytes 1048576 | tf_op jit(solution)/shard_map/pallas_call | solution.py:412
  2.1 1.5 %collective-permute-start = (s32[5,1,128]{2,1,0:T(1,128)S(1)}, s32[5,1,128]{2,1,0:T(1,128)S(1)}, u32[]{:S(2)}, u32[]{:S(2)}) collective-permute-start(s32[5,1,128]{2,1,0:T(1,128)S(1)} %get-tuple-element.40.ask_ref), channel_id=1, source_target_pairs={{0,1},{1,0},{2,3},{3,2},{4,5},{5,4},{6,7},{7,6},{8,9},{9,8},{10,11... | collective-permute-start | bytes 7688 | tf_op jit(solution)/shard_map/ppermute | solution.py:425
  3.6 0.6 %shard_map.69 = f32[328,256]{1,0:T(8,128)S(1)} custom-call(s32[1]{0:T(128)} %bitcast.me_ref, f32[320,1024]{1,0:T(8,128)S(1)} %get-tuple-element.37.state_ref, s32[1,1024]{1,0:T(1,128)S(1)} %get-tuple-element.38.level_ref, s32[1,1024]{1,0:T(1,128)S(1)} %get-tuple-element.43.morton_ref), custom_call_target="tpu_custom_call" | custom-call | flops 1000000 | bytes 1048576 | tf_op jit(solution)/shard_map/pallas_call | solution.py:412
  4.2 0.2 collective-permute-done
  4.5 8.7 %collective-permute-start.4 = (s32[3,1,128]{2,1,0:T(1,128)S(1)}, s32[3,1,128]{2,1,0:T(1,128)S(1)}, u32[]{:S(2)}, u32[]{:S(2)}) collective-permute-start(s32[3,1,128]{2,1,0:T(1,128)S(1)} %pad_add_fusion.1), channel_id=1, source_target_pairs={{0,4},{1,125},{2,6},{3,127},{4,8},{5,1},{6,10},{7,3},{8,12},{9,5},... | collective-permute-start | bytes 4616 | tf_op jit(solution)/shard_map/ppermute | solution.py:435
  13.1 0.8 %collective-permute-start.1 = (s32[4,1,128]{2,1,0:T(1,128)S(1)}, s32[4,1,128]{2,1,0:T(1,128)S(1)}, u32[]{:S(2)}, u32[]{:S(2)}) collective-permute-start(s32[4,1,128]{2,1,0:T(1,128)S(1)} %pad_add_fusion), channel_id=1, source_target_pairs={{0,2},{1,127},{2,4},{3,1},{4,6},{5,3},{6,8},{7,5},{8,10},{9,7},{10... | collective-permute-start | bytes 6152 | tf_op jit(solution)/shard_map/ppermute | solution.py:435
  13.9 1.9 %collective-permute-done.1 = s32[4,1,128]{2,1,0:T(1,128)S(1)} collective-permute-done((s32[4,1,128]{2,1,0:T(1,128)S(1)}, s32[4,1,128]{2,1,0:T(1,128)S(1)}, u32[]{:S(2)}, u32[]{:S(2)}) %collective-permute-start.1) | collective-permute-done | bytes 2080 | tf_op jit(solution)/shard_map/ppermute | solution.py:435
  15.9 1.2 %collective-permute-start.5 = (s32[3,1,128]{2,1,0:T(1,128)S(1)}, s32[3,1,128]{2,1,0:T(1,128)S(1)}, u32[]{:S(2)}, u32[]{:S(2)}) collective-permute-start(s32[3,1,128]{2,1,0:T(1,128)S(1)} %pad_add_fusion.2), channel_id=1, source_target_pairs={{0,1},{1,0},{2,3},{3,2},{4,5},{5,4},{6,7},{7,6},{8,9},{9,8},{10,11... | collective-permute-start | bytes 4616 | tf_op jit(solution)/shard_map/ppermute | solution.py:425
  17.1 0.6 %shard_map.71 = f32[328,256]{1,0:T(8,128)S(1)} custom-call(s32[1]{0:T(128)} %bitcast.me_ref, f32[320,1024]{1,0:T(8,128)S(1)} %get-tuple-element.37.state_ref, s32[1,1024]{1,0:T(1,128)S(1)} %get-tuple-element.38.level_ref, s32[1,1024]{1,0:T(1,128)S(1)} %get-tuple-element.43.morton_ref), custom_call_target="tpu_custom_call" | custom-call | flops 1000000000 | bytes 1048576 | tf_op jit(solution)/shard_map/pallas_call | solution.py:412
  17.8 0.9 %shard_map.70.home_ref = f32[4,328,128]{2,1,0:T(8,128)S(1)} custom-call(s32[1]{0:T(128)} %bitcast.me_ref, f32[320,1024]{1,0:T(8,128)S(1)} %get-tuple-element.37.state_ref, s32[1,1024]{1,0:T(1,128)S(1)} %get-tuple-element.38.level_ref, s32[1,1024]{1,0:T(1,128)S(1)} %get-tuple-element.43.morton_ref), custom_call_target="tpu_custom_call" | custom-call | flops 1000000 | bytes 1048576 | tf_op jit(solution)/shard_map/pallas_call | solution.py:412
  18.8 0.5 shard_map.72
  19.2 1.3 %collective-permute-done.2.far_ref = f32[328,256]{1,0:T(8,128)S(1)} collective-permute-done((f32[328,256]{1,0:T(8,128)S(1)}, f32[328,256]{1,0:T(8,128)S(1)}, u32[]{:S(2)}, u32[]{:S(2)}) %collective-permute-start.2) | collective-permute-done | bytes 335904 | tf_op jit(solution)/shard_map/ppermute | solution.py:430
  20.5 0.6 %shard_map.73 = (f32[4,328,128]{2,1,0:T(8,128)S(1)}, f32[4,80,128]{2,1,0:T(8,128)S(1)}) custom-call(s32[1]{0:T(128)} %bitcast.me_ref, f32[4,328,128]{2,1,0:T(8,128)S(1)} %shard_map.70.home_ref, f32[328,256]{1,0:T(8,128)S(1)} %collective-permute-done.2.far_ref, f32[328,256]{1,0:T(8,128)S(1)} %collective-permute-done.3.sib_ref, ...), custom_call_target="tpu_custom_call" | custom-call | flops 1000000 | bytes 1048576 | tf_op jit(solution)/shard_map/pallas_call | solution.py:412
  21.1 0.4 collective-permute-start.6
  21.4 0.5 shard_map.74
  22.0 0.6 %collective-permute-done.6 = f32[4,80,128]{2,1,0:T(8,128)S(1)} collective-permute-done((f32[4,80,128]{2,1,0:T(8,128)S(1)}, f32[4,80,128]{2,1,0:T(8,128)S(1)}, u32[]{:S(2)}, u32[]{:S(2)}) %collective-permute-start.6) | collective-permute-done | bytes 163872 | tf_op jit(solution)/shard_map/ppermute | solution.py:425
  22.6 5.5 %collective-permute-start.7 = (f32[4,80,128]{2,1,0:T(8,128)S(1)}, f32[4,80,128]{2,1,0:T(8,128)S(1)}, u32[]{:S(2)}, u32[]{:S(2)}) collective-permute-start(f32[4,80,128]{2,1,0:T(8,128)S(1)} %pad_maximum_fusion), channel_id=1, source_target_pairs={{0,2},{1,127},{2,4},{3,1},{4,6},{5,3},{6,8},{7,5},{8,10},{9,7},{10... | collective-permute-start | bytes 491528 | tf_op jit(solution)/shard_map/ppermute | solution.py:435
  28.2 2.2 %shard_map.75.part_ref = f32[4,320,128]{2,1,0:T(8,128)S(1)} custom-call(bf16[128,192]{1,0:T(8,128)(2,1)S(1)} %copy-done, f32[4,328,128]{2,1,0:T(8,128)S(1)} %get-tuple-element.48.fields_ref.start_ref, s32[6,512]{1,0:T(8,128)S(1)} %get-tuple-element.53.near_ref), custom_call_target="tpu_custom_call" | custom-call | flops 1000000000 | bytes 1048576 | tf_op jit(solution)/shard_map/pallas_call | solution.py:412
  30.5 3.4 %collective-permute-done.8.b_ref = f32[3,80,128]{2,1,0:T(8,128)S(1)} collective-permute-done((f32[3,80,128]{2,1,0:T(8,128)S(1)}, f32[3,80,128]{2,1,0:T(8,128)S(1)}, u32[]{:S(2)}, u32[]{:S(2)}) %collective-permute-start.8) | collective-permute-done | bytes 122912 | tf_op jit(solution)/shard_map/ppermute | solution.py:435
  33.9 2.0 %collective-permute-start.10 = (f32[3,80,128]{2,1,0:T(8,128)S(1)}, f32[3,80,128]{2,1,0:T(8,128)S(1)}, u32[]{:S(2)}, u32[]{:S(2)}) collective-permute-start(f32[3,80,128]{2,1,0:T(8,128)S(1)} %pad_maximum_fusion.3), channel_id=1, source_target_pairs={{0,1},{1,0},{2,3},{3,2},{4,5},{5,4},{6,7},{7,6},{8,9},{9,8},{10,11... | collective-permute-start | bytes 368648 | tf_op jit(solution)/shard_map/ppermute | solution.py:425
  36.0 1.2 %shard_map.76.part_ref = f32[4,320,128]{2,1,0:T(8,128)S(1)} custom-call(f32[4,320,128]{2,1,0:T(8,128)S(1)} %shard_map.75.part_ref, s32[6,512]{1,0:T(8,128)S(1)} %get-tuple-element.46.far_ref, s32[5,1,128]{2,1,0:T(1,128)S(1)} %get-tuple-element.40.ask_ref, f32[4,80,128]{2,1,0:T(8,128)S(1)} %collective-permute-done.7.a_ref, ...), custom_call_target="tpu_custom_call" | custom-call | flops 1000000000 | bytes 1048576 | tf_op jit(solution)/shard_map/pallas_call | solution.py:412
  37.2 1.3 %shard_map.77 = (f32[4,320,128]{2,1,0:T(8,128)S(1)}, f32[4,80,128]{2,1,0:T(8,128)S(1)}) custom-call(f32[4,328,128]{2,1,0:T(8,128)S(1)} %get-tuple-element.48.fields_ref.start_ref, f32[4,320,128]{2,1,0:T(8,128)S(1)} %shard_map.76.part_ref, bf16[6,384,512]{2,1,0:T(8,128)(2,1)S(1)} %get-tuple-element.59.rest_ref, ...), custom_call_target="tpu_custom_call" | custom-call | flops 1000000 | bytes 1048576 | tf_op jit(solution)/shard_map/pallas_call | solution.py:412
  38.5 0.2 collective-permute-start.11
  38.7 0.5 shard_map.78
  39.2 0.8 %collective-permute-done.11 = f32[4,80,128]{2,1,0:T(8,128)S(1)} collective-permute-done((f32[4,80,128]{2,1,0:T(8,128)S(1)}, f32[4,80,128]{2,1,0:T(8,128)S(1)}, u32[]{:S(2)}, u32[]{:S(2)}) %collective-permute-start.11) | collective-permute-done | bytes 163872 | tf_op jit(solution)/shard_map/ppermute | solution.py:425
  40.0 3.7 %collective-permute-start.12 = (f32[4,80,128]{2,1,0:T(8,128)S(1)}, f32[4,80,128]{2,1,0:T(8,128)S(1)}, u32[]{:S(2)}, u32[]{:S(2)}) collective-permute-start(f32[4,80,128]{2,1,0:T(8,128)S(1)} %pad_maximum_fusion.1), channel_id=1, source_target_pairs={{0,2},{1,127},{2,4},{3,1},{4,6},{5,3},{6,8},{7,5},{8,10},{9,7},{10... | collective-permute-start | bytes 491528 | tf_op jit(solution)/shard_map/ppermute | solution.py:435
  43.7 0.3 collective-permute-start.13
  44.0 2.2 %shard_map.79.part_ref = f32[4,320,128]{2,1,0:T(8,128)S(1)} custom-call(bf16[128,192]{1,0:T(8,128)(2,1)S(1)} %copy-done, f32[4,320,128]{2,1,0:T(8,128)S(1)} %get-tuple-element.60.fields_ref.section_ref, s32[6,512]{1,0:T(8,128)S(1)} %get-tuple-element.53.near_ref), custom_call_target="tpu_custom_call" | custom-call | flops 1000000000 | bytes 1048576 | tf_op jit(solution)/shard_map/pallas_call | solution.py:412
  46.3 3.0 %collective-permute-done.13.b_ref = f32[3,80,128]{2,1,0:T(8,128)S(1)} collective-permute-done((f32[3,80,128]{2,1,0:T(8,128)S(1)}, f32[3,80,128]{2,1,0:T(8,128)S(1)}, u32[]{:S(2)}, u32[]{:S(2)}) %collective-permute-start.13) | collective-permute-done | bytes 122912 | tf_op jit(solution)/shard_map/ppermute | solution.py:435
  49.3 3.2 %collective-permute-start.15 = (f32[3,80,128]{2,1,0:T(8,128)S(1)}, f32[3,80,128]{2,1,0:T(8,128)S(1)}, u32[]{:S(2)}, u32[]{:S(2)}) collective-permute-start(f32[3,80,128]{2,1,0:T(8,128)S(1)} %pad_maximum_fusion.5), channel_id=1, source_target_pairs={{0,1},{1,0},{2,3},{3,2},{4,5},{5,4},{6,7},{7,6},{8,9},{9,8},{10,11... | collective-permute-start | bytes 368648 | tf_op jit(solution)/shard_map/ppermute | solution.py:425
  52.6 1.2 %shard_map.80.part_ref = f32[4,320,128]{2,1,0:T(8,128)S(1)} custom-call(f32[4,320,128]{2,1,0:T(8,128)S(1)} %shard_map.79.part_ref, s32[6,512]{1,0:T(8,128)S(1)} %get-tuple-element.46.far_ref, s32[5,1,128]{2,1,0:T(1,128)S(1)} %get-tuple-element.40.ask_ref, f32[4,80,128]{2,1,0:T(8,128)S(1)} %collective-permute-done.12.a_ref, ...), custom_call_target="tpu_custom_call" | custom-call | flops 1000000000 | bytes 1048576 | tf_op jit(solution)/shard_map/pallas_call | solution.py:412
  53.8 1.7 %shard_map.81 = (f32[320,512]{1,0:T(8,128)}, f32[320,512]{1,0:T(8,128)}) custom-call(f32[4,328,128]{2,1,0:T(8,128)S(1)} %get-tuple-element.48.fields_ref.start_ref, f32[4,320,128]{2,1,0:T(8,128)S(1)} %get-tuple-element.60.fields_ref.section_ref, f32[4,320,128]{2,1,0:T(8,128)S(1)} %shard_map.80.part_ref, bf16[6,384,512]{2,1,0:T(8,128)(2,1)S(1)} %get-tuple-element.59.rest_ref, ...), custom_call_target="tpu_custom_call" | custom-call | flops 1000000 | bytes 1048576 | tf_op jit(solution)/shard_map/pallas_call | solution.py:412
  (39 shorter events, 0.5 us)
Async XLA Ops:
  2.1 2.3 %collective-permute-start = (s32[5,1,128]{2,1,0:T(1,128)S(1)}, s32[5,1,128]{2,1,0:T(1,128)S(1)}, u32[]{:S(2)}, u32[]{:S(2)}) collective-permute-start(s32[5,1,128]{2,1,0:T(1,128)S(1)} %get-tuple-element.40.ask_ref), channel_id=1, source_target_pairs={{0,1},{1,0},{2,3},{3,2},{4,5},{5,4},{6,7},{7,6},{8,9},{9,8},{10,11... | collective-permute-start | bytes 7688 | tf_op jit(solution)/shard_map/ppermute | solution.py:425
  4.5 9.4 %collective-permute-start.4 = (s32[3,1,128]{2,1,0:T(1,128)S(1)}, s32[3,1,128]{2,1,0:T(1,128)S(1)}, u32[]{:S(2)}, u32[]{:S(2)}) collective-permute-start(s32[3,1,128]{2,1,0:T(1,128)S(1)} %pad_add_fusion.1), channel_id=1, source_target_pairs={{0,4},{1,125},{2,6},{3,127},{4,8},{5,1},{6,10},{7,3},{8,12},{9,5},... | collective-permute-start | bytes 4616 | tf_op jit(solution)/shard_map/ppermute | solution.py:435
  13.1 2.7 %collective-permute-start.1 = (s32[4,1,128]{2,1,0:T(1,128)S(1)}, s32[4,1,128]{2,1,0:T(1,128)S(1)}, u32[]{:S(2)}, u32[]{:S(2)}) collective-permute-start(s32[4,1,128]{2,1,0:T(1,128)S(1)} %pad_add_fusion), channel_id=1, source_target_pairs={{0,2},{1,127},{2,4},{3,1},{4,6},{5,3},{6,8},{7,5},{8,10},{9,7},{10... | collective-permute-start | bytes 6152 | tf_op jit(solution)/shard_map/ppermute | solution.py:435
  13.9 6.6 %collective-permute-start.2 = (f32[328,256]{1,0:T(8,128)S(1)}, f32[328,256]{1,0:T(8,128)S(1)}, u32[]{:S(2)}, u32[]{:S(2)}) collective-permute-start(f32[328,256]{1,0:T(8,128)S(1)} %shard_map.69), channel_id=1, source_target_pairs={{0,127},{1,2},{2,1},{3,4},{4,3},{5,6},{6,5},{7,8},{8,7},{9,10},{10... | collective-permute-start | bytes 1007624 | tf_op jit(solution)/shard_map/ppermute | solution.py:430
  15.9 2.8 %collective-permute-start.5 = (s32[3,1,128]{2,1,0:T(1,128)S(1)}, s32[3,1,128]{2,1,0:T(1,128)S(1)}, u32[]{:S(2)}, u32[]{:S(2)}) collective-permute-start(s32[3,1,128]{2,1,0:T(1,128)S(1)} %pad_add_fusion.2), channel_id=1, source_target_pairs={{0,1},{1,0},{2,3},{3,2},{4,5},{5,4},{6,7},{7,6},{8,9},{9,8},{10,11... | collective-permute-start | bytes 4616 | tf_op jit(solution)/shard_map/ppermute | solution.py:425
  17.7 2.8 %collective-permute-start.3 = (f32[328,256]{1,0:T(8,128)S(1)}, f32[328,256]{1,0:T(8,128)S(1)}, u32[]{:S(2)}, u32[]{:S(2)}) collective-permute-start(f32[328,256]{1,0:T(8,128)S(1)} %shard_map.71), channel_id=1, source_target_pairs={{0,1},{1,0},{2,3},{3,2},{4,5},{5,4},{6,7},{7,6},{8,9},{9,8},{10,11... | collective-permute-start | bytes 1007624 | tf_op jit(solution)/shard_map/ppermute | solution.py:425
  21.1 1.5 %collective-permute-start.6 = (f32[4,80,128]{2,1,0:T(8,128)S(1)}, f32[4,80,128]{2,1,0:T(8,128)S(1)}, u32[]{:S(2)}, u32[]{:S(2)}) collective-permute-start(f32[4,80,128]{2,1,0:T(8,128)S(1)} %get-tuple-element.50), channel_id=1, source_target_pairs={{0,1},{1,0},{2,3},{3,2},{4,5},{5,4},{6,7},{7,6},{8,9},{9,8},{10,11... | collective-permute-start | bytes 491528 | tf_op jit(solution)/shard_map/ppermute | solution.py:425
  21.4 6.8 %copy-start = (bf16[128,192]{1,0:T(8,128)(2,1)S(1)}, bf16[128,192]{1,0:T(8,128)(2,1)}, u32[]{:S(2)}) copy-start(bf16[128,192]{1,0:T(8,128)(2,1)} %constant.13.clone.table_ref) | copy-start | bytes 147460
  22.6 11.3 %collective-permute-start.7 = (f32[4,80,128]{2,1,0:T(8,128)S(1)}, f32[4,80,128]{2,1,0:T(8,128)S(1)}, u32[]{:S(2)}, u32[]{:S(2)}) collective-permute-start(f32[4,80,128]{2,1,0:T(8,128)S(1)} %pad_maximum_fusion), channel_id=1, source_target_pairs={{0,2},{1,127},{2,4},{3,1},{4,6},{5,3},{6,8},{7,5},{8,10},{9,7},{10... | collective-permute-start | bytes 491528 | tf_op jit(solution)/shard_map/ppermute | solution.py:435
  28.1 5.8 %collective-permute-start.8 = (f32[3,80,128]{2,1,0:T(8,128)S(1)}, f32[3,80,128]{2,1,0:T(8,128)S(1)}, u32[]{:S(2)}, u32[]{:S(2)}) collective-permute-start(f32[3,80,128]{2,1,0:T(8,128)S(1)} %pad_maximum_fusion.2), channel_id=1, source_target_pairs={{0,4},{1,125},{2,6},{3,127},{4,8},{5,1},{6,10},{7,3},{8,12},{9,5},... | collective-permute-start | bytes 368648 | tf_op jit(solution)/shard_map/ppermute | solution.py:435
  30.4 5.5 %collective-permute-start.9 = (f32[1,80,128]{2,1,0:T(8,128)S(1)}, f32[1,80,128]{2,1,0:T(8,128)S(1)}, u32[]{:S(2)}, u32[]{:S(2)}) collective-permute-start(f32[1,80,128]{2,1,0:T(8,128)S(1)} %get-tuple-element.58), channel_id=1, source_target_pairs={{0,1},{1,0},{2,3},{3,2},{4,5},{5,4},{6,7},{7,6},{8,9},{9,8},{10,11... | collective-permute-start | bytes 122888 | tf_op jit(solution)/shard_map/ppermute | solution.py:425
  33.9 3.2 %collective-permute-start.10 = (f32[3,80,128]{2,1,0:T(8,128)S(1)}, f32[3,80,128]{2,1,0:T(8,128)S(1)}, u32[]{:S(2)}, u32[]{:S(2)}) collective-permute-start(f32[3,80,128]{2,1,0:T(8,128)S(1)} %pad_maximum_fusion.3), channel_id=1, source_target_pairs={{0,1},{1,0},{2,3},{3,2},{4,5},{5,4},{6,7},{7,6},{8,9},{9,8},{10,11... | collective-permute-start | bytes 368648 | tf_op jit(solution)/shard_map/ppermute | solution.py:425
  38.5 1.5 %collective-permute-start.11 = (f32[4,80,128]{2,1,0:T(8,128)S(1)}, f32[4,80,128]{2,1,0:T(8,128)S(1)}, u32[]{:S(2)}, u32[]{:S(2)}) collective-permute-start(f32[4,80,128]{2,1,0:T(8,128)S(1)} %get-tuple-element.62), channel_id=1, source_target_pairs={{0,1},{1,0},{2,3},{3,2},{4,5},{5,4},{6,7},{7,6},{8,9},{9,8},{10,11... | collective-permute-start | bytes 491528 | tf_op jit(solution)/shard_map/ppermute | solution.py:425
  40.0 9.3 %collective-permute-start.12 = (f32[4,80,128]{2,1,0:T(8,128)S(1)}, f32[4,80,128]{2,1,0:T(8,128)S(1)}, u32[]{:S(2)}, u32[]{:S(2)}) collective-permute-start(f32[4,80,128]{2,1,0:T(8,128)S(1)} %pad_maximum_fusion.1), channel_id=1, source_target_pairs={{0,2},{1,127},{2,4},{3,1},{4,6},{5,3},{6,8},{7,5},{8,10},{9,7},{10... | collective-permute-start | bytes 491528 | tf_op jit(solution)/shard_map/ppermute | solution.py:435
  43.7 5.6 %collective-permute-start.13 = (f32[3,80,128]{2,1,0:T(8,128)S(1)}, f32[3,80,128]{2,1,0:T(8,128)S(1)}, u32[]{:S(2)}, u32[]{:S(2)}) collective-permute-start(f32[3,80,128]{2,1,0:T(8,128)S(1)} %pad_maximum_fusion.4), channel_id=1, source_target_pairs={{0,4},{1,125},{2,6},{3,127},{4,8},{5,1},{6,10},{7,3},{8,12},{9,5},... | collective-permute-start | bytes 368648 | tf_op jit(solution)/shard_map/ppermute | solution.py:435
  46.2 6.4 %collective-permute-start.14 = (f32[1,80,128]{2,1,0:T(8,128)S(1)}, f32[1,80,128]{2,1,0:T(8,128)S(1)}, u32[]{:S(2)}, u32[]{:S(2)}) collective-permute-start(f32[1,80,128]{2,1,0:T(8,128)S(1)} %get-tuple-element.69), channel_id=1, source_target_pairs={{0,1},{1,0},{2,3},{3,2},{4,5},{5,4},{6,7},{7,6},{8,9},{9,8},{10,11... | collective-permute-start | bytes 122888 | tf_op jit(solution)/shard_map/ppermute | solution.py:425
  49.3 4.4 %collective-permute-start.15 = (f32[3,80,128]{2,1,0:T(8,128)S(1)}, f32[3,80,128]{2,1,0:T(8,128)S(1)}, u32[]{:S(2)}, u32[]{:S(2)}) collective-permute-start(f32[3,80,128]{2,1,0:T(8,128)S(1)} %pad_maximum_fusion.5), channel_id=1, source_target_pairs={{0,1},{1,0},{2,3},{3,2},{4,5},{5,4},{6,7},{7,6},{8,9},{9,8},{10,11... | collective-permute-start | bytes 368648 | tf_op jit(solution)/shard_map/ppermute | solution.py:425

commit v6 on v5

--- a/solution.py
+++ b/solution.py
@@ -275,14 +275,13 @@
     reply(wide(fields_ref, ROWS), ask, hot, got_ref, outs)
 
 
-def first_kernel(me_ref, home_ref, far_ref, sib_ref, ask_ref, hot_ref, start_ref, swap_ref, got_ref):
+def first_kernel(me_ref, home_ref, prior_ref, next_ref, sib_ref, ask_ref, hot_ref, start_ref, swap_ref, got_ref):
     even = (me_ref[0] & 1) == 0
     for c in range(2):
         spot = slice(128 * c, 128 * c + 128)
         sib = sib_ref[:, spot]
-        far = far_ref[:, spot]
-        start_ref[c] = home_ref[c] + jnp.where(even, far, sib)
-        start_ref[c + 2] = home_ref[c + 2] + jnp.where(even, sib, far)
+        start_ref[c] = home_ref[c] + jnp.where(even, prior_ref[:, spot], sib)
+        start_ref[c + 2] = home_ref[c + 2] + jnp.where(even, sib, next_ref[:, spot])
     reply(wide(start_ref, ROWS), ask_ref[4:8, :], hot_ref[...], got_ref, [swap_ref.at[t] for t in range(4)])
 
 
@@ -425,9 +424,14 @@
     return lax.ppermute(x, AXES, [(i, i ^ 1) for i in range(n)])
 
 
-def swap_chips(x):
+def to_next_chip(x):
     n = lax.axis_size(AXES)
-    return lax.ppermute(x, AXES, [(i, (i + (1 if i % 2 else -1)) % n) for i in range(n)])
+    return lax.ppermute(x, AXES, [(i, (i + 1) % n) for i in range(1, n, 2)])
+
+
+def to_prior_chip(x):
+    n = lax.axis_size(AXES)
+    return lax.ppermute(x, AXES, [(i, (i - 1) % n) for i in range(0, n, 2)])
 
 
 def outward(x, by):
@@ -475,9 +479,10 @@
     relay = [SM, VM, VM, VM]
     moved = ((MOVED_ROWS, HALF), F32)
     (to_far,) = call(far_kernel, [moved], (me, state, level, morton), relay)
+    from_prior = to_next_chip(to_far)
     got, to_far = lax.optimization_barrier((got, to_far))
     a, b = outward_pair((own_ask[0:2], own_ask[2:3]), got[1:5])
-    from_far = swap_chips(to_far)
+    from_next = to_prior_chip(to_far)
     a, morton = lax.optimization_barrier((a, morton))
     (to_sib,) = call(sib_kernel, [moved], (me, state, level, morton), relay, flops=10**9)
     from_sib = swap_cores(to_sib)
@@ -527,8 +532,8 @@
     start, swap = call(
         first_kernel,
         [((BLOCKS, MOVED_ROWS, 128), F32), swapped],
-        (me, home, from_far, from_sib, asked, reply_hot),
-        [SM, VM, VM, VM, VM, VM],
+        (me, home, from_prior, from_next, from_sib, asked, reply_hot),
+        [SM, VM, VM, VM, VM, VM, VM],
         [got_scratch],
     )
     ghosts = neighbours_of(start, swap)

time: 55.9 us -> 60.5 us (1.082)
  starting transfers between devices: 27.8 us -> 31.6 us
  waiting for transfers between devices: 11.2 us -> 12 us
    ppermute x1 -> x2, starting transfers between devices: 0.01 us -> 4.49 us  [the longest x1 3.21 us: to_next_chip(): return lax.ppermute(x, AXES, [(i, (i + 1) % n) for i in range(1, n, 2)])]
    ppermute x1 -> x2, waiting for transfers between devices: 1.27 us -> 3.89 us  [the longest x1 3.89 us: to_prior_chip(): return lax.ppermute(x, AXES, [(i, (i - 1) % n) for i in range(0, n, 2)])]
    ppermute x6, waiting for transfers between devices: 8.36 us -> 6.5 us  [outward(): lax.ppermute(x, AXES, [(i, (i + (by if i % 2 == 0 else -by)) % n) for i i...]
    ppermute x9, starting transfers between devices: 8.76 us -> 8.15 us  [swap_cores(): return lax.ppermute(x, AXES, [(i, i ^ 1) for i in range(n)])]
  transfers between devices with their start and end apart: 16 -> 17, of which waited for: 7 -> 6; matrix products, arithmetic and copies ran while one was open for 0% -> 0% of each run, Pallas kernels for 19% -> 17%
where the time goes in v6:
time: 60.5 us; the launch traced here: 60.3 us
  starting transfers between devices  31.6 us (52%)
  Pallas kernels  15.4 us (25%)
  waiting for transfers between devices  12 us (20%)
  between operations  1.12 us (2%)
    ppermute x6, starting transfers between devices, outward(): lax.ppermute(x, AXES, [(i, (i + (by if i % 2 == 0 else -by)) % n) for i i...  19 us
    pallas_call x14, Pallas kernels, call(): pl.pallas_call(kernel, out_shape=[jax.ShapeDtypeStruct(s, d) for s, d in...  15.4 us
    ppermute x9, starting transfers between devices, swap_cores(): return lax.ppermute(x, AXES, [(i, i ^ 1) for i in range(n)])  8.15 us
    ppermute x6, waiting for transfers between devices, outward(): lax.ppermute(x, AXES, [(i, (i + (by if i % 2 == 0 else -by)) % n) for i i...  6.5 us
    ppermute x1, waiting for transfers between devices, to_prior_chip(): return lax.ppermute(x, AXES, [(i, (i - 1) % n) for i in range(0, n, 2)])  3.89 us
    ppermute x1, starting transfers between devices, to_next_chip(): return lax.ppermute(x, AXES, [(i, (i + 1) % n) for i in range(1, n, 2)])  3.21 us
    ppermute x9, waiting for transfers between devices, swap_cores(): return lax.ppermute(x, AXES, [(i, i ^ 1) for i in range(n)])  1.61 us
    ppermute x1, starting transfers between devices, to_prior_chip(): return lax.ppermute(x, AXES, [(i, (i - 1) % n) for i in range(0, n, 2)])  1.28 us
  transfers between devices with their start and end apart: 17, of which 6 were waited for; matrix products, arithmetic and copies ran while one was open for 0% of the time, Pallas kernels for 17%

profile of v6, /device:TPU:1, one launch (start us, length us, event | category | flops | bytes accessed | tf_op | source)
XLA Modules:
  0.0 60.3 jit_solution(5638314646157255229)
XLA Ops:
  0.6 1.5 %shard_map.68 = (s32[3,1,128]{2,1,0:T(1,128)S(1)}, s32[5,1,128]{2,1,0:T(1,128)S(1)}, s32[6,512]{1,0:T(8,128)S(1)}, s32[6,512]{1,0:T(8,128)S(1)}, f32[320,1024]{1...) custom-call(s32[1]{0:T(128)} %bitcast.me_ref, s32[6,512]{1,0:T(8,128)} %links_hbm.1, f32[320,1024]{1,0:T(8,128)} %bitcast.22, ...), custom_call_target="tpu_custom_call" | custom-call | flops 1000000 | bytes 1048576 | tf_op jit(solution)/shard_map/pallas_call | solution.py:411
  2.1 1.5 %collective-permute-start = (s32[5,1,128]{2,1,0:T(1,128)S(1)}, s32[5,1,128]{2,1,0:T(1,128)S(1)}, u32[]{:S(2)}, u32[]{:S(2)}) collective-permute-start(s32[5,1,128]{2,1,0:T(1,128)S(1)} %get-tuple-element.40.ask_ref), channel_id=1, source_target_pairs={{0,1},{1,0},{2,3},{3,2},{4,5},{5,4},{6,7},{7,6},{8,9},{9,8},{10,11... | collective-permute-start | bytes 7688 | tf_op jit(solution)/shard_map/ppermute | solution.py:424
  3.6 0.6 shard_map.69
  4.2 3.2 %collective-permute-start.2 = (f32[328,256]{1,0:T(8,128)S(1)}, f32[328,256]{1,0:T(8,128)S(1)}, u32[]{:S(2)}, u32[]{:S(2)}) collective-permute-start(f32[328,256]{1,0:T(8,128)S(1)} %shard_map.69), channel_id=1, source_target_pairs={{1,2},{3,4},{5,6},{7,8},{9,10},{11,12},{13,14},{15,16},{17,18},{19... | collective-permute-start | bytes 1007624 | tf_op jit(solution)/shard_map/ppermute | solution.py:429
  7.5 8.4 %collective-permute-start.5 = (s32[3,1,128]{2,1,0:T(1,128)S(1)}, s32[3,1,128]{2,1,0:T(1,128)S(1)}, u32[]{:S(2)}, u32[]{:S(2)}) collective-permute-start(s32[3,1,128]{2,1,0:T(1,128)S(1)} %pad_add_fusion.1), channel_id=1, source_target_pairs={{0,4},{1,125},{2,6},{3,127},{4,8},{5,1},{6,10},{7,3},{8,12},{9,5},... | collective-permute-start | bytes 4616 | tf_op jit(solution)/shard_map/ppermute | solution.py:439
  15.8 1.1 %collective-permute-start.1 = (s32[4,1,128]{2,1,0:T(1,128)S(1)}, s32[4,1,128]{2,1,0:T(1,128)S(1)}, u32[]{:S(2)}, u32[]{:S(2)}) collective-permute-start(s32[4,1,128]{2,1,0:T(1,128)S(1)} %pad_add_fusion), channel_id=1, source_target_pairs={{0,2},{1,127},{2,4},{3,1},{4,6},{5,3},{6,8},{7,5},{8,10},{9,7},{10... | collective-permute-start | bytes 6152 | tf_op jit(solution)/shard_map/ppermute | solution.py:439
  16.9 1.3 %collective-permute-start.3 = (f32[328,256]{1,0:T(8,128)S(1)}, f32[328,256]{1,0:T(8,128)S(1)}, u32[]{:S(2)}, u32[]{:S(2)}) collective-permute-start(f32[328,256]{1,0:T(8,128)S(1)} %shard_map.69), channel_id=1, source_target_pairs={{0,127},{2,1},{4,3},{6,5},{8,7},{10,9},{12,11},{14,13},{16,15},{18... | collective-permute-start | bytes 1007624 | tf_op jit(solution)/shard_map/ppermute | solution.py:434
  18.2 0.4 collective-permute-done.1
  18.6 0.8 %collective-permute-start.6 = (s32[3,1,128]{2,1,0:T(1,128)S(1)}, s32[3,1,128]{2,1,0:T(1,128)S(1)}, u32[]{:S(2)}, u32[]{:S(2)}) collective-permute-start(s32[3,1,128]{2,1,0:T(1,128)S(1)} %pad_add_fusion.2), channel_id=1, source_target_pairs={{0,1},{1,0},{2,3},{3,2},{4,5},{5,4},{6,7},{7,6},{8,9},{9,8},{10,11... | collective-permute-start | bytes 4616 | tf_op jit(solution)/shard_map/ppermute | solution.py:424
  19.4 0.6 shard_map.71
  20.0 0.9 %shard_map.70.home_ref = f32[4,328,128]{2,1,0:T(8,128)S(1)} custom-call(s32[1]{0:T(128)} %bitcast.me_ref, f32[320,1024]{1,0:T(8,128)S(1)} %get-tuple-element.37.state_ref, s32[1,1024]{1,0:T(1,128)S(1)} %get-tuple-element.38.level_ref, s32[1,1024]{1,0:T(1,128)S(1)} %get-tuple-element.43.morton_ref), custom_call_target="tpu_custom_call" | custom-call | flops 1000000 | bytes 1048576 | tf_op jit(solution)/shard_map/pallas_call | solution.py:411
  21.0 0.5 shard_map.72
  21.5 3.9 %collective-permute-done.3.next_ref = f32[328,256]{1,0:T(8,128)S(1)} collective-permute-done((f32[328,256]{1,0:T(8,128)S(1)}, f32[328,256]{1,0:T(8,128)S(1)}, u32[]{:S(2)}, u32[]{:S(2)}) %collective-permute-start.3) | collective-permute-done | bytes 335904 | tf_op jit(solution)/shard_map/ppermute | solution.py:434
  25.4 0.5 shard_map.73
  26.0 0.5 shard_map.74
  26.6 0.8 %collective-permute-done.7 = f32[4,80,128]{2,1,0:T(8,128)S(1)} collective-permute-done((f32[4,80,128]{2,1,0:T(8,128)S(1)}, f32[4,80,128]{2,1,0:T(8,128)S(1)}, u32[]{:S(2)}, u32[]{:S(2)}) %collective-permute-start.7) | collective-permute-done | bytes 163872 | tf_op jit(solution)/shard_map/ppermute | solution.py:424
  27.4 5.5 %collective-permute-start.8 = (f32[4,80,128]{2,1,0:T(8,128)S(1)}, f32[4,80,128]{2,1,0:T(8,128)S(1)}, u32[]{:S(2)}, u32[]{:S(2)}) collective-permute-start(f32[4,80,128]{2,1,0:T(8,128)S(1)} %pad_maximum_fusion), channel_id=1, source_target_pairs={{0,2},{1,127},{2,4},{3,1},{4,6},{5,3},{6,8},{7,5},{8,10},{9,7},{10... | collective-permute-start | bytes 491528 | tf_op jit(solution)/shard_map/ppermute | solution.py:439
  33.1 2.2 %shard_map.75.part_ref = f32[4,320,128]{2,1,0:T(8,128)S(1)} custom-call(bf16[128,192]{1,0:T(8,128)(2,1)S(1)} %copy-done, f32[4,328,128]{2,1,0:T(8,128)S(1)} %get-tuple-element.48.fields_ref.start_ref, s32[6,512]{1,0:T(8,128)S(1)} %get-tuple-element.53.near_ref), custom_call_target="tpu_custom_call" | custom-call | flops 1000000000 | bytes 1048576 | tf_op jit(solution)/shard_map/pallas_call | solution.py:411
  35.3 3.2 %collective-permute-done.9.b_ref = f32[3,80,128]{2,1,0:T(8,128)S(1)} collective-permute-done((f32[3,80,128]{2,1,0:T(8,128)S(1)}, f32[3,80,128]{2,1,0:T(8,128)S(1)}, u32[]{:S(2)}, u32[]{:S(2)}) %collective-permute-start.9) | collective-permute-done | bytes 122912 | tf_op jit(solution)/shard_map/ppermute | solution.py:439
  38.6 2.2 %collective-permute-start.11 = (f32[3,80,128]{2,1,0:T(8,128)S(1)}, f32[3,80,128]{2,1,0:T(8,128)S(1)}, u32[]{:S(2)}, u32[]{:S(2)}) collective-permute-start(f32[3,80,128]{2,1,0:T(8,128)S(1)} %pad_maximum_fusion.3), channel_id=1, source_target_pairs={{0,1},{1,0},{2,3},{3,2},{4,5},{5,4},{6,7},{7,6},{8,9},{9,8},{10,11... | collective-permute-start | bytes 368648 | tf_op jit(solution)/shard_map/ppermute | solution.py:424
  40.8 1.2 %shard_map.76.part_ref = f32[4,320,128]{2,1,0:T(8,128)S(1)} custom-call(f32[4,320,128]{2,1,0:T(8,128)S(1)} %shard_map.75.part_ref, s32[6,512]{1,0:T(8,128)S(1)} %get-tuple-element.46.far_ref, s32[5,1,128]{2,1,0:T(1,128)S(1)} %get-tuple-element.40.ask_ref, f32[4,80,128]{2,1,0:T(8,128)S(1)} %collective-permute-done.8.a_ref, ...), custom_call_target="tpu_custom_call" | custom-call | flops 1000000000 | bytes 1048576 | tf_op jit(solution)/shard_map/pallas_call | solution.py:411
  42.0 1.3 %shard_map.77 = (f32[4,320,128]{2,1,0:T(8,128)S(1)}, f32[4,80,128]{2,1,0:T(8,128)S(1)}) custom-call(f32[4,328,128]{2,1,0:T(8,128)S(1)} %get-tuple-element.48.fields_ref.start_ref, f32[4,320,128]{2,1,0:T(8,128)S(1)} %shard_map.76.part_ref, bf16[6,384,512]{2,1,0:T(8,128)(2,1)S(1)} %get-tuple-element.59.rest_ref, ...), custom_call_target="tpu_custom_call" | custom-call | flops 1000000 | bytes 1048576 | tf_op jit(solution)/shard_map/pallas_call | solution.py:411
  43.3 0.2 collective-permute-start.12
  43.5 0.5 shard_map.78
  44.0 0.8 %collective-permute-done.12 = f32[4,80,128]{2,1,0:T(8,128)S(1)} collective-permute-done((f32[4,80,128]{2,1,0:T(8,128)S(1)}, f32[4,80,128]{2,1,0:T(8,128)S(1)}, u32[]{:S(2)}, u32[]{:S(2)}) %collective-permute-start.12) | collective-permute-done | bytes 163872 | tf_op jit(solution)/shard_map/ppermute | solution.py:424
  44.8 3.4 %collective-permute-start.13 = (f32[4,80,128]{2,1,0:T(8,128)S(1)}, f32[4,80,128]{2,1,0:T(8,128)S(1)}, u32[]{:S(2)}, u32[]{:S(2)}) collective-permute-start(f32[4,80,128]{2,1,0:T(8,128)S(1)} %pad_maximum_fusion.1), channel_id=1, source_target_pairs={{0,2},{1,127},{2,4},{3,1},{4,6},{5,3},{6,8},{7,5},{8,10},{9,7},{10... | collective-permute-start | bytes 491528 | tf_op jit(solution)/shard_map/ppermute | solution.py:439
  48.2 0.6 collective-permute-start.14
  48.8 2.2 %shard_map.79.part_ref = f32[4,320,128]{2,1,0:T(8,128)S(1)} custom-call(bf16[128,192]{1,0:T(8,128)(2,1)S(1)} %copy-done, f32[4,320,128]{2,1,0:T(8,128)S(1)} %get-tuple-element.60.fields_ref.section_ref, s32[6,512]{1,0:T(8,128)S(1)} %get-tuple-element.53.near_ref), custom_call_target="tpu_custom_call" | custom-call | flops 1000000000 | bytes 1048576 | tf_op jit(solution)/shard_map/pallas_call | solution.py:411
  51.1 2.9 %collective-permute-done.14.b_ref = f32[3,80,128]{2,1,0:T(8,128)S(1)} collective-permute-done((f32[3,80,128]{2,1,0:T(8,128)S(1)}, f32[3,80,128]{2,1,0:T(8,128)S(1)}, u32[]{:S(2)}, u32[]{:S(2)}) %collective-permute-start.14) | collective-permute-done | bytes 122912 | tf_op jit(solution)/shard_map/ppermute | solution.py:439
  54.1 3.2 %collective-permute-start.16 = (f32[3,80,128]{2,1,0:T(8,128)S(1)}, f32[3,80,128]{2,1,0:T(8,128)S(1)}, u32[]{:S(2)}, u32[]{:S(2)}) collective-permute-start(f32[3,80,128]{2,1,0:T(8,128)S(1)} %pad_maximum_fusion.5), channel_id=1, source_target_pairs={{0,1},{1,0},{2,3},{3,2},{4,5},{5,4},{6,7},{7,6},{8,9},{9,8},{10,11... | collective-permute-start | bytes 368648 | tf_op jit(solution)/shard_map/ppermute | solution.py:424
  57.2 1.2 %shard_map.80.part_ref = f32[4,320,128]{2,1,0:T(8,128)S(1)} custom-call(f32[4,320,128]{2,1,0:T(8,128)S(1)} %shard_map.79.part_ref, s32[6,512]{1,0:T(8,128)S(1)} %get-tuple-element.46.far_ref, s32[5,1,128]{2,1,0:T(1,128)S(1)} %get-tuple-element.40.ask_ref, f32[4,80,128]{2,1,0:T(8,128)S(1)} %collective-permute-done.13.a_ref, ...), custom_call_target="tpu_custom_call" | custom-call | flops 1000000000 | bytes 1048576 | tf_op jit(solution)/shard_map/pallas_call | solution.py:411
  58.4 1.7 %shard_map.81 = (f32[320,512]{1,0:T(8,128)}, f32[320,512]{1,0:T(8,128)}) custom-call(f32[4,328,128]{2,1,0:T(8,128)S(1)} %get-tuple-element.48.fields_ref.start_ref, f32[4,320,128]{2,1,0:T(8,128)S(1)} %get-tuple-element.60.fields_ref.section_ref, f32[4,320,128]{2,1,0:T(8,128)S(1)} %shard_map.80.part_ref, bf16[6,384,512]{2,1,0:T(8,128)(2,1)S(1)} %get-tuple-element.59.rest_ref, ...), custom_call_target="tpu_custom_call" | custom-call | flops 1000000 | bytes 1048576 | tf_op jit(solution)/shard_map/pallas_call | solution.py:411
  (41 shorter events, 0.6 us)
Async XLA Ops:
  2.1 5.3 %collective-permute-start = (s32[5,1,128]{2,1,0:T(1,128)S(1)}, s32[5,1,128]{2,1,0:T(1,128)S(1)}, u32[]{:S(2)}, u32[]{:S(2)}) collective-permute-start(s32[5,1,128]{2,1,0:T(1,128)S(1)} %get-tuple-element.40.ask_ref), channel_id=1, source_target_pairs={{0,1},{1,0},{2,3},{3,2},{4,5},{5,4},{6,7},{7,6},{8,9},{9,8},{10,11... | collective-permute-start | bytes 7688 | tf_op jit(solution)/shard_map/ppermute | solution.py:424
  4.2 17.3 %collective-permute-start.2 = (f32[328,256]{1,0:T(8,128)S(1)}, f32[328,256]{1,0:T(8,128)S(1)}, u32[]{:S(2)}, u32[]{:S(2)}) collective-permute-start(f32[328,256]{1,0:T(8,128)S(1)} %shard_map.69), channel_id=1, source_target_pairs={{1,2},{3,4},{5,6},{7,8},{9,10},{11,12},{13,14},{15,16},{17,18},{19... | collective-permute-start | bytes 1007624 | tf_op jit(solution)/shard_map/ppermute | solution.py:429
  7.5 10.7 %collective-permute-start.5 = (s32[3,1,128]{2,1,0:T(1,128)S(1)}, s32[3,1,128]{2,1,0:T(1,128)S(1)}, u32[]{:S(2)}, u32[]{:S(2)}) collective-permute-start(s32[3,1,128]{2,1,0:T(1,128)S(1)} %pad_add_fusion.1), channel_id=1, source_target_pairs={{0,4},{1,125},{2,6},{3,127},{4,8},{5,1},{6,10},{7,3},{8,12},{9,5},... | collective-permute-start | bytes 4616 | tf_op jit(solution)/shard_map/ppermute | solution.py:439
  15.8 2.7 %collective-permute-start.1 = (s32[4,1,128]{2,1,0:T(1,128)S(1)}, s32[4,1,128]{2,1,0:T(1,128)S(1)}, u32[]{:S(2)}, u32[]{:S(2)}) collective-permute-start(s32[4,1,128]{2,1,0:T(1,128)S(1)} %pad_add_fusion), channel_id=1, source_target_pairs={{0,2},{1,127},{2,4},{3,1},{4,6},{5,3},{6,8},{7,5},{8,10},{9,7},{10... | collective-permute-start | bytes 6152 | tf_op jit(solution)/shard_map/ppermute | solution.py:439
  16.9 8.5 %collective-permute-start.3 = (f32[328,256]{1,0:T(8,128)S(1)}, f32[328,256]{1,0:T(8,128)S(1)}, u32[]{:S(2)}, u32[]{:S(2)}) collective-permute-start(f32[328,256]{1,0:T(8,128)S(1)} %shard_map.69), channel_id=1, source_target_pairs={{0,127},{2,1},{4,3},{6,5},{8,7},{10,9},{12,11},{14,13},{16,15},{18... | collective-permute-start | bytes 1007624 | tf_op jit(solution)/shard_map/ppermute | solution.py:434
  18.6 2.4 %collective-permute-start.6 = (s32[3,1,128]{2,1,0:T(1,128)S(1)}, s32[3,1,128]{2,1,0:T(1,128)S(1)}, u32[]{:S(2)}, u32[]{:S(2)}) collective-permute-start(s32[3,1,128]{2,1,0:T(1,128)S(1)} %pad_add_fusion.2), channel_id=1, source_target_pairs={{0,1},{1,0},{2,3},{3,2},{4,5},{5,4},{6,7},{7,6},{8,9},{9,8},{10,11... | collective-permute-start | bytes 4616 | tf_op jit(solution)/shard_map/ppermute | solution.py:424
  19.9 5.4 %collective-permute-start.4 = (f32[328,256]{1,0:T(8,128)S(1)}, f32[328,256]{1,0:T(8,128)S(1)}, u32[]{:S(2)}, u32[]{:S(2)}) collective-permute-start(f32[328,256]{1,0:T(8,128)S(1)} %shard_map.71), channel_id=1, source_target_pairs={{0,1},{1,0},{2,3},{3,2},{4,5},{5,4},{6,7},{7,6},{8,9},{9,8},{10,11... | collective-permute-start | bytes 1007624 | tf_op jit(solution)/shard_map/ppermute | solution.py:424
  25.9 1.5 %collective-permute-start.7 = (f32[4,80,128]{2,1,0:T(8,128)S(1)}, f32[4,80,128]{2,1,0:T(8,128)S(1)}, u32[]{:S(2)}, u32[]{:S(2)}) collective-permute-start(f32[4,80,128]{2,1,0:T(8,128)S(1)} %get-tuple-element.50), channel_id=1, source_target_pairs={{0,1},{1,0},{2,3},{3,2},{4,5},{5,4},{6,7},{7,6},{8,9},{9,8},{10,11... | collective-permute-start | bytes 491528 | tf_op jit(solution)/shard_map/ppermute | solution.py:424
  26.0 7.0 %copy-start = (bf16[128,192]{1,0:T(8,128)(2,1)S(1)}, bf16[128,192]{1,0:T(8,128)(2,1)}, u32[]{:S(2)}) copy-start(bf16[128,192]{1,0:T(8,128)(2,1)} %constant.13.clone.table_ref) | copy-start | bytes 147460
  27.4 11.1 %collective-permute-start.8 = (f32[4,80,128]{2,1,0:T(8,128)S(1)}, f32[4,80,128]{2,1,0:T(8,128)S(1)}, u32[]{:S(2)}, u32[]{:S(2)}) collective-permute-start(f32[4,80,128]{2,1,0:T(8,128)S(1)} %pad_maximum_fusion), channel_id=1, source_target_pairs={{0,2},{1,127},{2,4},{3,1},{4,6},{5,3},{6,8},{7,5},{8,10},{9,7},{10... | collective-permute-start | bytes 491528 | tf_op jit(solution)/shard_map/ppermute | solution.py:439
  33.0 5.6 %collective-permute-start.9 = (f32[3,80,128]{2,1,0:T(8,128)S(1)}, f32[3,80,128]{2,1,0:T(8,128)S(1)}, u32[]{:S(2)}, u32[]{:S(2)}) collective-permute-start(f32[3,80,128]{2,1,0:T(8,128)S(1)} %pad_maximum_fusion.2), channel_id=1, source_target_pairs={{0,4},{1,125},{2,6},{3,127},{4,8},{5,1},{6,10},{7,3},{8,12},{9,5},... | collective-permute-start | bytes 368648 | tf_op jit(solution)/shard_map/ppermute | solution.py:439
  35.2 5.5 %collective-permute-start.10 = (f32[1,80,128]{2,1,0:T(8,128)S(1)}, f32[1,80,128]{2,1,0:T(8,128)S(1)}, u32[]{:S(2)}, u32[]{:S(2)}) collective-permute-start(f32[1,80,128]{2,1,0:T(8,128)S(1)} %get-tuple-element.58), channel_id=1, source_target_pairs={{0,1},{1,0},{2,3},{3,2},{4,5},{5,4},{6,7},{7,6},{8,9},{9,8},{10,11... | collective-permute-start | bytes 122888 | tf_op jit(solution)/shard_map/ppermute | solution.py:424
  38.6 3.4 %collective-permute-start.11 = (f32[3,80,128]{2,1,0:T(8,128)S(1)}, f32[3,80,128]{2,1,0:T(8,128)S(1)}, u32[]{:S(2)}, u32[]{:S(2)}) collective-permute-start(f32[3,80,128]{2,1,0:T(8,128)S(1)} %pad_maximum_fusion.3), channel_id=1, source_target_pairs={{0,1},{1,0},{2,3},{3,2},{4,5},{5,4},{6,7},{7,6},{8,9},{9,8},{10,11... | collective-permute-start | bytes 368648 | tf_op jit(solution)/shard_map/ppermute | solution.py:424
  43.3 1.5 %collective-permute-start.12 = (f32[4,80,128]{2,1,0:T(8,128)S(1)}, f32[4,80,128]{2,1,0:T(8,128)S(1)}, u32[]{:S(2)}, u32[]{:S(2)}) collective-permute-start(f32[4,80,128]{2,1,0:T(8,128)S(1)} %get-tuple-element.62), channel_id=1, source_target_pairs={{0,1},{1,0},{2,3},{3,2},{4,5},{5,4},{6,7},{7,6},{8,9},{9,8},{10,11... | collective-permute-start | bytes 491528 | tf_op jit(solution)/shard_map/ppermute | solution.py:424
  44.8 9.2 %collective-permute-start.13 = (f32[4,80,128]{2,1,0:T(8,128)S(1)}, f32[4,80,128]{2,1,0:T(8,128)S(1)}, u32[]{:S(2)}, u32[]{:S(2)}) collective-permute-start(f32[4,80,128]{2,1,0:T(8,128)S(1)} %pad_maximum_fusion.1), channel_id=1, source_target_pairs={{0,2},{1,127},{2,4},{3,1},{4,6},{5,3},{6,8},{7,5},{8,10},{9,7},{10... | collective-permute-start | bytes 491528 | tf_op jit(solution)/shard_map/ppermute | solution.py:439
  48.2 5.8 %collective-permute-start.14 = (f32[3,80,128]{2,1,0:T(8,128)S(1)}, f32[3,80,128]{2,1,0:T(8,128)S(1)}, u32[]{:S(2)}, u32[]{:S(2)}) collective-permute-start(f32[3,80,128]{2,1,0:T(8,128)S(1)} %pad_maximum_fusion.4), channel_id=1, source_target_pairs={{0,4},{1,125},{2,6},{3,127},{4,8},{5,1},{6,10},{7,3},{8,12},{9,5},... | collective-permute-start | bytes 368648 | tf_op jit(solution)/shard_map/ppermute | solution.py:439
  51.0 6.2 %collective-permute-start.15 = (f32[1,80,128]{2,1,0:T(8,128)S(1)}, f32[1,80,128]{2,1,0:T(8,128)S(1)}, u32[]{:S(2)}, u32[]{:S(2)}) collective-permute-start(f32[1,80,128]{2,1,0:T(8,128)S(1)} %get-tuple-element.69), channel_id=1, source_target_pairs={{0,1},{1,0},{2,3},{3,2},{4,5},{5,4},{6,7},{7,6},{8,9},{9,8},{10,11... | collective-permute-start | bytes 122888 | tf_op jit(solution)/shard_map/ppermute | solution.py:424
  54.1 4.4 %collective-permute-start.16 = (f32[3,80,128]{2,1,0:T(8,128)S(1)}, f32[3,80,128]{2,1,0:T(8,128)S(1)}, u32[]{:S(2)}, u32[]{:S(2)}) collective-permute-start(f32[3,80,128]{2,1,0:T(8,128)S(1)} %pad_maximum_fusion.5), channel_id=1, source_target_pairs={{0,1},{1,0},{2,3},{3,2},{4,5},{5,4},{6,7},{7,6},{8,9},{9,8},{10,11... | collective-permute-start | bytes 368648 | tf_op jit(solution)/shard_map/ppermute | solution.py:424

commit v7 on v5

--- a/solution.py
+++ b/solution.py
@@ -363,8 +363,8 @@
                 add_on_face(sum_ref, c, v, f, term[16 * v : 16 * v + 16])
 
 
-def direct_kernel(part_ref, far_ref, ask_ref, a_ref, b_ref, sib_ref, sum_ref):
-    lhs = ghost_rows([sib_ref[0], a_ref[2], a_ref[0], b_ref[1], b_ref[0]], ask_ref)
+def direct_kernel(part_ref, far_ref, ask_ref, own_ref, got_ref, b_ref, sib_ref, sum_ref):
+    lhs = ghost_rows([sib_ref[0], got_ref[0], own_ref[0], b_ref[1], b_ref[0]], ask_ref)
     sum_ref[...] = part_ref[...]
     add_ghosts(sum_ref, lhs, lambda f: one_hot_rows(5 * CAP, far_ref[f : f + 1, :] - 3 * CAP))
 
@@ -508,7 +508,9 @@
             [got_scratch],
             flops=10**9,
         )
-        a, b = outward_pair(own, got)
+        a_own = outward(own[0], 2)
+        b = outward(jnp.concatenate([own[1], got[2:4]], axis=0), 4)
+        a_got = outward(got[0:2], 2)
         (part,) = call(
             near_kernel,
             [blocks],
@@ -519,9 +521,9 @@
         )
         sib, part = lax.optimization_barrier((sib, part))
         sib = swap_cores(sib)
-        a, b, part = lax.optimization_barrier((a, b, part))
-        post = swap_back(a, b)
-        (part,) = call(direct_kernel, [blocks], (part, far, swap_ask, a, b, sib), flops=10**9)
+        a_own, a_got, b, part = lax.optimization_barrier((a_own, a_got, b, part))
+        post = swap_cores(jnp.concatenate([a_own[1:2], a_got[1:2], b[2:3]], axis=0))
+        (part,) = call(direct_kernel, [blocks], (part, far, swap_ask, a_own, a_got, b, sib), flops=10**9)
         return part, rest_hot, own_ask, post
 
     start, swap = call(

time: 55.9 us -> 55.4 us (level)
  waiting for transfers between devices: 11.2 us -> 7.2 us
  starting transfers between devices: 27.8 us -> 31.4 us
    ppermute x6 -> x8, waiting for transfers between devices: 8.36 us -> 4.35 us  [outward(): lax.ppermute(x, AXES, [(i, (i + (by if i % 2 == 0 else -by)) % n) for i i...]
    ppermute x9, starting transfers between devices: 8.76 us -> 12.1 us  [swap_cores(): return lax.ppermute(x, AXES, [(i, i ^ 1) for i in range(n)])]
    ppermute x6 -> x8, starting transfers between devices: 19 us -> 19.3 us  [outward(): lax.ppermute(x, AXES, [(i, (i + (by if i % 2 == 0 else -by)) % n) for i i...]
  transfers between devices with their start and end apart: 16 -> 18, of which waited for: 7 -> 8; matrix products, arithmetic and copies ran while one was open for 0% -> 0% of each run, Pallas kernels for 19% -> 19%
where the time goes in v7:
time: 55.4 us; the launch traced here: 55.3 us
  starting transfers between devices  31.4 us (57%)
  Pallas kernels  15.5 us (28%)
  waiting for transfers between devices  7.2 us (13%)
  between operations  1.05 us (2%)
    ppermute x8, starting transfers between devices, outward(): lax.ppermute(x, AXES, [(i, (i + (by if i % 2 == 0 else -by)) % n) for i i...  19.3 us
    pallas_call x14, Pallas kernels, call(): pl.pallas_call(kernel, out_shape=[jax.ShapeDtypeStruct(s, d) for s, d in...  15.5 us
    ppermute x9, starting transfers between devices, swap_cores(): return lax.ppermute(x, AXES, [(i, i ^ 1) for i in range(n)])  12.1 us
    ppermute x8, waiting for transfers between devices, outward(): lax.ppermute(x, AXES, [(i, (i + (by if i % 2 == 0 else -by)) % n) for i i...  4.35 us
    ppermute x9, waiting for transfers between devices, swap_cores(): return lax.ppermute(x, AXES, [(i, i ^ 1) for i in range(n)])  1.58 us
    ppermute x1, waiting for transfers between devices, swap_chips(): lax.ppermute(x, AXES, [(i, (i + (1 if i % 2 else -1)) % n) for i in range...  1.27 us
  transfers between devices with their start and end apart: 18, of which 8 were waited for; matrix products, arithmetic and copies ran while one was open for 0% of the time, Pallas kernels for 19%

profile of v7, /device:TPU:1, one launch (start us, length us, event | category | flops | bytes accessed | tf_op | source)
XLA Modules:
  0.0 55.3 jit_solution(11466027315905140370)
XLA Ops:
  0.6 1.5 %shard_map.68 = (s32[3,1,128]{2,1,0:T(1,128)S(1)}, s32[5,1,128]{2,1,0:T(1,128)S(1)}, s32[6,512]{1,0:T(8,128)S(1)}, s32[6,512]{1,0:T(8,128)S(1)}, f32[320,1024]{1...) custom-call(s32[1]{0:T(128)} %bitcast.me_ref, s32[6,512]{1,0:T(8,128)} %links_hbm.1, f32[320,1024]{1,0:T(8,128)} %bitcast.22, ...), custom_call_target="tpu_custom_call" | custom-call | flops 1000000 | bytes 1048576 | tf_op jit(solution)/shard_map/pallas_call | solution.py:412
  2.1 1.5 %collective-permute-start = (s32[5,1,128]{2,1,0:T(1,128)S(1)}, s32[5,1,128]{2,1,0:T(1,128)S(1)}, u32[]{:S(2)}, u32[]{:S(2)}) collective-permute-start(s32[5,1,128]{2,1,0:T(1,128)S(1)} %get-tuple-element.42.ask_ref), channel_id=1, source_target_pairs={{0,1},{1,0},{2,3},{3,2},{4,5},{5,4},{6,7},{7,6},{8,9},{9,8},{10,11... | collective-permute-start | bytes 7688 | tf_op jit(solution)/shard_map/ppermute | solution.py:425
  3.6 0.6 %shard_map.69 = f32[328,256]{1,0:T(8,128)S(1)} custom-call(s32[1]{0:T(128)} %bitcast.me_ref, f32[320,1024]{1,0:T(8,128)S(1)} %get-tuple-element.39.state_ref, s32[1,1024]{1,0:T(1,128)S(1)} %get-tuple-element.40.level_ref, s32[1,1024]{1,0:T(1,128)S(1)} %get-tuple-element.45.morton_ref), custom_call_target="tpu_custom_call" | custom-call | flops 1000000 | bytes 1048576 | tf_op jit(solution)/shard_map/pallas_call | solution.py:412
  4.5 8.7 %collective-permute-start.4 = (s32[3,1,128]{2,1,0:T(1,128)S(1)}, s32[3,1,128]{2,1,0:T(1,128)S(1)}, u32[]{:S(2)}, u32[]{:S(2)}) collective-permute-start(s32[3,1,128]{2,1,0:T(1,128)S(1)} %pad_add_fusion.1), channel_id=1, source_target_pairs={{0,4},{1,125},{2,6},{3,127},{4,8},{5,1},{6,10},{7,3},{8,12},{9,5},... | collective-permute-start | bytes 4616 | tf_op jit(solution)/shard_map/ppermute | solution.py:435
  13.1 0.8 %collective-permute-start.1 = (s32[4,1,128]{2,1,0:T(1,128)S(1)}, s32[4,1,128]{2,1,0:T(1,128)S(1)}, u32[]{:S(2)}, u32[]{:S(2)}) collective-permute-start(s32[4,1,128]{2,1,0:T(1,128)S(1)} %pad_add_fusion), channel_id=1, source_target_pairs={{0,2},{1,127},{2,4},{3,1},{4,6},{5,3},{6,8},{7,5},{8,10},{9,7},{10... | collective-permute-start | bytes 6152 | tf_op jit(solution)/shard_map/ppermute | solution.py:435
  13.9 1.9 %collective-permute-done.1 = s32[4,1,128]{2,1,0:T(1,128)S(1)} collective-permute-done((s32[4,1,128]{2,1,0:T(1,128)S(1)}, s32[4,1,128]{2,1,0:T(1,128)S(1)}, u32[]{:S(2)}, u32[]{:S(2)}) %collective-permute-start.1) | collective-permute-done | bytes 2080 | tf_op jit(solution)/shard_map/ppermute | solution.py:435
  15.9 1.2 %collective-permute-start.5 = (s32[3,1,128]{2,1,0:T(1,128)S(1)}, s32[3,1,128]{2,1,0:T(1,128)S(1)}, u32[]{:S(2)}, u32[]{:S(2)}) collective-permute-start(s32[3,1,128]{2,1,0:T(1,128)S(1)} %pad_add_fusion.2), channel_id=1, source_target_pairs={{0,1},{1,0},{2,3},{3,2},{4,5},{5,4},{6,7},{7,6},{8,9},{9,8},{10,11... | collective-permute-start | bytes 4616 | tf_op jit(solution)/shard_map/ppermute | solution.py:425
  17.1 0.6 %shard_map.71 = f32[328,256]{1,0:T(8,128)S(1)} custom-call(s32[1]{0:T(128)} %bitcast.me_ref, f32[320,1024]{1,0:T(8,128)S(1)} %get-tuple-element.39.state_ref, s32[1,1024]{1,0:T(1,128)S(1)} %get-tuple-element.40.level_ref, s32[1,1024]{1,0:T(1,128)S(1)} %get-tuple-element.45.morton_ref), custom_call_target="tpu_custom_call" | custom-call | flops 1000000000 | bytes 1048576 | tf_op jit(solution)/shard_map/pallas_call | solution.py:412
  17.8 0.9 %shard_map.70.home_ref = f32[4,328,128]{2,1,0:T(8,128)S(1)} custom-call(s32[1]{0:T(128)} %bitcast.me_ref, f32[320,1024]{1,0:T(8,128)S(1)} %get-tuple-element.39.state_ref, s32[1,1024]{1,0:T(1,128)S(1)} %get-tuple-element.40.level_ref, s32[1,1024]{1,0:T(1,128)S(1)} %get-tuple-element.45.morton_ref), custom_call_target="tpu_custom_call" | custom-call | flops 1000000 | bytes 1048576 | tf_op jit(solution)/shard_map/pallas_call | solution.py:412
  18.8 0.5 shard_map.72
  19.2 1.3 %collective-permute-done.2.far_ref = f32[328,256]{1,0:T(8,128)S(1)} collective-permute-done((f32[328,256]{1,0:T(8,128)S(1)}, f32[328,256]{1,0:T(8,128)S(1)}, u32[]{:S(2)}, u32[]{:S(2)}) %collective-permute-start.2) | collective-permute-done | bytes 335904 | tf_op jit(solution)/shard_map/ppermute | solution.py:430
  20.5 0.6 %shard_map.73 = (f32[4,328,128]{2,1,0:T(8,128)S(1)}, f32[4,80,128]{2,1,0:T(8,128)S(1)}) custom-call(s32[1]{0:T(128)} %bitcast.me_ref, f32[4,328,128]{2,1,0:T(8,128)S(1)} %shard_map.70.home_ref, f32[328,256]{1,0:T(8,128)S(1)} %collective-permute-done.2.far_ref, f32[328,256]{1,0:T(8,128)S(1)} %collective-permute-done.3.sib_ref, ...), custom_call_target="tpu_custom_call" | custom-call | flops 1000000 | bytes 1048576 | tf_op jit(solution)/shard_map/pallas_call | solution.py:412
  21.1 0.4 collective-permute-start.7
  21.4 0.5 shard_map.74
  22.0 0.6 %collective-permute-done.7 = f32[4,80,128]{2,1,0:T(8,128)S(1)} collective-permute-done((f32[4,80,128]{2,1,0:T(8,128)S(1)}, f32[4,80,128]{2,1,0:T(8,128)S(1)}, u32[]{:S(2)}, u32[]{:S(2)}) %collective-permute-start.7) | collective-permute-done | bytes 163872 | tf_op jit(solution)/shard_map/ppermute | solution.py:425
  22.6 3.7 %collective-permute-start.9 = (f32[3,80,128]{2,1,0:T(8,128)S(1)}, f32[3,80,128]{2,1,0:T(8,128)S(1)}, u32[]{:S(2)}, u32[]{:S(2)}) collective-permute-start(f32[3,80,128]{2,1,0:T(8,128)S(1)} %pad_maximum_fusion), channel_id=1, source_target_pairs={{0,4},{1,125},{2,6},{3,127},{4,8},{5,1},{6,10},{7,3},{8,12},{9,5},... | collective-permute-start | bytes 368648 | tf_op jit(solution)/shard_map/ppermute | solution.py:435
  26.3 1.9 %collective-permute-start.6 = (f32[2,80,128]{2,1,0:T(8,128)S(1)}, f32[2,80,128]{2,1,0:T(8,128)S(1)}, u32[]{:S(2)}, u32[]{:S(2)}) collective-permute-start(f32[2,80,128]{2,1,0:T(8,128)S(1)} %get-tuple-element.51), channel_id=1, source_target_pairs={{0,2},{1,127},{2,4},{3,1},{4,6},{5,3},{6,8},{7,5},{8,10},{9,7},{10... | collective-permute-start | bytes 245768 | tf_op jit(solution)/shard_map/ppermute | solution.py:435
  28.3 2.2 %shard_map.75.part_ref = f32[4,320,128]{2,1,0:T(8,128)S(1)} custom-call(bf16[128,192]{1,0:T(8,128)(2,1)S(1)} %copy-done, f32[4,328,128]{2,1,0:T(8,128)S(1)} %get-tuple-element.50.fields_ref.start_ref, s32[6,512]{1,0:T(8,128)S(1)} %get-tuple-element.55.near_ref), custom_call_target="tpu_custom_call" | custom-call | flops 1000000000 | bytes 1048576 | tf_op jit(solution)/shard_map/pallas_call | solution.py:412
  30.8 1.0 %collective-permute-done.8.got_ref = f32[2,80,128]{2,1,0:T(8,128)S(1)} collective-permute-done((f32[2,80,128]{2,1,0:T(8,128)S(1)}, f32[2,80,128]{2,1,0:T(8,128)S(1)}, u32[]{:S(2)}, u32[]{:S(2)}) %collective-permute-start.8) | collective-permute-done | bytes 81952 | tf_op jit(solution)/shard_map/ppermute | solution.py:435
  31.8 3.6 %collective-permute-start.11 = (f32[3,80,128]{2,1,0:T(8,128)S(1)}, f32[3,80,128]{2,1,0:T(8,128)S(1)}, u32[]{:S(2)}, u32[]{:S(2)}) collective-permute-start(f32[3,80,128]{2,1,0:T(8,128)S(1)} %pad_maximum_fusion.1), channel_id=1, source_target_pairs={{0,1},{1,0},{2,3},{3,2},{4,5},{5,4},{6,7},{7,6},{8,9},{9,8},{10,11... | collective-permute-start | bytes 368648 | tf_op jit(solution)/shard_map/ppermute | solution.py:425
  35.4 1.2 %shard_map.76.part_ref = f32[4,320,128]{2,1,0:T(8,128)S(1)} custom-call(f32[4,320,128]{2,1,0:T(8,128)S(1)} %shard_map.75.part_ref, s32[6,512]{1,0:T(8,128)S(1)} %get-tuple-element.48.far_ref, s32[5,1,128]{2,1,0:T(1,128)S(1)} %get-tuple-element.42.ask_ref, f32[2,80,128]{2,1,0:T(8,128)S(1)} %collective-permute-done.6.own_ref, ...), custom_call_target="tpu_custom_call" | custom-call | flops 1000000000 | bytes 1048576 | tf_op jit(solution)/shard_map/pallas_call | solution.py:412
  36.7 1.3 %shard_map.77 = (f32[4,320,128]{2,1,0:T(8,128)S(1)}, f32[4,80,128]{2,1,0:T(8,128)S(1)}) custom-call(f32[4,328,128]{2,1,0:T(8,128)S(1)} %get-tuple-element.50.fields_ref.start_ref, f32[4,320,128]{2,1,0:T(8,128)S(1)} %shard_map.76.part_ref, bf16[6,384,512]{2,1,0:T(8,128)(2,1)S(1)} %get-tuple-element.62.rest_ref, ...), custom_call_target="tpu_custom_call" | custom-call | flops 1000000 | bytes 1048576 | tf_op jit(solution)/shard_map/pallas_call | solution.py:412
  38.0 0.4 collective-permute-start.13
  38.3 0.5 shard_map.78
  38.9 0.7 %collective-permute-done.13 = f32[4,80,128]{2,1,0:T(8,128)S(1)} collective-permute-done((f32[4,80,128]{2,1,0:T(8,128)S(1)}, f32[4,80,128]{2,1,0:T(8,128)S(1)}, u32[]{:S(2)}, u32[]{:S(2)}) %collective-permute-start.13) | collective-permute-done | bytes 163872 | tf_op jit(solution)/shard_map/ppermute | solution.py:425
  39.6 1.1 %collective-permute-start.15 = (f32[3,80,128]{2,1,0:T(8,128)S(1)}, f32[3,80,128]{2,1,0:T(8,128)S(1)}, u32[]{:S(2)}, u32[]{:S(2)}) collective-permute-start(f32[3,80,128]{2,1,0:T(8,128)S(1)} %pad_maximum_fusion.2), channel_id=1, source_target_pairs={{0,4},{1,125},{2,6},{3,127},{4,8},{5,1},{6,10},{7,3},{8,12},{9,5},... | collective-permute-start | bytes 368648 | tf_op jit(solution)/shard_map/ppermute | solution.py:435
  40.7 3.1 %collective-permute-start.12 = (f32[2,80,128]{2,1,0:T(8,128)S(1)}, f32[2,80,128]{2,1,0:T(8,128)S(1)}, u32[]{:S(2)}, u32[]{:S(2)}) collective-permute-start(f32[2,80,128]{2,1,0:T(8,128)S(1)} %get-tuple-element.64), channel_id=1, source_target_pairs={{0,2},{1,127},{2,4},{3,1},{4,6},{5,3},{6,8},{7,5},{8,10},{9,7},{10... | collective-permute-start | bytes 245768 | tf_op jit(solution)/shard_map/ppermute | solution.py:435
  43.8 2.2 %shard_map.79.part_ref = f32[4,320,128]{2,1,0:T(8,128)S(1)} custom-call(bf16[128,192]{1,0:T(8,128)(2,1)S(1)} %copy-done, f32[4,320,128]{2,1,0:T(8,128)S(1)} %get-tuple-element.63.fields_ref.section_ref, s32[6,512]{1,0:T(8,128)S(1)} %get-tuple-element.55.near_ref), custom_call_target="tpu_custom_call" | custom-call | flops 1000000000 | bytes 1048576 | tf_op jit(solution)/shard_map/pallas_call | solution.py:412
  46.2 1.2 %collective-permute-done.14.got_ref = f32[2,80,128]{2,1,0:T(8,128)S(1)} collective-permute-done((f32[2,80,128]{2,1,0:T(8,128)S(1)}, f32[2,80,128]{2,1,0:T(8,128)S(1)}, u32[]{:S(2)}, u32[]{:S(2)}) %collective-permute-start.14) | collective-permute-done | bytes 81952 | tf_op jit(solution)/shard_map/ppermute | solution.py:435
  47.4 4.7 %collective-permute-start.17 = (f32[3,80,128]{2,1,0:T(8,128)S(1)}, f32[3,80,128]{2,1,0:T(8,128)S(1)}, u32[]{:S(2)}, u32[]{:S(2)}) collective-permute-start(f32[3,80,128]{2,1,0:T(8,128)S(1)} %pad_maximum_fusion.3), channel_id=1, source_target_pairs={{0,1},{1,0},{2,3},{3,2},{4,5},{5,4},{6,7},{7,6},{8,9},{9,8},{10,11... | collective-permute-start | bytes 368648 | tf_op jit(solution)/shard_map/ppermute | solution.py:425
  52.1 1.2 %shard_map.80.part_ref = f32[4,320,128]{2,1,0:T(8,128)S(1)} custom-call(f32[4,320,128]{2,1,0:T(8,128)S(1)} %shard_map.79.part_ref, s32[6,512]{1,0:T(8,128)S(1)} %get-tuple-element.48.far_ref, s32[5,1,128]{2,1,0:T(1,128)S(1)} %get-tuple-element.42.ask_ref, f32[2,80,128]{2,1,0:T(8,128)S(1)} %collective-permute-done.12.own_ref, ...), custom_call_target="tpu_custom_call" | custom-call | flops 1000000000 | bytes 1048576 | tf_op jit(solution)/shard_map/pallas_call | solution.py:412
  53.4 1.7 %shard_map.81 = (f32[320,512]{1,0:T(8,128)}, f32[320,512]{1,0:T(8,128)}) custom-call(f32[4,328,128]{2,1,0:T(8,128)S(1)} %get-tuple-element.50.fields_ref.start_ref, f32[4,320,128]{2,1,0:T(8,128)S(1)} %get-tuple-element.63.fields_ref.section_ref, f32[4,320,128]{2,1,0:T(8,128)S(1)} %shard_map.80.part_ref, bf16[6,384,512]{2,1,0:T(8,128)(2,1)S(1)} %get-tuple-element.62.rest_ref, ...), custom_call_target="tpu_custom_call" | custom-call | flops 1000000 | bytes 1048576 | tf_op jit(solution)/shard_map/pallas_call | solution.py:412
  (43 shorter events, 1.1 us)
Async XLA Ops:
  2.1 2.3 %collective-permute-start = (s32[5,1,128]{2,1,0:T(1,128)S(1)}, s32[5,1,128]{2,1,0:T(1,128)S(1)}, u32[]{:S(2)}, u32[]{:S(2)}) collective-permute-start(s32[5,1,128]{2,1,0:T(1,128)S(1)} %get-tuple-element.42.ask_ref), channel_id=1, source_target_pairs={{0,1},{1,0},{2,3},{3,2},{4,5},{5,4},{6,7},{7,6},{8,9},{9,8},{10,11... | collective-permute-start | bytes 7688 | tf_op jit(solution)/shard_map/ppermute | solution.py:425
  4.5 9.4 %collective-permute-start.4 = (s32[3,1,128]{2,1,0:T(1,128)S(1)}, s32[3,1,128]{2,1,0:T(1,128)S(1)}, u32[]{:S(2)}, u32[]{:S(2)}) collective-permute-start(s32[3,1,128]{2,1,0:T(1,128)S(1)} %pad_add_fusion.1), channel_id=1, source_target_pairs={{0,4},{1,125},{2,6},{3,127},{4,8},{5,1},{6,10},{7,3},{8,12},{9,5},... | collective-permute-start | bytes 4616 | tf_op jit(solution)/shard_map/ppermute | solution.py:435
  13.1 2.7 %collective-permute-start.1 = (s32[4,1,128]{2,1,0:T(1,128)S(1)}, s32[4,1,128]{2,1,0:T(1,128)S(1)}, u32[]{:S(2)}, u32[]{:S(2)}) collective-permute-start(s32[4,1,128]{2,1,0:T(1,128)S(1)} %pad_add_fusion), channel_id=1, source_target_pairs={{0,2},{1,127},{2,4},{3,1},{4,6},{5,3},{6,8},{7,5},{8,10},{9,7},{10... | collective-permute-start | bytes 6152 | tf_op jit(solution)/shard_map/ppermute | solution.py:435
  13.9 6.6 %collective-permute-start.2 = (f32[328,256]{1,0:T(8,128)S(1)}, f32[328,256]{1,0:T(8,128)S(1)}, u32[]{:S(2)}, u32[]{:S(2)}) collective-permute-start(f32[328,256]{1,0:T(8,128)S(1)} %shard_map.69), channel_id=1, source_target_pairs={{0,127},{1,2},{2,1},{3,4},{4,3},{5,6},{6,5},{7,8},{8,7},{9,10},{10... | collective-permute-start | bytes 1007624 | tf_op jit(solution)/shard_map/ppermute | solution.py:430
  15.9 2.8 %collective-permute-start.5 = (s32[3,1,128]{2,1,0:T(1,128)S(1)}, s32[3,1,128]{2,1,0:T(1,128)S(1)}, u32[]{:S(2)}, u32[]{:S(2)}) collective-permute-start(s32[3,1,128]{2,1,0:T(1,128)S(1)} %pad_add_fusion.2), channel_id=1, source_target_pairs={{0,1},{1,0},{2,3},{3,2},{4,5},{5,4},{6,7},{7,6},{8,9},{9,8},{10,11... | collective-permute-start | bytes 4616 | tf_op jit(solution)/shard_map/ppermute | solution.py:425
  17.7 2.8 %collective-permute-start.3 = (f32[328,256]{1,0:T(8,128)S(1)}, f32[328,256]{1,0:T(8,128)S(1)}, u32[]{:S(2)}, u32[]{:S(2)}) collective-permute-start(f32[328,256]{1,0:T(8,128)S(1)} %shard_map.71), channel_id=1, source_target_pairs={{0,1},{1,0},{2,3},{3,2},{4,5},{5,4},{6,7},{7,6},{8,9},{9,8},{10,11... | collective-permute-start | bytes 1007624 | tf_op jit(solution)/shard_map/ppermute | solution.py:425
  21.1 1.5 %collective-permute-start.7 = (f32[4,80,128]{2,1,0:T(8,128)S(1)}, f32[4,80,128]{2,1,0:T(8,128)S(1)}, u32[]{:S(2)}, u32[]{:S(2)}) collective-permute-start(f32[4,80,128]{2,1,0:T(8,128)S(1)} %get-tuple-element.52), channel_id=1, source_target_pairs={{0,1},{1,0},{2,3},{3,2},{4,5},{5,4},{6,7},{7,6},{8,9},{9,8},{10,11... | collective-permute-start | bytes 491528 | tf_op jit(solution)/shard_map/ppermute | solution.py:425
  21.4 6.8 %copy-start = (bf16[128,192]{1,0:T(8,128)(2,1)S(1)}, bf16[128,192]{1,0:T(8,128)(2,1)}, u32[]{:S(2)}) copy-start(bf16[128,192]{1,0:T(8,128)(2,1)} %constant.13.clone.table_ref) | copy-start | bytes 147460
  22.6 9.2 %collective-permute-start.9 = (f32[3,80,128]{2,1,0:T(8,128)S(1)}, f32[3,80,128]{2,1,0:T(8,128)S(1)}, u32[]{:S(2)}, u32[]{:S(2)}) collective-permute-start(f32[3,80,128]{2,1,0:T(8,128)S(1)} %pad_maximum_fusion), channel_id=1, source_target_pairs={{0,4},{1,125},{2,6},{3,127},{4,8},{5,1},{6,10},{7,3},{8,12},{9,5},... | collective-permute-start | bytes 368648 | tf_op jit(solution)/shard_map/ppermute | solution.py:435
  26.3 4.5 %collective-permute-start.6 = (f32[2,80,128]{2,1,0:T(8,128)S(1)}, f32[2,80,128]{2,1,0:T(8,128)S(1)}, u32[]{:S(2)}, u32[]{:S(2)}) collective-permute-start(f32[2,80,128]{2,1,0:T(8,128)S(1)} %get-tuple-element.51), channel_id=1, source_target_pairs={{0,2},{1,127},{2,4},{3,1},{4,6},{5,3},{6,8},{7,5},{8,10},{9,7},{10... | collective-permute-start | bytes 245768 | tf_op jit(solution)/shard_map/ppermute | solution.py:435
  28.2 3.6 %collective-permute-start.8 = (f32[2,80,128]{2,1,0:T(8,128)S(1)}, f32[2,80,128]{2,1,0:T(8,128)S(1)}, u32[]{:S(2)}, u32[]{:S(2)}) collective-permute-start(f32[2,80,128]{2,1,0:T(8,128)S(1)} %get-tuple-element.79), channel_id=1, source_target_pairs={{0,2},{1,127},{2,4},{3,1},{4,6},{5,3},{6,8},{7,5},{8,10},{9,7},{10... | collective-permute-start | bytes 245768 | tf_op jit(solution)/shard_map/ppermute | solution.py:435
  30.5 4.9 %collective-permute-start.10 = (f32[1,80,128]{2,1,0:T(8,128)S(1)}, f32[1,80,128]{2,1,0:T(8,128)S(1)}, u32[]{:S(2)}, u32[]{:S(2)}) collective-permute-start(f32[1,80,128]{2,1,0:T(8,128)S(1)} %get-tuple-element.61), channel_id=1, source_target_pairs={{0,1},{1,0},{2,3},{3,2},{4,5},{5,4},{6,7},{7,6},{8,9},{9,8},{10,11... | collective-permute-start | bytes 122888 | tf_op jit(solution)/shard_map/ppermute | solution.py:425
  31.8 4.8 %collective-permute-start.11 = (f32[3,80,128]{2,1,0:T(8,128)S(1)}, f32[3,80,128]{2,1,0:T(8,128)S(1)}, u32[]{:S(2)}, u32[]{:S(2)}) collective-permute-start(f32[3,80,128]{2,1,0:T(8,128)S(1)} %pad_maximum_fusion.1), channel_id=1, source_target_pairs={{0,1},{1,0},{2,3},{3,2},{4,5},{5,4},{6,7},{7,6},{8,9},{9,8},{10,11... | collective-permute-start | bytes 368648 | tf_op jit(solution)/shard_map/ppermute | solution.py:425
  38.0 1.7 %collective-permute-start.13 = (f32[4,80,128]{2,1,0:T(8,128)S(1)}, f32[4,80,128]{2,1,0:T(8,128)S(1)}, u32[]{:S(2)}, u32[]{:S(2)}) collective-permute-start(f32[4,80,128]{2,1,0:T(8,128)S(1)} %get-tuple-element.65), channel_id=1, source_target_pairs={{0,1},{1,0},{2,3},{3,2},{4,5},{5,4},{6,7},{7,6},{8,9},{9,8},{10,11... | collective-permute-start | bytes 491528 | tf_op jit(solution)/shard_map/ppermute | solution.py:425
  39.6 7.7 %collective-permute-start.15 = (f32[3,80,128]{2,1,0:T(8,128)S(1)}, f32[3,80,128]{2,1,0:T(8,128)S(1)}, u32[]{:S(2)}, u32[]{:S(2)}) collective-permute-start(f32[3,80,128]{2,1,0:T(8,128)S(1)} %pad_maximum_fusion.2), channel_id=1, source_target_pairs={{0,4},{1,125},{2,6},{3,127},{4,8},{5,1},{6,10},{7,3},{8,12},{9,5},... | collective-permute-start | bytes 368648 | tf_op jit(solution)/shard_map/ppermute | solution.py:435
  40.7 5.4 %collective-permute-start.12 = (f32[2,80,128]{2,1,0:T(8,128)S(1)}, f32[2,80,128]{2,1,0:T(8,128)S(1)}, u32[]{:S(2)}, u32[]{:S(2)}) collective-permute-start(f32[2,80,128]{2,1,0:T(8,128)S(1)} %get-tuple-element.64), channel_id=1, source_target_pairs={{0,2},{1,127},{2,4},{3,1},{4,6},{5,3},{6,8},{7,5},{8,10},{9,7},{10... | collective-permute-start | bytes 245768 | tf_op jit(solution)/shard_map/ppermute | solution.py:435
  43.8 3.6 %collective-permute-start.14 = (f32[2,80,128]{2,1,0:T(8,128)S(1)}, f32[2,80,128]{2,1,0:T(8,128)S(1)}, u32[]{:S(2)}, u32[]{:S(2)}) collective-permute-start(f32[2,80,128]{2,1,0:T(8,128)S(1)} %get-tuple-element.77), channel_id=1, source_target_pairs={{0,2},{1,127},{2,4},{3,1},{4,6},{5,3},{6,8},{7,5},{8,10},{9,7},{10... | collective-permute-start | bytes 245768 | tf_op jit(solution)/shard_map/ppermute | solution.py:435
  46.0 6.1 %collective-permute-start.16 = (f32[1,80,128]{2,1,0:T(8,128)S(1)}, f32[1,80,128]{2,1,0:T(8,128)S(1)}, u32[]{:S(2)}, u32[]{:S(2)}) collective-permute-start(f32[1,80,128]{2,1,0:T(8,128)S(1)} %get-tuple-element.73), channel_id=1, source_target_pairs={{0,1},{1,0},{2,3},{3,2},{4,5},{5,4},{6,7},{7,6},{8,9},{9,8},{10,11... | collective-permute-start | bytes 122888 | tf_op jit(solution)/shard_map/ppermute | solution.py:425
  47.4 6.0 %collective-permute-start.17 = (f32[3,80,128]{2,1,0:T(8,128)S(1)}, f32[3,80,128]{2,1,0:T(8,128)S(1)}, u32[]{:S(2)}, u32[]{:S(2)}) collective-permute-start(f32[3,80,128]{2,1,0:T(8,128)S(1)} %pad_maximum_fusion.3), channel_id=1, source_target_pairs={{0,1},{1,0},{2,3},{3,2},{4,5},{5,4},{6,7},{7,6},{8,9},{9,8},{10,11... | collective-permute-start | bytes 368648 | tf_op jit(solution)/shard_map/ppermute | solution.py:425

commit v8 on v7

--- a/solution.py
+++ b/solution.py
@@ -246,14 +246,14 @@
     return jnp.concatenate([ask[t : t + 1, :] for t in range(ask.shape[0])], axis=1)
 
 
-def reply(fields, ask, hot, got_ref, outs):
-    chunks = ask.shape[0]
+def gather(fields, hot):
     high, low = split(fields)
     both = dot(jnp.concatenate([high, low], axis=0), hot)
-    for t in range(chunks):
-        spot = slice(CAP * t, CAP * t + CAP)
-        got_ref[t] = both[0:ROWS, spot] + both[ROWS:, spot]
-    for t in range(chunks):
+    return both[0:ROWS] + both[ROWS:]
+
+
+def pick_faces(got_ref, ask, outs):
+    for t in range(ask.shape[0]):
         face = ask[t : t + 1, :] >> 9
         for v in range(FIELDS):
             x = trace(got_ref, t, v, 0)
@@ -262,10 +262,26 @@
             outs[t][16 * v : 16 * v + 16, :] = x
 
 
-def hot_kernel(far_ref, ask_ref, rest_ref, reply_ref):
+def reply(fields, ask, hot, got_ref, outs):
+    got = gather(fields, hot)
+    for t in range(ask.shape[0]):
+        got_ref[t] = got[:, CAP * t : CAP * t + CAP]
+    pick_faces(got_ref, ask, outs)
+
+
+def hot_kernel(me_ref, far_ref, ask_ref, home_ref, sib_ref, rest_ref, reply_ref, base_ref, pre_ref):
+    even = (me_ref[0] & 1) == 0
+    for c in range(2):
+        sib = sib_ref[:, 128 * c : 128 * c + 128]
+        base_ref[c] = home_ref[c] + jnp.where(even, 0.0, sib)
+        base_ref[c + 2] = home_ref[c + 2] + jnp.where(even, sib, 0.0)
+    hot = one_hot_rows(NEW_DEV, asked_code(ask_ref[4:8, :]) & (NEW_DEV - 1))
+    reply_ref[...] = hot
+    got = gather(wide(base_ref, ROWS), hot)
+    for t in range(4):
+        pre_ref[t] = got[:, CAP * t : CAP * t + CAP]
     for f in range(6):
         rest_ref[f] = one_hot_rows(3 * CAP, far_ref[f : f + 1, :])
-    reply_ref[...] = one_hot_rows(NEW_DEV, asked_code(ask_ref[4:8, :]) & (NEW_DEV - 1))
 
 
 def own_kernel(fields_ref, ask_ref, a_ref, b_ref, sib_ref, got_ref):
@@ -275,15 +291,16 @@
     reply(wide(fields_ref, ROWS), ask, hot, got_ref, outs)
 
 
-def first_kernel(me_ref, home_ref, far_ref, sib_ref, ask_ref, hot_ref, start_ref, swap_ref, got_ref):
-    even = (me_ref[0] & 1) == 0
+def first_kernel(me_ref, base_ref, pre_ref, far_ref, ask_ref, hot_ref, start_ref, swap_ref, got_ref):
+    odd = me_ref[0] & 1
+    got = gather(far_ref[0:ROWS, :], hot_ref[pl.ds(pl.multiple_of(odd * HALF, HALF), HALF), :])
+    for t in range(4):
+        got_ref[t] = pre_ref[t] + got[:, CAP * t : CAP * t + CAP]
+    pick_faces(got_ref, ask_ref[4:8, :], [swap_ref.at[t] for t in range(4)])
     for c in range(2):
-        spot = slice(128 * c, 128 * c + 128)
-        sib = sib_ref[:, spot]
-        far = far_ref[:, spot]
-        start_ref[c] = home_ref[c] + jnp.where(even, far, sib)
-        start_ref[c + 2] = home_ref[c + 2] + jnp.where(even, sib, far)
-    reply(wide(start_ref, ROWS), ask_ref[4:8, :], hot_ref[...], got_ref, [swap_ref.at[t] for t in range(4)])
+        far = far_ref[:, 128 * c : 128 * c + 128]
+        start_ref[c] = base_ref[c] + jnp.where(odd == 0, far, 0.0)
+        start_ref[c + 2] = base_ref[c + 2] + jnp.where(odd == 0, 0.0, far)
 
 
 def near_kernel(table_ref, fields_ref, near_ref, part_ref, high_ref, low_ref):
@@ -487,10 +504,16 @@
         [post[1], post[0], post[2], got[0], a[2], a[0], b[1], b[0]], axis=0
     )
 
-    rest_hot, reply_hot = call(
+    rest_hot, reply_hot, base, pre = call(
         hot_kernel,
-        [((6, 3 * CAP, NEW_DEV), BF16), ((NEW_DEV, 4 * CAP), BF16)],
-        (far, asked),
+        [
+            ((6, 3 * CAP, NEW_DEV), BF16),
+            ((NEW_DEV, 4 * CAP), BF16),
+            ((BLOCKS, MOVED_ROWS, 128), F32),
+            ((4, ROWS, CAP), F32),
+        ],
+        (me, far, asked, home, from_sib),
+        [SM, VM, VM, VM, VM],
         flops=10**9,
     )
     swapped = ((4, TRACE_ROWS, CAP), F32)
@@ -529,7 +552,7 @@
     start, swap = call(
         first_kernel,
         [((BLOCKS, MOVED_ROWS, 128), F32), swapped],
-        (me, home, from_far, from_sib, asked, reply_hot),
+        (me, base, pre, from_far, asked, reply_hot),
         [SM, VM, VM, VM, VM, VM],
         [got_scratch],
     )

time: 55.4 us -> 55.3 us (level)
    ppermute x1, waiting for transfers between devices: 1.27 us -> 0.17 us  [swap_chips(): lax.ppermute(x, AXES, [(i, (i + (1 if i % 2 else -1)) % n) for i in range...]
    ppermute x9, waiting for transfers between devices: 1.58 us -> 2.25 us  [swap_cores(): return lax.ppermute(x, AXES, [(i, i ^ 1) for i in range(n)])]
  transfers between devices with their start and end apart: 18 -> 18, of which waited for: 8 -> 9; matrix products, arithmetic and copies ran while one was open for 0% -> 0% of each run, Pallas kernels for 19% -> 20%
where the time goes in v8:
time: 55.3 us; the launch traced here: 55.1 us
  starting transfers between devices  31.4 us (57%)
  Pallas kernels  15.8 us (29%)
  waiting for transfers between devices  6.77 us (12%)
  between operations  1.04 us (2%)
    ppermute x8, starting transfers between devices, outward(): lax.ppermute(x, AXES, [(i, (i + (by if i % 2 == 0 else -by)) % n) for i i...  19.5 us
    pallas_call x14, Pallas kernels, call(): pl.pallas_call(kernel, out_shape=[jax.ShapeDtypeStruct(s, d) for s, d in...  15.8 us
    ppermute x9, starting transfers between devices, swap_cores(): return lax.ppermute(x, AXES, [(i, i ^ 1) for i in range(n)])  11.9 us
    ppermute x8, waiting for transfers between devices, outward(): lax.ppermute(x, AXES, [(i, (i + (by if i % 2 == 0 else -by)) % n) for i i...  4.35 us
    ppermute x9, waiting for transfers between devices, swap_cores(): return lax.ppermute(x, AXES, [(i, i ^ 1) for i in range(n)])  2.25 us
  transfers between devices with their start and end apart: 18, of which 9 were waited for; matrix products, arithmetic and copies ran while one was open for 0% of the time, Pallas kernels for 20%

profile of v8, /device:TPU:1, one launch (start us, length us, event | category | flops | bytes accessed | tf_op | source)
XLA Modules:
  0.0 55.1 jit_solution(9848993137684897806)
XLA Ops:
  0.6 1.5 %shard_map.68 = (s32[3,1,128]{2,1,0:T(1,128)S(1)}, s32[5,1,128]{2,1,0:T(1,128)S(1)}, s32[6,512]{1,0:T(8,128)S(1)}, s32[6,512]{1,0:T(8,128)S(1)}, f32[320,1024]{1...) custom-call(s32[1]{0:T(128)} %bitcast.me_ref, s32[6,512]{1,0:T(8,128)} %links_hbm.1, f32[320,1024]{1,0:T(8,128)} %bitcast.22, ...), custom_call_target="tpu_custom_call" | custom-call | flops 1000000 | bytes 1048576 | tf_op jit(solution)/shard_map/pallas_call | solution.py:429
  2.1 1.5 %collective-permute-start = (s32[5,1,128]{2,1,0:T(1,128)S(1)}, s32[5,1,128]{2,1,0:T(1,128)S(1)}, u32[]{:S(2)}, u32[]{:S(2)}) collective-permute-start(s32[5,1,128]{2,1,0:T(1,128)S(1)} %get-tuple-element.43.ask_ref), channel_id=1, source_target_pairs={{0,1},{1,0},{2,3},{3,2},{4,5},{5,4},{6,7},{7,6},{8,9},{9,8},{10,11... | collective-permute-start | bytes 7688 | tf_op jit(solution)/shard_map/ppermute | solution.py:442
  3.6 0.6 %shard_map.69 = f32[328,256]{1,0:T(8,128)S(1)} custom-call(s32[1]{0:T(128)} %bitcast.me_ref, f32[320,1024]{1,0:T(8,128)S(1)} %get-tuple-element.44.state_ref, s32[1,1024]{1,0:T(1,128)S(1)} %get-tuple-element.45.level_ref, s32[1,1024]{1,0:T(1,128)S(1)} %get-tuple-element.49.morton_ref), custom_call_target="tpu_custom_call" | custom-call | flops 1000000 | bytes 1048576 | tf_op jit(solution)/shard_map/pallas_call | solution.py:429
  4.5 8.7 %collective-permute-start.2 = (s32[3,1,128]{2,1,0:T(1,128)S(1)}, s32[3,1,128]{2,1,0:T(1,128)S(1)}, u32[]{:S(2)}, u32[]{:S(2)}) collective-permute-start(s32[3,1,128]{2,1,0:T(1,128)S(1)} %pad_add_fusion.1), channel_id=1, source_target_pairs={{0,4},{1,125},{2,6},{3,127},{4,8},{5,1},{6,10},{7,3},{8,12},{9,5},... | collective-permute-start | bytes 4616 | tf_op jit(solution)/shard_map/ppermute | solution.py:452
  13.1 0.8 %collective-permute-start.1 = (s32[4,1,128]{2,1,0:T(1,128)S(1)}, s32[4,1,128]{2,1,0:T(1,128)S(1)}, u32[]{:S(2)}, u32[]{:S(2)}) collective-permute-start(s32[4,1,128]{2,1,0:T(1,128)S(1)} %pad_add_fusion), channel_id=1, source_target_pairs={{0,2},{1,127},{2,4},{3,1},{4,6},{5,3},{6,8},{7,5},{8,10},{9,7},{10... | collective-permute-start | bytes 6152 | tf_op jit(solution)/shard_map/ppermute | solution.py:452
  13.9 1.9 %collective-permute-done.1 = s32[4,1,128]{2,1,0:T(1,128)S(1)} collective-permute-done((s32[4,1,128]{2,1,0:T(1,128)S(1)}, s32[4,1,128]{2,1,0:T(1,128)S(1)}, u32[]{:S(2)}, u32[]{:S(2)}) %collective-permute-start.1) | collective-permute-done | bytes 2080 | tf_op jit(solution)/shard_map/ppermute | solution.py:452
  15.9 1.2 %collective-permute-start.3 = (s32[3,1,128]{2,1,0:T(1,128)S(1)}, s32[3,1,128]{2,1,0:T(1,128)S(1)}, u32[]{:S(2)}, u32[]{:S(2)}) collective-permute-start(s32[3,1,128]{2,1,0:T(1,128)S(1)} %pad_add_fusion.2), channel_id=1, source_target_pairs={{0,1},{1,0},{2,3},{3,2},{4,5},{5,4},{6,7},{7,6},{8,9},{9,8},{10,11... | collective-permute-start | bytes 4616 | tf_op jit(solution)/shard_map/ppermute | solution.py:442
  17.1 0.6 %shard_map.71 = f32[328,256]{1,0:T(8,128)S(1)} custom-call(s32[1]{0:T(128)} %bitcast.me_ref, f32[320,1024]{1,0:T(8,128)S(1)} %get-tuple-element.44.state_ref, s32[1,1024]{1,0:T(1,128)S(1)} %get-tuple-element.45.level_ref, s32[1,1024]{1,0:T(1,128)S(1)} %get-tuple-element.49.morton_ref), custom_call_target="tpu_custom_call" | custom-call | flops 1000000000 | bytes 1048576 | tf_op jit(solution)/shard_map/pallas_call | solution.py:429
  17.8 0.9 %shard_map.70.home_ref = f32[4,328,128]{2,1,0:T(8,128)S(1)} custom-call(s32[1]{0:T(128)} %bitcast.me_ref, f32[320,1024]{1,0:T(8,128)S(1)} %get-tuple-element.44.state_ref, s32[1,1024]{1,0:T(1,128)S(1)} %get-tuple-element.45.level_ref, s32[1,1024]{1,0:T(1,128)S(1)} %get-tuple-element.49.morton_ref), custom_call_target="tpu_custom_call" | custom-call | flops 1000000 | bytes 1048576 | tf_op jit(solution)/shard_map/pallas_call | solution.py:429
  18.7 0.7 %collective-permute-done.4.sib_ref = f32[328,256]{1,0:T(8,128)S(1)} collective-permute-done((f32[328,256]{1,0:T(8,128)S(1)}, f32[328,256]{1,0:T(8,128)S(1)}, u32[]{:S(2)}, u32[]{:S(2)}) %collective-permute-start.4) | collective-permute-done | bytes 335904 | tf_op jit(solution)/shard_map/ppermute | solution.py:442
  19.4 0.9 %shard_map.72 = (bf16[6,384,512]{2,1,0:T(8,128)(2,1)S(1)}, bf16[512,512]{1,0:T(8,128)(2,1)S(1)}, f32[4,328,128]{2,1,0:T(8,128)S(1)}, f32[4,320,128]{2,1,0:T(8,128)S(1)}) custom-call(s32[1]{0:T(128)} %bitcast.me_ref, s32[6,512]{1,0:T(8,128)S(1)} %get-tuple-element.41.far_ref, s32[8,128]{1,0:T(8,128)S(1)} %concatenate.27.ask_ref, ...), custom_call_target="tpu_custom_call" | custom-call | flops 1000000000 | bytes 1048576 | tf_op jit(solution)/shard_map/pallas_call | solution.py:429
  20.5 0.4 shard_map.73
  20.9 0.4 collective-permute-start.7
  21.3 0.5 shard_map.74
  21.8 0.6 %collective-permute-done.7 = f32[4,80,128]{2,1,0:T(8,128)S(1)} collective-permute-done((f32[4,80,128]{2,1,0:T(8,128)S(1)}, f32[4,80,128]{2,1,0:T(8,128)S(1)}, u32[]{:S(2)}, u32[]{:S(2)}) %collective-permute-start.7) | collective-permute-done | bytes 163872 | tf_op jit(solution)/shard_map/ppermute | solution.py:442
  22.4 4.4 %collective-permute-start.9 = (f32[3,80,128]{2,1,0:T(8,128)S(1)}, f32[3,80,128]{2,1,0:T(8,128)S(1)}, u32[]{:S(2)}, u32[]{:S(2)}) collective-permute-start(f32[3,80,128]{2,1,0:T(8,128)S(1)} %pad_maximum_fusion), channel_id=1, source_target_pairs={{0,4},{1,125},{2,6},{3,127},{4,8},{5,1},{6,10},{7,3},{8,12},{9,5},... | collective-permute-start | bytes 368648 | tf_op jit(solution)/shard_map/ppermute | solution.py:452
  26.9 1.2 %collective-permute-start.6 = (f32[2,80,128]{2,1,0:T(8,128)S(1)}, f32[2,80,128]{2,1,0:T(8,128)S(1)}, u32[]{:S(2)}, u32[]{:S(2)}) collective-permute-start(f32[2,80,128]{2,1,0:T(8,128)S(1)} %get-tuple-element.55), channel_id=1, source_target_pairs={{0,2},{1,127},{2,4},{3,1},{4,6},{5,3},{6,8},{7,5},{8,10},{9,7},{10... | collective-permute-start | bytes 245768 | tf_op jit(solution)/shard_map/ppermute | solution.py:452
  28.1 2.2 %shard_map.75.part_ref = f32[4,320,128]{2,1,0:T(8,128)S(1)} custom-call(bf16[128,192]{1,0:T(8,128)(2,1)S(1)} %copy-done, f32[4,328,128]{2,1,0:T(8,128)S(1)} %get-tuple-element.54.fields_ref.start_ref, s32[6,512]{1,0:T(8,128)S(1)} %get-tuple-element.59.near_ref), custom_call_target="tpu_custom_call" | custom-call | flops 1000000000 | bytes 1048576 | tf_op jit(solution)/shard_map/pallas_call | solution.py:429
  30.7 1.0 %collective-permute-done.8.got_ref = f32[2,80,128]{2,1,0:T(8,128)S(1)} collective-permute-done((f32[2,80,128]{2,1,0:T(8,128)S(1)}, f32[2,80,128]{2,1,0:T(8,128)S(1)}, u32[]{:S(2)}, u32[]{:S(2)}) %collective-permute-start.8) | collective-permute-done | bytes 81952 | tf_op jit(solution)/shard_map/ppermute | solution.py:452
  31.7 3.6 %collective-permute-start.11 = (f32[3,80,128]{2,1,0:T(8,128)S(1)}, f32[3,80,128]{2,1,0:T(8,128)S(1)}, u32[]{:S(2)}, u32[]{:S(2)}) collective-permute-start(f32[3,80,128]{2,1,0:T(8,128)S(1)} %pad_maximum_fusion.1), channel_id=1, source_target_pairs={{0,1},{1,0},{2,3},{3,2},{4,5},{5,4},{6,7},{7,6},{8,9},{9,8},{10,11... | collective-permute-start | bytes 368648 | tf_op jit(solution)/shard_map/ppermute | solution.py:442
  35.3 1.2 %shard_map.76.part_ref = f32[4,320,128]{2,1,0:T(8,128)S(1)} custom-call(f32[4,320,128]{2,1,0:T(8,128)S(1)} %shard_map.75.part_ref, s32[6,512]{1,0:T(8,128)S(1)} %get-tuple-element.41.far_ref, s32[5,1,128]{2,1,0:T(1,128)S(1)} %get-tuple-element.43.ask_ref, f32[2,80,128]{2,1,0:T(8,128)S(1)} %collective-permute-done.6.own_ref, ...), custom_call_target="tpu_custom_call" | custom-call | flops 1000000000 | bytes 1048576 | tf_op jit(solution)/shard_map/pallas_call | solution.py:429
  36.5 1.3 %shard_map.77 = (f32[4,320,128]{2,1,0:T(8,128)S(1)}, f32[4,80,128]{2,1,0:T(8,128)S(1)}) custom-call(f32[4,328,128]{2,1,0:T(8,128)S(1)} %get-tuple-element.54.fields_ref.start_ref, f32[4,320,128]{2,1,0:T(8,128)S(1)} %shard_map.76.part_ref, bf16[6,384,512]{2,1,0:T(8,128)(2,1)S(1)} %get-tuple-element.66.rest_ref, ...), custom_call_target="tpu_custom_call" | custom-call | flops 1000000 | bytes 1048576 | tf_op jit(solution)/shard_map/pallas_call | solution.py:429
  37.8 0.4 collective-permute-start.13
  38.2 0.5 shard_map.78
  38.7 0.8 %collective-permute-done.13 = f32[4,80,128]{2,1,0:T(8,128)S(1)} collective-permute-done((f32[4,80,128]{2,1,0:T(8,128)S(1)}, f32[4,80,128]{2,1,0:T(8,128)S(1)}, u32[]{:S(2)}, u32[]{:S(2)}) %collective-permute-start.13) | collective-permute-done | bytes 163872 | tf_op jit(solution)/shard_map/ppermute | solution.py:442
  39.5 1.5 %collective-permute-start.15 = (f32[3,80,128]{2,1,0:T(8,128)S(1)}, f32[3,80,128]{2,1,0:T(8,128)S(1)}, u32[]{:S(2)}, u32[]{:S(2)}) collective-permute-start(f32[3,80,128]{2,1,0:T(8,128)S(1)} %pad_maximum_fusion.2), channel_id=1, source_target_pairs={{0,4},{1,125},{2,6},{3,127},{4,8},{5,1},{6,10},{7,3},{8,12},{9,5},... | collective-permute-start | bytes 368648 | tf_op jit(solution)/shard_map/ppermute | solution.py:452
  41.0 2.7 %collective-permute-start.12 = (f32[2,80,128]{2,1,0:T(8,128)S(1)}, f32[2,80,128]{2,1,0:T(8,128)S(1)}, u32[]{:S(2)}, u32[]{:S(2)}) collective-permute-start(f32[2,80,128]{2,1,0:T(8,128)S(1)} %get-tuple-element.68), channel_id=1, source_target_pairs={{0,2},{1,127},{2,4},{3,1},{4,6},{5,3},{6,8},{7,5},{8,10},{9,7},{10... | collective-permute-start | bytes 245768 | tf_op jit(solution)/shard_map/ppermute | solution.py:452
  43.8 2.2 %shard_map.79.part_ref = f32[4,320,128]{2,1,0:T(8,128)S(1)} custom-call(bf16[128,192]{1,0:T(8,128)(2,1)S(1)} %copy-done, f32[4,320,128]{2,1,0:T(8,128)S(1)} %get-tuple-element.67.fields_ref.section_ref, s32[6,512]{1,0:T(8,128)S(1)} %get-tuple-element.59.near_ref), custom_call_target="tpu_custom_call" | custom-call | flops 1000000000 | bytes 1048576 | tf_op jit(solution)/shard_map/pallas_call | solution.py:429
  46.2 1.2 %collective-permute-done.14.got_ref = f32[2,80,128]{2,1,0:T(8,128)S(1)} collective-permute-done((f32[2,80,128]{2,1,0:T(8,128)S(1)}, f32[2,80,128]{2,1,0:T(8,128)S(1)}, u32[]{:S(2)}, u32[]{:S(2)}) %collective-permute-start.14) | collective-permute-done | bytes 81952 | tf_op jit(solution)/shard_map/ppermute | solution.py:452
  47.4 4.6 %collective-permute-start.17 = (f32[3,80,128]{2,1,0:T(8,128)S(1)}, f32[3,80,128]{2,1,0:T(8,128)S(1)}, u32[]{:S(2)}, u32[]{:S(2)}) collective-permute-start(f32[3,80,128]{2,1,0:T(8,128)S(1)} %pad_maximum_fusion.3), channel_id=1, source_target_pairs={{0,1},{1,0},{2,3},{3,2},{4,5},{5,4},{6,7},{7,6},{8,9},{9,8},{10,11... | collective-permute-start | bytes 368648 | tf_op jit(solution)/shard_map/ppermute | solution.py:442
  52.0 1.2 %shard_map.80.part_ref = f32[4,320,128]{2,1,0:T(8,128)S(1)} custom-call(f32[4,320,128]{2,1,0:T(8,128)S(1)} %shard_map.79.part_ref, s32[6,512]{1,0:T(8,128)S(1)} %get-tuple-element.41.far_ref, s32[5,1,128]{2,1,0:T(1,128)S(1)} %get-tuple-element.43.ask_ref, f32[2,80,128]{2,1,0:T(8,128)S(1)} %collective-permute-done.12.own_ref, ...), custom_call_target="tpu_custom_call" | custom-call | flops 1000000000 | bytes 1048576 | tf_op jit(solution)/shard_map/pallas_call | solution.py:429
  53.2 1.7 %shard_map.81 = (f32[320,512]{1,0:T(8,128)}, f32[320,512]{1,0:T(8,128)}) custom-call(f32[4,328,128]{2,1,0:T(8,128)S(1)} %get-tuple-element.54.fields_ref.start_ref, f32[4,320,128]{2,1,0:T(8,128)S(1)} %get-tuple-element.67.fields_ref.section_ref, f32[4,320,128]{2,1,0:T(8,128)S(1)} %shard_map.80.part_ref, bf16[6,384,512]{2,1,0:T(8,128)(2,1)S(1)} %get-tuple-element.66.rest_ref, ...), custom_call_target="tpu_custom_call" | custom-call | flops 1000000 | bytes 1048576 | tf_op jit(solution)/shard_map/pallas_call | solution.py:429
  (43 shorter events, 1.3 us)
Async XLA Ops:
  2.1 2.3 %collective-permute-start = (s32[5,1,128]{2,1,0:T(1,128)S(1)}, s32[5,1,128]{2,1,0:T(1,128)S(1)}, u32[]{:S(2)}, u32[]{:S(2)}) collective-permute-start(s32[5,1,128]{2,1,0:T(1,128)S(1)} %get-tuple-element.43.ask_ref), channel_id=1, source_target_pairs={{0,1},{1,0},{2,3},{3,2},{4,5},{5,4},{6,7},{7,6},{8,9},{9,8},{10,11... | collective-permute-start | bytes 7688 | tf_op jit(solution)/shard_map/ppermute | solution.py:442
  4.5 9.4 %collective-permute-start.2 = (s32[3,1,128]{2,1,0:T(1,128)S(1)}, s32[3,1,128]{2,1,0:T(1,128)S(1)}, u32[]{:S(2)}, u32[]{:S(2)}) collective-permute-start(s32[3,1,128]{2,1,0:T(1,128)S(1)} %pad_add_fusion.1), channel_id=1, source_target_pairs={{0,4},{1,125},{2,6},{3,127},{4,8},{5,1},{6,10},{7,3},{8,12},{9,5},... | collective-permute-start | bytes 4616 | tf_op jit(solution)/shard_map/ppermute | solution.py:452
  13.1 2.7 %collective-permute-start.1 = (s32[4,1,128]{2,1,0:T(1,128)S(1)}, s32[4,1,128]{2,1,0:T(1,128)S(1)}, u32[]{:S(2)}, u32[]{:S(2)}) collective-permute-start(s32[4,1,128]{2,1,0:T(1,128)S(1)} %pad_add_fusion), channel_id=1, source_target_pairs={{0,2},{1,127},{2,4},{3,1},{4,6},{5,3},{6,8},{7,5},{8,10},{9,7},{10... | collective-permute-start | bytes 6152 | tf_op jit(solution)/shard_map/ppermute | solution.py:452
  13.9 6.6 %collective-permute-start.5 = (f32[328,256]{1,0:T(8,128)S(1)}, f32[328,256]{1,0:T(8,128)S(1)}, u32[]{:S(2)}, u32[]{:S(2)}) collective-permute-start(f32[328,256]{1,0:T(8,128)S(1)} %shard_map.69), channel_id=1, source_target_pairs={{0,127},{1,2},{2,1},{3,4},{4,3},{5,6},{6,5},{7,8},{8,7},{9,10},{10... | collective-permute-start | bytes 1007624 | tf_op jit(solution)/shard_map/ppermute | solution.py:447
  15.9 2.8 %collective-permute-start.3 = (s32[3,1,128]{2,1,0:T(1,128)S(1)}, s32[3,1,128]{2,1,0:T(1,128)S(1)}, u32[]{:S(2)}, u32[]{:S(2)}) collective-permute-start(s32[3,1,128]{2,1,0:T(1,128)S(1)} %pad_add_fusion.2), channel_id=1, source_target_pairs={{0,1},{1,0},{2,3},{3,2},{4,5},{5,4},{6,7},{7,6},{8,9},{9,8},{10,11... | collective-permute-start | bytes 4616 | tf_op jit(solution)/shard_map/ppermute | solution.py:442
  17.7 1.7 %collective-permute-start.4 = (f32[328,256]{1,0:T(8,128)S(1)}, f32[328,256]{1,0:T(8,128)S(1)}, u32[]{:S(2)}, u32[]{:S(2)}) collective-permute-start(f32[328,256]{1,0:T(8,128)S(1)} %shard_map.71), channel_id=1, source_target_pairs={{0,1},{1,0},{2,3},{3,2},{4,5},{5,4},{6,7},{7,6},{8,9},{9,8},{10,11... | collective-permute-start | bytes 1007624 | tf_op jit(solution)/shard_map/ppermute | solution.py:442
  20.9 1.5 %collective-permute-start.7 = (f32[4,80,128]{2,1,0:T(8,128)S(1)}, f32[4,80,128]{2,1,0:T(8,128)S(1)}, u32[]{:S(2)}, u32[]{:S(2)}) collective-permute-start(f32[4,80,128]{2,1,0:T(8,128)S(1)} %get-tuple-element.56), channel_id=1, source_target_pairs={{0,1},{1,0},{2,3},{3,2},{4,5},{5,4},{6,7},{7,6},{8,9},{9,8},{10,11... | collective-permute-start | bytes 491528 | tf_op jit(solution)/shard_map/ppermute | solution.py:442
  21.3 6.8 %copy-start = (bf16[128,192]{1,0:T(8,128)(2,1)S(1)}, bf16[128,192]{1,0:T(8,128)(2,1)}, u32[]{:S(2)}) copy-start(bf16[128,192]{1,0:T(8,128)(2,1)} %constant.13.clone.table_ref) | copy-start | bytes 147460
  22.4 9.2 %collective-permute-start.9 = (f32[3,80,128]{2,1,0:T(8,128)S(1)}, f32[3,80,128]{2,1,0:T(8,128)S(1)}, u32[]{:S(2)}, u32[]{:S(2)}) collective-permute-start(f32[3,80,128]{2,1,0:T(8,128)S(1)} %pad_maximum_fusion), channel_id=1, source_target_pairs={{0,4},{1,125},{2,6},{3,127},{4,8},{5,1},{6,10},{7,3},{8,12},{9,5},... | collective-permute-start | bytes 368648 | tf_op jit(solution)/shard_map/ppermute | solution.py:452
  26.9 3.8 %collective-permute-start.6 = (f32[2,80,128]{2,1,0:T(8,128)S(1)}, f32[2,80,128]{2,1,0:T(8,128)S(1)}, u32[]{:S(2)}, u32[]{:S(2)}) collective-permute-start(f32[2,80,128]{2,1,0:T(8,128)S(1)} %get-tuple-element.55), channel_id=1, source_target_pairs={{0,2},{1,127},{2,4},{3,1},{4,6},{5,3},{6,8},{7,5},{8,10},{9,7},{10... | collective-permute-start | bytes 245768 | tf_op jit(solution)/shard_map/ppermute | solution.py:452
  28.1 3.6 %collective-permute-start.8 = (f32[2,80,128]{2,1,0:T(8,128)S(1)}, f32[2,80,128]{2,1,0:T(8,128)S(1)}, u32[]{:S(2)}, u32[]{:S(2)}) collective-permute-start(f32[2,80,128]{2,1,0:T(8,128)S(1)} %get-tuple-element.83), channel_id=1, source_target_pairs={{0,2},{1,127},{2,4},{3,1},{4,6},{5,3},{6,8},{7,5},{8,10},{9,7},{10... | collective-permute-start | bytes 245768 | tf_op jit(solution)/shard_map/ppermute | solution.py:452
  30.3 5.0 %collective-permute-start.10 = (f32[1,80,128]{2,1,0:T(8,128)S(1)}, f32[1,80,128]{2,1,0:T(8,128)S(1)}, u32[]{:S(2)}, u32[]{:S(2)}) collective-permute-start(f32[1,80,128]{2,1,0:T(8,128)S(1)} %get-tuple-element.65), channel_id=1, source_target_pairs={{0,1},{1,0},{2,3},{3,2},{4,5},{5,4},{6,7},{7,6},{8,9},{9,8},{10,11... | collective-permute-start | bytes 122888 | tf_op jit(solution)/shard_map/ppermute | solution.py:442
  31.7 4.8 %collective-permute-start.11 = (f32[3,80,128]{2,1,0:T(8,128)S(1)}, f32[3,80,128]{2,1,0:T(8,128)S(1)}, u32[]{:S(2)}, u32[]{:S(2)}) collective-permute-start(f32[3,80,128]{2,1,0:T(8,128)S(1)} %pad_maximum_fusion.1), channel_id=1, source_target_pairs={{0,1},{1,0},{2,3},{3,2},{4,5},{5,4},{6,7},{7,6},{8,9},{9,8},{10,11... | collective-permute-start | bytes 368648 | tf_op jit(solution)/shard_map/ppermute | solution.py:442
  37.8 1.7 %collective-permute-start.13 = (f32[4,80,128]{2,1,0:T(8,128)S(1)}, f32[4,80,128]{2,1,0:T(8,128)S(1)}, u32[]{:S(2)}, u32[]{:S(2)}) collective-permute-start(f32[4,80,128]{2,1,0:T(8,128)S(1)} %get-tuple-element.69), channel_id=1, source_target_pairs={{0,1},{1,0},{2,3},{3,2},{4,5},{5,4},{6,7},{7,6},{8,9},{9,8},{10,11... | collective-permute-start | bytes 491528 | tf_op jit(solution)/shard_map/ppermute | solution.py:442
  39.5 7.8 %collective-permute-start.15 = (f32[3,80,128]{2,1,0:T(8,128)S(1)}, f32[3,80,128]{2,1,0:T(8,128)S(1)}, u32[]{:S(2)}, u32[]{:S(2)}) collective-permute-start(f32[3,80,128]{2,1,0:T(8,128)S(1)} %pad_maximum_fusion.2), channel_id=1, source_target_pairs={{0,4},{1,125},{2,6},{3,127},{4,8},{5,1},{6,10},{7,3},{8,12},{9,5},... | collective-permute-start | bytes 368648 | tf_op jit(solution)/shard_map/ppermute | solution.py:452
  41.0 5.1 %collective-permute-start.12 = (f32[2,80,128]{2,1,0:T(8,128)S(1)}, f32[2,80,128]{2,1,0:T(8,128)S(1)}, u32[]{:S(2)}, u32[]{:S(2)}) collective-permute-start(f32[2,80,128]{2,1,0:T(8,128)S(1)} %get-tuple-element.68), channel_id=1, source_target_pairs={{0,2},{1,127},{2,4},{3,1},{4,6},{5,3},{6,8},{7,5},{8,10},{9,7},{10... | collective-permute-start | bytes 245768 | tf_op jit(solution)/shard_map/ppermute | solution.py:452
  43.8 3.6 %collective-permute-start.14 = (f32[2,80,128]{2,1,0:T(8,128)S(1)}, f32[2,80,128]{2,1,0:T(8,128)S(1)}, u32[]{:S(2)}, u32[]{:S(2)}) collective-permute-start(f32[2,80,128]{2,1,0:T(8,128)S(1)} %get-tuple-element.81), channel_id=1, source_target_pairs={{0,2},{1,127},{2,4},{3,1},{4,6},{5,3},{6,8},{7,5},{8,10},{9,7},{10... | collective-permute-start | bytes 245768 | tf_op jit(solution)/shard_map/ppermute | solution.py:452
  46.1 5.9 %collective-permute-start.16 = (f32[1,80,128]{2,1,0:T(8,128)S(1)}, f32[1,80,128]{2,1,0:T(8,128)S(1)}, u32[]{:S(2)}, u32[]{:S(2)}) collective-permute-start(f32[1,80,128]{2,1,0:T(8,128)S(1)} %get-tuple-element.77), channel_id=1, source_target_pairs={{0,1},{1,0},{2,3},{3,2},{4,5},{5,4},{6,7},{7,6},{8,9},{9,8},{10,11... | collective-permute-start | bytes 122888 | tf_op jit(solution)/shard_map/ppermute | solution.py:442
  47.4 5.8 %collective-permute-start.17 = (f32[3,80,128]{2,1,0:T(8,128)S(1)}, f32[3,80,128]{2,1,0:T(8,128)S(1)}, u32[]{:S(2)}, u32[]{:S(2)}) collective-permute-start(f32[3,80,128]{2,1,0:T(8,128)S(1)} %pad_maximum_fusion.3), channel_id=1, source_target_pairs={{0,1},{1,0},{2,3},{3,2},{4,5},{5,4},{6,7},{7,6},{8,9},{9,8},{10,11... | collective-permute-start | bytes 368648 | tf_op jit(solution)/shard_map/ppermute | solution.py:442

commit v9 on v8

--- a/solution.py
+++ b/solution.py
@@ -149,10 +149,18 @@
     b = lax.broadcasted_iota(I32, (8, NEW_DEV), 0)
     step_of = jnp.where(b < 3, b + 2, jnp.where(b == 3, 1, 3 - b))
     masks = [jnp.where(gap[f : f + 1, :] == step_of, 1.0, 0.0) for f in range(6)]
-    k = lax.broadcasted_iota(I32, (NEW_DEV, NEW_DEV), 0)
-    j = lax.broadcasted_iota(I32, (NEW_DEV, NEW_DEV), 1)
+    k = lax.broadcasted_iota(I32, (128, 128), 0)
+    j = lax.broadcasted_iota(I32, (128, 128), 1)
     upper = jnp.where(k <= j, 1.0, 0.0).astype(BF16)
-    counts = dot(jnp.concatenate(masks, axis=0).astype(BF16), upper)
+    every = jnp.concatenate(masks, axis=0)
+    blocks = [every[:, 128 * q : 128 * q + 128] for q in range(BLOCKS)]
+    inside = dot(jnp.concatenate(blocks, axis=0).astype(BF16), upper)
+    before = jnp.zeros((48, 1), F32)
+    counts = []
+    for q in range(BLOCKS):
+        counts.append(inside[48 * q : 48 * q + 48] + before)
+        before = counts[-1][:, 127:128]
+    counts = jnp.concatenate(counts, axis=1)
     offset = jnp.full((8, 1), -1.0, F32)
     bf = b.astype(F32)
     total = jnp.zeros((16, CAP), F32)
@@ -370,20 +378,28 @@
     return jnp.concatenate([high, low], axis=0)
 
 
-def add_ghosts(sum_ref, lhs, hot_of, blocks=range(BLOCKS)):
+def add_ghosts(part_ref, sum_ref, lhs, hot_of, blocks=range(BLOCKS)):
+    for c in blocks:
+        for v in range(FIELDS):
+            rows = slice(DOFS * v + 16, DOFS * v + 48)
+            sum_ref[c, rows, :] = part_ref[c, rows, :]
     for f in range(6):
         both = dot(lhs, hot_of(f))
         for i, c in enumerate(blocks):
             spot = slice(128 * i, 128 * i + 128)
             term = both[0:TRACE_ROWS, spot] + both[TRACE_ROWS:, spot]
             for v in range(FIELDS):
-                add_on_face(sum_ref, c, v, f, term[16 * v : 16 * v + 16])
+                x = term[16 * v : 16 * v + 16]
+                if f < 2:
+                    rows = slice(DOFS * v + 48 * f, DOFS * v + 48 * f + 16)
+                    sum_ref[c, rows, :] = part_ref[c, rows, :] + x
+                else:
+                    add_on_face(sum_ref, c, v, f, x)
 
 
 def direct_kernel(part_ref, far_ref, ask_ref, own_ref, got_ref, b_ref, sib_ref, sum_ref):
     lhs = ghost_rows([sib_ref[0], got_ref[0], own_ref[0], b_ref[1], b_ref[0]], ask_ref)
-    sum_ref[...] = part_ref[...]
-    add_ghosts(sum_ref, lhs, lambda f: one_hot_rows(5 * CAP, far_ref[f : f + 1, :] - 3 * CAP))
+    add_ghosts(part_ref, sum_ref, lhs, lambda f: one_hot_rows(5 * CAP, far_ref[f : f + 1, :] - 3 * CAP))
 
 
 def metric_of(start_ref, c):
@@ -393,8 +409,7 @@
 def second_kernel(start_ref, part_ref, rest_ref, own_ask_ref, post_ref, ask_ref, hot_ref,
                   section_ref, swap_ref, sum_ref, got_ref):
     lhs = ghost_rows([post_ref[1], post_ref[0], post_ref[2]], own_ask_ref)
-    sum_ref[...] = part_ref[...]
-    add_ghosts(sum_ref, lhs, lambda f: rest_ref[f])
+    add_ghosts(part_ref, sum_ref, lhs, lambda f: rest_ref[f])
     for c in range(BLOCKS):
         section_ref[c] = start_ref[c, 0:ROWS, :] - (DT * metric_of(start_ref, c)) * sum_ref[c]
     reply(wide(section_ref, ROWS), ask_ref[4:8, :], hot_ref[...], got_ref, [swap_ref.at[t] for t in range(4)])
@@ -403,11 +418,10 @@
 def last_kernel(start_ref, section_ref, part_ref, rest_ref, own_ask_ref, post_ref,
                 state_hbm, rate_hbm, sum_ref, state_ref, rate_ref, sems):
     lhs = ghost_rows([post_ref[1], post_ref[0], post_ref[2]], own_ask_ref)
-    sum_ref[...] = part_ref[...]
     copies = []
     for half in range(2):
         pair = (2 * half, 2 * half + 1)
-        add_ghosts(sum_ref, lhs, lambda f: rest_ref[f, :, HALF * half : HALF * half + HALF], pair)
+        add_ghosts(part_ref, sum_ref, lhs, lambda f: rest_ref[f, :, HALF * half : HALF * half + HALF], pair)
         for c in pair:
             rate = -metric_of(start_ref, c) * sum_ref[c]
             rate_ref[c] = rate

time: 55.3 us -> 55.4 us (level)
  no operation moved by 1% of the time
where the time goes in v9:
time: 55.4 us; the launch traced here: 55.2 us
  starting transfers between devices  31.4 us (57%)
  Pallas kernels  15.9 us (29%)
  waiting for transfers between devices  6.78 us (12%)
  between operations  1.03 us (2%)
    ppermute x8, starting transfers between devices, outward(): lax.ppermute(x, AXES, [(i, (i + (by if i % 2 == 0 else -by)) % n) for i i...  19.5 us
    pallas_call x14, Pallas kernels, call(): pl.pallas_call(kernel, out_shape=[jax.ShapeDtypeStruct(s, d) for s, d in...  15.9 us
    ppermute x9, starting transfers between devices, swap_cores(): return lax.ppermute(x, AXES, [(i, i ^ 1) for i in range(n)])  11.9 us
    ppermute x8, waiting for transfers between devices, outward(): lax.ppermute(x, AXES, [(i, (i + (by if i % 2 == 0 else -by)) % n) for i i...  4.35 us
    ppermute x9, waiting for transfers between devices, swap_cores(): return lax.ppermute(x, AXES, [(i, i ^ 1) for i in range(n)])  2.26 us
  transfers between devices with their start and end apart: 18, of which 9 were waited for; matrix products, arithmetic and copies ran while one was open for 0% of the time, Pallas kernels for 20%

profile of v9, /device:TPU:1, one launch (start us, length us, event | category | flops | bytes accessed | tf_op | source)
XLA Modules:
  0.0 55.2 jit_solution(17248658774924866074)
XLA Ops:
  0.6 1.6 %shard_map.68 = (s32[3,1,128]{2,1,0:T(1,128)S(1)}, s32[5,1,128]{2,1,0:T(1,128)S(1)}, s32[6,512]{1,0:T(8,128)S(1)}, s32[6,512]{1,0:T(8,128)S(1)}, f32[320,1024]{1...) custom-call(s32[1]{0:T(128)} %bitcast.me_ref, s32[6,512]{1,0:T(8,128)} %links_hbm.1, f32[320,1024]{1,0:T(8,128)} %bitcast.22, ...), custom_call_target="tpu_custom_call" | custom-call | flops 1000000 | bytes 1048576 | tf_op jit(solution)/shard_map/pallas_call | solution.py:443
  2.2 1.5 %collective-permute-start = (s32[5,1,128]{2,1,0:T(1,128)S(1)}, s32[5,1,128]{2,1,0:T(1,128)S(1)}, u32[]{:S(2)}, u32[]{:S(2)}) collective-permute-start(s32[5,1,128]{2,1,0:T(1,128)S(1)} %get-tuple-element.43.ask_ref), channel_id=1, source_target_pairs={{0,1},{1,0},{2,3},{3,2},{4,5},{5,4},{6,7},{7,6},{8,9},{9,8},{10,11... | collective-permute-start | bytes 7688 | tf_op jit(solution)/shard_map/ppermute | solution.py:456
  3.7 0.6 %shard_map.69 = f32[328,256]{1,0:T(8,128)S(1)} custom-call(s32[1]{0:T(128)} %bitcast.me_ref, f32[320,1024]{1,0:T(8,128)S(1)} %get-tuple-element.44.state_ref, s32[1,1024]{1,0:T(1,128)S(1)} %get-tuple-element.45.level_ref, s32[1,1024]{1,0:T(1,128)S(1)} %get-tuple-element.49.morton_ref), custom_call_target="tpu_custom_call" | custom-call | flops 1000000 | bytes 1048576 | tf_op jit(solution)/shard_map/pallas_call | solution.py:443
  4.6 8.7 %collective-permute-start.2 = (s32[3,1,128]{2,1,0:T(1,128)S(1)}, s32[3,1,128]{2,1,0:T(1,128)S(1)}, u32[]{:S(2)}, u32[]{:S(2)}) collective-permute-start(s32[3,1,128]{2,1,0:T(1,128)S(1)} %pad_add_fusion.1), channel_id=1, source_target_pairs={{0,4},{1,125},{2,6},{3,127},{4,8},{5,1},{6,10},{7,3},{8,12},{9,5},... | collective-permute-start | bytes 4616 | tf_op jit(solution)/shard_map/ppermute | solution.py:466
  13.2 0.8 %collective-permute-start.1 = (s32[4,1,128]{2,1,0:T(1,128)S(1)}, s32[4,1,128]{2,1,0:T(1,128)S(1)}, u32[]{:S(2)}, u32[]{:S(2)}) collective-permute-start(s32[4,1,128]{2,1,0:T(1,128)S(1)} %pad_add_fusion), channel_id=1, source_target_pairs={{0,2},{1,127},{2,4},{3,1},{4,6},{5,3},{6,8},{7,5},{8,10},{9,7},{10... | collective-permute-start | bytes 6152 | tf_op jit(solution)/shard_map/ppermute | solution.py:466
  14.0 1.9 %collective-permute-done.1 = s32[4,1,128]{2,1,0:T(1,128)S(1)} collective-permute-done((s32[4,1,128]{2,1,0:T(1,128)S(1)}, s32[4,1,128]{2,1,0:T(1,128)S(1)}, u32[]{:S(2)}, u32[]{:S(2)}) %collective-permute-start.1) | collective-permute-done | bytes 2080 | tf_op jit(solution)/shard_map/ppermute | solution.py:466
  16.0 1.2 %collective-permute-start.3 = (s32[3,1,128]{2,1,0:T(1,128)S(1)}, s32[3,1,128]{2,1,0:T(1,128)S(1)}, u32[]{:S(2)}, u32[]{:S(2)}) collective-permute-start(s32[3,1,128]{2,1,0:T(1,128)S(1)} %pad_add_fusion.2), channel_id=1, source_target_pairs={{0,1},{1,0},{2,3},{3,2},{4,5},{5,4},{6,7},{7,6},{8,9},{9,8},{10,11... | collective-permute-start | bytes 4616 | tf_op jit(solution)/shard_map/ppermute | solution.py:456
  17.2 0.6 %shard_map.71 = f32[328,256]{1,0:T(8,128)S(1)} custom-call(s32[1]{0:T(128)} %bitcast.me_ref, f32[320,1024]{1,0:T(8,128)S(1)} %get-tuple-element.44.state_ref, s32[1,1024]{1,0:T(1,128)S(1)} %get-tuple-element.45.level_ref, s32[1,1024]{1,0:T(1,128)S(1)} %get-tuple-element.49.morton_ref), custom_call_target="tpu_custom_call" | custom-call | flops 1000000000 | bytes 1048576 | tf_op jit(solution)/shard_map/pallas_call | solution.py:443
  17.9 0.9 %shard_map.70.home_ref = f32[4,328,128]{2,1,0:T(8,128)S(1)} custom-call(s32[1]{0:T(128)} %bitcast.me_ref, f32[320,1024]{1,0:T(8,128)S(1)} %get-tuple-element.44.state_ref, s32[1,1024]{1,0:T(1,128)S(1)} %get-tuple-element.45.level_ref, s32[1,1024]{1,0:T(1,128)S(1)} %get-tuple-element.49.morton_ref), custom_call_target="tpu_custom_call" | custom-call | flops 1000000 | bytes 1048576 | tf_op jit(solution)/shard_map/pallas_call | solution.py:443
  18.8 0.7 %collective-permute-done.4.sib_ref = f32[328,256]{1,0:T(8,128)S(1)} collective-permute-done((f32[328,256]{1,0:T(8,128)S(1)}, f32[328,256]{1,0:T(8,128)S(1)}, u32[]{:S(2)}, u32[]{:S(2)}) %collective-permute-start.4) | collective-permute-done | bytes 335904 | tf_op jit(solution)/shard_map/ppermute | solution.py:456
  19.5 0.9 %shard_map.72 = (bf16[6,384,512]{2,1,0:T(8,128)(2,1)S(1)}, bf16[512,512]{1,0:T(8,128)(2,1)S(1)}, f32[4,328,128]{2,1,0:T(8,128)S(1)}, f32[4,320,128]{2,1,0:T(8,128)S(1)}) custom-call(s32[1]{0:T(128)} %bitcast.me_ref, s32[6,512]{1,0:T(8,128)S(1)} %get-tuple-element.41.far_ref, s32[8,128]{1,0:T(8,128)S(1)} %concatenate.27.ask_ref, ...), custom_call_target="tpu_custom_call" | custom-call | flops 1000000000 | bytes 1048576 | tf_op jit(solution)/shard_map/pallas_call | solution.py:443
  20.6 0.4 shard_map.73
  21.0 0.4 collective-permute-start.7
  21.4 0.5 shard_map.74
  21.9 0.6 %collective-permute-done.7 = f32[4,80,128]{2,1,0:T(8,128)S(1)} collective-permute-done((f32[4,80,128]{2,1,0:T(8,128)S(1)}, f32[4,80,128]{2,1,0:T(8,128)S(1)}, u32[]{:S(2)}, u32[]{:S(2)}) %collective-permute-start.7) | collective-permute-done | bytes 163872 | tf_op jit(solution)/shard_map/ppermute | solution.py:456
  22.5 4.4 %collective-permute-start.9 = (f32[3,80,128]{2,1,0:T(8,128)S(1)}, f32[3,80,128]{2,1,0:T(8,128)S(1)}, u32[]{:S(2)}, u32[]{:S(2)}) collective-permute-start(f32[3,80,128]{2,1,0:T(8,128)S(1)} %pad_maximum_fusion), channel_id=1, source_target_pairs={{0,4},{1,125},{2,6},{3,127},{4,8},{5,1},{6,10},{7,3},{8,12},{9,5},... | collective-permute-start | bytes 368648 | tf_op jit(solution)/shard_map/ppermute | solution.py:466
  27.0 1.2 %collective-permute-start.6 = (f32[2,80,128]{2,1,0:T(8,128)S(1)}, f32[2,80,128]{2,1,0:T(8,128)S(1)}, u32[]{:S(2)}, u32[]{:S(2)}) collective-permute-start(f32[2,80,128]{2,1,0:T(8,128)S(1)} %get-tuple-element.55), channel_id=1, source_target_pairs={{0,2},{1,127},{2,4},{3,1},{4,6},{5,3},{6,8},{7,5},{8,10},{9,7},{10... | collective-permute-start | bytes 245768 | tf_op jit(solution)/shard_map/ppermute | solution.py:466
  28.2 2.2 %shard_map.75.part_ref = f32[4,320,128]{2,1,0:T(8,128)S(1)} custom-call(bf16[128,192]{1,0:T(8,128)(2,1)S(1)} %copy-done, f32[4,328,128]{2,1,0:T(8,128)S(1)} %get-tuple-element.54.fields_ref.start_ref, s32[6,512]{1,0:T(8,128)S(1)} %get-tuple-element.59.near_ref), custom_call_target="tpu_custom_call" | custom-call | flops 1000000000 | bytes 1048576 | tf_op jit(solution)/shard_map/pallas_call | solution.py:443
  30.8 1.0 %collective-permute-done.8.got_ref = f32[2,80,128]{2,1,0:T(8,128)S(1)} collective-permute-done((f32[2,80,128]{2,1,0:T(8,128)S(1)}, f32[2,80,128]{2,1,0:T(8,128)S(1)}, u32[]{:S(2)}, u32[]{:S(2)}) %collective-permute-start.8) | collective-permute-done | bytes 81952 | tf_op jit(solution)/shard_map/ppermute | solution.py:466
  31.8 3.6 %collective-permute-start.11 = (f32[3,80,128]{2,1,0:T(8,128)S(1)}, f32[3,80,128]{2,1,0:T(8,128)S(1)}, u32[]{:S(2)}, u32[]{:S(2)}) collective-permute-start(f32[3,80,128]{2,1,0:T(8,128)S(1)} %pad_maximum_fusion.1), channel_id=1, source_target_pairs={{0,1},{1,0},{2,3},{3,2},{4,5},{5,4},{6,7},{7,6},{8,9},{9,8},{10,11... | collective-permute-start | bytes 368648 | tf_op jit(solution)/shard_map/ppermute | solution.py:456
  35.4 1.2 %shard_map.76.part_ref = f32[4,320,128]{2,1,0:T(8,128)S(1)} custom-call(f32[4,320,128]{2,1,0:T(8,128)S(1)} %shard_map.75.part_ref, s32[6,512]{1,0:T(8,128)S(1)} %get-tuple-element.41.far_ref, s32[5,1,128]{2,1,0:T(1,128)S(1)} %get-tuple-element.43.ask_ref, f32[2,80,128]{2,1,0:T(8,128)S(1)} %collective-permute-done.6.own_ref, ...), custom_call_target="tpu_custom_call" | custom-call | flops 1000000000 | bytes 1048576 | tf_op jit(solution)/shard_map/pallas_call | solution.py:443
  36.6 1.3 %shard_map.77 = (f32[4,320,128]{2,1,0:T(8,128)S(1)}, f32[4,80,128]{2,1,0:T(8,128)S(1)}) custom-call(f32[4,328,128]{2,1,0:T(8,128)S(1)} %get-tuple-element.54.fields_ref.start_ref, f32[4,320,128]{2,1,0:T(8,128)S(1)} %shard_map.76.part_ref, bf16[6,384,512]{2,1,0:T(8,128)(2,1)S(1)} %get-tuple-element.66.rest_ref, ...), custom_call_target="tpu_custom_call" | custom-call | flops 1000000 | bytes 1048576 | tf_op jit(solution)/shard_map/pallas_call | solution.py:443
  37.9 0.4 collective-permute-start.13
  38.3 0.5 shard_map.78
  38.8 0.8 %collective-permute-done.13 = f32[4,80,128]{2,1,0:T(8,128)S(1)} collective-permute-done((f32[4,80,128]{2,1,0:T(8,128)S(1)}, f32[4,80,128]{2,1,0:T(8,128)S(1)}, u32[]{:S(2)}, u32[]{:S(2)}) %collective-permute-start.13) | collective-permute-done | bytes 163872 | tf_op jit(solution)/shard_map/ppermute | solution.py:456
  39.6 1.5 %collective-permute-start.15 = (f32[3,80,128]{2,1,0:T(8,128)S(1)}, f32[3,80,128]{2,1,0:T(8,128)S(1)}, u32[]{:S(2)}, u32[]{:S(2)}) collective-permute-start(f32[3,80,128]{2,1,0:T(8,128)S(1)} %pad_maximum_fusion.2), channel_id=1, source_target_pairs={{0,4},{1,125},{2,6},{3,127},{4,8},{5,1},{6,10},{7,3},{8,12},{9,5},... | collective-permute-start | bytes 368648 | tf_op jit(solution)/shard_map/ppermute | solution.py:466
  41.1 2.7 %collective-permute-start.12 = (f32[2,80,128]{2,1,0:T(8,128)S(1)}, f32[2,80,128]{2,1,0:T(8,128)S(1)}, u32[]{:S(2)}, u32[]{:S(2)}) collective-permute-start(f32[2,80,128]{2,1,0:T(8,128)S(1)} %get-tuple-element.68), channel_id=1, source_target_pairs={{0,2},{1,127},{2,4},{3,1},{4,6},{5,3},{6,8},{7,5},{8,10},{9,7},{10... | collective-permute-start | bytes 245768 | tf_op jit(solution)/shard_map/ppermute | solution.py:466
  43.9 2.2 %shard_map.79.part_ref = f32[4,320,128]{2,1,0:T(8,128)S(1)} custom-call(bf16[128,192]{1,0:T(8,128)(2,1)S(1)} %copy-done, f32[4,320,128]{2,1,0:T(8,128)S(1)} %get-tuple-element.67.fields_ref.section_ref, s32[6,512]{1,0:T(8,128)S(1)} %get-tuple-element.59.near_ref), custom_call_target="tpu_custom_call" | custom-call | flops 1000000000 | bytes 1048576 | tf_op jit(solution)/shard_map/pallas_call | solution.py:443
  46.2 1.2 %collective-permute-done.14.got_ref = f32[2,80,128]{2,1,0:T(8,128)S(1)} collective-permute-done((f32[2,80,128]{2,1,0:T(8,128)S(1)}, f32[2,80,128]{2,1,0:T(8,128)S(1)}, u32[]{:S(2)}, u32[]{:S(2)}) %collective-permute-start.14) | collective-permute-done | bytes 81952 | tf_op jit(solution)/shard_map/ppermute | solution.py:466
  47.5 4.6 %collective-permute-start.17 = (f32[3,80,128]{2,1,0:T(8,128)S(1)}, f32[3,80,128]{2,1,0:T(8,128)S(1)}, u32[]{:S(2)}, u32[]{:S(2)}) collective-permute-start(f32[3,80,128]{2,1,0:T(8,128)S(1)} %pad_maximum_fusion.3), channel_id=1, source_target_pairs={{0,1},{1,0},{2,3},{3,2},{4,5},{5,4},{6,7},{7,6},{8,9},{9,8},{10,11... | collective-permute-start | bytes 368648 | tf_op jit(solution)/shard_map/ppermute | solution.py:456
  52.1 1.2 %shard_map.80.part_ref = f32[4,320,128]{2,1,0:T(8,128)S(1)} custom-call(f32[4,320,128]{2,1,0:T(8,128)S(1)} %shard_map.79.part_ref, s32[6,512]{1,0:T(8,128)S(1)} %get-tuple-element.41.far_ref, s32[5,1,128]{2,1,0:T(1,128)S(1)} %get-tuple-element.43.ask_ref, f32[2,80,128]{2,1,0:T(8,128)S(1)} %collective-permute-done.12.own_ref, ...), custom_call_target="tpu_custom_call" | custom-call | flops 1000000000 | bytes 1048576 | tf_op jit(solution)/shard_map/pallas_call | solution.py:443
  53.3 1.7 %shard_map.81 = (f32[320,512]{1,0:T(8,128)}, f32[320,512]{1,0:T(8,128)}) custom-call(f32[4,328,128]{2,1,0:T(8,128)S(1)} %get-tuple-element.54.fields_ref.start_ref, f32[4,320,128]{2,1,0:T(8,128)S(1)} %get-tuple-element.67.fields_ref.section_ref, f32[4,320,128]{2,1,0:T(8,128)S(1)} %shard_map.80.part_ref, bf16[6,384,512]{2,1,0:T(8,128)(2,1)S(1)} %get-tuple-element.66.rest_ref, ...), custom_call_target="tpu_custom_call" | custom-call | flops 1000000 | bytes 1048576 | tf_op jit(solution)/shard_map/pallas_call | solution.py:443
  (43 shorter events, 1.3 us)
Async XLA Ops:
  2.2 2.3 %collective-permute-start = (s32[5,1,128]{2,1,0:T(1,128)S(1)}, s32[5,1,128]{2,1,0:T(1,128)S(1)}, u32[]{:S(2)}, u32[]{:S(2)}) collective-permute-start(s32[5,1,128]{2,1,0:T(1,128)S(1)} %get-tuple-element.43.ask_ref), channel_id=1, source_target_pairs={{0,1},{1,0},{2,3},{3,2},{4,5},{5,4},{6,7},{7,6},{8,9},{9,8},{10,11... | collective-permute-start | bytes 7688 | tf_op jit(solution)/shard_map/ppermute | solution.py:456
  4.6 9.4 %collective-permute-start.2 = (s32[3,1,128]{2,1,0:T(1,128)S(1)}, s32[3,1,128]{2,1,0:T(1,128)S(1)}, u32[]{:S(2)}, u32[]{:S(2)}) collective-permute-start(s32[3,1,128]{2,1,0:T(1,128)S(1)} %pad_add_fusion.1), channel_id=1, source_target_pairs={{0,4},{1,125},{2,6},{3,127},{4,8},{5,1},{6,10},{7,3},{8,12},{9,5},... | collective-permute-start | bytes 4616 | tf_op jit(solution)/shard_map/ppermute | solution.py:466
  13.2 2.7 %collective-permute-start.1 = (s32[4,1,128]{2,1,0:T(1,128)S(1)}, s32[4,1,128]{2,1,0:T(1,128)S(1)}, u32[]{:S(2)}, u32[]{:S(2)}) collective-permute-start(s32[4,1,128]{2,1,0:T(1,128)S(1)} %pad_add_fusion), channel_id=1, source_target_pairs={{0,2},{1,127},{2,4},{3,1},{4,6},{5,3},{6,8},{7,5},{8,10},{9,7},{10... | collective-permute-start | bytes 6152 | tf_op jit(solution)/shard_map/ppermute | solution.py:466
  14.0 6.6 %collective-permute-start.5 = (f32[328,256]{1,0:T(8,128)S(1)}, f32[328,256]{1,0:T(8,128)S(1)}, u32[]{:S(2)}, u32[]{:S(2)}) collective-permute-start(f32[328,256]{1,0:T(8,128)S(1)} %shard_map.69), channel_id=1, source_target_pairs={{0,127},{1,2},{2,1},{3,4},{4,3},{5,6},{6,5},{7,8},{8,7},{9,10},{10... | collective-permute-start | bytes 1007624 | tf_op jit(solution)/shard_map/ppermute | solution.py:461
  16.0 2.8 %collective-permute-start.3 = (s32[3,1,128]{2,1,0:T(1,128)S(1)}, s32[3,1,128]{2,1,0:T(1,128)S(1)}, u32[]{:S(2)}, u32[]{:S(2)}) collective-permute-start(s32[3,1,128]{2,1,0:T(1,128)S(1)} %pad_add_fusion.2), channel_id=1, source_target_pairs={{0,1},{1,0},{2,3},{3,2},{4,5},{5,4},{6,7},{7,6},{8,9},{9,8},{10,11... | collective-permute-start | bytes 4616 | tf_op jit(solution)/shard_map/ppermute | solution.py:456
  17.8 1.7 %collective-permute-start.4 = (f32[328,256]{1,0:T(8,128)S(1)}, f32[328,256]{1,0:T(8,128)S(1)}, u32[]{:S(2)}, u32[]{:S(2)}) collective-permute-start(f32[328,256]{1,0:T(8,128)S(1)} %shard_map.71), channel_id=1, source_target_pairs={{0,1},{1,0},{2,3},{3,2},{4,5},{5,4},{6,7},{7,6},{8,9},{9,8},{10,11... | collective-permute-start | bytes 1007624 | tf_op jit(solution)/shard_map/ppermute | solution.py:456
  21.0 1.5 %collective-permute-start.7 = (f32[4,80,128]{2,1,0:T(8,128)S(1)}, f32[4,80,128]{2,1,0:T(8,128)S(1)}, u32[]{:S(2)}, u32[]{:S(2)}) collective-permute-start(f32[4,80,128]{2,1,0:T(8,128)S(1)} %get-tuple-element.56), channel_id=1, source_target_pairs={{0,1},{1,0},{2,3},{3,2},{4,5},{5,4},{6,7},{7,6},{8,9},{9,8},{10,11... | collective-permute-start | bytes 491528 | tf_op jit(solution)/shard_map/ppermute | solution.py:456
  21.4 6.8 %copy-start = (bf16[128,192]{1,0:T(8,128)(2,1)S(1)}, bf16[128,192]{1,0:T(8,128)(2,1)}, u32[]{:S(2)}) copy-start(bf16[128,192]{1,0:T(8,128)(2,1)} %constant.13.clone.table_ref) | copy-start | bytes 147460
  22.5 9.2 %collective-permute-start.9 = (f32[3,80,128]{2,1,0:T(8,128)S(1)}, f32[3,80,128]{2,1,0:T(8,128)S(1)}, u32[]{:S(2)}, u32[]{:S(2)}) collective-permute-start(f32[3,80,128]{2,1,0:T(8,128)S(1)} %pad_maximum_fusion), channel_id=1, source_target_pairs={{0,4},{1,125},{2,6},{3,127},{4,8},{5,1},{6,10},{7,3},{8,12},{9,5},... | collective-permute-start | bytes 368648 | tf_op jit(solution)/shard_map/ppermute | solution.py:466
  27.0 3.8 %collective-permute-start.6 = (f32[2,80,128]{2,1,0:T(8,128)S(1)}, f32[2,80,128]{2,1,0:T(8,128)S(1)}, u32[]{:S(2)}, u32[]{:S(2)}) collective-permute-start(f32[2,80,128]{2,1,0:T(8,128)S(1)} %get-tuple-element.55), channel_id=1, source_target_pairs={{0,2},{1,127},{2,4},{3,1},{4,6},{5,3},{6,8},{7,5},{8,10},{9,7},{10... | collective-permute-start | bytes 245768 | tf_op jit(solution)/shard_map/ppermute | solution.py:466
  28.2 3.6 %collective-permute-start.8 = (f32[2,80,128]{2,1,0:T(8,128)S(1)}, f32[2,80,128]{2,1,0:T(8,128)S(1)}, u32[]{:S(2)}, u32[]{:S(2)}) collective-permute-start(f32[2,80,128]{2,1,0:T(8,128)S(1)} %get-tuple-element.83), channel_id=1, source_target_pairs={{0,2},{1,127},{2,4},{3,1},{4,6},{5,3},{6,8},{7,5},{8,10},{9,7},{10... | collective-permute-start | bytes 245768 | tf_op jit(solution)/shard_map/ppermute | solution.py:466
  30.4 5.0 %collective-permute-start.10 = (f32[1,80,128]{2,1,0:T(8,128)S(1)}, f32[1,80,128]{2,1,0:T(8,128)S(1)}, u32[]{:S(2)}, u32[]{:S(2)}) collective-permute-start(f32[1,80,128]{2,1,0:T(8,128)S(1)} %get-tuple-element.65), channel_id=1, source_target_pairs={{0,1},{1,0},{2,3},{3,2},{4,5},{5,4},{6,7},{7,6},{8,9},{9,8},{10,11... | collective-permute-start | bytes 122888 | tf_op jit(solution)/shard_map/ppermute | solution.py:456
  31.8 4.8 %collective-permute-start.11 = (f32[3,80,128]{2,1,0:T(8,128)S(1)}, f32[3,80,128]{2,1,0:T(8,128)S(1)}, u32[]{:S(2)}, u32[]{:S(2)}) collective-permute-start(f32[3,80,128]{2,1,0:T(8,128)S(1)} %pad_maximum_fusion.1), channel_id=1, source_target_pairs={{0,1},{1,0},{2,3},{3,2},{4,5},{5,4},{6,7},{7,6},{8,9},{9,8},{10,11... | collective-permute-start | bytes 368648 | tf_op jit(solution)/shard_map/ppermute | solution.py:456
  37.9 1.7 %collective-permute-start.13 = (f32[4,80,128]{2,1,0:T(8,128)S(1)}, f32[4,80,128]{2,1,0:T(8,128)S(1)}, u32[]{:S(2)}, u32[]{:S(2)}) collective-permute-start(f32[4,80,128]{2,1,0:T(8,128)S(1)} %get-tuple-element.69), channel_id=1, source_target_pairs={{0,1},{1,0},{2,3},{3,2},{4,5},{5,4},{6,7},{7,6},{8,9},{9,8},{10,11... | collective-permute-start | bytes 491528 | tf_op jit(solution)/shard_map/ppermute | solution.py:456
  39.6 7.8 %collective-permute-start.15 = (f32[3,80,128]{2,1,0:T(8,128)S(1)}, f32[3,80,128]{2,1,0:T(8,128)S(1)}, u32[]{:S(2)}, u32[]{:S(2)}) collective-permute-start(f32[3,80,128]{2,1,0:T(8,128)S(1)} %pad_maximum_fusion.2), channel_id=1, source_target_pairs={{0,4},{1,125},{2,6},{3,127},{4,8},{5,1},{6,10},{7,3},{8,12},{9,5},... | collective-permute-start | bytes 368648 | tf_op jit(solution)/shard_map/ppermute | solution.py:466
  41.1 5.1 %collective-permute-start.12 = (f32[2,80,128]{2,1,0:T(8,128)S(1)}, f32[2,80,128]{2,1,0:T(8,128)S(1)}, u32[]{:S(2)}, u32[]{:S(2)}) collective-permute-start(f32[2,80,128]{2,1,0:T(8,128)S(1)} %get-tuple-element.68), channel_id=1, source_target_pairs={{0,2},{1,127},{2,4},{3,1},{4,6},{5,3},{6,8},{7,5},{8,10},{9,7},{10... | collective-permute-start | bytes 245768 | tf_op jit(solution)/shard_map/ppermute | solution.py:466
  43.8 3.6 %collective-permute-start.14 = (f32[2,80,128]{2,1,0:T(8,128)S(1)}, f32[2,80,128]{2,1,0:T(8,128)S(1)}, u32[]{:S(2)}, u32[]{:S(2)}) collective-permute-start(f32[2,80,128]{2,1,0:T(8,128)S(1)} %get-tuple-element.81), channel_id=1, source_target_pairs={{0,2},{1,127},{2,4},{3,1},{4,6},{5,3},{6,8},{7,5},{8,10},{9,7},{10... | collective-permute-start | bytes 245768 | tf_op jit(solution)/shard_map/ppermute | solution.py:466
  46.1 5.9 %collective-permute-start.16 = (f32[1,80,128]{2,1,0:T(8,128)S(1)}, f32[1,80,128]{2,1,0:T(8,128)S(1)}, u32[]{:S(2)}, u32[]{:S(2)}) collective-permute-start(f32[1,80,128]{2,1,0:T(8,128)S(1)} %get-tuple-element.77), channel_id=1, source_target_pairs={{0,1},{1,0},{2,3},{3,2},{4,5},{5,4},{6,7},{7,6},{8,9},{9,8},{10,11... | collective-permute-start | bytes 122888 | tf_op jit(solution)/shard_map/ppermute | solution.py:456
  47.5 5.8 %collective-permute-start.17 = (f32[3,80,128]{2,1,0:T(8,128)S(1)}, f32[3,80,128]{2,1,0:T(8,128)S(1)}, u32[]{:S(2)}, u32[]{:S(2)}) collective-permute-start(f32[3,80,128]{2,1,0:T(8,128)S(1)} %pad_maximum_fusion.3), channel_id=1, source_target_pairs={{0,1},{1,0},{2,3},{3,2},{4,5},{5,4},{6,7},{7,6},{8,9},{9,8},{10,11... | collective-permute-start | bytes 368648 | tf_op jit(solution)/shard_map/ppermute | solution.py:456

commit v10 on v8

--- a/solution.py
+++ b/solution.py
@@ -380,8 +380,8 @@
                 add_on_face(sum_ref, c, v, f, term[16 * v : 16 * v + 16])
 
 
-def direct_kernel(part_ref, far_ref, ask_ref, own_ref, got_ref, b_ref, sib_ref, sum_ref):
-    lhs = ghost_rows([sib_ref[0], got_ref[0], own_ref[0], b_ref[1], b_ref[0]], ask_ref)
+def direct_kernel(part_ref, far_ref, ask_ref, a_ref, b_ref, sib_ref, sum_ref):
+    lhs = ghost_rows([sib_ref[0], a_ref[2], a_ref[0], b_ref[1], b_ref[0]], ask_ref)
     sum_ref[...] = part_ref[...]
     add_ghosts(sum_ref, lhs, lambda f: one_hot_rows(5 * CAP, far_ref[f : f + 1, :] - 3 * CAP))
 
@@ -531,9 +531,7 @@
             [got_scratch],
             flops=10**9,
         )
-        a_own = outward(own[0], 2)
-        b = outward(jnp.concatenate([own[1], got[2:4]], axis=0), 4)
-        a_got = outward(got[0:2], 2)
+        a, b = outward_pair(own, got)
         (part,) = call(
             near_kernel,
             [blocks],
@@ -544,9 +542,9 @@
         )
         sib, part = lax.optimization_barrier((sib, part))
         sib = swap_cores(sib)
-        a_own, a_got, b, part = lax.optimization_barrier((a_own, a_got, b, part))
-        post = swap_cores(jnp.concatenate([a_own[1:2], a_got[1:2], b[2:3]], axis=0))
-        (part,) = call(direct_kernel, [blocks], (part, far, swap_ask, a_own, a_got, b, sib), flops=10**9)
+        a, b, part = lax.optimization_barrier((a, b, part))
+        post = swap_back(a, b)
+        (part,) = call(direct_kernel, [blocks], (part, far, swap_ask, a, b, sib), flops=10**9)
         return part, rest_hot, own_ask, post
 
     start, swap = call(

time: 55.3 us -> 55.7 us (level)
  waiting for transfers between devices: 6.77 us -> 10.8 us
  starting transfers between devices: 31.4 us -> 27.8 us
    ppermute x8 -> x6, waiting for transfers between devices: 4.35 us -> 8.36 us  [outward(): lax.ppermute(x, AXES, [(i, (i + (by if i % 2 == 0 else -by)) % n) for i i...]
    ppermute x9, starting transfers between devices: 11.9 us -> 8.76 us  [swap_cores(): return lax.ppermute(x, AXES, [(i, i ^ 1) for i in range(n)])]
    ppermute x8 -> x6, starting transfers between devices: 19.5 us -> 19 us  [outward(): lax.ppermute(x, AXES, [(i, (i + (by if i % 2 == 0 else -by)) % n) for i i...]
  transfers between devices with their start and end apart: 18 -> 16, of which waited for: 9 -> 8; matrix products, arithmetic and copies ran while one was open for 0% -> 0% of each run, Pallas kernels for 20% -> 19%
where the time goes in v10:
time: 55.7 us; the launch traced here: 55.6 us
  starting transfers between devices  27.8 us (50%)
  Pallas kernels  15.8 us (28%)
  waiting for transfers between devices  10.8 us (19%)
  between operations  1.03 us (2%)
    ppermute x6, starting transfers between devices, outward(): lax.ppermute(x, AXES, [(i, (i + (by if i % 2 == 0 else -by)) % n) for i i...  19 us
    pallas_call x14, Pallas kernels, call(): pl.pallas_call(kernel, out_shape=[jax.ShapeDtypeStruct(s, d) for s, d in...  15.8 us
    ppermute x9, starting transfers between devices, swap_cores(): return lax.ppermute(x, AXES, [(i, i ^ 1) for i in range(n)])  8.76 us
    ppermute x6, waiting for transfers between devices, outward(): lax.ppermute(x, AXES, [(i, (i + (by if i % 2 == 0 else -by)) % n) for i i...  8.36 us
    ppermute x9, waiting for transfers between devices, swap_cores(): return lax.ppermute(x, AXES, [(i, i ^ 1) for i in range(n)])  2.25 us
  transfers between devices with their start and end apart: 16, of which 8 were waited for; matrix products, arithmetic and copies ran while one was open for 0% of the time, Pallas kernels for 19%

profile of v10, /device:TPU:1, one launch (start us, length us, event | category | flops | bytes accessed | tf_op | source)
XLA Modules:
  0.0 55.6 jit_solution(10643500223206075253)
XLA Ops:
  0.6 1.5 %shard_map.68 = (s32[3,1,128]{2,1,0:T(1,128)S(1)}, s32[5,1,128]{2,1,0:T(1,128)S(1)}, s32[6,512]{1,0:T(8,128)S(1)}, s32[6,512]{1,0:T(8,128)S(1)}, f32[320,1024]{1...) custom-call(s32[1]{0:T(128)} %bitcast.me_ref, s32[6,512]{1,0:T(8,128)} %links_hbm.1, f32[320,1024]{1,0:T(8,128)} %bitcast.22, ...), custom_call_target="tpu_custom_call" | custom-call | flops 1000000 | bytes 1048576 | tf_op jit(solution)/shard_map/pallas_call | solution.py:429
  2.1 1.5 %collective-permute-start = (s32[5,1,128]{2,1,0:T(1,128)S(1)}, s32[5,1,128]{2,1,0:T(1,128)S(1)}, u32[]{:S(2)}, u32[]{:S(2)}) collective-permute-start(s32[5,1,128]{2,1,0:T(1,128)S(1)} %get-tuple-element.41.ask_ref), channel_id=1, source_target_pairs={{0,1},{1,0},{2,3},{3,2},{4,5},{5,4},{6,7},{7,6},{8,9},{9,8},{10,11... | collective-permute-start | bytes 7688 | tf_op jit(solution)/shard_map/ppermute | solution.py:442
  3.6 0.6 %shard_map.69 = f32[328,256]{1,0:T(8,128)S(1)} custom-call(s32[1]{0:T(128)} %bitcast.me_ref, f32[320,1024]{1,0:T(8,128)S(1)} %get-tuple-element.42.state_ref, s32[1,1024]{1,0:T(1,128)S(1)} %get-tuple-element.43.level_ref, s32[1,1024]{1,0:T(1,128)S(1)} %get-tuple-element.47.morton_ref), custom_call_target="tpu_custom_call" | custom-call | flops 1000000 | bytes 1048576 | tf_op jit(solution)/shard_map/pallas_call | solution.py:429
  4.2 0.2 collective-permute-done
  4.5 8.7 %collective-permute-start.2 = (s32[3,1,128]{2,1,0:T(1,128)S(1)}, s32[3,1,128]{2,1,0:T(1,128)S(1)}, u32[]{:S(2)}, u32[]{:S(2)}) collective-permute-start(s32[3,1,128]{2,1,0:T(1,128)S(1)} %pad_add_fusion.1), channel_id=1, source_target_pairs={{0,4},{1,125},{2,6},{3,127},{4,8},{5,1},{6,10},{7,3},{8,12},{9,5},... | collective-permute-start | bytes 4616 | tf_op jit(solution)/shard_map/ppermute | solution.py:452
  13.1 0.8 %collective-permute-start.1 = (s32[4,1,128]{2,1,0:T(1,128)S(1)}, s32[4,1,128]{2,1,0:T(1,128)S(1)}, u32[]{:S(2)}, u32[]{:S(2)}) collective-permute-start(s32[4,1,128]{2,1,0:T(1,128)S(1)} %pad_add_fusion), channel_id=1, source_target_pairs={{0,2},{1,127},{2,4},{3,1},{4,6},{5,3},{6,8},{7,5},{8,10},{9,7},{10... | collective-permute-start | bytes 6152 | tf_op jit(solution)/shard_map/ppermute | solution.py:452
  13.9 1.9 %collective-permute-done.1 = s32[4,1,128]{2,1,0:T(1,128)S(1)} collective-permute-done((s32[4,1,128]{2,1,0:T(1,128)S(1)}, s32[4,1,128]{2,1,0:T(1,128)S(1)}, u32[]{:S(2)}, u32[]{:S(2)}) %collective-permute-start.1) | collective-permute-done | bytes 2080 | tf_op jit(solution)/shard_map/ppermute | solution.py:452
  15.9 1.2 %collective-permute-start.3 = (s32[3,1,128]{2,1,0:T(1,128)S(1)}, s32[3,1,128]{2,1,0:T(1,128)S(1)}, u32[]{:S(2)}, u32[]{:S(2)}) collective-permute-start(s32[3,1,128]{2,1,0:T(1,128)S(1)} %pad_add_fusion.2), channel_id=1, source_target_pairs={{0,1},{1,0},{2,3},{3,2},{4,5},{5,4},{6,7},{7,6},{8,9},{9,8},{10,11... | collective-permute-start | bytes 4616 | tf_op jit(solution)/shard_map/ppermute | solution.py:442
  17.1 0.6 %shard_map.71 = f32[328,256]{1,0:T(8,128)S(1)} custom-call(s32[1]{0:T(128)} %bitcast.me_ref, f32[320,1024]{1,0:T(8,128)S(1)} %get-tuple-element.42.state_ref, s32[1,1024]{1,0:T(1,128)S(1)} %get-tuple-element.43.level_ref, s32[1,1024]{1,0:T(1,128)S(1)} %get-tuple-element.47.morton_ref), custom_call_target="tpu_custom_call" | custom-call | flops 1000000000 | bytes 1048576 | tf_op jit(solution)/shard_map/pallas_call | solution.py:429
  17.8 0.9 %shard_map.70.home_ref = f32[4,328,128]{2,1,0:T(8,128)S(1)} custom-call(s32[1]{0:T(128)} %bitcast.me_ref, f32[320,1024]{1,0:T(8,128)S(1)} %get-tuple-element.42.state_ref, s32[1,1024]{1,0:T(1,128)S(1)} %get-tuple-element.43.level_ref, s32[1,1024]{1,0:T(1,128)S(1)} %get-tuple-element.47.morton_ref), custom_call_target="tpu_custom_call" | custom-call | flops 1000000 | bytes 1048576 | tf_op jit(solution)/shard_map/pallas_call | solution.py:429
  18.7 0.7 %collective-permute-done.4.sib_ref = f32[328,256]{1,0:T(8,128)S(1)} collective-permute-done((f32[328,256]{1,0:T(8,128)S(1)}, f32[328,256]{1,0:T(8,128)S(1)}, u32[]{:S(2)}, u32[]{:S(2)}) %collective-permute-start.4) | collective-permute-done | bytes 335904 | tf_op jit(solution)/shard_map/ppermute | solution.py:442
  19.4 0.9 %shard_map.72 = (bf16[6,384,512]{2,1,0:T(8,128)(2,1)S(1)}, bf16[512,512]{1,0:T(8,128)(2,1)S(1)}, f32[4,328,128]{2,1,0:T(8,128)S(1)}, f32[4,320,128]{2,1,0:T(8,128)S(1)}) custom-call(s32[1]{0:T(128)} %bitcast.me_ref, s32[6,512]{1,0:T(8,128)S(1)} %get-tuple-element.39.far_ref, s32[8,128]{1,0:T(8,128)S(1)} %concatenate.33.ask_ref, ...), custom_call_target="tpu_custom_call" | custom-call | flops 1000000000 | bytes 1048576 | tf_op jit(solution)/shard_map/pallas_call | solution.py:429
  20.5 0.4 shard_map.73
  20.9 0.4 collective-permute-start.6
  21.3 0.5 shard_map.74
  21.8 0.6 %collective-permute-done.6 = f32[4,80,128]{2,1,0:T(8,128)S(1)} collective-permute-done((f32[4,80,128]{2,1,0:T(8,128)S(1)}, f32[4,80,128]{2,1,0:T(8,128)S(1)}, u32[]{:S(2)}, u32[]{:S(2)}) %collective-permute-start.6) | collective-permute-done | bytes 163872 | tf_op jit(solution)/shard_map/ppermute | solution.py:442
  22.5 5.5 %collective-permute-start.7 = (f32[4,80,128]{2,1,0:T(8,128)S(1)}, f32[4,80,128]{2,1,0:T(8,128)S(1)}, u32[]{:S(2)}, u32[]{:S(2)}) collective-permute-start(f32[4,80,128]{2,1,0:T(8,128)S(1)} %pad_maximum_fusion), channel_id=1, source_target_pairs={{0,2},{1,127},{2,4},{3,1},{4,6},{5,3},{6,8},{7,5},{8,10},{9,7},{10... | collective-permute-start | bytes 491528 | tf_op jit(solution)/shard_map/ppermute | solution.py:452
  28.1 2.2 %shard_map.75.part_ref = f32[4,320,128]{2,1,0:T(8,128)S(1)} custom-call(bf16[128,192]{1,0:T(8,128)(2,1)S(1)} %copy-done, f32[4,328,128]{2,1,0:T(8,128)S(1)} %get-tuple-element.52.fields_ref.start_ref, s32[6,512]{1,0:T(8,128)S(1)} %get-tuple-element.57.near_ref), custom_call_target="tpu_custom_call" | custom-call | flops 1000000000 | bytes 1048576 | tf_op jit(solution)/shard_map/pallas_call | solution.py:429
  30.4 3.4 %collective-permute-done.8.b_ref = f32[3,80,128]{2,1,0:T(8,128)S(1)} collective-permute-done((f32[3,80,128]{2,1,0:T(8,128)S(1)}, f32[3,80,128]{2,1,0:T(8,128)S(1)}, u32[]{:S(2)}, u32[]{:S(2)}) %collective-permute-start.8) | collective-permute-done | bytes 122912 | tf_op jit(solution)/shard_map/ppermute | solution.py:452
  33.8 2.0 %collective-permute-start.10 = (f32[3,80,128]{2,1,0:T(8,128)S(1)}, f32[3,80,128]{2,1,0:T(8,128)S(1)}, u32[]{:S(2)}, u32[]{:S(2)}) collective-permute-start(f32[3,80,128]{2,1,0:T(8,128)S(1)} %pad_maximum_fusion.3), channel_id=1, source_target_pairs={{0,1},{1,0},{2,3},{3,2},{4,5},{5,4},{6,7},{7,6},{8,9},{9,8},{10,11... | collective-permute-start | bytes 368648 | tf_op jit(solution)/shard_map/ppermute | solution.py:442
  35.8 1.2 %shard_map.76.part_ref = f32[4,320,128]{2,1,0:T(8,128)S(1)} custom-call(f32[4,320,128]{2,1,0:T(8,128)S(1)} %shard_map.75.part_ref, s32[6,512]{1,0:T(8,128)S(1)} %get-tuple-element.39.far_ref, s32[5,1,128]{2,1,0:T(1,128)S(1)} %get-tuple-element.41.ask_ref, f32[4,80,128]{2,1,0:T(8,128)S(1)} %collective-permute-done.7.a_ref, ...), custom_call_target="tpu_custom_call" | custom-call | flops 1000000000 | bytes 1048576 | tf_op jit(solution)/shard_map/pallas_call | solution.py:429
  37.1 1.3 %shard_map.77 = (f32[4,320,128]{2,1,0:T(8,128)S(1)}, f32[4,80,128]{2,1,0:T(8,128)S(1)}) custom-call(f32[4,328,128]{2,1,0:T(8,128)S(1)} %get-tuple-element.52.fields_ref.start_ref, f32[4,320,128]{2,1,0:T(8,128)S(1)} %shard_map.76.part_ref, bf16[6,384,512]{2,1,0:T(8,128)(2,1)S(1)} %get-tuple-element.63.rest_ref, ...), custom_call_target="tpu_custom_call" | custom-call | flops 1000000 | bytes 1048576 | tf_op jit(solution)/shard_map/pallas_call | solution.py:429
  38.3 0.2 collective-permute-start.11
  38.5 0.5 shard_map.78
  39.1 0.8 %collective-permute-done.11 = f32[4,80,128]{2,1,0:T(8,128)S(1)} collective-permute-done((f32[4,80,128]{2,1,0:T(8,128)S(1)}, f32[4,80,128]{2,1,0:T(8,128)S(1)}, u32[]{:S(2)}, u32[]{:S(2)}) %collective-permute-start.11) | collective-permute-done | bytes 163872 | tf_op jit(solution)/shard_map/ppermute | solution.py:442
  39.9 3.7 %collective-permute-start.12 = (f32[4,80,128]{2,1,0:T(8,128)S(1)}, f32[4,80,128]{2,1,0:T(8,128)S(1)}, u32[]{:S(2)}, u32[]{:S(2)}) collective-permute-start(f32[4,80,128]{2,1,0:T(8,128)S(1)} %pad_maximum_fusion.1), channel_id=1, source_target_pairs={{0,2},{1,127},{2,4},{3,1},{4,6},{5,3},{6,8},{7,5},{8,10},{9,7},{10... | collective-permute-start | bytes 491528 | tf_op jit(solution)/shard_map/ppermute | solution.py:452
  43.5 0.3 collective-permute-start.13
  43.8 2.2 %shard_map.79.part_ref = f32[4,320,128]{2,1,0:T(8,128)S(1)} custom-call(bf16[128,192]{1,0:T(8,128)(2,1)S(1)} %copy-done, f32[4,320,128]{2,1,0:T(8,128)S(1)} %get-tuple-element.64.fields_ref.section_ref, s32[6,512]{1,0:T(8,128)S(1)} %get-tuple-element.57.near_ref), custom_call_target="tpu_custom_call" | custom-call | flops 1000000000 | bytes 1048576 | tf_op jit(solution)/shard_map/pallas_call | solution.py:429
  46.2 3.0 %collective-permute-done.13.b_ref = f32[3,80,128]{2,1,0:T(8,128)S(1)} collective-permute-done((f32[3,80,128]{2,1,0:T(8,128)S(1)}, f32[3,80,128]{2,1,0:T(8,128)S(1)}, u32[]{:S(2)}, u32[]{:S(2)}) %collective-permute-start.13) | collective-permute-done | bytes 122912 | tf_op jit(solution)/shard_map/ppermute | solution.py:452
  49.2 3.2 %collective-permute-start.15 = (f32[3,80,128]{2,1,0:T(8,128)S(1)}, f32[3,80,128]{2,1,0:T(8,128)S(1)}, u32[]{:S(2)}, u32[]{:S(2)}) collective-permute-start(f32[3,80,128]{2,1,0:T(8,128)S(1)} %pad_maximum_fusion.5), channel_id=1, source_target_pairs={{0,1},{1,0},{2,3},{3,2},{4,5},{5,4},{6,7},{7,6},{8,9},{9,8},{10,11... | collective-permute-start | bytes 368648 | tf_op jit(solution)/shard_map/ppermute | solution.py:442
  52.4 1.2 %shard_map.80.part_ref = f32[4,320,128]{2,1,0:T(8,128)S(1)} custom-call(f32[4,320,128]{2,1,0:T(8,128)S(1)} %shard_map.79.part_ref, s32[6,512]{1,0:T(8,128)S(1)} %get-tuple-element.39.far_ref, s32[5,1,128]{2,1,0:T(1,128)S(1)} %get-tuple-element.41.ask_ref, f32[4,80,128]{2,1,0:T(8,128)S(1)} %collective-permute-done.12.a_ref, ...), custom_call_target="tpu_custom_call" | custom-call | flops 1000000000 | bytes 1048576 | tf_op jit(solution)/shard_map/pallas_call | solution.py:429
  53.7 1.7 %shard_map.81 = (f32[320,512]{1,0:T(8,128)}, f32[320,512]{1,0:T(8,128)}) custom-call(f32[4,328,128]{2,1,0:T(8,128)S(1)} %get-tuple-element.52.fields_ref.start_ref, f32[4,320,128]{2,1,0:T(8,128)S(1)} %get-tuple-element.64.fields_ref.section_ref, f32[4,320,128]{2,1,0:T(8,128)S(1)} %shard_map.80.part_ref, bf16[6,384,512]{2,1,0:T(8,128)(2,1)S(1)} %get-tuple-element.63.rest_ref, ...), custom_call_target="tpu_custom_call" | custom-call | flops 1000000 | bytes 1048576 | tf_op jit(solution)/shard_map/pallas_call | solution.py:429
  (39 shorter events, 0.7 us)
Async XLA Ops:
  2.1 2.3 %collective-permute-start = (s32[5,1,128]{2,1,0:T(1,128)S(1)}, s32[5,1,128]{2,1,0:T(1,128)S(1)}, u32[]{:S(2)}, u32[]{:S(2)}) collective-permute-start(s32[5,1,128]{2,1,0:T(1,128)S(1)} %get-tuple-element.41.ask_ref), channel_id=1, source_target_pairs={{0,1},{1,0},{2,3},{3,2},{4,5},{5,4},{6,7},{7,6},{8,9},{9,8},{10,11... | collective-permute-start | bytes 7688 | tf_op jit(solution)/shard_map/ppermute | solution.py:442
  4.5 9.4 %collective-permute-start.2 = (s32[3,1,128]{2,1,0:T(1,128)S(1)}, s32[3,1,128]{2,1,0:T(1,128)S(1)}, u32[]{:S(2)}, u32[]{:S(2)}) collective-permute-start(s32[3,1,128]{2,1,0:T(1,128)S(1)} %pad_add_fusion.1), channel_id=1, source_target_pairs={{0,4},{1,125},{2,6},{3,127},{4,8},{5,1},{6,10},{7,3},{8,12},{9,5},... | collective-permute-start | bytes 4616 | tf_op jit(solution)/shard_map/ppermute | solution.py:452
  13.1 2.7 %collective-permute-start.1 = (s32[4,1,128]{2,1,0:T(1,128)S(1)}, s32[4,1,128]{2,1,0:T(1,128)S(1)}, u32[]{:S(2)}, u32[]{:S(2)}) collective-permute-start(s32[4,1,128]{2,1,0:T(1,128)S(1)} %pad_add_fusion), channel_id=1, source_target_pairs={{0,2},{1,127},{2,4},{3,1},{4,6},{5,3},{6,8},{7,5},{8,10},{9,7},{10... | collective-permute-start | bytes 6152 | tf_op jit(solution)/shard_map/ppermute | solution.py:452
  13.9 6.6 %collective-permute-start.5 = (f32[328,256]{1,0:T(8,128)S(1)}, f32[328,256]{1,0:T(8,128)S(1)}, u32[]{:S(2)}, u32[]{:S(2)}) collective-permute-start(f32[328,256]{1,0:T(8,128)S(1)} %shard_map.69), channel_id=1, source_target_pairs={{0,127},{1,2},{2,1},{3,4},{4,3},{5,6},{6,5},{7,8},{8,7},{9,10},{10... | collective-permute-start | bytes 1007624 | tf_op jit(solution)/shard_map/ppermute | solution.py:447
  15.9 2.8 %collective-permute-start.3 = (s32[3,1,128]{2,1,0:T(1,128)S(1)}, s32[3,1,128]{2,1,0:T(1,128)S(1)}, u32[]{:S(2)}, u32[]{:S(2)}) collective-permute-start(s32[3,1,128]{2,1,0:T(1,128)S(1)} %pad_add_fusion.2), channel_id=1, source_target_pairs={{0,1},{1,0},{2,3},{3,2},{4,5},{5,4},{6,7},{7,6},{8,9},{9,8},{10,11... | collective-permute-start | bytes 4616 | tf_op jit(solution)/shard_map/ppermute | solution.py:442
  17.7 1.7 %collective-permute-start.4 = (f32[328,256]{1,0:T(8,128)S(1)}, f32[328,256]{1,0:T(8,128)S(1)}, u32[]{:S(2)}, u32[]{:S(2)}) collective-permute-start(f32[328,256]{1,0:T(8,128)S(1)} %shard_map.71), channel_id=1, source_target_pairs={{0,1},{1,0},{2,3},{3,2},{4,5},{5,4},{6,7},{7,6},{8,9},{9,8},{10,11... | collective-permute-start | bytes 1007624 | tf_op jit(solution)/shard_map/ppermute | solution.py:442
  20.9 1.5 %collective-permute-start.6 = (f32[4,80,128]{2,1,0:T(8,128)S(1)}, f32[4,80,128]{2,1,0:T(8,128)S(1)}, u32[]{:S(2)}, u32[]{:S(2)}) collective-permute-start(f32[4,80,128]{2,1,0:T(8,128)S(1)} %get-tuple-element.54), channel_id=1, source_target_pairs={{0,1},{1,0},{2,3},{3,2},{4,5},{5,4},{6,7},{7,6},{8,9},{9,8},{10,11... | collective-permute-start | bytes 491528 | tf_op jit(solution)/shard_map/ppermute | solution.py:442
  21.3 6.8 %copy-start = (bf16[128,192]{1,0:T(8,128)(2,1)S(1)}, bf16[128,192]{1,0:T(8,128)(2,1)}, u32[]{:S(2)}) copy-start(bf16[128,192]{1,0:T(8,128)(2,1)} %constant.13.clone.table_ref) | copy-start | bytes 147460
  22.5 11.3 %collective-permute-start.7 = (f32[4,80,128]{2,1,0:T(8,128)S(1)}, f32[4,80,128]{2,1,0:T(8,128)S(1)}, u32[]{:S(2)}, u32[]{:S(2)}) collective-permute-start(f32[4,80,128]{2,1,0:T(8,128)S(1)} %pad_maximum_fusion), channel_id=1, source_target_pairs={{0,2},{1,127},{2,4},{3,1},{4,6},{5,3},{6,8},{7,5},{8,10},{9,7},{10... | collective-permute-start | bytes 491528 | tf_op jit(solution)/shard_map/ppermute | solution.py:452
  28.0 5.8 %collective-permute-start.8 = (f32[3,80,128]{2,1,0:T(8,128)S(1)}, f32[3,80,128]{2,1,0:T(8,128)S(1)}, u32[]{:S(2)}, u32[]{:S(2)}) collective-permute-start(f32[3,80,128]{2,1,0:T(8,128)S(1)} %pad_maximum_fusion.2), channel_id=1, source_target_pairs={{0,4},{1,125},{2,6},{3,127},{4,8},{5,1},{6,10},{7,3},{8,12},{9,5},... | collective-permute-start | bytes 368648 | tf_op jit(solution)/shard_map/ppermute | solution.py:452
  30.3 5.5 %collective-permute-start.9 = (f32[1,80,128]{2,1,0:T(8,128)S(1)}, f32[1,80,128]{2,1,0:T(8,128)S(1)}, u32[]{:S(2)}, u32[]{:S(2)}) collective-permute-start(f32[1,80,128]{2,1,0:T(8,128)S(1)} %get-tuple-element.62), channel_id=1, source_target_pairs={{0,1},{1,0},{2,3},{3,2},{4,5},{5,4},{6,7},{7,6},{8,9},{9,8},{10,11... | collective-permute-start | bytes 122888 | tf_op jit(solution)/shard_map/ppermute | solution.py:442
  33.8 3.2 %collective-permute-start.10 = (f32[3,80,128]{2,1,0:T(8,128)S(1)}, f32[3,80,128]{2,1,0:T(8,128)S(1)}, u32[]{:S(2)}, u32[]{:S(2)}) collective-permute-start(f32[3,80,128]{2,1,0:T(8,128)S(1)} %pad_maximum_fusion.3), channel_id=1, source_target_pairs={{0,1},{1,0},{2,3},{3,2},{4,5},{5,4},{6,7},{7,6},{8,9},{9,8},{10,11... | collective-permute-start | bytes 368648 | tf_op jit(solution)/shard_map/ppermute | solution.py:442
  38.3 1.5 %collective-permute-start.11 = (f32[4,80,128]{2,1,0:T(8,128)S(1)}, f32[4,80,128]{2,1,0:T(8,128)S(1)}, u32[]{:S(2)}, u32[]{:S(2)}) collective-permute-start(f32[4,80,128]{2,1,0:T(8,128)S(1)} %get-tuple-element.66), channel_id=1, source_target_pairs={{0,1},{1,0},{2,3},{3,2},{4,5},{5,4},{6,7},{7,6},{8,9},{9,8},{10,11... | collective-permute-start | bytes 491528 | tf_op jit(solution)/shard_map/ppermute | solution.py:442
  39.9 9.3 %collective-permute-start.12 = (f32[4,80,128]{2,1,0:T(8,128)S(1)}, f32[4,80,128]{2,1,0:T(8,128)S(1)}, u32[]{:S(2)}, u32[]{:S(2)}) collective-permute-start(f32[4,80,128]{2,1,0:T(8,128)S(1)} %pad_maximum_fusion.1), channel_id=1, source_target_pairs={{0,2},{1,127},{2,4},{3,1},{4,6},{5,3},{6,8},{7,5},{8,10},{9,7},{10... | collective-permute-start | bytes 491528 | tf_op jit(solution)/shard_map/ppermute | solution.py:452
  43.5 5.6 %collective-permute-start.13 = (f32[3,80,128]{2,1,0:T(8,128)S(1)}, f32[3,80,128]{2,1,0:T(8,128)S(1)}, u32[]{:S(2)}, u32[]{:S(2)}) collective-permute-start(f32[3,80,128]{2,1,0:T(8,128)S(1)} %pad_maximum_fusion.4), channel_id=1, source_target_pairs={{0,4},{1,125},{2,6},{3,127},{4,8},{5,1},{6,10},{7,3},{8,12},{9,5},... | collective-permute-start | bytes 368648 | tf_op jit(solution)/shard_map/ppermute | solution.py:452
  46.1 6.4 %collective-permute-start.14 = (f32[1,80,128]{2,1,0:T(8,128)S(1)}, f32[1,80,128]{2,1,0:T(8,128)S(1)}, u32[]{:S(2)}, u32[]{:S(2)}) collective-permute-start(f32[1,80,128]{2,1,0:T(8,128)S(1)} %get-tuple-element.73), channel_id=1, source_target_pairs={{0,1},{1,0},{2,3},{3,2},{4,5},{5,4},{6,7},{7,6},{8,9},{9,8},{10,11... | collective-permute-start | bytes 122888 | tf_op jit(solution)/shard_map/ppermute | solution.py:442
  49.2 4.4 %collective-permute-start.15 = (f32[3,80,128]{2,1,0:T(8,128)S(1)}, f32[3,80,128]{2,1,0:T(8,128)S(1)}, u32[]{:S(2)}, u32[]{:S(2)}) collective-permute-start(f32[3,80,128]{2,1,0:T(8,128)S(1)} %pad_maximum_fusion.5), channel_id=1, source_target_pairs={{0,1},{1,0},{2,3},{3,2},{4,5},{5,4},{6,7},{7,6},{8,9},{9,8},{10,11... | collective-permute-start | bytes 368648 | tf_op jit(solution)/shard_map/ppermute | solution.py:442
